TPU v7x, 128 devices: a whole 4x4x4 slice. The times are simulated.
128 devices in a mesh: gx: 16 (over x, y), gy: 8 (over z, core).
Axes of the slice: x: 4, y: 4, z: 4, core: 2. Of those that a mesh axis runs over, the one named last changes fastest.
Arguments:
- estimate: float32 [64, 1024, 2048], P(None, 'gx', 'gy'), may hold values from 0.1 to 8
- measured: float32 [64, 1024, 2048], P('gy', None, 'gx'), may hold values from 0.1 to 14
- z_interp: float32 [64, 64], replicated, may hold values from 0 to 0.95, as said below
- r_interp: float32 [1024, 1024], replicated, may hold values from 0 to 0.95, as said below
- psf_z: float32 [32], replicated, may hold values from 0.004 to 0.25
- psf_r: float32 [32], replicated, may hold values from 0.004 to 0.25
- psf_u: float32 [32], replicated, may hold values from 0.004 to 0.25
Outputs:
- updated: float32 [64, 1024, 2048], P(None, 'gx', 'gy')
Inputs may be any that keep to these rules, and one draw needn't show every extreme that they name: `z_interp`: nonzero only at [i, i], equal to 1 - o_i, and at [i, i + 1], equal to o_i (where i + 1 < 64), with every o_i between 0.05 and 0.95. `r_interp`: nonzero only at [i, i], equal to 1 - o_i, and at [i, i + 1], equal to o_i (where i + 1 < 1024), with every o_i between 0.05 and 0.95.
All inputs are finite; a program needn't handle non-finite values.
Results may differ from a plain program's by a relative error of at most 0.00005.
Values sent between devices are 32-bit elements; how exact they have to be, the bound alone decides.
No kernel may reach another device: no remote copies, remote signals or barrier semaphores. Data moves between devices by JAX's collectives and lax.ppermute only.
A program may use at most 128 MiB of HBM per device.

v0:
```python
import jax
import jax.numpy as jnp
from jax import lax
from jax.sharding import PartitionSpec as P

background = 0.25
HIGH = lax.Precision.HIGHEST


def with_halo(cells, sides, width):
    for axis, dim in sides:
        count = lax.axis_size(axis)
        ends = count - 1
        head = lax.slice_in_dim(cells, 0, width, axis=dim)
        tail = lax.slice_in_dim(cells, cells.shape[dim] - width, cells.shape[dim], axis=dim)
        cells = jnp.concatenate(
            [
                lax.ppermute(tail, axis, [(i, (i + 1) % count) for i in range(ends)]),
                cells,
                lax.ppermute(head, axis, [((i + 1) % count, i) for i in range(ends)]),
            ],
            axis=dim,
        )
    return cells


def toeplitz(kernel, height, breadth, offset):
    distance = (
        lax.broadcasted_iota(jnp.int32, (height, breadth), 1)
        - lax.broadcasted_iota(jnp.int32, (height, breadth), 0)
        + offset
    )
    picks = (
        distance[:, :, None] == lax.broadcasted_iota(jnp.int32, (1, 1, kernel.shape[0]), 2)
    ).astype(jnp.float32)
    return jnp.einsum("abk,k->ab", picks, kernel, precision=HIGH)


def choose_block(count):
    for candidate in (128, 64, 32):
        return candidate
    return count


def windows(vector, block, blocks):
    stacked = vector[: (blocks + 1) * block].reshape(blocks + 1, block)
    return jnp.concatenate([stacked[:blocks], stacked[1:, :32]], axis=1)


def row_tables(kernel, main_diag, upper_diag, count, block, forward):
    blocks = count // block
    if forward:
        leading = toeplitz(kernel, block, block + 32, 0)
        shifted = toeplitz(kernel, block, block + 32, -1)
        near_diag = lax.slice_in_dim(
            jnp.pad(main_diag, (16, block + 32)), 0, count + block + 32, axis=0
        )
        near_upper = lax.slice_in_dim(
            jnp.pad(upper_diag, (16, block + 32)), 0, count + block + 32, axis=0
        )
        near_diag = windows(near_diag, block, blocks)
        near_upper = windows(near_upper, block, blocks)
        return leading[None] * near_diag[:, None, :] + shifted[None] * near_upper[:, None, :]
    reverse = kernel[::-1]
    leading = toeplitz(reverse, block, block + 32, -1)
    shifted = toeplitz(reverse, block, block + 32, 0)
    own_diag = main_diag.reshape(blocks, block)
    own_upper = lax.slice_in_dim(upper_diag, 0, count, axis=0).reshape(blocks, block)
    return leading[None] * own_diag[:, :, None] + shifted[None] * own_upper[:, :, None]


def apply_rows(field, tables):
    blocks = tables.shape[0]
    block = tables.shape[1]
    count = blocks * block
    depth = field.shape[0]
    width = field.shape[2]
    leading = field[:, :count].reshape(depth, blocks, block, width)
    middle = field[:, block:count].reshape(depth, blocks - 1, block, width)[:, :, :32]
    closing = field[:, count : count + 32][:, None]
    trailing = jnp.concatenate([middle, closing], axis=1)
    result = jnp.einsum("bsw,ybwc->ybsc", tables[:, :, :block], leading, precision=HIGH)
    result = result + jnp.einsum("bsw,ybwc->ybsc", tables[:, :, block:], trailing, precision=HIGH)
    return result.reshape(depth, count, width)


def apply_columns(field, table):
    return jnp.einsum("abw,sw->abs", field, table, precision=HIGH)


def shards(estimate, measured, z_interp, r_interp, psf_z, psf_r, psf_u):
    depth = estimate.shape[0]
    mix_z = jnp.dot(toeplitz(psf_z, depth, depth, 16), z_interp, precision=HIGH)
    main_diag = jnp.diagonal(r_interp)
    upper_diag = jnp.pad(jnp.diagonal(r_interp, 1), (1, 0))
    mixed = jnp.einsum("yz,zrc->yrc", mix_z, estimate, precision=HIGH)
    total_rows = r_interp.shape[0]
    slab = measured.shape[2]
    row_block = choose_block(total_rows)
    rows_out = row_tables(psf_r, main_diag, upper_diag, total_rows, row_block, True)
    rows_back = row_tables(psf_r, main_diag, upper_diag, total_rows, row_block, False)
    slab_block = choose_block(slab)
    planes = lax.all_to_all(mixed, "gy", split_axis=0, concat_axis=2, tiled=True)
    arrived = lax.all_to_all(planes, "gx", split_axis=2, concat_axis=1, tiled=True)
    view = apply_rows(jnp.pad(arrived, ((0, 0), (16, 16), (0, 0))), rows_out)
    padded = with_halo(view, (("gx", 2),), 16)
    blurred = apply_columns(padded, toeplitz(psf_u, slab_block, slab_block + 32, 0))
    ratio = measured / (blurred + background)
    margin = with_halo(ratio, (("gx", 2),), 16)
    spread = apply_columns(margin, toeplitz(psf_u[::-1], slab_block, slab_block + 32, -1))
    spread = apply_rows(jnp.pad(spread, ((0, 0), (16, 16), (0, 0))), rows_back)
    owned = lax.all_to_all(
        lax.all_to_all(spread, "gx", split_axis=1, concat_axis=2, tiled=True),
        "gy",
        split_axis=2,
        concat_axis=0,
        tiled=True,
    )
    back = jnp.einsum("yz,yrc->zrc", mix_z, owned, precision=HIGH)
    return estimate * back


def solution(mesh):
    in_specs = (P(None, "gx", "gy"), P("gy", None, "gx"), P(), P(), P(), P(), P())
    out_specs = P(None, "gx", "gy")
    return jax.shard_map(shards, mesh=mesh, in_specs=in_specs, out_specs=out_specs, check_vma=False)
```

profile of v0, /device:TPU:1, one launch (start us, length us, event | category | flops | bytes accessed | tf_op | source)
XLA Modules:
  0.0 456.0 jit_solution(6425849735286490592)
XLA Ops:
  3.7 8.4 %fusion.18 = f32[64,64,256]{2,0,1:T(8,128)S(1)} fusion(f32[64,64,1]{1,0,2:T(8,128)S(1)} %convolution_bitcast_fusion, f32[64,64,256]{2,1,0:T(8,128)} %param.7), kind=kOutput, calls=%fused_computation.27 | convolution fusion | flops 805306368 | bytes 8404992 | tf_op jit(solution)/shard_map/yz,zrc->yrc/dot_general | solution.py:96
  14.5 56.0 %all_to_all.72 = f32[64,64,256]{2,1,0:T(8,128)} all-to-all(f32[64,64,256]{2,1,0:T(8,128)S(1)} %copy.92), channel_id=1, replica_groups=mesh['gx'=16,'gy'=8] {'gy'}, dimensions={0} | all-to-all | bytes 8388608 | tf_op jit(solution)/shard_map/all_to_all | solution.py:103
  70.5 7.0 %copy.130 = f32[8,64,8,256]{1,0,3,2:T(8,128)} copy(f32[8,64,8,256]{3,1,0,2:T(8,128)} %bitcast.129) | data formatting | bytes 8388608 | tf_op jit(solution)/shard_map/all_to_all | solution.py:103
  77.5 13.3 %reshape.119 = f32[16,1,65536]{2,1,0:T(1,128)} reshape(f32[2048,8,64]{2,1,0:T(8,128)} %bitcast.125) | data formatting | bytes 8388608
  90.7 7.0 %all-to-all-start.1 = ((f32[16,1,65536]{2,1,0:T(1,128)}), f32[16,1,65536]{2,1,0:T(1,128)}, u32[]{:S(2)}, u32[]{:S(2)}) async-start(f32[16,1,65536]{2,1,0:T(1,128)} %reshape.119), calls=%async_computation.1 | async-start | bytes 8388608 | tf_op jit(solution)/shard_map/all_to_all | solution.py:104
  97.8 20.0 %gather_fusion.1 = f32[1023]{0:T(1024)S(1)} fusion(f32[1024,1024]{1,0:T(8,128)} %param.10, s32[1023]{0:T(1024)S(1)} %bitcast.119), kind=kCustom, calls=%fused_computation.1 | custom fusion | bytes 16368 | tf_op jit(solution)/shard_map/jit(diagonal)/gather | solution.py:95
  118.0 17.4 %gather_fusion = f32[1024]{0:T(1024)S(1)} fusion(f32[1024,1024]{1,0:T(8,128)} %param.10, s32[1024]{0:T(1024)S(1)} %bitcast.120), kind=kCustom, calls=%fused_computation | custom fusion | bytes 16384 | tf_op jit(solution)/shard_map/jit(diagonal)/cond/branch_0_fun/gather | solution.py:94
  137.7 14.3 %all-to-all-done.1 = f32[16,1,65536]{2,1,0:T(1,128)} async-done(((f32[16,1,65536]{2,1,0:T(1,128)}), f32[16,1,65536]{2,1,0:T(1,128)}, u32[]{:S(2)}, u32[]{:S(2)}) %all-to-all-start.1) | async-done | bytes 4194336 | tf_op jit(solution)/shard_map/all_to_all | solution.py:104
  152.5 13.7 %reduce = f32[16,65536]{1,0:T(8,128)} reduce(f32[16,1,65536]{2,1,0:T(1,128)} %all-to-all-done.1, f32[]{:T(128)} %broadcast.93), dimensions={1}, to_apply=%all_to_all.56.reduce_sub_computation | reduce | bytes 8388612 | tf_op jit(solution)/shard_map/all_to_all | solution.py:104
  166.3 6.9 %reshape.120 = f32[2048,8,64]{2,1,0:T(8,128)} reshape(f32[16,65536]{1,0:T(8,128)} %reduce) | data formatting | bytes 8388608
  173.2 7.0 %copy.96 = f32[8,16,64,128]{3,2,1,0:T(8,128)} copy(f32[8,16,64,128]{2,0,3,1:T(8,128)} %bitcast.126) | data formatting | bytes 8388608 | tf_op jit(solution)/shard_map/all_to_all | solution.py:104
  193.8 5.4 %copy.101 = f32[8,1024,128]{1,2,0:T(8,128)} copy(f32[8,1024,128]{2,1,0:T(8,128)} %bitcast.133) | data formatting | bytes 8388608 | tf_op jit(solution)/shard_map/reshape | solution.py:84
  203.1 5.8 %copy.104 = f32[8,1024,128]{1,2,0:T(8,128)} copy(f32[8,1024,128]{2,1,0:T(8,128)} %param.8) | data formatting | bytes 8388608 | tf_op args[1]
  210.5 7.1 %collective-permute-done.1 = f32[8,1024,16]{1,2,0:T(8,128)S(1)} collective-permute-done((f32[8,1024,16]{1,2,0:T(8,128)S(1)}, f32[8,1024,16]{1,2,0:T(8,128)S(1)}, u32[]{:S(2)}, u32[]{:S(2)}) %collective-permute-start.1) | collective-permute-done | bytes 524320 | tf_op jit(solution)/shard_map/ppermute | solution.py:20
  217.6 9.6 %add_divide_fusion = f32[8,1024,128]{1,2,0:T(8,128)S(1)} fusion(f32[8,1024,128]{1,2,0:T(8,128)} %copy.104, f32[128,160,1]{0,1,2:T(8,128)S(1)} %bitcast.143, f32[8,1024,16]{1,2,0:T(8,128)S(1)} %collective-permute-done.1, f32[8,1024,128]{1,2,0:T(8,128)} %copy.101, f32[8,1024,16]{1,2,0:T(8,128)S(1)} %collective-permute-done), kind=kOutput, calls=%fused_computation.21 | convolution fusion | flops 2017984512 | bytes 13713408 | tf_op jit(solution)/shard_map/abw,sw->abs/dot_general | solution.py:88
  244.0 15.4 %fusion.6 = f32[8,1024,128]{2,1,0:T(8,128)S(1)} fusion(f32[128,160,1]{0,1,2:T(8,128)S(1)} %bitcast.140, f32[8,1024,16]{1,2,0:T(8,128)S(1)} %collective-permute-done.3, f32[8,1024,128]{1,2,0:T(8,128)} %copy-done.4, f32[8,1024,16]{1,2,0:T(8,128)S(1)} %collective-permute-done.2), kind=kOutput, calls=%fused_computation.8 | convolution fusion | flops 2015887360 | bytes 9519104 | tf_op jit(solution)/shard_map/abw,sw->abs/dot_general | solution.py:88
  271.5 59.4 %all_to_all.73 = f32[8,1024,128]{2,0,1:T(8,128)} all-to-all(f32[8,1024,128]{2,0,1:T(8,128)S(1)} %copy.109), channel_id=1, replica_groups=mesh['gx'=16,'gy'=8] {'gx'}, dimensions={1} | all-to-all | bytes 8388608 | tf_op jit(solution)/shard_map/all_to_all | solution.py:113
  330.9 6.9 %copy.137 = f32[8,64,16,128]{1,0,3,2:T(8,128)} copy(f32[8,64,16,128]{3,0,1,2:T(8,128)} %bitcast.130) | data formatting | bytes 8388608 | tf_op jit(solution)/shard_map/all_to_all | solution.py:113
  337.8 9.8 %reshape.121 = f32[8,1,131072]{2,1,0:T(1,128)} reshape(f32[2048,8,64]{2,1,0:T(8,128)} %bitcast.127) | data formatting | bytes 8388608
  347.6 63.9 %all_to_all.74 = f32[8,1,131072]{2,1,0:T(1,128)} all-to-all(f32[8,1,131072]{2,1,0:T(1,128)} %reshape.121), channel_id=1, replica_groups=mesh['gx'=16,'gy'=8] {'gy'}, dimensions={0} | all-to-all | bytes 8388608 | tf_op jit(solution)/shard_map/all_to_all | solution.py:112
  411.5 13.7 %reduce.1 = f32[8,131072]{1,0:T(8,128)} reduce(f32[8,1,131072]{2,1,0:T(1,128)} %all_to_all.74, f32[]{:T(128)} %broadcast.93), dimensions={1}, to_apply=%all_to_all.64.reduce_sub_computation | reduce | bytes 8388612 | tf_op jit(solution)/shard_map/all_to_all | solution.py:112
  425.2 8.7 %reshape.122 = f32[2048,8,64]{2,1,0:T(8,128)} reshape(f32[8,131072]{1,0:T(8,128)} %reduce.1) | data formatting | bytes 8388608
  433.9 7.8 %copy.113 = f32[8,8,64,256]{3,1,0,2:T(8,128)} copy(f32[8,8,64,256]{2,1,3,0:T(8,128)} %bitcast.128) | data formatting | bytes 8388608 | tf_op jit(solution)/shard_map/all_to_all | solution.py:112
  441.8 9.2 %copy_multiply_fusion = f32[64,64,256]{2,0,1:T(8,128)S(1)} fusion(f32[64,64,256]{2,1,0:T(8,128)} %param.7, f32[64,64,1]{1,0,2:T(8,128)S(1)} %convolution_bitcast_fusion, f32[8,8,64,256]{3,1,0,2:T(8,128)} %copy.113), kind=kOutput, calls=%fused_computation.29 | convolution fusion | flops 806354944 | bytes 12599296 | tf_op jit(solution)/shard_map/yz,yrc->zrc/dot_general | solution.py:119
  (69 shorter events, 61.5 us)
Async XLA Ops:
  0.0 3.5 copy-start
  90.7 61.3 %all-to-all-start.1 = ((f32[16,1,65536]{2,1,0:T(1,128)}), f32[16,1,65536]{2,1,0:T(1,128)}, u32[]{:S(2)}, u32[]{:S(2)}) async-start(f32[16,1,65536]{2,1,0:T(1,128)} %reshape.119), calls=%async_computation.1 | async-start | bytes 8388608 | tf_op jit(solution)/shard_map/all_to_all | solution.py:104
  97.8 37.6 %copy-start.5 = (f32[32]{0:T(128)S(1)}, f32[32]{0:T(128)}, u32[]{:S(2)}) copy-start(f32[32]{0:T(128)} %param.12) | copy-start | bytes 388
  180.2 3.4 copy-start.3
  200.4 10.1 %collective-permute-start = (f32[8,1024,16]{1,2,0:T(8,128)S(1)}, f32[8,1024,16]{1,2,0:T(8,128)S(1)}, u32[]{:S(2)}, u32[]{:S(2)}) collective-permute-start(f32[8,1024,16]{1,2,0:T(8,128)S(1)} %get-tuple-element.7), channel_id=1, source_target_pairs={{0,8},{8,16},{16,24},{24,32},{32,40},{40,48},{48,56},{56,64},{64,7... | collective-permute-start | bytes 1572872 | tf_op jit(solution)/shard_map/ppermute | solution.py:18
  201.7 15.9 %collective-permute-start.1 = (f32[8,1024,16]{1,2,0:T(8,128)S(1)}, f32[8,1024,16]{1,2,0:T(8,128)S(1)}, u32[]{:S(2)}, u32[]{:S(2)}) collective-permute-start(f32[8,1024,16]{1,2,0:T(8,128)S(1)} %get-tuple-element.8), channel_id=1, source_target_pairs={{8,0},{16,8},{24,16},{32,24},{40,32},{48,40},{56,48},{64,56},{72,6... | collective-permute-start | bytes 1572872 | tf_op jit(solution)/shard_map/ppermute | solution.py:20
  203.1 5.8 %copy-start.6 = (f32[32]{0:T(128)S(1)}, f32[32]{0:T(128)}, u32[]{:S(2)}) copy-start(f32[32]{0:T(128)} %param.13) | copy-start | bytes 388
  227.2 2.0 copy-start.4
  229.3 10.8 %collective-permute-start.2 = (f32[8,1024,16]{1,2,0:T(8,128)S(1)}, f32[8,1024,16]{1,2,0:T(8,128)S(1)}, u32[]{:S(2)}, u32[]{:S(2)}) collective-permute-start(f32[8,1024,16]{1,2,0:T(8,128)S(1)} %get-tuple-element.5), channel_id=1, source_target_pairs={{0,8},{8,16},{16,24},{24,32},{32,40},{40,48},{48,56},{56,64},{64,7... | collective-permute-start | bytes 1572872 | tf_op jit(solution)/shard_map/ppermute | solution.py:18
  232.4 11.6 %collective-permute-start.3 = (f32[8,1024,16]{1,2,0:T(8,128)S(1)}, f32[8,1024,16]{1,2,0:T(8,128)S(1)}, u32[]{:S(2)}, u32[]{:S(2)}) collective-permute-start(f32[8,1024,16]{1,2,0:T(8,128)S(1)} %get-tuple-element.6), channel_id=1, source_target_pairs={{8,0},{16,8},{24,16},{32,24},{40,32},{48,40},{56,48},{64,56},{72,6... | collective-permute-start | bytes 1572872 | tf_op jit(solution)/shard_map/ppermute | solution.py:20
  259.4 2.0 copy-start.2
  261.4 3.9 slice-start
  441.8 13.7 %copy-start.1 = (f32[64,64]{1,0:T(8,128)S(1)}, f32[64,64]{1,0:T(8,128)}, u32[]{:S(2)}) copy-start(f32[64,64]{1,0:T(8,128)} %param.9) | copy-start | bytes 49156
where the time goes:
time: 464 us; the launch traced here: 456 us
  blocking collectives  179 us (39%)
  local copies, waits for them, and re-layouts  138 us (30%)
  matrix products  65.8 us (14%)
  waiting for transfers between devices  29.5 us (6%)
  other arithmetic  28 us (6%)
  starting transfers between devices  14.1 us (3%)
    all_to_all x1, blocking collectives, shards(): lax.all_to_all(lax.all_to_all(spread, 'gx', split_axis=1, concat_axis=2,...  63.9 us
    all_to_all x1, blocking collectives, shards(): lax.all_to_all(spread, 'gx', split_axis=1, concat_axis=2, tiled=True)  59.4 us
    all_to_all x1, blocking collectives, shards(): lax.all_to_all(mixed, 'gy', split_axis=0, concat_axis=2, tiled=True)  56 us
    unnamed x19, local copies, waits for them, and re-layouts  49 us
    dot_general x2, matrix products, apply_columns(): return jnp.einsum('abw,sw->abs', field, table, precision=HIGH)  25 us
    gather x1, local copies, waits for them, and re-layouts, shards(): upper_diag = jnp.pad(jnp.diagonal(r_interp, 1), (1, 0))  20 us
    gather x1, local copies, waits for them, and re-layouts, shards(): main_diag = jnp.diagonal(r_interp)  17.4 us
    all_to_all x1, waiting for transfers between devices, shards(): lax.all_to_all(planes, 'gx', split_axis=2, concat_axis=1, tiled=True)  14.3 us
  transfers between devices with their start and end apart: 5, of which 4 were waited for; matrix products, arithmetic and copies ran while one was open for 11% of the time, Pallas kernels for 0%

commit v1 on v0

v1 whole, which is shorter than its diff:
```python
import functools

import jax
import jax.numpy as jnp
from jax import lax
from jax.experimental import pallas as pl
from jax.experimental.pallas import tpu as pltpu
from jax.sharding import PartitionSpec as P

background = 0.25
HIGH = lax.Precision.HIGHEST
F32 = jnp.float32
BF = jnp.bfloat16
AXES = ("gx", "gy")
MIB = 1024 * 1024


def split(x):
    hi = x.astype(BF)
    return hi, (x - hi.astype(F32)).astype(BF)


def split_table(x):
    hi = lax.reduce_precision(x, 8, 7)
    return hi.astype(BF), (x - hi).astype(BF)


def dot(a, b):
    return jnp.dot(a, b, preferred_element_type=F32)


def dot3(ah, al, bh, bl):
    return dot(ah, bh) + dot(ah, bl) + dot(al, bh)


def taps(kernel, distance):
    total = jnp.zeros(distance.shape, F32)
    for k in range(kernel.shape[0]):
        total = total + jnp.where(distance == k, kernel[k], 0.0)
    return total


def grid_of(rows, cols):
    i = lax.broadcasted_iota(jnp.int32, (rows, cols), 0)
    j = lax.broadcasted_iota(jnp.int32, (rows, cols), 1)
    return i, j


def shift_perm(axis_of, d):
    if axis_of == "gx":
        return [(i * 8 + j, (i + d) * 8 + j) for i in range(16) for j in range(8) if 0 <= i + d < 16]
    return [(i * 8 + j, i * 8 + j + d) for i in range(16) for j in range(8) if 0 <= j + d < 8]


def position(x, y, z, c):
    return ((x % 4) * 4 + y % 4) * 8 + (z % 4) * 2 + c % 2


def piece_perm(k):
    k1, k2 = k // 4, k % 4
    pairs = []
    for x in range(4):
        for y in range(4):
            for z in range(4):
                for c in range(2):
                    pairs.append((position(x, y, z, c), position(x + z + 2 * c + k1, y + 2 * c + k2, x, y // 2)))
    return pairs


def row_kernel(ah_ref, al_ref, up_ref, own_ref, down_ref, out_ref):
    ah, al = ah_ref[...], al_ref[...]
    wide = jnp.concatenate([ah, ah], axis=1)
    for z in range(out_ref.shape[0]):
        x = jnp.concatenate([up_ref[z], own_ref[z], down_ref[z]], axis=0)
        xh, xl = split(x)
        out_ref[z] = dot(wide, jnp.concatenate([xh, xl], axis=0)) + dot(al, xh)


def row_mix(table, up, own, down):
    ah, al = split_table(table)
    depth, rows, cols = own.shape
    step = 8
    block = lambda r: pl.BlockSpec((step, r, cols), lambda i: (i, 0, 0))
    whole = pl.BlockSpec(ah.shape, lambda i: (0, 0))
    return pl.pallas_call(
        row_kernel,
        grid=(depth // step,),
        in_specs=[whole, whole, block(16), block(rows), block(16)],
        out_specs=block(rows),
        out_shape=jax.ShapeDtypeStruct(own.shape, F32),
        compiler_params=pltpu.CompilerParams(vmem_limit_bytes=32 * MIB),
    )(ah, al, up, own, down)


def column_part(x, left, right, u, ul, ur):
    rows, depth = x.shape[1], x.shape[0]
    xh, xl = split(x.reshape(depth * rows, x.shape[2]))
    total = dot3(xh, xl, u[0], u[1])
    for edge, table in ((left, ul), (right, ur)):
        eh, el = split(edge.reshape(depth * rows, 16))
        total = total + dot3(eh, el, table[0], table[1])
    return total


def column_depth_kernel(uh_ref, ul_ref, eh_ref, el_ref, kh_ref, kl_ref, left_ref, right_ref, x_ref, out_ref):
    u = (uh_ref[...], ul_ref[...])
    lt = (eh_ref[:16], el_ref[:16])
    rt = (eh_ref[16:], el_ref[16:])
    y = column_part(x_ref[...], left_ref[...], right_ref[...], u, lt, rt)
    yh, yl = split(y)
    out_ref[...] = dot3(kh_ref[...], kl_ref[...], yh, yl).reshape(out_ref.shape)


def column_kernel(uh_ref, ul_ref, eh_ref, el_ref, left_ref, right_ref, x_ref, out_ref):
    u = (uh_ref[...], ul_ref[...])
    lt = (eh_ref[:16], el_ref[:16])
    rt = (eh_ref[16:], el_ref[16:])
    out_ref[...] = column_part(x_ref[...], left_ref[...], right_ref[...], u, lt, rt).reshape(out_ref.shape)


def column_mix(main, edges, depth_table, left, right, x):
    depth, rows, cols = x.shape
    tables = [*split_table(main), *split_table(edges)]
    body = column_kernel
    if depth_table is not None:
        tables += [*split_table(depth_table)]
        body = column_depth_kernel
    block = lambda c: pl.BlockSpec((depth, 8, c), lambda i: (0, i, 0))
    whole = lambda t: pl.BlockSpec(t.shape, lambda i: (0, 0))
    return pl.pallas_call(
        body,
        grid=(rows // 8,),
        in_specs=[whole(t) for t in tables] + [block(16), block(16), block(cols)],
        out_specs=block(cols),
        out_shape=jax.ShapeDtypeStruct(x.shape, F32),
        compiler_params=pltpu.CompilerParams(vmem_limit_bytes=32 * MIB),
    )(*tables, left, right, x)


def ratio_kernel(place_ref, blur_ref, *refs):
    pieces, out_ref = refs[:-1], refs[-1]
    for k, piece in enumerate(pieces):
        planes = pl.ds(pl.multiple_of(place_ref[k, 0] * 8, 8), 8)
        cols = pl.ds(pl.multiple_of(place_ref[k, 1] * 128, 128), 128)
        out_ref[planes, :, cols] = piece[...] / (blur_ref[planes, :, cols] + background)


def ratio_of(place, blurred, pieces):
    vmem = pl.BlockSpec(memory_space=pltpu.VMEM)
    return pl.pallas_call(
        ratio_kernel,
        in_specs=[pl.BlockSpec(memory_space=pltpu.SMEM), vmem] + [vmem] * len(pieces),
        out_specs=vmem,
        out_shape=jax.ShapeDtypeStruct(blurred.shape, F32),
        compiler_params=pltpu.CompilerParams(vmem_limit_bytes=48 * MIB),
    )(place, blurred, *pieces)


def depth_update_kernel(kh_ref, kl_ref, est_ref, x_ref, out_ref):
    xh, xl = split(x_ref[...].reshape(-1, x_ref.shape[2]))
    back = dot3(kh_ref[...], kl_ref[...], xh, xl)
    out_ref[...] = est_ref[...] * back.reshape(out_ref.shape)


def depth_update(table, est, x):
    depth, rows, cols = x.shape
    kh, kl = split_table(table)
    block = pl.BlockSpec((depth, 8, cols), lambda i: (0, i, 0))
    whole = pl.BlockSpec(kh.shape, lambda i: (0, 0))
    return pl.pallas_call(
        depth_update_kernel,
        grid=(rows // 8,),
        in_specs=[whole, whole, block, block],
        out_specs=block,
        out_shape=jax.ShapeDtypeStruct(x.shape, F32),
        compiler_params=pltpu.CompilerParams(vmem_limit_bytes=32 * MIB),
    )(kh, kl, est, x)


def column_edges(x):
    width = x.shape[2]
    send = lambda part, d: jnp.transpose(
        lax.ppermute(jnp.transpose(part, (0, 2, 1)), AXES, shift_perm("gy", d)), (0, 2, 1)
    )
    return send(x[:, :, width - 16 :], 1), send(x[:, :, :16], -1)


def row_edges(x):
    rows = x.shape[1]
    return (
        lax.ppermute(x[:, rows - 16 :], AXES, shift_perm("gx", 1)),
        lax.ppermute(x[:, :16], AXES, shift_perm("gx", -1)),
    )


def shards(estimate, measured, z_interp, r_interp, psf_z, psf_r, psf_u):
    depth, rows, width = estimate.shape
    gx, gy = lax.axis_index("gx"), lax.axis_index("gy")
    x, y, z, c = gx // 4, gx % 4, gy // 2, gy % 2

    up, down = row_edges(estimate)
    pieces, place = [], []
    for k in range(16):
        k1, k2 = k // 4, k % 4
        target = ((x + z + 2 * c + k1) % 4) * 4 + (y + 2 * c + k2) % 4
        part = lax.dynamic_slice(measured, (0, target * rows, 0), (8, rows, 128))
        pieces.append(lax.ppermute(part, AXES, piece_perm(k)))
        q = (y - 2 * c - k2) % 4
        half, core = q % 2, q // 2
        place.append(jnp.stack([((x - z - 2 * core - k1) % 4) * 2 + core, half]))
    place = jnp.stack(place).astype(jnp.int32)

    i, j = grid_of(depth, depth)
    mix_z = jnp.dot(taps(psf_z, j - i + 16), z_interp, precision=HIGH)
    eye = jnp.eye(8, dtype=F32)
    total = r_interp.shape[0]
    first = jnp.clip(gx * rows - 64, 0, total - 192)
    band = lax.dynamic_slice(r_interp, (first, 0), (192, total))
    i, j = grid_of(192, total)
    i = i + first
    main = jnp.sum(jnp.where(i == j, band, 0.0), axis=0)
    upper = jnp.sum(jnp.where(i + 1 == j, band, 0.0), axis=0)
    window = lambda v: lax.dynamic_slice(jnp.pad(v, (16, 16)), (gx * rows,), (rows + 32,))
    main, upper = window(main), window(upper)
    i, j = grid_of(rows, rows + 32)
    rows_out = taps(psf_r, j - i) * main[None] + taps(psf_r, j - 1 - i) * upper[None]
    rows_back = taps(psf_r, i - j + 32) * main[16 : 16 + rows, None]
    rows_back = rows_back + taps(psf_r, i - j + 31) * upper[16 : 16 + rows, None]
    i, j = grid_of(width + 32, width)
    out_u = taps(psf_u, i - j)
    back_u = taps(psf_u, j - i + 32)
    edges_of = lambda t: jnp.concatenate([t[:16], t[width + 16 :]], axis=0)

    mixed = row_mix(rows_out, up, estimate, down)
    left, right = column_edges(mixed)
    blurred = column_mix(out_u[16 : 16 + width], edges_of(out_u), jnp.kron(mix_z, eye), left, right, mixed)
    ratio = ratio_of(place, blurred, pieces)
    left, right = column_edges(ratio)
    spread = column_mix(back_u[16 : 16 + width], edges_of(back_u), None, left, right, ratio)
    up, down = row_edges(spread)
    spread = row_mix(rows_back, up, spread, down)
    return depth_update(jnp.kron(mix_z.T, eye), estimate, spread)


def solution(mesh):
    in_specs = (P(None, "gx", "gy"), P("gy", None, "gx"), P(), P(), P(), P(), P())
    out_specs = P(None, "gx", "gy")
    return jax.shard_map(shards, mesh=mesh, in_specs=in_specs, out_specs=out_specs, check_vma=False)
```

time: 464 us -> 343 us (0.74)
  the two profiles are of different devices: /device:TPU:1 before, /device:TPU:15 now
where the time goes in v1:
time: 343 us; the launch traced here: 340 us
  other arithmetic  97.3 us (28%)
  starting transfers between devices  86.1 us (25%)
  local copies, waits for them, and re-layouts  83.4 us (24%)
  Pallas kernels  42 us (12%)
  matrix products  20.1 us (6%)
  waiting for transfers between devices  9.27 us (3%)
    ppermute x16, starting transfers between devices, shards(): pieces.append(lax.ppermute(part, AXES, piece_perm(k)))  61 us
    convert_element_type x10, other arithmetic, split_table(): return (hi.astype(BF), (x - hi).astype(BF))  41.9 us
    add x2, other arithmetic, taps(): total = total + jnp.where(distance == k, kernel[k], 0.0)  40.2 us
    pallas_call x2, Pallas kernels, column_mix(): pl.pallas_call(body, grid=(rows // 8,), in_specs=[whole(t) for t in table...  24.6 us
    dot_general x1, matrix products, shards(): mix_z = jnp.dot(taps(psf_z, j - i + 16), z_interp, precision=HIGH)  20.1 us
    unnamed x90, local copies, waits for them, and re-layouts  18.9 us
    transpose x6, local copies, waits for them, and re-layouts, column_edges(): jnp.transpose(part, (0, 2, 1))  15.7 us
    ppermute x4, starting transfers between devices, column_edges(): lax.ppermute(jnp.transpose(part, (0, 2, 1)), AXES, shift_perm('gy', d))  14.6 us
  transfers between devices with their start and end apart: 24, of which 2 were waited for; matrix products, arithmetic and copies ran while one was open for 49% of the time, Pallas kernels for 6%

profile of v1, /device:TPU:15, one launch (start us, length us, event | category | flops | bytes accessed | tf_op | source)
XLA Modules:
  0.0 339.9 jit_solution(6561173661552511565)
XLA Ops:
  8.6 4.2 %constant_dynamic-slice_fusion = (f32[8,64,128]{2,1,0:T(8,128)}, f32[8,64,128]{2,1,0:T(8,128)}, f32[8,64,128]{2,1,0:T(8,128)}, f32[8,64,128]{2,1,0:T(8,128)}, f3...) fusion(f32[8,1024,128]{2,1,0:T(8,128)} %param.8, ...), kind=kLoop, calls=%fused_computation.403 | loop fusion | bytes 8388672 | tf_op jit(solution)/shard_map/dynamic_slice | solution.py:206
  12.9 9.4 %collective-permute-start.4 = (f32[8,64,128]{2,1,0:T(8,128)}, f32[8,64,128]{2,1,0:T(8,128)S(1)}, u32[]{:S(2)}, u32[]{:S(2)}) collective-permute-start(f32[8,64,128]{2,1,0:T(8,128)} %get-tuple-element.29), channel_id=1, source_target_pairs={{0,0},{1,80},{2,32},{3,112},{4,64},{5,16},{6,96},{7,48},{8,8},{9,8... | collective-permute-start | bytes 786440 | tf_op jit(solution)/shard_map/ppermute | solution.py:207
  29.2 20.1 %fusion.202 = f32[64,64]{1,0:T(8,128)S(1)} fusion(f32[64,64]{1,0:T(8,128)S(1)} %copy-done, f32[]{:T(128)} %bitcast.31, f32[]{:T(128)} %bitcast.30, f32[]{:T(128)} %bitcast.29, f32[]{:T(128)} %bitcast.28, f32[]{:T(128)} %bitcast.27, f32[]{:T(128)} %bitcast.26, f32[]{:T(128)} %bitcast.25, f32[]{:T(128)} %bitcast.24, f32[]{:T(128)} %bitcast.23, f32[]{:T(128)} %bitcast.22, ...), kind=kOutput, calls=%fused_computation.239 | convolution fusion | flops 3543040 | bytes 32896 | tf_op jit(solution)/shard_map/dot_general | solution.py:214
  49.5 20.1 %select_add_fusion = f32[288,256]{1,0:T(8,128)S(1)} fusion(f32[]{:T(128)} %bitcast.96, f32[]{:T(128)} %bitcast.95, f32[]{:T(128)} %bitcast.94, f32[]{:T(128)} %bitcast.93, f32[]{:T(128)} %bitcast.92, f32[]{:T(128)} %bitcast.91, f32[]{:T(128)} %bitcast.90, f32[]{:T(128)} %bitcast.89, f32[]{:T(128)} %bitcast.88, f32[]{:T(128)} %bitcast.87, f32[]{:T(128)} %bitcast.86, ...), kind=kLoop, calls=%fused_computation.20 | loop fusion | flops 7077888 | bytes 295040 | tf_op jit(solution)/shard_map/add | solution.py:39
  70.4 12.0 %broadcast_multiply_fusion = (f32[64,8,64,8]{3,2,1,0:T(8,128)}, f32[64,8,64,8]{3,2,1,0:T(8,128)}) fusion(f32[64,64]{1,0:T(8,128)S(1)} %fusion.202, f32[8,8]{1,0:T(8,128)S(1)} %fusion.396, f32[64,64]{1,0:T(8,128)S(1)} %copy.36), kind=kLoop, calls=%fused_computation | loop fusion | flops 524288 | bytes 2130176 | tf_op jit(solution)/shard_map/jit(kron)/mul | solution.py:236
  85.0 20.2 %select_add_fusion.1 = f32[288,256]{1,0:T(8,128)S(1)} fusion(f32[]{:T(128)} %bitcast.96, f32[]{:T(128)} %bitcast.95, f32[]{:T(128)} %bitcast.94, f32[]{:T(128)} %bitcast.93, f32[]{:T(128)} %bitcast.92, f32[]{:T(128)} %bitcast.91, f32[]{:T(128)} %bitcast.90, f32[]{:T(128)} %bitcast.89, f32[]{:T(128)} %bitcast.88, f32[]{:T(128)} %bitcast.87, f32[]{:T(128)} %bitcast.86, ...), kind=kLoop, calls=%fused_computation.54 | loop fusion | flops 7151616 | bytes 295040 | tf_op jit(solution)/shard_map/add | solution.py:39
  105.2 20.1 %fusion.71 = (bf16[64,96]{1,0:T(8,128)(2,1)S(1)}, f32[64,96]{1,0:T(8,128)S(1)}) fusion(f32[96]{0:T(128)S(1)} %get-tuple-element.165, s32[96]{0:T(128)S(1)} %iota_add_fusion.1, f32[96]{0:T(128)S(1)} %get-tuple-element.166, f32[]{:T(128)} %bitcast.64, f32[]{:T(128)} %bitcast.63, f32[]{:T(128)} %bitcast.62, f32[]{:T(128)} %bitcast.61, f32[]{:T(128)} %bitcast.60, ...), kind=kLoop, calls=%fused_computation.101 | loop fusion | flops 1216512 | bytes 38144 | tf_op jit(solution)/shard_map/convert_element_type | solution.py:25
  126.0 6.8 %collective-permute-start.7 = (f32[8,64,128]{2,1,0:T(8,128)}, f32[8,64,128]{2,1,0:T(8,128)S(1)}, u32[]{:S(2)}, u32[]{:S(2)}) collective-permute-start(f32[8,64,128]{2,1,0:T(8,128)} %get-tuple-element.26), channel_id=1, source_target_pairs={{0,24},{1,72},{2,56},{3,104},{4,88},{5,8},{6,120},{7,40},{8,0},{9,... | collective-permute-start | bytes 786440 | tf_op jit(solution)/shard_map/ppermute | solution.py:207
  139.7 4.4 %collective-permute-start.9 = (f32[8,64,128]{2,1,0:T(8,128)}, f32[8,64,128]{2,1,0:T(8,128)S(1)}, u32[]{:S(2)}, u32[]{:S(2)}) collective-permute-start(f32[8,64,128]{2,1,0:T(8,128)} %get-tuple-element.24), channel_id=1, source_target_pairs={{0,40},{1,120},{2,72},{3,24},{4,104},{5,56},{6,8},{7,88},{8,48},{9... | collective-permute-start | bytes 786440 | tf_op jit(solution)/shard_map/ppermute | solution.py:207
  154.1 6.2 %collective-permute-start.12 = (f32[8,64,128]{2,1,0:T(8,128)}, f32[8,64,128]{2,1,0:T(8,128)S(1)}, u32[]{:S(2)}, u32[]{:S(2)}) collective-permute-start(f32[8,64,128]{2,1,0:T(8,128)} %get-tuple-element.21), channel_id=1, source_target_pairs={{0,64},{1,16},{2,96},{3,48},{4,0},{5,80},{6,32},{7,112},{8,72},{9,... | collective-permute-start | bytes 786440 | tf_op jit(solution)/shard_map/ppermute | solution.py:207
  165.1 6.0 %collective-permute-start.2 = (f32[64,16,64]{2,1,0:T(8,128)}, f32[64,16,64]{2,1,0:T(8,128)}, u32[]{:S(2)}, u32[]{:S(2)}) collective-permute-start(f32[64,16,64]{2,1,0:T(8,128)} %copy.37), channel_id=1, source_target_pairs={{0,1},{1,2},{2,3},{3,4},{4,5},{5,6},{6,7},{8,9},{9,10},{10,11},{11... | collective-permute-start | bytes 786440 | tf_op jit(solution)/shard_map/ppermute | solution.py:183
  174.7 13.5 %mul.304 = f32[512,512]{1,0:T(8,128)} reshape(f32[64,8,64,8]{3,2,1,0:T(8,128)} %get-tuple-element.51) | data formatting | bytes 2097152 | tf_op jit(solution)/shard_map/jit(kron)/mul | solution.py:236
  189.1 4.5 %collective-permute-start.15 = (f32[8,64,128]{2,1,0:T(8,128)}, f32[8,64,128]{2,1,0:T(8,128)}, u32[]{:S(2)}, u32[]{:S(2)}) collective-permute-start(f32[8,64,128]{2,1,0:T(8,128)} %get-tuple-element.18), channel_id=1, source_target_pairs={{0,88},{1,8},{2,120},{3,40},{4,24},{5,72},{6,56},{7,104},{8,64},{9... | collective-permute-start | bytes 786440 | tf_op jit(solution)/shard_map/ppermute | solution.py:207
  198.0 5.3 %collective-permute-start.17 = (f32[8,64,128]{2,1,0:T(8,128)}, f32[8,64,128]{2,1,0:T(8,128)}, u32[]{:S(2)}, u32[]{:S(2)}) collective-permute-start(f32[8,64,128]{2,1,0:T(8,128)} %get-tuple-element.16), channel_id=1, source_target_pairs={{0,104},{1,56},{2,8},{3,88},{4,40},{5,120},{6,72},{7,24},{8,112},{... | collective-permute-start | bytes 786440 | tf_op jit(solution)/shard_map/ppermute | solution.py:207
  203.3 5.6 %collective-permute-start.18 = (f32[8,64,128]{2,1,0:T(8,128)}, f32[8,64,128]{2,1,0:T(8,128)}, u32[]{:S(2)}, u32[]{:S(2)}) collective-permute-start(f32[8,64,128]{2,1,0:T(8,128)} %get-tuple-element.30), channel_id=1, source_target_pairs={{0,112},{1,32},{2,16},{3,64},{4,48},{5,96},{6,80},{7,0},{8,120},{9... | collective-permute-start | bytes 786440 | tf_op jit(solution)/shard_map/ppermute | solution.py:207
  208.9 5.0 %collective-permute-start.19 = (f32[8,64,128]{2,1,0:T(8,128)}, f32[8,64,128]{2,1,0:T(8,128)}, u32[]{:S(2)}, u32[]{:S(2)}) collective-permute-start(f32[8,64,128]{2,1,0:T(8,128)} %get-tuple-element.15), channel_id=1, source_target_pairs={{0,120},{1,40},{2,24},{3,72},{4,56},{5,104},{6,88},{7,8},{8,96},{9... | collective-permute-start | bytes 786440 | tf_op jit(solution)/shard_map/ppermute | solution.py:207
  223.8 17.4 %shard_map.74.blur_ref = f32[64,64,256]{2,1,0:T(8,128)S(1)} custom-call(bf16[256,256]{1,0:T(8,128)(2,1)S(1)} %get-tuple-element.42.uh_ref, bf16[256,256]{1,0:T(8,128)(2,1)S(1)} %get-tuple-element.41.ul_ref, bf16[32,256]{1,0:T(8,128)(2,1)S(1)} %get-tuple-element.48.eh_ref, bf16[32,256]{1,0:T(8,128)(2,1)S(1)} %get-tuple-element.47.el_ref, ...), custom_call_target="tpu_custom_call" | custom-call | tf_op jit(solution)/shard_map/pallas_call | solution.py:130
  243.4 5.2 %shard_map.75.x_ref = f32[64,64,256]{2,1,0:T(8,128)} custom-call(s32[16,2]{1,0:T(8,128)S(1)} %stack.223.place_ref, f32[64,64,256]{2,1,0:T(8,128)} %copy-done.9, f32[8,64,128]{2,1,0:T(8,128)S(1)} %copy-done.13, f32[8,64,128]{2,1,0:T(8,128)S(1)} %copy-done.15, f32[8,64,128]{2,1,0:T(8,128)S(1)} %copy-done.17, f32[8,64,128]{2,1,0:T(8,128)S(1)} %copy-done.19, ...), custom_call_target="tpu_custom_call" | custom-call | tf_op jit(solution)/shard_map/pallas_call | solution.py:150
  248.6 4.2 %slice_bitcast_fusion = (f32[64,16,64]{1,2,0:T(8,128)S(1)}, f32[64,16,64]{1,2,0:T(8,128)}) fusion(f32[64,64,256]{2,1,0:T(8,128)} %shard_map.75.x_ref), kind=kLoop, calls=%fused_computation.2 | loop fusion | bytes 1048576 | tf_op jit(solution)/shard_map/transpose | solution.py:183
  264.8 7.8 %collective-permute-done.21 = f32[64,16,64]{2,1,0:T(8,128)} collective-permute-done((f32[64,16,64]{2,1,0:T(8,128)}, f32[64,16,64]{2,1,0:T(8,128)}, u32[]{:S(2)}, u32[]{:S(2)}) %collective-permute-start.21) | collective-permute-done | bytes 262176 | tf_op jit(solution)/shard_map/ppermute | solution.py:183
  279.3 7.2 %shard_map.76.own_ref = f32[64,64,256]{2,1,0:T(8,128)S(1)} custom-call(bf16[256,256]{1,0:T(8,128)(2,1)S(1)} %get-tuple-element.46.uh_ref, bf16[256,256]{1,0:T(8,128)(2,1)S(1)} %get-tuple-element.45.ul_ref, bf16[32,256]{1,0:T(8,128)(2,1)S(1)} %get-tuple-element.50.eh_ref, bf16[32,256]{1,0:T(8,128)(2,1)S(1)} %get-tuple-element.49.el_ref, ...), custom_call_target="tpu_custom_call" | custom-call | tf_op jit(solution)/shard_map/pallas_call | solution.py:130
  295.5 12.6 %mul.137 = f32[512,512]{1,0:T(8,128)S(1)} reshape(f32[64,8,64,8]{3,2,1,0:T(8,128)} %get-tuple-element.52) | data formatting | bytes 2097152 | tf_op jit(solution)/shard_map/jit(kron)/mul | solution.py:242
  308.1 20.1 %fusion.68 = (bf16[64,96]{1,0:T(8,128)(2,1)S(1)}, f32[64,96]{1,0:T(8,128)S(1)}) fusion(f32[64]{0:T(128)S(1)} %slice.529, f32[64]{0:T(128)S(1)} %slice.528, f32[]{:T(128)} %bitcast.64, f32[]{:T(128)} %bitcast.63, f32[]{:T(128)} %bitcast.62, f32[]{:T(128)} %bitcast.61, f32[]{:T(128)} %bitcast.60, f32[]{:T(128)} %bitcast.59, f32[]{:T(128)} %bitcast.58, ...), kind=kLoop, calls=%fused_computation.98 | loop fusion | flops 1222656 | bytes 37504 | tf_op jit(solution)/shard_map/convert_element_type | solution.py:25
  333.4 6.5 %shard_map.78 = f32[64,64,256]{2,1,0:T(8,128)} custom-call(bf16[512,512]{1,0:T(8,128)(2,1)S(1)} %get-tuple-element.38.kh_ref, bf16[512,512]{1,0:T(8,128)(2,1)S(1)} %get-tuple-element.37.kl_ref, f32[64,64,256]{2,1,0:T(8,128)S(1)} %copy-done.6, f32[64,64,256]{2,1,0:T(8,128)S(1)} %shard_map.77.x_ref), custom_call_target="tpu_custom_call" | custom-call | tf_op jit(solution)/shard_map/pallas_call | solution.py:170
  (175 shorter events, 93.9 us)
Async XLA Ops:
  3.0 122.9 %collective-permute-start = (f32[64,16,256]{2,1,0:T(8,128)}, f32[64,16,256]{2,1,0:T(8,128)S(1)}, u32[]{:S(2)}, u32[]{:S(2)}) collective-permute-start(f32[64,16,256]{2,1,0:T(8,128)} %get-tuple-element.34), channel_id=1, source_target_pairs={{0,8},{1,9},{2,10},{3,11},{4,12},{5,13},{6,14},{7,15},{8,16},{9,17... | collective-permute-start | bytes 3145736 | tf_op jit(solution)/shard_map/ppermute | solution.py:191
  6.2 126.5 %collective-permute-start.1 = (f32[64,16,256]{2,1,0:T(8,128)}, f32[64,16,256]{2,1,0:T(8,128)S(1)}, u32[]{:S(2)}, u32[]{:S(2)}) collective-permute-start(f32[64,16,256]{2,1,0:T(8,128)} %get-tuple-element.33), channel_id=1, source_target_pairs={{8,0},{9,1},{10,2},{11,3},{12,4},{13,5},{14,6},{15,7},{16,8},{17,9... | collective-permute-start | bytes 3145736 | tf_op jit(solution)/shard_map/ppermute | solution.py:192
  12.9 126.9 %collective-permute-start.4 = (f32[8,64,128]{2,1,0:T(8,128)}, f32[8,64,128]{2,1,0:T(8,128)S(1)}, u32[]{:S(2)}, u32[]{:S(2)}) collective-permute-start(f32[8,64,128]{2,1,0:T(8,128)} %get-tuple-element.29), channel_id=1, source_target_pairs={{0,0},{1,80},{2,32},{3,112},{4,64},{5,16},{6,96},{7,48},{8,8},{9,8... | collective-permute-start | bytes 786440 | tf_op jit(solution)/shard_map/ppermute | solution.py:207
  22.2 121.9 %collective-permute-start.5 = (f32[8,64,128]{2,1,0:T(8,128)}, f32[8,64,128]{2,1,0:T(8,128)S(1)}, u32[]{:S(2)}, u32[]{:S(2)}) collective-permute-start(f32[8,64,128]{2,1,0:T(8,128)} %get-tuple-element.28), channel_id=1, source_target_pairs={{0,8},{1,88},{2,40},{3,120},{4,72},{5,24},{6,104},{7,56},{8,16},{9... | collective-permute-start | bytes 786440 | tf_op jit(solution)/shard_map/ppermute | solution.py:207
  22.6 123.5 %collective-permute-start.6 = (f32[8,64,128]{2,1,0:T(8,128)}, f32[8,64,128]{2,1,0:T(8,128)S(1)}, u32[]{:S(2)}, u32[]{:S(2)}) collective-permute-start(f32[8,64,128]{2,1,0:T(8,128)} %get-tuple-element.27), channel_id=1, source_target_pairs={{0,16},{1,64},{2,48},{3,96},{4,80},{5,0},{6,112},{7,32},{8,24},{9,... | collective-permute-start | bytes 786440 | tf_op jit(solution)/shard_map/ppermute | solution.py:207
  126.0 28.1 %collective-permute-start.7 = (f32[8,64,128]{2,1,0:T(8,128)}, f32[8,64,128]{2,1,0:T(8,128)S(1)}, u32[]{:S(2)}, u32[]{:S(2)}) collective-permute-start(f32[8,64,128]{2,1,0:T(8,128)} %get-tuple-element.26), channel_id=1, source_target_pairs={{0,24},{1,72},{2,56},{3,104},{4,88},{5,8},{6,120},{7,40},{8,0},{9,... | collective-permute-start | bytes 786440 | tf_op jit(solution)/shard_map/ppermute | solution.py:207
  132.8 27.5 %collective-permute-start.8 = (f32[8,64,128]{2,1,0:T(8,128)}, f32[8,64,128]{2,1,0:T(8,128)S(1)}, u32[]{:S(2)}, u32[]{:S(2)}) collective-permute-start(f32[8,64,128]{2,1,0:T(8,128)} %get-tuple-element.25), channel_id=1, source_target_pairs={{0,32},{1,112},{2,64},{3,16},{4,96},{5,48},{6,0},{7,80},{8,40},{9,... | collective-permute-start | bytes 786440 | tf_op jit(solution)/shard_map/ppermute | solution.py:207
  139.7 22.7 %collective-permute-start.9 = (f32[8,64,128]{2,1,0:T(8,128)}, f32[8,64,128]{2,1,0:T(8,128)S(1)}, u32[]{:S(2)}, u32[]{:S(2)}) collective-permute-start(f32[8,64,128]{2,1,0:T(8,128)} %get-tuple-element.24), channel_id=1, source_target_pairs={{0,40},{1,120},{2,72},{3,24},{4,104},{5,56},{6,8},{7,88},{8,48},{9... | collective-permute-start | bytes 786440 | tf_op jit(solution)/shard_map/ppermute | solution.py:207
  144.2 20.9 %collective-permute-start.10 = (f32[8,64,128]{2,1,0:T(8,128)}, f32[8,64,128]{2,1,0:T(8,128)S(1)}, u32[]{:S(2)}, u32[]{:S(2)}) collective-permute-start(f32[8,64,128]{2,1,0:T(8,128)} %get-tuple-element.23), channel_id=1, source_target_pairs={{0,48},{1,96},{2,80},{3,0},{4,112},{5,32},{6,16},{7,64},{8,56},{9,... | collective-permute-start | bytes 786440 | tf_op jit(solution)/shard_map/ppermute | solution.py:207
  146.1 25.0 %collective-permute-start.11 = (f32[8,64,128]{2,1,0:T(8,128)}, f32[8,64,128]{2,1,0:T(8,128)S(1)}, u32[]{:S(2)}, u32[]{:S(2)}) collective-permute-start(f32[8,64,128]{2,1,0:T(8,128)} %get-tuple-element.22), channel_id=1, source_target_pairs={{0,56},{1,104},{2,88},{3,8},{4,120},{5,40},{6,24},{7,72},{8,32},{9... | collective-permute-start | bytes 786440 | tf_op jit(solution)/shard_map/ppermute | solution.py:207
  154.1 34.3 %collective-permute-start.12 = (f32[8,64,128]{2,1,0:T(8,128)}, f32[8,64,128]{2,1,0:T(8,128)S(1)}, u32[]{:S(2)}, u32[]{:S(2)}) collective-permute-start(f32[8,64,128]{2,1,0:T(8,128)} %get-tuple-element.21), channel_id=1, source_target_pairs={{0,64},{1,16},{2,96},{3,48},{4,0},{5,80},{6,32},{7,112},{8,72},{9,... | collective-permute-start | bytes 786440 | tf_op jit(solution)/shard_map/ppermute | solution.py:207
  160.3 33.3 %collective-permute-start.13 = (f32[8,64,128]{2,1,0:T(8,128)}, f32[8,64,128]{2,1,0:T(8,128)S(1)}, u32[]{:S(2)}, u32[]{:S(2)}) collective-permute-start(f32[8,64,128]{2,1,0:T(8,128)} %get-tuple-element.20), channel_id=1, source_target_pairs={{0,72},{1,24},{2,104},{3,56},{4,8},{5,88},{6,40},{7,120},{8,80},{9... | collective-permute-start | bytes 786440 | tf_op jit(solution)/shard_map/ppermute | solution.py:207
  162.5 34.8 %collective-permute-start.14 = (f32[8,64,128]{2,1,0:T(8,128)}, f32[8,64,128]{2,1,0:T(8,128)S(1)}, u32[]{:S(2)}, u32[]{:S(2)}) collective-permute-start(f32[8,64,128]{2,1,0:T(8,128)} %get-tuple-element.19), channel_id=1, source_target_pairs={{0,80},{1,0},{2,112},{3,32},{4,16},{5,64},{6,48},{7,96},{8,88},{9,... | collective-permute-start | bytes 786440 | tf_op jit(solution)/shard_map/ppermute | solution.py:207
  165.1 38.2 %collective-permute-start.2 = (f32[64,16,64]{2,1,0:T(8,128)}, f32[64,16,64]{2,1,0:T(8,128)}, u32[]{:S(2)}, u32[]{:S(2)}) collective-permute-start(f32[64,16,64]{2,1,0:T(8,128)} %copy.37), channel_id=1, source_target_pairs={{0,1},{1,2},{2,3},{3,4},{4,5},{5,6},{6,7},{8,9},{9,10},{10,11},{11... | collective-permute-start | bytes 786440 | tf_op jit(solution)/shard_map/ppermute | solution.py:183
  171.1 37.8 %collective-permute-start.3 = (f32[64,16,64]{2,1,0:T(8,128)S(1)}, f32[64,16,64]{2,1,0:T(8,128)}, u32[]{:S(2)}, u32[]{:S(2)}) collective-permute-start(f32[64,16,64]{2,1,0:T(8,128)S(1)} %copy.39), channel_id=1, source_target_pairs={{1,0},{2,1},{3,2},{4,3},{5,4},{6,5},{7,6},{9,8},{10,9},{11,10},{12... | collective-permute-start | bytes 786440 | tf_op jit(solution)/shard_map/ppermute | solution.py:183
  189.1 54.1 %collective-permute-start.15 = (f32[8,64,128]{2,1,0:T(8,128)}, f32[8,64,128]{2,1,0:T(8,128)}, u32[]{:S(2)}, u32[]{:S(2)}) collective-permute-start(f32[8,64,128]{2,1,0:T(8,128)} %get-tuple-element.18), channel_id=1, source_target_pairs={{0,88},{1,8},{2,120},{3,40},{4,24},{5,72},{6,56},{7,104},{8,64},{9... | collective-permute-start | bytes 786440 | tf_op jit(solution)/shard_map/ppermute | solution.py:207
  194.3 48.9 %collective-permute-start.16 = (f32[8,64,128]{2,1,0:T(8,128)}, f32[8,64,128]{2,1,0:T(8,128)}, u32[]{:S(2)}, u32[]{:S(2)}) collective-permute-start(f32[8,64,128]{2,1,0:T(8,128)} %get-tuple-element.17), channel_id=1, source_target_pairs={{0,96},{1,48},{2,0},{3,80},{4,32},{5,112},{6,64},{7,16},{8,104},{9... | collective-permute-start | bytes 786440 | tf_op jit(solution)/shard_map/ppermute | solution.py:207
  198.0 45.3 %collective-permute-start.17 = (f32[8,64,128]{2,1,0:T(8,128)}, f32[8,64,128]{2,1,0:T(8,128)}, u32[]{:S(2)}, u32[]{:S(2)}) collective-permute-start(f32[8,64,128]{2,1,0:T(8,128)} %get-tuple-element.16), channel_id=1, source_target_pairs={{0,104},{1,56},{2,8},{3,88},{4,40},{5,120},{6,72},{7,24},{8,112},{... | collective-permute-start | bytes 786440 | tf_op jit(solution)/shard_map/ppermute | solution.py:207
  203.3 40.0 %collective-permute-start.18 = (f32[8,64,128]{2,1,0:T(8,128)}, f32[8,64,128]{2,1,0:T(8,128)}, u32[]{:S(2)}, u32[]{:S(2)}) collective-permute-start(f32[8,64,128]{2,1,0:T(8,128)} %get-tuple-element.30), channel_id=1, source_target_pairs={{0,112},{1,32},{2,16},{3,64},{4,48},{5,96},{6,80},{7,0},{8,120},{9... | collective-permute-start | bytes 786440 | tf_op jit(solution)/shard_map/ppermute | solution.py:207
  208.9 34.4 %collective-permute-start.19 = (f32[8,64,128]{2,1,0:T(8,128)}, f32[8,64,128]{2,1,0:T(8,128)}, u32[]{:S(2)}, u32[]{:S(2)}) collective-permute-start(f32[8,64,128]{2,1,0:T(8,128)} %get-tuple-element.15), channel_id=1, source_target_pairs={{0,120},{1,40},{2,24},{3,72},{4,56},{5,104},{6,88},{7,8},{8,96},{9... | collective-permute-start | bytes 786440 | tf_op jit(solution)/shard_map/ppermute | solution.py:207
  255.1 8.0 %collective-permute-start.20 = (f32[64,16,64]{2,1,0:T(8,128)S(1)}, f32[64,16,64]{2,1,0:T(8,128)}, u32[]{:S(2)}, u32[]{:S(2)}) collective-permute-start(f32[64,16,64]{2,1,0:T(8,128)S(1)} %copy.41), channel_id=1, source_target_pairs={{0,1},{1,2},{2,3},{3,4},{4,5},{5,6},{6,7},{8,9},{9,10},{10,11},{11... | collective-permute-start | bytes 786440 | tf_op jit(solution)/shard_map/ppermute | solution.py:183
  258.4 14.2 %collective-permute-start.21 = (f32[64,16,64]{2,1,0:T(8,128)}, f32[64,16,64]{2,1,0:T(8,128)}, u32[]{:S(2)}, u32[]{:S(2)}) collective-permute-start(f32[64,16,64]{2,1,0:T(8,128)} %copy.43), channel_id=1, source_target_pairs={{1,0},{2,1},{3,2},{4,3},{5,4},{6,5},{7,6},{9,8},{10,9},{11,10},{12... | collective-permute-start | bytes 786440 | tf_op jit(solution)/shard_map/ppermute | solution.py:183
  290.0 38.3 %collective-permute-start.22 = (f32[64,16,256]{2,1,0:T(8,128)}, f32[64,16,256]{2,1,0:T(8,128)S(1)}, u32[]{:S(2)}, u32[]{:S(2)}) collective-permute-start(f32[64,16,256]{2,1,0:T(8,128)} %get-tuple-element.12), channel_id=1, source_target_pairs={{0,8},{1,9},{2,10},{3,11},{4,12},{5,13},{6,14},{7,15},{8,16},{9,17... | collective-permute-start | bytes 3145736 | tf_op jit(solution)/shard_map/ppermute | solution.py:191
  291.9 36.4 %collective-permute-start.23 = (f32[64,16,256]{2,1,0:T(8,128)}, f32[64,16,256]{2,1,0:T(8,128)S(1)}, u32[]{:S(2)}, u32[]{:S(2)}) collective-permute-start(f32[64,16,256]{2,1,0:T(8,128)} %get-tuple-element.11), channel_id=1, source_target_pairs={{8,0},{9,1},{10,2},{11,3},{12,4},{13,5},{14,6},{15,7},{16,8},{17,9... | collective-permute-start | bytes 3145736 | tf_op jit(solution)/shard_map/ppermute | solution.py:192
  (45 other events, 576.8 us)

commit v2 on v1

v2 whole, which is shorter than its diff:
```python
import functools

import jax
import jax.numpy as jnp
from jax import lax
from jax.experimental import pallas as pl
from jax.experimental.pallas import tpu as pltpu
from jax.sharding import PartitionSpec as P

background = 0.25
HIGH = lax.Precision.HIGHEST
F32 = jnp.float32
BF = jnp.bfloat16
AXES = ("gx", "gy")
MIB = 1024 * 1024


def split(x):
    hi = x.astype(BF)
    return hi, (x - hi.astype(F32)).astype(BF)


def dot(a, b):
    return jnp.dot(a, b, preferred_element_type=F32)


def dot3(ah, al, bh, bl):
    return dot(ah, bh) + dot(ah, bl) + dot(al, bh)


def shift_perm(axis_of, d):
    if axis_of == "gx":
        return [(i * 8 + j, (i + d) * 8 + j) for i in range(16) for j in range(8) if 0 <= i + d < 16]
    return [(i * 8 + j, i * 8 + j + d) for i in range(16) for j in range(8) if 0 <= j + d < 8]


def position(x, y, z, c):
    return ((x % 4) * 4 + y % 4) * 8 + (z % 4) * 2 + c % 2


def core_swap():
    return [(d, d ^ 1) for d in range(128)]


def target_of(x, y, z, c, k):
    k1, k2 = k // 2, k % 2
    side, half = y // 2, y % 2
    parity = c ^ (x & 1)
    return (x + z + 2 * c + k1) % 4, 2 * (half ^ k2 ^ side) + parity


def source_of(x, y, z, c, k):
    k1, k2 = k // 2, k % 2
    core = (y & 1) ^ (z & 1)
    return (x - z - 2 * core - k1) % 4, core, (y // 2) ^ k2 ^ c


def piece_perm(k):
    pairs = []
    for x in range(4):
        for y in range(4):
            for z in range(4):
                for c in range(2):
                    tx, ty = target_of(x, y, z, c, k)
                    pairs.append((position(x, y, z, c), position(tx, ty, x, y // 2)))
    return pairs


def table_kernel(pz_ref, pr_ref, pu_ref, zi_ref, main_ref, upper_ref, mcol_ref, ucol_ref, *outs):
    (ro_h, ro_l, rb_h, rb_l, uo_h, uo_l, uoe_h, uoe_l, ub_h, ub_l, ube_h, ube_l, kz_h, kz_l, kt_h, kt_l) = outs

    def grid_of(rows, cols):
        return (
            lax.broadcasted_iota(jnp.int32, (rows, cols), 0),
            lax.broadcasted_iota(jnp.int32, (rows, cols), 1),
        )

    def taps(ref, distance):
        total = jnp.zeros(distance.shape, F32)
        for k in range(32):
            total = jnp.where(distance == k, ref[k], total)
        return total

    def put(value, high, low):
        h, l = split(value)
        high[...] = h
        low[...] = l

    rows, wide = ro_h.shape
    i, j = grid_of(rows, wide)
    put(taps(pr_ref, j - i) * main_ref[...] + taps(pr_ref, j - 1 - i) * upper_ref[...], ro_h, ro_l)
    put(taps(pr_ref, i - j + 32) * mcol_ref[...] + taps(pr_ref, i - j + 31) * ucol_ref[...], rb_h, rb_l)
    width = uo_h.shape[0]
    i, j = grid_of(width, width)
    put(taps(pu_ref, i + 16 - j), uo_h, uo_l)
    put(taps(pu_ref, j - i + 16), ub_h, ub_l)
    i, j = grid_of(16, width)
    for sign, high, low in ((1, uoe_h, uoe_l), (-1, ube_h, ube_l)):
        for side, start in ((0, 0), (1, width + 16)):
            distance = i + start - j if sign > 0 else j - i - start + 32
            h, l = split(taps(pu_ref, distance))
            for q in range(8):
                at = pl.ds(side * 128 + q * 16, 16)
                high[at, :] = h
                low[at, :] = l
    depth = zi_ref.shape[0]
    i, j = grid_of(depth, depth)
    mix = jnp.dot(taps(pz_ref, j - i + 16), zi_ref[...], precision=HIGH, preferred_element_type=F32)
    big = depth * 8
    i, j = grid_of(big, depth)
    spread = (i // 8 == j).astype(BF)
    i, j = grid_of(depth, big)
    gather = (j // 8 == i).astype(BF)
    i, j = grid_of(big, big)
    same = (i % 8) == (j % 8)
    for value, high, low in ((mix, kz_h, kz_l), (mix.T, kt_h, kt_l)):
        for part, ref in zip(split(value), (high, low)):
            grown = dot(dot(spread, part).astype(BF), gather)
            ref[...] = jnp.where(same, grown, 0.0).astype(BF)


def make_tables(psf_z, psf_r, psf_u, z_interp, main, upper, rows, width):
    depth = z_interp.shape[0]
    shapes = [(rows, rows + 32)] * 4 + [(width, width)] * 8 + [(depth * 8, depth * 8)] * 4
    smem = pl.BlockSpec(memory_space=pltpu.SMEM)
    vmem = pl.BlockSpec(memory_space=pltpu.VMEM)
    own = slice(16, 16 + rows)
    return pl.pallas_call(
        table_kernel,
        in_specs=[smem] * 3 + [vmem] * 5,
        out_specs=[vmem] * len(shapes),
        out_shape=[jax.ShapeDtypeStruct(s, BF) for s in shapes],
        compiler_params=pltpu.CompilerParams(vmem_limit_bytes=32 * MIB),
    )(psf_z, psf_r, psf_u, z_interp, main[None], upper[None], main[own, None], upper[own, None])


def packed(planes):
    lane = lax.broadcasted_iota(jnp.int32, planes[0][:, :128].shape, 1) // 16
    left = right = None
    for q, x in enumerate(planes):
        a, b = x[:, :128], x[:, x.shape[1] - 128 :]
        a = pltpu.roll(a, 16 * q, 1) if q else a
        b = pltpu.roll(b, (16 * q + 16) % 128, 1) if q != 7 else b
        left = a if q == 0 else jnp.where(lane == q, a, left)
        right = b if q == 0 else jnp.where(lane == q, b, right)
    return left, right


def row_product(wide, low, up, own, down):
    xh, xl = split(jnp.concatenate([up, own, down], axis=0))
    return dot(wide, jnp.concatenate([xh, xl], axis=0)) + dot(low, xh)


def row_kernel(ah_ref, al_ref, up_ref, own_ref, down_ref, out_ref, left_ref, right_ref):
    ah, al = ah_ref[...], al_ref[...]
    wide = jnp.concatenate([ah, ah], axis=1)
    planes = []
    for z in range(8):
        planes.append(row_product(wide, al, up_ref[z], own_ref[z], down_ref[z]))
        out_ref[z] = planes[-1]
    left_ref[0], right_ref[0] = packed(planes)


def row_mix(table, up, own, down):
    depth, rows, cols = own.shape
    block = lambda r: pl.BlockSpec((8, r, cols), lambda i: (i, 0, 0))
    edge = pl.BlockSpec((1, rows, 128), lambda i: (i, 0, 0))
    whole = pl.BlockSpec(table[0].shape, lambda i: (0, 0))
    edge_shape = jax.ShapeDtypeStruct((depth // 8, rows, 128), F32)
    return pl.pallas_call(
        row_kernel,
        grid=(depth // 8,),
        in_specs=[whole, whole, block(16), block(rows), block(16)],
        out_specs=[block(rows), edge, edge],
        out_shape=[jax.ShapeDtypeStruct(own.shape, F32), edge_shape, edge_shape],
        compiler_params=pltpu.CompilerParams(vmem_limit_bytes=32 * MIB),
    )(*table, up, own, down)


def column_part(x, left, right, main, edges):
    depth, rows, cols = x.shape
    xh, xl = split(x.reshape(depth * rows, cols))
    total = dot3(xh, xl, main[0], main[1])
    both = jnp.concatenate([left, right], axis=2)
    lane = (lax.broadcasted_iota(jnp.int32, (8, rows, 256), 2) % 128) // 16
    spaced = jnp.stack([jnp.where(lane == q, both, 0.0) for q in range(8)], axis=1)
    eh, el = split(spaced.reshape(depth * rows, 256))
    return total + dot3(eh, el, edges[0], edges[1])


def column_depth_kernel(uh_ref, ul_ref, eh_ref, el_ref, kh_ref, kl_ref, left_ref, right_ref, x_ref, out_ref):
    tables = ((uh_ref[...], ul_ref[...]), (eh_ref[...], el_ref[...]))
    yh, yl = split(column_part(x_ref[...], left_ref[...], right_ref[...], *tables))
    out_ref[...] = dot3(kh_ref[...], kl_ref[...], yh, yl).reshape(out_ref.shape)


def column_kernel(uh_ref, ul_ref, eh_ref, el_ref, left_ref, right_ref, x_ref, out_ref):
    tables = ((uh_ref[...], ul_ref[...]), (eh_ref[...], el_ref[...]))
    out_ref[...] = column_part(x_ref[...], left_ref[...], right_ref[...], *tables).reshape(out_ref.shape)


def column_mix(body, tables, left, right, x):
    depth, rows, cols = x.shape
    block = lambda d, c: pl.BlockSpec((d, 8, c), lambda i: (0, i, 0))
    whole = lambda t: pl.BlockSpec(t.shape, lambda i: (0, 0))
    return pl.pallas_call(
        body,
        grid=(rows // 8,),
        in_specs=[whole(t) for t in tables] + [block(depth // 8, 128), block(depth // 8, 128), block(depth, cols)],
        out_specs=block(depth, cols),
        out_shape=jax.ShapeDtypeStruct(x.shape, F32),
        compiler_params=pltpu.CompilerParams(vmem_limit_bytes=32 * MIB),
    )(*tables, left, right, x)


def ratio_kernel(place_ref, blur_ref, *refs):
    pieces, (out_ref, left_ref, right_ref) = refs[:-3], refs[-3:]
    for k, piece in enumerate(pieces):
        cols = pl.ds(pl.multiple_of(place_ref[k, 2] * 128, 128), 128)
        for part in range(2):
            planes = pl.ds(pl.multiple_of(place_ref[k, part] * 8, 8), 8)
            out_ref[planes, :, cols] = piece[part] / (blur_ref[planes, :, cols] + background)
    for g in range(left_ref.shape[0]):
        left_ref[g], right_ref[g] = packed([out_ref[8 * g + q] for q in range(8)])


def ratio_of(place, blurred, pieces):
    depth, rows, cols = blurred.shape
    vmem = pl.BlockSpec(memory_space=pltpu.VMEM)
    edge_shape = jax.ShapeDtypeStruct((depth // 8, rows, 128), F32)
    return pl.pallas_call(
        ratio_kernel,
        in_specs=[pl.BlockSpec(memory_space=pltpu.SMEM), vmem] + [vmem] * len(pieces),
        out_specs=[vmem] * 3,
        out_shape=[jax.ShapeDtypeStruct(blurred.shape, F32), edge_shape, edge_shape],
        compiler_params=pltpu.CompilerParams(vmem_limit_bytes=48 * MIB),
    )(place, blurred, *pieces)


def final_kernel(ah_ref, al_ref, kh_ref, kl_ref, up_ref, own_ref, down_ref, est_ref, out_ref, mixed):
    step = pl.program_id(0)
    half = pl.num_programs(0) // 2

    @pl.when(step < half)
    def _():
        ah, al = ah_ref[...], al_ref[...]
        wide = jnp.concatenate([ah, ah], axis=1)
        first = pl.multiple_of(step * 8, 8)
        for z in range(8):
            mixed[first + z] = row_product(wide, al, up_ref[z], own_ref[z], down_ref[z])

    @pl.when(step >= half)
    def _():
        rows = pl.ds(pl.multiple_of((step - half) * 8, 8), 8)
        xh, xl = split(mixed[:, rows, :].reshape(-1, mixed.shape[2]))
        back = dot3(kh_ref[...], kl_ref[...], xh, xl)
        out_ref[...] = est_ref[...] * back.reshape(out_ref.shape)


def final_update(row_table, depth_table, up, own, down, est):
    depth, rows, cols = own.shape
    half = depth // 8
    block = lambda r: pl.BlockSpec((8, r, cols), lambda i: (jnp.minimum(i, half - 1), 0, 0))
    tile = pl.BlockSpec((depth, 8, cols), lambda i: (0, jnp.maximum(i - half, 0), 0))
    whole = lambda t: pl.BlockSpec(t.shape, lambda i: (0, 0))
    return pl.pallas_call(
        final_kernel,
        grid=(half + rows // 8,),
        in_specs=[whole(t) for t in (*row_table, *depth_table)] + [block(16), block(rows), block(16), tile],
        out_specs=tile,
        out_shape=jax.ShapeDtypeStruct(own.shape, F32),
        scratch_shapes=[pltpu.VMEM(own.shape, F32)],
        compiler_params=pltpu.CompilerParams(vmem_limit_bytes=40 * MIB),
    )(*row_table, *depth_table, up, own, down, est)


def column_edges(left, right):
    return lax.ppermute(right, AXES, shift_perm("gy", 1)), lax.ppermute(left, AXES, shift_perm("gy", -1))


def row_edges(x):
    rows = x.shape[1]
    return (
        lax.ppermute(x[:, rows - 16 :], AXES, shift_perm("gx", 1)),
        lax.ppermute(x[:, :16], AXES, shift_perm("gx", -1)),
    )


def shards(estimate, measured, z_interp, r_interp, psf_z, psf_r, psf_u):
    depth, rows, width = estimate.shape
    gx, gy = lax.axis_index("gx"), lax.axis_index("gy")
    x, y, z, c = gx // 4, gx % 4, gy // 2, gy % 2

    up, down = row_edges(estimate)
    blocks = measured.reshape(8, 8, 2, rows, 128)
    parity = c ^ (x & 1)
    take = lambda side: lax.dynamic_index_in_dim(blocks, side, axis=2, keepdims=False)
    kept, swapped = take(parity), lax.ppermute(take(1 - parity), AXES, core_swap())
    pieces, place = [], []
    for k in range(8):
        tx, ty = target_of(x, y, z, c, k)
        slot = tx * 2 + ty // 2
        part = jnp.stack([lax.dynamic_index_in_dim(p, slot, axis=1, keepdims=False) for p in (kept, swapped)])
        pieces.append(lax.ppermute(part, AXES, piece_perm(k)))
        pair, core, half = source_of(x, y, z, c, k)
        place.append(jnp.stack([pair * 2 + core, pair * 2 + 1 - core, half]))
    place = jnp.stack(place).astype(jnp.int32)

    total = r_interp.shape[0]
    first = jnp.clip(gx * rows - 64, 0, total - 192)
    band = lax.dynamic_slice(r_interp, (first, 0), (192, total))
    i = lax.broadcasted_iota(jnp.int32, (192, total), 0) + first
    j = lax.broadcasted_iota(jnp.int32, (192, total), 1)
    main = jnp.sum(jnp.where(i == j, band, 0.0), axis=0)
    upper = jnp.sum(jnp.where(i + 1 == j, band, 0.0), axis=0)
    window = lambda v: lax.dynamic_slice(jnp.pad(v, (16, 16)), (gx * rows,), (rows + 32,))
    tables = make_tables(psf_z, psf_r, psf_u, z_interp, window(main), window(upper), rows, width)
    rows_out, rows_back, cols_out, cols_back = tables[:2], tables[2:4], tables[4:8], tables[8:12]
    depth_out, depth_back = tables[12:14], tables[14:16]

    mixed, left, right = row_mix(rows_out, up, estimate, down)
    left, right = column_edges(left, right)
    blurred = column_mix(column_depth_kernel, (*cols_out, *depth_out), left, right, mixed)
    ratio, left, right = ratio_of(place, blurred, pieces)
    left, right = column_edges(left, right)
    spread = column_mix(column_kernel, cols_back, left, right, ratio)
    up, down = row_edges(spread)
    return final_update(rows_back, depth_back, up, spread, down, estimate)


def solution(mesh):
    in_specs = (P(None, "gx", "gy"), P("gy", None, "gx"), P(), P(), P(), P(), P())
    out_specs = P(None, "gx", "gy")
    return jax.shard_map(shards, mesh=mesh, in_specs=in_specs, out_specs=out_specs, check_vma=False)
```

time: 343 us -> 230 us (0.67)
  the two profiles are of different devices: /device:TPU:15 before, /device:TPU:33 now
where the time goes in v2:
time: 230 us; the launch traced here: 229 us
  starting transfers between devices  81.5 us (35%)
  waiting for transfers between devices  73.1 us (32%)
  Pallas kernels  42.9 us (19%)
  local copies, waits for them, and re-layouts  22.8 us (10%)
  other arithmetic  7.81 us (3%)
    ppermute x8, starting transfers between devices, shards(): pieces.append(lax.ppermute(part, AXES, piece_perm(k)))  36.7 us
    ppermute x2, waiting for transfers between devices, row_edges(): lax.ppermute(x[:, rows - 16:], AXES, shift_perm('gx', 1))  34.5 us
    ppermute x8, waiting for transfers between devices, shards(): pieces.append(lax.ppermute(part, AXES, piece_perm(k)))  24.9 us
    ppermute x2, starting transfers between devices, row_edges(): lax.ppermute(x[:, rows - 16:], AXES, shift_perm('gx', 1))  21.4 us
    pallas_call x2, Pallas kernels, column_mix(): pl.pallas_call(body, grid=(rows // 8,), in_specs=[whole(t) for t in table...  20.6 us
    ppermute x2, starting transfers between devices, column_edges(): lax.ppermute(right, AXES, shift_perm('gy', 1))  16.3 us
    unnamed x74, local copies, waits for them, and re-layouts  12.5 us
    pallas_call x1, Pallas kernels, final_update(): pl.pallas_call(final_kernel, grid=(half + rows // 8,), in_specs=[whole(t)...  9.48 us
  transfers between devices with their start and end apart: 17, of which 9 were waited for; matrix products, arithmetic and copies ran while one was open for 6% of the time, Pallas kernels for 9%

profile of v2, /device:TPU:33, one launch (start us, length us, event | category | flops | bytes accessed | tf_op | source)
XLA Modules:
  0.0 229.1 jit_solution(15174145563970072832)
XLA Ops:
  0.0 3.4 %copy_bitcast_fusion = f32[8,8,64,128]{3,2,0,1:T(8,128)} fusion(f32[8,8,2,64,128]{4,3,2,1,0:T(8,128)} %bitcast.85, s32[]{:T(128)S(6)} %select_n.203), kind=kLoop, calls=%fused_computation | loop fusion | bytes 4194308 | tf_op jit(solution)/shard_map/jit(dynamic_index_in_dim)/squeeze | solution.py:297
  5.6 3.3 %collective-permute-start = (f32[64,16,256]{2,1,0:T(8,128)}, f32[64,16,256]{2,1,0:T(8,128)S(1)}, u32[]{:S(2)}, u32[]{:S(2)}) collective-permute-start(f32[64,16,256]{2,1,0:T(8,128)} %get-tuple-element.62), channel_id=1, source_target_pairs={{0,8},{1,9},{2,10},{3,11},{4,12},{5,13},{6,14},{7,15},{8,16},{9,17... | collective-permute-start | bytes 3145736 | tf_op jit(solution)/shard_map/ppermute | solution.py:284
  12.4 3.0 %shard_map.73 = (bf16[64,96]{1,0:T(8,128)(2,1)S(1)}, bf16[64,96]{1,0:T(8,128)(2,1)S(1)}, bf16[64,96]{1,0:T(8,128)(2,1)S(1)}, bf16[64,96]{1,0:T(8,128)(2,1)S(1)},...) custom-call(f32[32]{0:T(128)S(1)} %copy-done.34, ...), custom_call_target="tpu_custom_call" | custom-call | tf_op jit(solution)/shard_map/pallas_call | solution.py:128
  17.8 13.8 %collective-permute-done.up_ref = f32[64,16,256]{2,1,0:T(8,128)S(1)} collective-permute-done((f32[64,16,256]{2,1,0:T(8,128)}, f32[64,16,256]{2,1,0:T(8,128)S(1)}, u32[]{:S(2)}, u32[]{:S(2)}) %collective-permute-start) | collective-permute-done | bytes 1048608 | tf_op jit(solution)/shard_map/ppermute | solution.py:284
  31.7 3.8 %collective-permute-done.1.down_ref = f32[64,16,256]{2,1,0:T(8,128)S(1)} collective-permute-done((f32[64,16,256]{2,1,0:T(8,128)}, f32[64,16,256]{2,1,0:T(8,128)S(1)}, u32[]{:S(2)}, u32[]{:S(2)}) %collective-permute-start.1) | collective-permute-done | bytes 1048608 | tf_op jit(solution)/shard_map/ppermute | solution.py:285
  35.5 3.5 %shard_map.74 = (f32[64,64,256]{2,1,0:T(8,128)S(1)}, f32[8,64,128]{2,1,0:T(8,128)S(1)}, f32[8,64,128]{2,1,0:T(8,128)S(1)}) custom-call(bf16[64,96]{1,0:T(8,128)(2,1)S(1)} %get-tuple-element.41.ah_ref, bf16[64,96]{1,0:T(8,128)(2,1)S(1)} %get-tuple-element.42.al_ref, f32[64,16,256]{2,1,0:T(8,128)S(1)} %collective-permute-done.up_ref, ...), custom_call_target="tpu_custom_call" | custom-call | tf_op jit(solution)/shard_map/pallas_call | solution.py:170
  39.1 4.5 %collective-permute-start.2 = (f32[8,64,128]{2,1,0:T(8,128)S(1)}, f32[8,64,128]{2,1,0:T(8,128)S(1)}, u32[]{:S(2)}, u32[]{:S(2)}) collective-permute-start(f32[8,64,128]{2,1,0:T(8,128)S(1)} %get-tuple-element.43), channel_id=1, source_target_pairs={{0,1},{1,2},{2,3},{3,4},{4,5},{5,6},{6,7},{8,9},{9,10},{10,11},{11... | collective-permute-start | bytes 786440 | tf_op jit(solution)/shard_map/ppermute | solution.py:278
  49.5 9.4 %collective-permute-start.6 = (f32[2,8,64,128]{3,2,1,0:T(8,128)S(1)}, f32[2,8,64,128]{3,2,1,0:T(8,128)S(1)}, u32[]{:S(2)}, u32[]{:S(2)}) collective-permute-start(f32[2,8,64,128]{3,2,1,0:T(8,128)S(1)} %pad_maximum_fusion.1), channel_id=1, source_target_pairs={{0,16},{1,88},{2,48},{3,120},{4,80},{5,24},{6,112},{7,56},{8,0},{9... | collective-permute-start | bytes 1572872 | tf_op jit(solution)/shard_map/ppermute | solution.py:304
  65.1 7.3 %collective-permute-start.8 = (f32[2,8,64,128]{3,2,1,0:T(8,128)}, f32[2,8,64,128]{3,2,1,0:T(8,128)}, u32[]{:S(2)}, u32[]{:S(2)}) collective-permute-start(f32[2,8,64,128]{3,2,1,0:T(8,128)} %pad_maximum_fusion.3), channel_id=1, source_target_pairs={{0,48},{1,120},{2,80},{3,24},{4,112},{5,56},{6,16},{7,88},{8,32},{... | collective-permute-start | bytes 1572872 | tf_op jit(solution)/shard_map/ppermute | solution.py:304
  76.0 3.5 %collective-permute-start.10 = (f32[2,8,64,128]{3,2,1,0:T(8,128)}, f32[2,8,64,128]{3,2,1,0:T(8,128)}, u32[]{:S(2)}, u32[]{:S(2)}) collective-permute-start(f32[2,8,64,128]{3,2,1,0:T(8,128)} %pad_maximum_fusion.5), channel_id=1, source_target_pairs={{0,80},{1,24},{2,112},{3,56},{4,16},{5,88},{6,48},{7,120},{8,64},{... | collective-permute-start | bytes 1572872 | tf_op jit(solution)/shard_map/ppermute | solution.py:304
  79.5 6.3 %collective-permute-start.11 = (f32[2,8,64,128]{3,2,1,0:T(8,128)}, f32[2,8,64,128]{3,2,1,0:T(8,128)}, u32[]{:S(2)}, u32[]{:S(2)}) collective-permute-start(f32[2,8,64,128]{3,2,1,0:T(8,128)} %pad_maximum_fusion.6), channel_id=1, source_target_pairs={{0,96},{1,40},{2,0},{3,72},{4,32},{5,104},{6,64},{7,8},{8,112},{9,... | collective-permute-start | bytes 1572872 | tf_op jit(solution)/shard_map/ppermute | solution.py:304
  85.7 2.9 %collective-permute-done.7.refs_2_ = f32[2,8,64,128]{3,2,1,0:T(8,128)S(1)} collective-permute-done((f32[2,8,64,128]{3,2,1,0:T(8,128)S(1)}, f32[2,8,64,128]{3,2,1,0:T(8,128)S(1)}, u32[]{:S(2)}, u32[]{:S(2)}) %collective-permute-start.7) | collective-permute-done | bytes 524320 | tf_op jit(solution)/shard_map/ppermute | solution.py:304
  89.5 3.4 %collective-permute-start.12 = (f32[2,8,64,128]{3,2,1,0:T(8,128)}, f32[2,8,64,128]{3,2,1,0:T(8,128)}, u32[]{:S(2)}, u32[]{:S(2)}) collective-permute-start(f32[2,8,64,128]{3,2,1,0:T(8,128)} %pad_maximum_fusion.7), channel_id=1, source_target_pairs={{0,112},{1,56},{2,16},{3,88},{4,48},{5,120},{6,80},{7,24},{8,96},{... | collective-permute-start | bytes 1572872 | tf_op jit(solution)/shard_map/ppermute | solution.py:304
  102.4 15.3 %shard_map.75.blur_ref = f32[64,64,256]{2,1,0:T(8,128)S(1)} custom-call(bf16[256,256]{1,0:T(8,128)(2,1)S(1)} %copy-done.22, bf16[256,256]{1,0:T(8,128)(2,1)S(1)} %copy-done.24, bf16[256,256]{1,0:T(8,128)(2,1)S(1)} %copy-done.26, bf16[256,256]{1,0:T(8,128)(2,1)S(1)} %copy-done.28, bf16[512,512]{1,0:T(8,128)(2,1)S(1)} %copy-done.8, ...), custom_call_target="tpu_custom_call" | custom-call | tf_op jit(solution)/shard_map/pallas_call | solution.py:206
  119.8 9.5 %collective-permute-done.11.refs_6_ = f32[2,8,64,128]{3,2,1,0:T(8,128)} collective-permute-done((f32[2,8,64,128]{3,2,1,0:T(8,128)}, f32[2,8,64,128]{3,2,1,0:T(8,128)}, u32[]{:S(2)}, u32[]{:S(2)}) %collective-permute-start.11) | collective-permute-done | bytes 524320 | tf_op jit(solution)/shard_map/ppermute | solution.py:304
  129.2 12.5 %collective-permute-done.12.refs_7_ = f32[2,8,64,128]{3,2,1,0:T(8,128)} collective-permute-done((f32[2,8,64,128]{3,2,1,0:T(8,128)}, f32[2,8,64,128]{3,2,1,0:T(8,128)}, u32[]{:S(2)}, u32[]{:S(2)}) %collective-permute-start.12) | collective-permute-done | bytes 524320 | tf_op jit(solution)/shard_map/ppermute | solution.py:304
  141.7 6.4 %shard_map.76 = (f32[64,64,256]{2,1,0:T(8,128)}, f32[8,64,128]{2,1,0:T(8,128)S(1)}, f32[8,64,128]{2,1,0:T(8,128)S(1)}) custom-call(s32[8,3]{1,0:T(8,128)S(1)} %stack.193.place_ref, f32[64,64,256]{2,1,0:T(8,128)} %copy-done.3, f32[2,8,64,128]{3,2,1,0:T(8,128)S(1)} %collective-permute-done.5.refs_0_, f32[2,8,64,128]{3,2,1,0:T(8,128)S(1)} %collective-permute-done.6.refs_1_, ...), custom_call_target="tpu_custom_call" | custom-call | tf_op jit(solution)/shard_map/pallas_call | solution.py:231
  148.2 11.8 %collective-permute-start.13 = (f32[8,64,128]{2,1,0:T(8,128)S(1)}, f32[8,64,128]{2,1,0:T(8,128)S(1)}, u32[]{:S(2)}, u32[]{:S(2)}) collective-permute-start(f32[8,64,128]{2,1,0:T(8,128)S(1)} %get-tuple-element.46), channel_id=1, source_target_pairs={{0,1},{1,2},{2,3},{3,4},{4,5},{5,6},{6,7},{8,9},{9,10},{10,11},{11... | collective-permute-start | bytes 786440 | tf_op jit(solution)/shard_map/ppermute | solution.py:278
  163.2 4.4 %collective-permute-done.14.right_ref = f32[8,64,128]{2,1,0:T(8,128)S(1)} collective-permute-done((f32[8,64,128]{2,1,0:T(8,128)S(1)}, f32[8,64,128]{2,1,0:T(8,128)S(1)}, u32[]{:S(2)}, u32[]{:S(2)}) %collective-permute-start.14) | collective-permute-done | bytes 262176 | tf_op jit(solution)/shard_map/ppermute | solution.py:278
  169.9 5.3 %shard_map.77.own_ref = f32[64,64,256]{2,1,0:T(8,128)S(1)} custom-call(bf16[256,256]{1,0:T(8,128)(2,1)S(1)} %get-tuple-element.31.uh_ref, bf16[256,256]{1,0:T(8,128)(2,1)S(1)} %copy-done.16, bf16[256,256]{1,0:T(8,128)(2,1)S(1)} %copy-done.18, bf16[256,256]{1,0:T(8,128)(2,1)S(1)} %copy-done.20, f32[8,64,128]{2,1,0:T(8,128)S(1)} %collective-permute-done.13.left_ref, ...), custom_call_target="tpu_custom_call" | custom-call | tf_op jit(solution)/shard_map/pallas_call | solution.py:206
  175.4 18.1 %collective-permute-start.15 = (f32[64,16,256]{2,1,0:T(8,128)S(1)}, f32[64,16,256]{2,1,0:T(8,128)S(1)}, u32[]{:S(2)}, u32[]{:S(2)}) collective-permute-start(f32[64,16,256]{2,1,0:T(8,128)S(1)} %get-tuple-element.52), channel_id=1, source_target_pairs={{0,8},{1,9},{2,10},{3,11},{4,12},{5,13},{6,14},{7,15},{8,16},{9,17... | collective-permute-start | bytes 3145736 | tf_op jit(solution)/shard_map/ppermute | solution.py:284
  194.8 20.7 %collective-permute-done.15.up_ref = f32[64,16,256]{2,1,0:T(8,128)S(1)} collective-permute-done((f32[64,16,256]{2,1,0:T(8,128)S(1)}, f32[64,16,256]{2,1,0:T(8,128)S(1)}, u32[]{:S(2)}, u32[]{:S(2)}) %collective-permute-start.15) | collective-permute-done | bytes 1048608 | tf_op jit(solution)/shard_map/ppermute | solution.py:284
  215.4 4.2 %collective-permute-done.16.down_ref = f32[64,16,256]{2,1,0:T(8,128)S(1)} collective-permute-done((f32[64,16,256]{2,1,0:T(8,128)S(1)}, f32[64,16,256]{2,1,0:T(8,128)S(1)}, u32[]{:S(2)}, u32[]{:S(2)}) %collective-permute-start.16) | collective-permute-done | bytes 1048608 | tf_op jit(solution)/shard_map/ppermute | solution.py:285
  219.6 9.5 %shard_map.78 = f32[64,64,256]{2,1,0:T(8,128)} custom-call(bf16[64,96]{1,0:T(8,128)(2,1)S(1)} %copy-done.31, bf16[64,96]{1,0:T(8,128)(2,1)S(1)} %copy-done.33, bf16[512,512]{1,0:T(8,128)(2,1)S(1)} %get-tuple-element.29.kh_ref, bf16[512,512]{1,0:T(8,128)(2,1)S(1)} %get-tuple-element.30.kl_ref, f32[64,16,256]{2,1,0:T(8,128)S(1)} %collective-permute-done.15.up_ref, ...), custom_call_target="tpu_custom_call" | custom-call | tf_op jit(solution)/shard_map/pallas_call | solution.py:266
  (116 shorter events, 42.7 us)
Async XLA Ops:
  3.4 42.1 %collective-permute-start.4 = (f32[8,8,64,128]{3,2,0,1:T(8,128)}, f32[8,8,64,128]{3,2,0,1:T(8,128)}, u32[]{:S(2)}, u32[]{:S(2)}) collective-permute-start(f32[8,8,64,128]{3,2,0,1:T(8,128)} %copy_bitcast_fusion), channel_id=1, source_target_pairs={{0,1},{1,0},{2,3},{3,2},{4,5},{5,4},{6,7},{7,6},{8,9},{9,8},{10,11... | collective-permute-start | bytes 6291464 | tf_op jit(solution)/shard_map/ppermute | solution.py:298
  5.6 26.1 %collective-permute-start = (f32[64,16,256]{2,1,0:T(8,128)}, f32[64,16,256]{2,1,0:T(8,128)S(1)}, u32[]{:S(2)}, u32[]{:S(2)}) collective-permute-start(f32[64,16,256]{2,1,0:T(8,128)} %get-tuple-element.62), channel_id=1, source_target_pairs={{0,8},{1,9},{2,10},{3,11},{4,12},{5,13},{6,14},{7,15},{8,16},{9,17... | collective-permute-start | bytes 3145736 | tf_op jit(solution)/shard_map/ppermute | solution.py:284
  8.9 26.6 %collective-permute-start.1 = (f32[64,16,256]{2,1,0:T(8,128)}, f32[64,16,256]{2,1,0:T(8,128)S(1)}, u32[]{:S(2)}, u32[]{:S(2)}) collective-permute-start(f32[64,16,256]{2,1,0:T(8,128)} %get-tuple-element.61), channel_id=1, source_target_pairs={{8,0},{9,1},{10,2},{11,3},{12,4},{13,5},{14,6},{15,7},{16,8},{17,9... | collective-permute-start | bytes 3145736 | tf_op jit(solution)/shard_map/ppermute | solution.py:285
  39.1 26.1 %collective-permute-start.2 = (f32[8,64,128]{2,1,0:T(8,128)S(1)}, f32[8,64,128]{2,1,0:T(8,128)S(1)}, u32[]{:S(2)}, u32[]{:S(2)}) collective-permute-start(f32[8,64,128]{2,1,0:T(8,128)S(1)} %get-tuple-element.43), channel_id=1, source_target_pairs={{0,1},{1,2},{2,3},{3,4},{4,5},{5,6},{6,7},{8,9},{9,10},{10,11},{11... | collective-permute-start | bytes 786440 | tf_op jit(solution)/shard_map/ppermute | solution.py:278
  43.6 28.8 %collective-permute-start.3 = (f32[8,64,128]{2,1,0:T(8,128)S(1)}, f32[8,64,128]{2,1,0:T(8,128)S(1)}, u32[]{:S(2)}, u32[]{:S(2)}) collective-permute-start(f32[8,64,128]{2,1,0:T(8,128)S(1)} %get-tuple-element.44), channel_id=1, source_target_pairs={{1,0},{2,1},{3,2},{4,3},{5,4},{6,5},{7,6},{9,8},{10,9},{11,10},{12... | collective-permute-start | bytes 786440 | tf_op jit(solution)/shard_map/ppermute | solution.py:278
  47.2 48.4 %copy-start.8 = (bf16[512,512]{1,0:T(8,128)(2,1)S(1)}, bf16[512,512]{1,0:T(8,128)(2,1)}, u32[]{:S(2)}) copy-start(bf16[512,512]{1,0:T(8,128)(2,1)} %copy-done.7) | copy-start | bytes 1572868
  47.2 48.4 %copy-start.10 = (bf16[512,512]{1,0:T(8,128)(2,1)S(1)}, bf16[512,512]{1,0:T(8,128)(2,1)}, u32[]{:S(2)}) copy-start(bf16[512,512]{1,0:T(8,128)(2,1)} %copy-done.9) | copy-start | bytes 1572868
  47.3 28.7 %collective-permute-start.5 = (f32[2,8,64,128]{3,2,1,0:T(8,128)S(1)}, f32[2,8,64,128]{3,2,1,0:T(8,128)S(1)}, u32[]{:S(2)}, u32[]{:S(2)}) collective-permute-start(f32[2,8,64,128]{3,2,1,0:T(8,128)S(1)} %pad_maximum_fusion), channel_id=1, source_target_pairs={{0,0},{1,72},{2,32},{3,104},{4,64},{5,8},{6,96},{7,40},{8,16},{9,8... | collective-permute-start | bytes 1572872 | tf_op jit(solution)/shard_map/ppermute | solution.py:304
  49.5 30.0 %collective-permute-start.6 = (f32[2,8,64,128]{3,2,1,0:T(8,128)S(1)}, f32[2,8,64,128]{3,2,1,0:T(8,128)S(1)}, u32[]{:S(2)}, u32[]{:S(2)}) collective-permute-start(f32[2,8,64,128]{3,2,1,0:T(8,128)S(1)} %pad_maximum_fusion.1), channel_id=1, source_target_pairs={{0,16},{1,88},{2,48},{3,120},{4,80},{5,24},{6,112},{7,56},{8,0},{9... | collective-permute-start | bytes 1572872 | tf_op jit(solution)/shard_map/ppermute | solution.py:304
  58.9 29.7 %collective-permute-start.7 = (f32[2,8,64,128]{3,2,1,0:T(8,128)S(1)}, f32[2,8,64,128]{3,2,1,0:T(8,128)S(1)}, u32[]{:S(2)}, u32[]{:S(2)}) collective-permute-start(f32[2,8,64,128]{3,2,1,0:T(8,128)S(1)} %pad_maximum_fusion.2), channel_id=1, source_target_pairs={{0,32},{1,104},{2,64},{3,8},{4,96},{5,40},{6,0},{7,72},{8,48},{9,1... | collective-permute-start | bytes 1572872 | tf_op jit(solution)/shard_map/ppermute | solution.py:304
  65.1 54.6 %collective-permute-start.8 = (f32[2,8,64,128]{3,2,1,0:T(8,128)}, f32[2,8,64,128]{3,2,1,0:T(8,128)}, u32[]{:S(2)}, u32[]{:S(2)}) collective-permute-start(f32[2,8,64,128]{3,2,1,0:T(8,128)} %pad_maximum_fusion.3), channel_id=1, source_target_pairs={{0,48},{1,120},{2,80},{3,24},{4,112},{5,56},{6,16},{7,88},{8,32},{... | collective-permute-start | bytes 1572872 | tf_op jit(solution)/shard_map/ppermute | solution.py:304
  73.1 46.7 %collective-permute-start.9 = (f32[2,8,64,128]{3,2,1,0:T(8,128)}, f32[2,8,64,128]{3,2,1,0:T(8,128)}, u32[]{:S(2)}, u32[]{:S(2)}) collective-permute-start(f32[2,8,64,128]{3,2,1,0:T(8,128)} %pad_maximum_fusion.4), channel_id=1, source_target_pairs={{0,64},{1,8},{2,96},{3,40},{4,0},{5,72},{6,32},{7,104},{8,80},{9,2... | collective-permute-start | bytes 1572872 | tf_op jit(solution)/shard_map/ppermute | solution.py:304
  76.0 43.8 %collective-permute-start.10 = (f32[2,8,64,128]{3,2,1,0:T(8,128)}, f32[2,8,64,128]{3,2,1,0:T(8,128)}, u32[]{:S(2)}, u32[]{:S(2)}) collective-permute-start(f32[2,8,64,128]{3,2,1,0:T(8,128)} %pad_maximum_fusion.5), channel_id=1, source_target_pairs={{0,80},{1,24},{2,112},{3,56},{4,16},{5,88},{6,48},{7,120},{8,64},{... | collective-permute-start | bytes 1572872 | tf_op jit(solution)/shard_map/ppermute | solution.py:304
  79.5 49.8 %collective-permute-start.11 = (f32[2,8,64,128]{3,2,1,0:T(8,128)}, f32[2,8,64,128]{3,2,1,0:T(8,128)}, u32[]{:S(2)}, u32[]{:S(2)}) collective-permute-start(f32[2,8,64,128]{3,2,1,0:T(8,128)} %pad_maximum_fusion.6), channel_id=1, source_target_pairs={{0,96},{1,40},{2,0},{3,72},{4,32},{5,104},{6,64},{7,8},{8,112},{9,... | collective-permute-start | bytes 1572872 | tf_op jit(solution)/shard_map/ppermute | solution.py:304
  89.5 52.3 %collective-permute-start.12 = (f32[2,8,64,128]{3,2,1,0:T(8,128)}, f32[2,8,64,128]{3,2,1,0:T(8,128)}, u32[]{:S(2)}, u32[]{:S(2)}) collective-permute-start(f32[2,8,64,128]{3,2,1,0:T(8,128)} %pad_maximum_fusion.7), channel_id=1, source_target_pairs={{0,112},{1,56},{2,16},{3,88},{4,48},{5,120},{6,80},{7,24},{8,96},{... | collective-permute-start | bytes 1572872 | tf_op jit(solution)/shard_map/ppermute | solution.py:304
  119.7 47.9 %copy-start.16 = (bf16[256,256]{1,0:T(8,128)(2,1)S(1)}, bf16[256,256]{1,0:T(8,128)(2,1)}, u32[]{:S(2)}) copy-start(bf16[256,256]{1,0:T(8,128)(2,1)} %copy-done.15) | copy-start | bytes 393220
  119.7 47.9 %copy-start.18 = (bf16[256,256]{1,0:T(8,128)(2,1)S(1)}, bf16[256,256]{1,0:T(8,128)(2,1)}, u32[]{:S(2)}) copy-start(bf16[256,256]{1,0:T(8,128)(2,1)} %copy-done.17) | copy-start | bytes 393220
  119.7 47.9 %copy-start.20 = (bf16[256,256]{1,0:T(8,128)(2,1)S(1)}, bf16[256,256]{1,0:T(8,128)(2,1)}, u32[]{:S(2)}) copy-start(bf16[256,256]{1,0:T(8,128)(2,1)} %copy-done.19) | copy-start | bytes 393220
  148.2 15.1 %collective-permute-start.13 = (f32[8,64,128]{2,1,0:T(8,128)S(1)}, f32[8,64,128]{2,1,0:T(8,128)S(1)}, u32[]{:S(2)}, u32[]{:S(2)}) collective-permute-start(f32[8,64,128]{2,1,0:T(8,128)S(1)} %get-tuple-element.46), channel_id=1, source_target_pairs={{0,1},{1,2},{2,3},{3,4},{4,5},{5,6},{6,7},{8,9},{9,10},{10,11},{11... | collective-permute-start | bytes 786440 | tf_op jit(solution)/shard_map/ppermute | solution.py:278
  160.0 7.7 %collective-permute-start.14 = (f32[8,64,128]{2,1,0:T(8,128)S(1)}, f32[8,64,128]{2,1,0:T(8,128)S(1)}, u32[]{:S(2)}, u32[]{:S(2)}) collective-permute-start(f32[8,64,128]{2,1,0:T(8,128)S(1)} %get-tuple-element.47), channel_id=1, source_target_pairs={{1,0},{2,1},{3,2},{4,3},{5,4},{6,5},{7,6},{9,8},{10,9},{11,10},{12... | collective-permute-start | bytes 786440 | tf_op jit(solution)/shard_map/ppermute | solution.py:278
  169.8 49.7 %copy-start.31 = (bf16[64,96]{1,0:T(8,128)(2,1)S(1)}, bf16[64,96]{1,0:T(8,128)(2,1)}, u32[]{:S(2)}) copy-start(bf16[64,96]{1,0:T(8,128)(2,1)} %copy-done.30) | copy-start | bytes 36868
  169.8 49.7 %copy-start.33 = (bf16[64,96]{1,0:T(8,128)(2,1)S(1)}, bf16[64,96]{1,0:T(8,128)(2,1)}, u32[]{:S(2)}) copy-start(bf16[64,96]{1,0:T(8,128)(2,1)} %copy-done.32) | copy-start | bytes 36868
  175.4 40.1 %collective-permute-start.15 = (f32[64,16,256]{2,1,0:T(8,128)S(1)}, f32[64,16,256]{2,1,0:T(8,128)S(1)}, u32[]{:S(2)}, u32[]{:S(2)}) collective-permute-start(f32[64,16,256]{2,1,0:T(8,128)S(1)} %get-tuple-element.52), channel_id=1, source_target_pairs={{0,8},{1,9},{2,10},{3,11},{4,12},{5,13},{6,14},{7,15},{8,16},{9,17... | collective-permute-start | bytes 3145736 | tf_op jit(solution)/shard_map/ppermute | solution.py:284
  193.5 26.1 %collective-permute-start.16 = (f32[64,16,256]{2,1,0:T(8,128)S(1)}, f32[64,16,256]{2,1,0:T(8,128)S(1)}, u32[]{:S(2)}, u32[]{:S(2)}) collective-permute-start(f32[64,16,256]{2,1,0:T(8,128)S(1)} %get-tuple-element.51), channel_id=1, source_target_pairs={{8,0},{9,1},{10,2},{11,3},{12,4},{13,5},{14,6},{15,7},{16,8},{17,9... | collective-permute-start | bytes 3145736 | tf_op jit(solution)/shard_map/ppermute | solution.py:285
  (30 other events, 444.3 us)

commit v3 on v2

v3 whole, which is shorter than its diff:
```python
import functools

import jax
import jax.numpy as jnp
from jax import lax
from jax.experimental import pallas as pl
from jax.experimental.pallas import tpu as pltpu
from jax.sharding import PartitionSpec as P

background = 0.25
HIGH = lax.Precision.HIGHEST
F32 = jnp.float32
BF = jnp.bfloat16
AXES = ("gx", "gy")
MIB = 1024 * 1024


def split(x):
    hi = x.astype(BF)
    return hi, (x - hi.astype(F32)).astype(BF)


def dot(a, b):
    return jnp.dot(a, b, preferred_element_type=F32)


def thrice(a, b):
    (ah, al), (bh, bl) = a, b
    return dot(jnp.concatenate([ah, ah, al], axis=1), jnp.concatenate([bh, bl, bh], axis=0))


def shift_perm(axis_of, d):
    if axis_of == "gx":
        return [(i * 8 + j, (i + d) * 8 + j) for i in range(16) for j in range(8) if 0 <= i + d < 16]
    return [(i * 8 + j, i * 8 + j + d) for i in range(16) for j in range(8) if 0 <= j + d < 8]


def position(x, y, z, c):
    return ((x % 4) * 4 + y % 4) * 8 + (z % 4) * 2 + c % 2


def core_swap():
    return [(d, d ^ 1) for d in range(128)]


def target_of(x, y, z, c, k):
    k1, k2 = k // 2, k % 2
    side, half = y >> 1, y & 1
    parity = c ^ (x & 1)
    return (x + z + 2 * c + k1) & 3, 2 * (half ^ k2 ^ side) + parity


def source_of(x, y, z, c, k):
    k1, k2 = k // 2, k % 2
    core = (y & 1) ^ (z & 1)
    return (x - z - 2 * core - k1) & 3, core, (y >> 1) ^ k2 ^ c


def piece_perm(k):
    pairs = []
    for x in range(4):
        for y in range(4):
            for z in range(4):
                for c in range(2):
                    tx, ty = target_of(x, y, z, c, k)
                    pairs.append((position(x, y, z, c), position(tx, ty, x, y // 2)))
    return pairs


def table_kernel(pz_ref, pr_ref, pu_ref, zi_ref, main_ref, upper_ref, mcol_ref, ucol_ref, *outs):
    ro_ref, rb_ref, re_ref, uo_ref, uoe_ref, ub_ref, ube_ref, zo_ref, zb_ref = outs

    def grid_of(rows, cols):
        return (
            lax.broadcasted_iota(jnp.int32, (rows, cols), 0),
            lax.broadcasted_iota(jnp.int32, (rows, cols), 1),
        )

    def taps(ref, distance):
        total = jnp.zeros(distance.shape, F32)
        for k in range(32):
            total = jnp.where(distance == k, ref[k], total)
        return total

    def left_table(value):
        h, l = split(value)
        return jnp.concatenate([h, h, l], axis=1)

    def right_table(value):
        h, l = split(value)
        return jnp.concatenate([h, l, h], axis=0)

    rows = rb_ref.shape[0]
    i, j = grid_of(rows, rows + 32)
    ro_ref[...] = left_table(taps(pr_ref, j - i) * main_ref[...] + taps(pr_ref, j - 1 - i) * upper_ref[...])
    back = taps(pr_ref, i - j + 32) * mcol_ref[...] + taps(pr_ref, i - j + 31) * ucol_ref[...]
    rb_ref[...] = left_table(back[:, 16 : 16 + rows])
    re_ref[0] = left_table(back[:16, :16])
    re_ref[1] = left_table(back[rows - 16 :, rows + 16 :])

    width = uo_ref.shape[1]
    i, j = grid_of(width, width)
    uo_ref[...] = right_table(taps(pu_ref, i + 16 - j))
    ub_ref[...] = right_table(taps(pu_ref, j - i + 16))
    a, b = i % 16, j % 16
    same = i // 16 == j // 16
    left = i < 128
    uoe_ref[...] = right_table(jnp.where(same, taps(pu_ref, jnp.where(left, a - b, a - b + 32)), 0.0))
    ube_ref[...] = right_table(jnp.where(same, taps(pu_ref, jnp.where(left, b - a + 32, b - a)), 0.0))

    depth = zi_ref.shape[0]
    i, j = grid_of(depth, depth)
    mix = jnp.dot(taps(pz_ref, j - i + 16), zi_ref[...], precision=HIGH, preferred_element_type=F32)
    zo_ref[...] = left_table(mix)
    zb_ref[...] = left_table(mix.T)


def make_tables(psf_z, psf_r, psf_u, z_interp, main, upper, rows, width):
    depth = z_interp.shape[0]
    shapes = [(rows, 3 * (rows + 32)), (rows, 3 * rows), (2, 16, 48)] + [(3 * width, width)] * 4
    shapes += [(depth, 3 * depth)] * 2
    smem = pl.BlockSpec(memory_space=pltpu.SMEM)
    vmem = pl.BlockSpec(memory_space=pltpu.VMEM)
    own = slice(16, 16 + rows)
    return pl.pallas_call(
        table_kernel,
        in_specs=[smem] * 3 + [vmem] * 5,
        out_specs=[vmem] * len(shapes),
        out_shape=[jax.ShapeDtypeStruct(s, BF) for s in shapes],
        **params(32, 3),
    )(psf_z, psf_r, psf_u, z_interp, main[None], upper[None], main[own, None], upper[own, None])


def packed(planes):
    lane = lax.broadcasted_iota(jnp.int32, planes[0][:, :128].shape, 1) // 16
    left = right = None
    for q, x in enumerate(planes):
        a, b = x[:, :128], x[:, x.shape[1] - 128 :]
        a = pltpu.roll(a, 16 * q, 1) if q else a
        b = pltpu.roll(b, (16 * q + 16) % 128, 1) if q != 7 else b
        left = a if q == 0 else jnp.where(lane == q, a, left)
        right = b if q == 0 else jnp.where(lane == q, b, right)
    return left, right


def edge_sums(left, right, table):
    h, l = split(jnp.concatenate([left, right], axis=1))
    total = dot(jnp.concatenate([h, h, l], axis=1), table)
    return total[:, :128], total[:, 128:]


def unpacked(left, right, q):
    lane = lax.broadcasted_iota(jnp.int32, left.shape, 1)
    a = pltpu.roll(left, (128 - 16 * q) % 128, 1) if q else left
    b = pltpu.roll(right, 112 - 16 * q, 1) if q != 7 else right
    return jnp.concatenate([jnp.where(lane < 16, a, 0.0), jnp.where(lane >= 112, b, 0.0)], axis=1)


def across(x, table):
    h, l = split(x)
    return dot(jnp.concatenate([h, h, l], axis=1), table)


def along(table, x):
    h, l = split(x)
    return dot(table, jnp.concatenate([h, l, h], axis=0))


def row_kernel(table_ref, up_ref, own_ref, down_ref, after_ref, out_ref, left_ref, right_ref):
    table = table_ref[...]
    planes = []
    for z in range(8):
        planes.append(along(table, jnp.concatenate([up_ref[z], own_ref[z], down_ref[z]], axis=0)))
        out_ref[z] = planes[-1]
    left_ref[0], right_ref[0] = packed(planes)


def params(mib, us):
    return dict(
        compiler_params=pltpu.CompilerParams(vmem_limit_bytes=mib * MIB),
        cost_estimate=pl.CostEstimate(flops=0, transcendentals=0, bytes_accessed=us * 3_000_000),
    )


def whole(t):
    return pl.BlockSpec(t.shape, lambda i: (0,) * t.ndim)


def row_mix(table, up, own, down, after):
    depth, rows, cols = own.shape
    block = lambda r: pl.BlockSpec((8, r, cols), lambda i: (i, 0, 0))
    edge = pl.BlockSpec((1, rows, 128), lambda i: (i, 0, 0))
    edge_shape = jax.ShapeDtypeStruct((depth // 8, rows, 128), F32)
    return pl.pallas_call(
        row_kernel,
        grid=(depth // 8,),
        in_specs=[whole(table), block(16), block(rows), block(16), ANY],
        out_specs=[block(rows), edge, edge],
        out_shape=[jax.ShapeDtypeStruct(own.shape, F32), edge_shape, edge_shape],
        **params(32, 4),
    )(table, up, own, down, after)


def blur_kernel(u_ref, e_ref, m_ref, left_ref, right_ref, x_ref, out_ref):
    depth, rows, cols = x_ref.shape
    total = across(x_ref[...].reshape(depth * rows, cols), u_ref[...]).reshape(depth, rows, cols)
    groups = depth // 8
    left, right = edge_sums(
        left_ref[...].reshape(groups * rows, 128), right_ref[...].reshape(groups * rows, 128), e_ref[...]
    )
    left, right = left.reshape(groups, rows, 128), right.reshape(groups, rows, 128)
    extra = [unpacked(left[g], right[g], q) for g in range(groups) for q in range(8)]
    total = jnp.transpose(total + jnp.stack(extra), (1, 0, 2))
    table = m_ref[...]
    for r in range(rows):
        out_ref[r] = along(table, total[r])


def blur(u, e, m, left, right, x):
    depth, rows, cols = x.shape
    block = lambda d, c: pl.BlockSpec((d, 8, c), lambda i: (0, i, 0))
    return pl.pallas_call(
        blur_kernel,
        grid=(rows // 8,),
        in_specs=[whole(u), whole(e), whole(m), block(depth // 8, 128), block(depth // 8, 128), block(depth, cols)],
        out_specs=pl.BlockSpec((8, depth, cols), lambda i: (i, 0, 0)),
        out_shape=jax.ShapeDtypeStruct((rows, depth, cols), F32),
        **params(32, 8),
    )(u, e, m, left, right, x)


def ratio_kernel(place_ref, blur_ref, *refs):
    pieces, (out_ref, top_ref, bottom_ref, left_ref, right_ref) = refs[:-5], refs[-5:]
    rows = out_ref.shape[0]
    for k, piece in enumerate(pieces):
        pair, core, half = source_of(*(place_ref[a] for a in range(4)), k)
        cols = pl.ds(pl.multiple_of(half * 128, 128), 128)
        for part in range(2):
            planes = pl.ds(pl.multiple_of((pair * 2 + (core ^ part)) * 8, 8), 8)
            seen = jnp.transpose(piece[part], (1, 0, 2))
            out_ref[:, planes, cols] = seen / (blur_ref[:, planes, cols] + background)
    top_ref[...] = out_ref[:16]
    bottom_ref[...] = out_ref[rows - 16 :]
    for g in range(left_ref.shape[0]):
        left_ref[g], right_ref[g] = packed([out_ref[8 * g + q] for q in range(8)])


def ratio_of(place, blurred, pieces):
    rows, depth, cols = blurred.shape
    vmem = pl.BlockSpec(memory_space=pltpu.VMEM)
    shapes = [blurred.shape] + [(16, depth, cols)] * 2 + [(rows // 8, depth, 128)] * 2
    return pl.pallas_call(
        ratio_kernel,
        in_specs=[pl.BlockSpec(memory_space=pltpu.SMEM), vmem] + [vmem] * len(pieces),
        out_specs=[vmem] * 5,
        out_shape=[jax.ShapeDtypeStruct(s, F32) for s in shapes],
        **params(48, 7),
    )(place, blurred, *pieces)


def spread_tile(ratio, left, right, u, e, m):
    rows, depth, cols = ratio.shape
    total = across(ratio.reshape(rows * depth, cols), u).reshape(rows, depth, cols)
    left, right = edge_sums(left, right, e)
    planes = [along(m, total[q] + unpacked(left, right, q)) for q in range(rows)]
    return jnp.transpose(jnp.stack(planes), (1, 0, 2))


def own_kernel(u_ref, e_ref, m_ref, a_ref, left_ref, right_ref, x_ref, est_ref, out_ref, kept):
    step = pl.program_id(0)
    half = pl.num_programs(0) // 2

    @pl.when(step < half)
    def _():
        rows = pl.ds(pl.multiple_of(step * 8, 8), 8)
        kept[:, rows, :] = spread_tile(x_ref[...], left_ref[0], right_ref[0], u_ref[...], e_ref[...], m_ref[...])

    @pl.when(step >= half)
    def _():
        first = pl.multiple_of((step - half) * 8, 8)
        table = a_ref[...]
        for z in range(8):
            out_ref[z] = est_ref[z] * along(table, kept[first + z])


def own_update(u, e, m, a, left, right, ratio, est):
    rows, depth, cols = ratio.shape
    half = rows // 8
    early = lambda i: (jnp.minimum(i, half - 1), 0, 0)
    late = lambda i: (jnp.maximum(i - half, 0), 0, 0)
    return pl.pallas_call(
        own_kernel,
        grid=(half + depth // 8,),
        in_specs=[whole(u), whole(e), whole(m), whole(a)]
        + [pl.BlockSpec((1, depth, 128), early)] * 2
        + [pl.BlockSpec((8, depth, cols), early), pl.BlockSpec((8, rows, cols), late)],
        out_specs=pl.BlockSpec((8, rows, cols), late),
        out_shape=jax.ShapeDtypeStruct(est.shape, F32),
        scratch_shapes=[pltpu.VMEM(est.shape, F32)],
        **params(40, 11),
    )(u, e, m, a, left, right, ratio, est)


def edge_kernel(u_ref, e_ref, m_ref, a_ref, above_ref, below_ref, up_ref, down_ref, est_ref, part_ref, out_ref, kept):
    side, step = pl.program_id(0), pl.program_id(1)
    rows = pl.ds(pl.multiple_of(step * 8, 8), 8)
    for s, x_ref, c_ref in ((0, up_ref, above_ref), (1, down_ref, below_ref)):

        @pl.when(side == s)
        def _(x_ref=x_ref, c_ref=c_ref):
            kept[:, rows, :] = spread_tile(x_ref[...], c_ref[0, 0], c_ref[1, 0], u_ref[...], e_ref[...], m_ref[...])

    @pl.when(step == 1)
    def _():
        table = a_ref[0]
        for z in range(est_ref.shape[0]):
            out_ref[z] = part_ref[z] + est_ref[z] * along(table, kept[z])


def edge_update(u, e, m, a, above, below, up, down, est, part):
    depth, rows, cols = est.shape
    step = rows // 16 - 1
    tile = pl.BlockSpec((depth, 16, cols), lambda s, i: (0, s * step, 0))
    fixed = lambda t: pl.BlockSpec(t.shape, lambda s, i: (0,) * t.ndim)
    first, second = lambda s, i: jnp.maximum(i, s), lambda s, i: i * s
    return pl.pallas_call(
        edge_kernel,
        grid=(2, 2),
        in_specs=[fixed(u), fixed(e), fixed(m), pl.BlockSpec((1, 16, 48), lambda s, i: (s, 0, 0))]
        + [pl.BlockSpec((2, 1, depth, 128), lambda s, i, at=at: (0, at(s, i), 0, 0)) for at in (first, second)]
        + [pl.BlockSpec((8, depth, cols), lambda s, i, at=at: (at(s, i), 0, 0)) for at in (first, second)]
        + [tile, tile],
        out_specs=tile,
        out_shape=jax.ShapeDtypeStruct(est.shape, F32),
        scratch_shapes=[pltpu.VMEM((depth, 16, cols), F32)],
        input_output_aliases={9: 0},
        **params(40, 6),
    )(u, e, m, a, above, below, up, down, est, part)


def send(x, axis, d):
    return lax.ppermute(x, AXES, shift_perm(axis, d))


def column_edges(left, right):
    return send(right, "gy", 1), send(left, "gy", -1)


ANY = pl.BlockSpec(memory_space=pl.ANY)
SMEM = pl.BlockSpec(memory_space=pltpu.SMEM)


def run_copies(pairs, sems):
    copies = [pltpu.make_async_copy(src, dst, sems.at[n]) for n, (src, dst) in enumerate(pairs)]
    for copy in copies:
        copy.start()
    for copy in copies:
        copy.wait()


def copy_call(body, count, shapes, inputs, us):
    return pl.pallas_call(
        body,
        in_specs=[SMEM] + [ANY] * (len(inputs) - 1),
        out_specs=[ANY] * len(shapes),
        out_shape=[jax.ShapeDtypeStruct(s, F32) for s in shapes],
        scratch_shapes=[pltpu.SemaphoreType.DMA((count,))],
        **params(56, us),
    )(*inputs)


def row_ends(place, est):
    def body(place_ref, est_ref, top_ref, bottom_ref, sems):
        rows = est_ref.shape[1]
        pairs = [(est_ref.at[:, :16], top_ref), (est_ref.at[:, rows - 16 :], bottom_ref)]
        run_copies(pairs, sems)

    depth, _, cols = est.shape
    return copy_call(body, 2, [(depth, 16, cols)] * 2, (place, est), 2)


def far_half(place, measured, rows):
    def body(place_ref, measured_ref, out_ref, sems):
        other = 1 - (place_ref[3] ^ (place_ref[0] & 1))
        run_copies([(measured_ref.at[:, :, other], out_ref)], sems)

    return copy_call(body, 1, [(8, 8, rows, 128)], (place, measured.reshape(8, 8, 2, rows, 128)), 2)[0]


def pieces_of(place, measured, far, rows, steps, after):
    def body(place_ref, measured_ref, far_ref, *refs):
        outs, sems = refs[len(after) : -1], refs[-1]
        pairs = []
        for k, out in zip(steps, outs):
            tx, ty = target_of(*(place_ref[a] for a in range(4)), k)
            pairs.append((measured_ref.at[:, tx * 4 + ty], out.at[0]))
            pairs.append((far_ref.at[:, tx * 2 + (ty >> 1)], out.at[1]))
        run_copies(pairs, sems)

    inputs = (place, measured.reshape(8, 16, rows, 128), far, *after)
    return copy_call(body, 2 * len(steps), [(2, 8, rows, 128)] * len(steps), inputs, 3)


def diagonal_windows(r_interp, gx, rows):
    total = r_interp.shape[0]
    first = jnp.clip(gx * rows - 64, 0, total - 192)
    band = lax.dynamic_slice(r_interp, (first, 0), (192, total))
    i = lax.broadcasted_iota(jnp.int32, (192, total), 0) + first
    j = lax.broadcasted_iota(jnp.int32, (192, total), 1)
    main = jnp.sum(jnp.where(i == j, band, 0.0), axis=0)
    upper = jnp.sum(jnp.where(i + 1 == j, band, 0.0), axis=0)
    window = lambda v: lax.dynamic_slice(jnp.pad(v, (16, 16)), (gx * rows,), (rows + 32,))
    return window(main), window(upper)


def forward(tables, up, estimate, down, column_edges, after):
    mixed, left, right = row_mix(tables[0], up, estimate, down, after)
    return blur(tables[3], tables[4], tables[7], *column_edges(left, right), mixed)


def backward(tables, ratio, top, bottom, left, right, estimate, column_edges, row_edges):
    rb, re, ub, ube, zb = tables[1], tables[2], tables[5], tables[6], tables[8]
    up, down = row_edges(top, bottom)
    left, right = column_edges(left, right)
    groups = left.shape[0]
    both = jnp.stack([left, right])
    above, below = row_edges(both[:, :2], both[:, groups - 2 :])
    part = own_update(ub, ube, zb, rb, left, right, ratio, estimate)
    return edge_update(ub, ube, zb, re, above, below, up, down, estimate, part)


def shards(estimate, measured, z_interp, r_interp, psf_z, psf_r, psf_u):
    depth, rows, width = estimate.shape
    gx, gy = lax.axis_index("gx"), lax.axis_index("gy")
    place = jnp.stack([gx // 4, gx % 4, gy // 2, gy % 2]).astype(jnp.int32)
    row_edges = lambda top, bottom: (send(bottom, "gx", 1), send(top, "gx", -1))
    up, down = row_edges(*row_ends(place, estimate))
    far = lax.ppermute(far_half(place, measured, rows), AXES, core_swap())
    main, upper = diagonal_windows(r_interp, gx, rows)
    tables = make_tables(psf_z, psf_r, psf_u, z_interp, main, upper, rows, width)
    ship = lambda parts, steps: [lax.ppermute(p, AXES, piece_perm(k)) for p, k in zip(parts, steps)]
    early, late = range(6), range(6, 8)
    pieces = ship(pieces_of(place, measured, far, rows, early, ()), early)
    blurred = forward(tables, up, estimate, down, column_edges, pieces[0])
    pieces += ship(pieces_of(place, measured, far, rows, late, (blurred,)), late)
    ratio, top, bottom, left, right = ratio_of(place, blurred, pieces)
    return backward(tables, ratio, top, bottom, left, right, estimate, column_edges, row_edges)


def solution(mesh):
    in_specs = (P(None, "gx", "gy"), P("gy", None, "gx"), P(), P(), P(), P(), P())
    out_specs = P(None, "gx", "gy")
    return jax.shard_map(shards, mesh=mesh, in_specs=in_specs, out_specs=out_specs, check_vma=False)
```

time: 230 us -> 438 us (1.90)
  the two profiles are of different devices: /device:TPU:33 before, /device:TPU:69 now
where the time goes in v3:
time: 438 us; the launch traced here: 434 us
  Pallas kernels  300 us (68%)
  starting transfers between devices  90.5 us (21%)
  waiting for transfers between devices  33.8 us (8%)
  local copies, waits for them, and re-layouts  6.84 us (2%)
    pallas_call x4, Pallas kernels, copy_call(): pl.pallas_call(body, in_specs=[SMEM] + [ANY] * (len(inputs) - 1), out_spe...  261 us
    ppermute x8, starting transfers between devices, shards(): lax.ppermute(p, AXES, piece_perm(k))  46.9 us
    ppermute x10, starting transfers between devices, send(): return lax.ppermute(x, AXES, shift_perm(axis, d))  42.9 us
    ppermute x8, waiting for transfers between devices, shards(): lax.ppermute(p, AXES, piece_perm(k))  25.2 us
    pallas_call x1, Pallas kernels, own_update(): pl.pallas_call(own_kernel, grid=(half + depth // 8,), in_specs=[whole(u),...  11.2 us
  transfers between devices with their start and end apart: 19, of which 6 were waited for; matrix products, arithmetic and copies ran while one was open for 0% of the time, Pallas kernels for 51%

profile of v3, /device:TPU:69, one launch (start us, length us, event | category | flops | bytes accessed | tf_op | source)
XLA Modules:
  0.0 433.8 jit_solution(2942343647106777500)
XLA Ops:
  0.6 65.3 %shard_map.75 = f32[8,8,64,128]{3,2,1,0:T(8,128)} custom-call(s32[4]{0:T(128)} %pad_add_fusion.place_ref, f32[8,8,2,64,128]{4,3,2,1,0:T(8,128)} %bitcast.18), custom_call_target="tpu_custom_call" | custom-call | bytes 6000000 | tf_op jit(solution)/shard_map/pallas_call | solution.py:362
  66.7 65.3 %shard_map.74 = (f32[64,16,256]{2,1,0:T(8,128)}, f32[64,16,256]{2,1,0:T(8,128)}) custom-call(s32[4]{0:T(128)} %pad_add_fusion.place_ref, f32[64,64,256]{2,1,0:T(8,128)} %est_ref.5), custom_call_target="tpu_custom_call" | custom-call | bytes 6000000 | tf_op jit(solution)/shard_map/pallas_call | solution.py:362
  132.0 3.3 collective-permute-start
  135.4 4.2 collective-permute-start.1
  141.1 97.2 %shard_map.76 = (f32[2,8,64,128]{3,2,1,0:T(8,128)}, f32[2,8,64,128]{3,2,1,0:T(8,128)}, f32[2,8,64,128]{3,2,1,0:T(8,128)}, f32[2,8,64,128]{3,2,1,0:T(8,128)}, f32...) custom-call(s32[4]{0:T(128)} %pad_add_fusion.place_ref, f32[8,16,64,128]{3,2,1,0:T(8,128)} %bitcast.19, ...), custom_call_target="tpu_custom_call" | custom-call | bytes 9000000 | tf_op jit(solution)/shard_map/pallas_call | solution.py:362
  240.3 3.0 collective-permute-start.6
  243.3 5.8 %collective-permute-start.7 = (f32[2,8,64,128]{3,2,1,0:T(8,128)}, f32[2,8,64,128]{3,2,1,0:T(8,128)}, u32[]{:S(2)}, u32[]{:S(2)}) collective-permute-start(f32[2,8,64,128]{3,2,1,0:T(8,128)} %get-tuple-element.47), channel_id=1, source_target_pairs={{0,32},{1,104},{2,64},{3,8},{4,96},{5,40},{6,0},{7,72},{8,48},{9,1... | collective-permute-start | bytes 1572872 | tf_op jit(solution)/shard_map/ppermute | solution.py:441
  249.5 2.8 shard_map.73
  252.3 11.2 %collective-permute-done.3.after_ref.refs_0_ = f32[2,8,64,128]{3,2,1,0:T(8,128)S(1)} collective-permute-done((f32[2,8,64,128]{3,2,1,0:T(8,128)}, f32[2,8,64,128]{3,2,1,0:T(8,128)S(1)}, u32[]{:S(2)}, u32[]{:S(2)}) %collective-permute-start.3) | collective-permute-done | bytes 524320 | tf_op jit(solution)/shard_map/ppermute | solution.py:441
  265.6 3.8 shard_map.77
  271.3 7.0 %collective-permute-start.5 = (f32[8,64,128]{2,1,0:T(8,128)S(1)}, f32[8,64,128]{2,1,0:T(8,128)S(1)}, u32[]{:S(2)}, u32[]{:S(2)}) collective-permute-start(f32[8,64,128]{2,1,0:T(8,128)S(1)} %get-tuple-element.44), channel_id=1, source_target_pairs={{1,0},{2,1},{3,2},{4,3},{5,4},{6,5},{7,6},{9,8},{10,9},{11,10},{12... | collective-permute-start | bytes 786440 | tf_op jit(solution)/shard_map/ppermute | solution.py:342
  284.6 5.6 %collective-permute-start.10 = (f32[2,8,64,128]{3,2,1,0:T(8,128)S(1)}, f32[2,8,64,128]{3,2,1,0:T(8,128)S(1)}, u32[]{:S(2)}, u32[]{:S(2)}) collective-permute-start(f32[2,8,64,128]{3,2,1,0:T(8,128)S(1)} %copy-done.9), channel_id=1, source_target_pairs={{0,80},{1,24},{2,112},{3,56},{4,16},{5,88},{6,48},{7,120},{8,64},{... | collective-permute-start | bytes 1572872 | tf_op jit(solution)/shard_map/ppermute | solution.py:441
  290.2 7.5 %shard_map.78.refs_0_.blur_ref = f32[64,64,256]{2,1,0:T(8,128)S(1)} custom-call(bf16[768,256]{1,0:T(8,128)(2,1)S(1)} %get-tuple-element.36.u_ref, bf16[768,256]{1,0:T(8,128)(2,1)S(1)} %get-tuple-element.37.e_ref, bf16[64,192]{1,0:T(8,128)(2,1)S(1)} %get-tuple-element.38.m_ref, f32[8,64,128]{2,1,0:T(8,128)S(1)} %collective-permute-done.4.left_ref, ...), custom_call_target="tpu_custom_call" | custom-call | bytes 24000000 | tf_op jit(solution)/shard_map/pallas_call | solution.py:222
  299.7 33.7 %shard_map.79 = (f32[2,8,64,128]{3,2,1,0:T(8,128)}, f32[2,8,64,128]{3,2,1,0:T(8,128)}) custom-call(s32[4]{0:T(128)} %pad_add_fusion.place_ref, f32[8,16,64,128]{3,2,1,0:T(8,128)} %bitcast.20, f32[8,8,64,128]{3,2,1,0:T(8,128)} %collective-permute-done.2.far_ref, f32[64,64,256]{2,1,0:T(8,128)} %copy-done.2), custom_call_target="tpu_custom_call" | custom-call | bytes 9000000 | tf_op jit(solution)/shard_map/pallas_call | solution.py:362
  333.5 24.5 %collective-permute-start.11 = (f32[2,8,64,128]{3,2,1,0:T(8,128)}, f32[2,8,64,128]{3,2,1,0:T(8,128)S(1)}, u32[]{:S(2)}, u32[]{:S(2)}) collective-permute-start(f32[2,8,64,128]{3,2,1,0:T(8,128)} %get-tuple-element.51), channel_id=1, source_target_pairs={{0,96},{1,40},{2,0},{3,72},{4,32},{5,104},{6,64},{7,8},{8,112},{9,... | collective-permute-start | bytes 1572872 | tf_op jit(solution)/shard_map/ppermute | solution.py:441
  360.3 7.0 %collective-permute-done.11.refs_6_ = f32[2,8,64,128]{3,2,1,0:T(8,128)S(1)} collective-permute-done((f32[2,8,64,128]{3,2,1,0:T(8,128)}, f32[2,8,64,128]{3,2,1,0:T(8,128)S(1)}, u32[]{:S(2)}, u32[]{:S(2)}) %collective-permute-start.11) | collective-permute-done | bytes 524320 | tf_op jit(solution)/shard_map/ppermute | solution.py:441
  367.2 7.1 %collective-permute-done.12.refs_7_ = f32[2,8,64,128]{3,2,1,0:T(8,128)S(1)} collective-permute-done((f32[2,8,64,128]{3,2,1,0:T(8,128)}, f32[2,8,64,128]{3,2,1,0:T(8,128)S(1)}, u32[]{:S(2)}, u32[]{:S(2)}) %collective-permute-start.12) | collective-permute-done | bytes 524320 | tf_op jit(solution)/shard_map/ppermute | solution.py:441
  374.3 6.9 %shard_map.80 = (f32[64,64,256]{2,1,0:T(8,128)}, f32[16,64,256]{2,1,0:T(8,128)S(1)}, f32[16,64,256]{2,1,0:T(8,128)}, f32[8,64,128]{2,1,0:T(8,128)S(1)}, f32[8,64,128]{2,1,0:T(8,128)S(1)}) custom-call(s32[4]{0:T(128)S(1)} %copy-done.5, f32[64,64,256]{2,1,0:T(8,128)} %copy-done.2, f32[2,8,64,128]{3,2,1,0:T(8,128)S(1)} %collective-permute-done.3.after_ref.refs_0_, ...), custom_call_target="tpu_custom_call" | custom-call | bytes 21000000 | tf_op jit(solution)/shard_map/pallas_call | solution.py:252
  383.2 5.5 %collective-permute-start.18 = (f32[16,64,256]{2,1,0:T(8,128)S(1)}, f32[16,64,256]{2,1,0:T(8,128)S(1)}, u32[]{:S(2)}, u32[]{:S(2)}) collective-permute-start(f32[16,64,256]{2,1,0:T(8,128)S(1)} %get-tuple-element.56), channel_id=1, source_target_pairs={{8,0},{9,1},{10,2},{11,3},{12,4},{13,5},{14,6},{15,7},{16,8},{17,9... | collective-permute-start | bytes 3145736 | tf_op jit(solution)/shard_map/ppermute | solution.py:342
  388.6 11.9 %collective-permute-start.13 = (f32[8,64,128]{2,1,0:T(8,128)S(1)}, f32[8,64,128]{2,1,0:T(8,128)S(1)}, u32[]{:S(2)}, u32[]{:S(2)}) collective-permute-start(f32[8,64,128]{2,1,0:T(8,128)S(1)} %get-tuple-element.53), channel_id=1, source_target_pairs={{0,1},{1,2},{2,3},{3,4},{4,5},{5,6},{6,7},{8,9},{9,10},{10,11},{11... | collective-permute-start | bytes 786440 | tf_op jit(solution)/shard_map/ppermute | solution.py:342
  403.8 4.7 %collective-permute-done.14.right_ref = f32[8,64,128]{2,1,0:T(8,128)S(1)} collective-permute-done((f32[8,64,128]{2,1,0:T(8,128)S(1)}, f32[8,64,128]{2,1,0:T(8,128)S(1)}, u32[]{:S(2)}, u32[]{:S(2)}) %collective-permute-start.14) | collective-permute-done | bytes 262176 | tf_op jit(solution)/shard_map/ppermute | solution.py:342
  410.5 3.4 collective-permute-start.15
  416.0 11.2 %shard_map.81.part_ref = f32[64,64,256]{2,1,0:T(8,128)} custom-call(bf16[768,256]{1,0:T(8,128)(2,1)S(1)} %get-tuple-element.32.u_ref, bf16[768,256]{1,0:T(8,128)(2,1)S(1)} %get-tuple-element.33.e_ref, bf16[64,192]{1,0:T(8,128)(2,1)S(1)} %get-tuple-element.34.m_ref, bf16[64,192]{1,0:T(8,128)(2,1)S(1)} %get-tuple-element.57.a_ref, ...), custom_call_target="tpu_custom_call" | custom-call | bytes 33000000 | tf_op jit(solution)/shard_map/pallas_call | solution.py:291
  427.2 6.6 %shard_map.82 = f32[64,64,256]{2,1,0:T(8,128)} custom-call(bf16[768,256]{1,0:T(8,128)(2,1)S(1)} %get-tuple-element.32.u_ref, bf16[768,256]{1,0:T(8,128)(2,1)S(1)} %get-tuple-element.33.e_ref, bf16[64,192]{1,0:T(8,128)(2,1)S(1)} %get-tuple-element.34.m_ref, bf16[2,16,48]{2,1,0:T(8,128)(2,1)S(1)} %get-tuple-element.35.a_ref, ...), custom_call_target="tpu_custom_call", output_to_operand_aliasing={{}: (9, {})} | custom-call | bytes 18000000 | tf_op jit(solution)/shard_map/pallas_call | solution.py:326
  (54 shorter events, 29.1 us)
Async XLA Ops:
  65.9 75.2 %collective-permute-start.2 = (f32[8,8,64,128]{3,2,1,0:T(8,128)}, f32[8,8,64,128]{3,2,1,0:T(8,128)}, u32[]{:S(2)}, u32[]{:S(2)}) collective-permute-start(f32[8,8,64,128]{3,2,1,0:T(8,128)} %shard_map.75), channel_id=1, source_target_pairs={{0,1},{1,0},{2,3},{3,2},{4,5},{5,4},{6,7},{7,6},{8,9},{9,8},{10,11... | collective-permute-start | bytes 6291464 | tf_op jit(solution)/shard_map/ppermute | solution.py:438
  132.0 117.4 %copy-start.4 = (f32[64,64]{1,0:T(8,128)S(1)}, f32[64,64]{1,0:T(8,128)}, u32[]{:S(2)}) copy-start(f32[64,64]{1,0:T(8,128)} %zi_ref.1) | copy-start | bytes 49156
  132.0 117.4 %copy-start.6 = (f32[32]{0:T(128)S(1)}, f32[32]{0:T(128)}, u32[]{:S(2)}) copy-start(f32[32]{0:T(128)} %pz_ref.1) | copy-start | bytes 388
  132.0 117.4 %copy-start.7 = (f32[32]{0:T(128)S(1)}, f32[32]{0:T(128)}, u32[]{:S(2)}) copy-start(f32[32]{0:T(128)} %pr_ref.1) | copy-start | bytes 388
  132.0 117.4 %copy-start.8 = (f32[32]{0:T(128)S(1)}, f32[32]{0:T(128)}, u32[]{:S(2)}) copy-start(f32[32]{0:T(128)} %pu_ref.1) | copy-start | bytes 388
  132.0 120.2 %collective-permute-start = (f32[64,16,256]{2,1,0:T(8,128)}, f32[64,16,256]{2,1,0:T(8,128)S(1)}, u32[]{:S(2)}, u32[]{:S(2)}) collective-permute-start(f32[64,16,256]{2,1,0:T(8,128)} %get-tuple-element.40), channel_id=1, source_target_pairs={{0,8},{1,9},{2,10},{3,11},{4,12},{5,13},{6,14},{7,15},{8,16},{9,17... | collective-permute-start | bytes 3145736 | tf_op jit(solution)/shard_map/ppermute | solution.py:342
  135.4 116.9 %collective-permute-start.1 = (f32[64,16,256]{2,1,0:T(8,128)}, f32[64,16,256]{2,1,0:T(8,128)S(1)}, u32[]{:S(2)}, u32[]{:S(2)}) collective-permute-start(f32[64,16,256]{2,1,0:T(8,128)} %get-tuple-element.41), channel_id=1, source_target_pairs={{8,0},{9,1},{10,2},{11,3},{12,4},{13,5},{14,6},{15,7},{16,8},{17,9... | collective-permute-start | bytes 3145736 | tf_op jit(solution)/shard_map/ppermute | solution.py:342
  238.3 25.2 %collective-permute-start.3 = (f32[2,8,64,128]{3,2,1,0:T(8,128)}, f32[2,8,64,128]{3,2,1,0:T(8,128)S(1)}, u32[]{:S(2)}, u32[]{:S(2)}) collective-permute-start(f32[2,8,64,128]{3,2,1,0:T(8,128)} %get-tuple-element.42), channel_id=1, source_target_pairs={{0,0},{1,72},{2,32},{3,104},{4,64},{5,8},{6,96},{7,40},{8,16},{9,8... | collective-permute-start | bytes 1572872 | tf_op jit(solution)/shard_map/ppermute | solution.py:441
  240.3 93.2 %collective-permute-start.6 = (f32[2,8,64,128]{3,2,1,0:T(8,128)}, f32[2,8,64,128]{3,2,1,0:T(8,128)S(1)}, u32[]{:S(2)}, u32[]{:S(2)}) collective-permute-start(f32[2,8,64,128]{3,2,1,0:T(8,128)} %get-tuple-element.46), channel_id=1, source_target_pairs={{0,16},{1,88},{2,48},{3,120},{4,80},{5,24},{6,112},{7,56},{8,0},{9... | collective-permute-start | bytes 1572872 | tf_op jit(solution)/shard_map/ppermute | solution.py:441
  243.3 114.7 %collective-permute-start.7 = (f32[2,8,64,128]{3,2,1,0:T(8,128)}, f32[2,8,64,128]{3,2,1,0:T(8,128)}, u32[]{:S(2)}, u32[]{:S(2)}) collective-permute-start(f32[2,8,64,128]{3,2,1,0:T(8,128)} %get-tuple-element.47), channel_id=1, source_target_pairs={{0,32},{1,104},{2,64},{3,8},{4,96},{5,40},{6,0},{7,72},{8,48},{9,1... | collective-permute-start | bytes 1572872 | tf_op jit(solution)/shard_map/ppermute | solution.py:441
  269.4 10.8 %collective-permute-start.4 = (f32[8,64,128]{2,1,0:T(8,128)S(1)}, f32[8,64,128]{2,1,0:T(8,128)S(1)}, u32[]{:S(2)}, u32[]{:S(2)}) collective-permute-start(f32[8,64,128]{2,1,0:T(8,128)S(1)} %get-tuple-element.43), channel_id=1, source_target_pairs={{0,1},{1,2},{2,3},{3,4},{4,5},{5,6},{6,7},{8,9},{9,10},{10,11},{11... | collective-permute-start | bytes 786440 | tf_op jit(solution)/shard_map/ppermute | solution.py:342
  271.3 13.3 %collective-permute-start.5 = (f32[8,64,128]{2,1,0:T(8,128)S(1)}, f32[8,64,128]{2,1,0:T(8,128)S(1)}, u32[]{:S(2)}, u32[]{:S(2)}) collective-permute-start(f32[8,64,128]{2,1,0:T(8,128)S(1)} %get-tuple-element.44), channel_id=1, source_target_pairs={{1,0},{2,1},{3,2},{4,3},{5,4},{6,5},{7,6},{9,8},{10,9},{11,10},{12... | collective-permute-start | bytes 786440 | tf_op jit(solution)/shard_map/ppermute | solution.py:342
  278.3 81.9 %collective-permute-start.8 = (f32[2,8,64,128]{3,2,1,0:T(8,128)}, f32[2,8,64,128]{3,2,1,0:T(8,128)S(1)}, u32[]{:S(2)}, u32[]{:S(2)}) collective-permute-start(f32[2,8,64,128]{3,2,1,0:T(8,128)} %get-tuple-element.48), channel_id=1, source_target_pairs={{0,48},{1,120},{2,80},{3,24},{4,112},{5,56},{6,16},{7,88},{8,32},{... | collective-permute-start | bytes 1572872 | tf_op jit(solution)/shard_map/ppermute | solution.py:441
  280.2 80.0 %collective-permute-start.9 = (f32[2,8,64,128]{3,2,1,0:T(8,128)}, f32[2,8,64,128]{3,2,1,0:T(8,128)S(1)}, u32[]{:S(2)}, u32[]{:S(2)}) collective-permute-start(f32[2,8,64,128]{3,2,1,0:T(8,128)} %get-tuple-element.49), channel_id=1, source_target_pairs={{0,64},{1,8},{2,96},{3,40},{4,0},{5,72},{6,32},{7,104},{8,80},{9,2... | collective-permute-start | bytes 1572872 | tf_op jit(solution)/shard_map/ppermute | solution.py:441
  284.6 75.6 %collective-permute-start.10 = (f32[2,8,64,128]{3,2,1,0:T(8,128)S(1)}, f32[2,8,64,128]{3,2,1,0:T(8,128)S(1)}, u32[]{:S(2)}, u32[]{:S(2)}) collective-permute-start(f32[2,8,64,128]{3,2,1,0:T(8,128)S(1)} %copy-done.9), channel_id=1, source_target_pairs={{0,80},{1,24},{2,112},{3,56},{4,16},{5,88},{6,48},{7,120},{8,64},{... | collective-permute-start | bytes 1572872 | tf_op jit(solution)/shard_map/ppermute | solution.py:441
  299.7 74.6 %copy-start.5 = (s32[4]{0:T(128)S(1)}, s32[4]{0:T(128)}, u32[]{:S(2)}) copy-start(s32[4]{0:T(128)} %pad_add_fusion.place_ref) | copy-start | bytes 52
  333.5 33.8 %collective-permute-start.11 = (f32[2,8,64,128]{3,2,1,0:T(8,128)}, f32[2,8,64,128]{3,2,1,0:T(8,128)S(1)}, u32[]{:S(2)}, u32[]{:S(2)}) collective-permute-start(f32[2,8,64,128]{3,2,1,0:T(8,128)} %get-tuple-element.51), channel_id=1, source_target_pairs={{0,96},{1,40},{2,0},{3,72},{4,32},{5,104},{6,64},{7,8},{8,112},{9,... | collective-permute-start | bytes 1572872 | tf_op jit(solution)/shard_map/ppermute | solution.py:441
  358.0 16.3 %collective-permute-start.12 = (f32[2,8,64,128]{3,2,1,0:T(8,128)}, f32[2,8,64,128]{3,2,1,0:T(8,128)S(1)}, u32[]{:S(2)}, u32[]{:S(2)}) collective-permute-start(f32[2,8,64,128]{3,2,1,0:T(8,128)} %get-tuple-element.52), channel_id=1, source_target_pairs={{0,112},{1,56},{2,16},{3,88},{4,48},{5,120},{6,80},{7,24},{8,96},{... | collective-permute-start | bytes 1572872 | tf_op jit(solution)/shard_map/ppermute | solution.py:441
  381.2 46.0 %collective-permute-start.17 = (f32[16,64,256]{2,1,0:T(8,128)}, f32[16,64,256]{2,1,0:T(8,128)S(1)}, u32[]{:S(2)}, u32[]{:S(2)}) collective-permute-start(f32[16,64,256]{2,1,0:T(8,128)} %get-tuple-element.55), channel_id=1, source_target_pairs={{0,8},{1,9},{2,10},{3,11},{4,12},{5,13},{6,14},{7,15},{8,16},{9,17... | collective-permute-start | bytes 3145736 | tf_op jit(solution)/shard_map/ppermute | solution.py:342
  383.2 44.1 %collective-permute-start.18 = (f32[16,64,256]{2,1,0:T(8,128)S(1)}, f32[16,64,256]{2,1,0:T(8,128)S(1)}, u32[]{:S(2)}, u32[]{:S(2)}) collective-permute-start(f32[16,64,256]{2,1,0:T(8,128)S(1)} %get-tuple-element.56), channel_id=1, source_target_pairs={{8,0},{9,1},{10,2},{11,3},{12,4},{13,5},{14,6},{15,7},{16,8},{17,9... | collective-permute-start | bytes 3145736 | tf_op jit(solution)/shard_map/ppermute | solution.py:342
  388.6 15.2 %collective-permute-start.13 = (f32[8,64,128]{2,1,0:T(8,128)S(1)}, f32[8,64,128]{2,1,0:T(8,128)S(1)}, u32[]{:S(2)}, u32[]{:S(2)}) collective-permute-start(f32[8,64,128]{2,1,0:T(8,128)S(1)} %get-tuple-element.53), channel_id=1, source_target_pairs={{0,1},{1,2},{2,3},{3,4},{4,5},{5,6},{6,7},{8,9},{9,10},{10,11},{11... | collective-permute-start | bytes 786440 | tf_op jit(solution)/shard_map/ppermute | solution.py:342
  400.5 8.0 %collective-permute-start.14 = (f32[8,64,128]{2,1,0:T(8,128)S(1)}, f32[8,64,128]{2,1,0:T(8,128)S(1)}, u32[]{:S(2)}, u32[]{:S(2)}) collective-permute-start(f32[8,64,128]{2,1,0:T(8,128)S(1)} %get-tuple-element.54), channel_id=1, source_target_pairs={{1,0},{2,1},{3,2},{4,3},{5,4},{6,5},{7,6},{9,8},{10,9},{11,10},{12... | collective-permute-start | bytes 786440 | tf_op jit(solution)/shard_map/ppermute | solution.py:342
  408.6 18.7 %collective-permute-start.16 = (f32[2,2,64,128]{3,2,1,0:T(8,128)S(1)}, f32[2,2,64,128]{3,2,1,0:T(8,128)S(1)}, u32[]{:S(2)}, u32[]{:S(2)}) collective-permute-start(f32[2,2,64,128]{3,2,1,0:T(8,128)S(1)} %get-tuple-element.61), channel_id=1, source_target_pairs={{8,0},{9,1},{10,2},{11,3},{12,4},{13,5},{14,6},{15,7},{16,8},{17,9... | collective-permute-start | bytes 393224 | tf_op jit(solution)/shard_map/ppermute | solution.py:342
  410.5 16.8 %collective-permute-start.15 = (f32[2,2,64,128]{3,2,1,0:T(8,128)S(1)}, f32[2,2,64,128]{3,2,1,0:T(8,128)S(1)}, u32[]{:S(2)}, u32[]{:S(2)}) collective-permute-start(f32[2,2,64,128]{3,2,1,0:T(8,128)S(1)} %get-tuple-element.62), channel_id=1, source_target_pairs={{0,8},{1,9},{2,10},{3,11},{4,12},{5,13},{6,14},{7,15},{8,16},{9,17... | collective-permute-start | bytes 393224 | tf_op jit(solution)/shard_map/ppermute | solution.py:342
  (5 other events, 81.2 us)

commit v4 on v3

--- a/solution.py
+++ b/solution.py
@@ -230,8 +230,7 @@
 
 
 def ratio_kernel(place_ref, blur_ref, *refs):
-    pieces, (out_ref, top_ref, bottom_ref, left_ref, right_ref) = refs[:-5], refs[-5:]
-    rows = out_ref.shape[0]
+    pieces, (out_ref, left_ref, right_ref) = refs[:-3], refs[-3:]
     for k, piece in enumerate(pieces):
         pair, core, half = source_of(*(place_ref[a] for a in range(4)), k)
         cols = pl.ds(pl.multiple_of(half * 128, 128), 128)
@@ -239,8 +238,6 @@
             planes = pl.ds(pl.multiple_of((pair * 2 + (core ^ part)) * 8, 8), 8)
             seen = jnp.transpose(piece[part], (1, 0, 2))
             out_ref[:, planes, cols] = seen / (blur_ref[:, planes, cols] + background)
-    top_ref[...] = out_ref[:16]
-    bottom_ref[...] = out_ref[rows - 16 :]
     for g in range(left_ref.shape[0]):
         left_ref[g], right_ref[g] = packed([out_ref[8 * g + q] for q in range(8)])
 
@@ -248,11 +245,11 @@
 def ratio_of(place, blurred, pieces):
     rows, depth, cols = blurred.shape
     vmem = pl.BlockSpec(memory_space=pltpu.VMEM)
-    shapes = [blurred.shape] + [(16, depth, cols)] * 2 + [(rows // 8, depth, 128)] * 2
+    shapes = [blurred.shape] + [(rows // 8, depth, 128)] * 2
     return pl.pallas_call(
         ratio_kernel,
         in_specs=[pl.BlockSpec(memory_space=pltpu.SMEM), vmem] + [vmem] * len(pieces),
-        out_specs=[vmem] * 5,
+        out_specs=[vmem] * 3,
         out_shape=[jax.ShapeDtypeStruct(s, F32) for s in shapes],
         **params(48, 7),
     )(place, blurred, *pieces)
@@ -266,76 +263,99 @@
     return jnp.transpose(jnp.stack(planes), (1, 0, 2))
 
 
-def own_kernel(u_ref, e_ref, m_ref, a_ref, left_ref, right_ref, x_ref, est_ref, out_ref, kept):
+def ends_kernel(u_ref, e_ref, m_ref, left_ref, right_ref, x_ref, top_ref, bottom_ref):
     step = pl.program_id(0)
-    half = pl.num_programs(0) // 2
-
-    @pl.when(step < half)
+    tile = spread_tile(x_ref[...], left_ref[0], right_ref[0], u_ref[...], e_ref[...], m_ref[...])
+    for s, ref in ((0, top_ref), (2, bottom_ref)):
+        for t in range(2):
+
+            @pl.when(step == s + t)
+            def _(ref=ref, t=t):
+                ref[:, 8 * t : 8 * t + 8, :] = tile
+
+
+def spread_ends(u, e, m, left, right, ratio):
+    rows, depth, cols = ratio.shape
+    at = lambda i: (jnp.where(i < 2, i, rows // 8 - 4 + i), 0, 0)
+    end = pl.BlockSpec((depth, 16, cols), lambda i: (0, 0, 0))
+    return pl.pallas_call(
+        ends_kernel,
+        grid=(4,),
+        in_specs=[whole(u), whole(e), whole(m)]
+        + [pl.BlockSpec((1, depth, 128), at)] * 2
+        + [pl.BlockSpec((8, depth, cols), at)],
+        out_specs=[end, end],
+        out_shape=[jax.ShapeDtypeStruct((depth, 16, cols), F32)] * 2,
+        **params(40, 4),
+    )(u, e, m, left, right, ratio)
+
+
+def own_kernel(u_ref, e_ref, m_ref, a_ref, left_ref, right_ref, x_ref, top_ref, bottom_ref, est_ref, out_ref, kept):
+    step = pl.program_id(0)
+    inner = kept.shape[1] // 8
+
+    @pl.when(step < inner)
     def _():
         rows = pl.ds(pl.multiple_of(step * 8, 8), 8)
         kept[:, rows, :] = spread_tile(x_ref[...], left_ref[0], right_ref[0], u_ref[...], e_ref[...], m_ref[...])
 
-    @pl.when(step >= half)
+    @pl.when(step >= inner)
     def _():
-        first = pl.multiple_of((step - half) * 8, 8)
+        first = pl.multiple_of((step - inner) * 8, 8)
         table = a_ref[...]
         for z in range(8):
-            out_ref[z] = est_ref[z] * along(table, kept[first + z])
-
-
-def own_update(u, e, m, a, left, right, ratio, est):
+            x = jnp.concatenate([top_ref[z], kept[first + z], bottom_ref[z]], axis=0)
+            out_ref[z] = est_ref[z] * along(table, x)
+
+
+def own_update(u, e, m, a, left, right, ratio, top, bottom, est):
     rows, depth, cols = ratio.shape
-    half = rows // 8
-    early = lambda i: (jnp.minimum(i, half - 1), 0, 0)
-    late = lambda i: (jnp.maximum(i - half, 0), 0, 0)
+    inner = rows // 8 - 4
+    early = lambda i: (jnp.minimum(i, inner - 1) + 2, 0, 0)
+    late = lambda i: (jnp.maximum(i - inner, 0), 0, 0)
     return pl.pallas_call(
         own_kernel,
-        grid=(half + depth // 8,),
+        grid=(inner + depth // 8,),
         in_specs=[whole(u), whole(e), whole(m), whole(a)]
         + [pl.BlockSpec((1, depth, 128), early)] * 2
-        + [pl.BlockSpec((8, depth, cols), early), pl.BlockSpec((8, rows, cols), late)],
+        + [pl.BlockSpec((8, depth, cols), early)]
+        + [pl.BlockSpec((8, 16, cols), late)] * 2
+        + [pl.BlockSpec((8, rows, cols), late)],
         out_specs=pl.BlockSpec((8, rows, cols), late),
         out_shape=jax.ShapeDtypeStruct(est.shape, F32),
-        scratch_shapes=[pltpu.VMEM(est.shape, F32)],
-        **params(40, 11),
-    )(u, e, m, a, left, right, ratio, est)
-
-
-def edge_kernel(u_ref, e_ref, m_ref, a_ref, above_ref, below_ref, up_ref, down_ref, est_ref, part_ref, out_ref, kept):
-    side, step = pl.program_id(0), pl.program_id(1)
-    rows = pl.ds(pl.multiple_of(step * 8, 8), 8)
-    for s, x_ref, c_ref in ((0, up_ref, above_ref), (1, down_ref, below_ref)):
+        scratch_shapes=[pltpu.VMEM((depth, rows - 32, cols), F32)],
+        **params(40, 8),
+    )(u, e, m, a, left, right, ratio, top, bottom, est)
+
+
+def edge_kernel(a_ref, up_ref, down_ref, est_ref, part_ref, out_ref):
+    side = pl.program_id(0)
+    for s, x_ref in ((0, up_ref), (1, down_ref)):
 
         @pl.when(side == s)
-        def _(x_ref=x_ref, c_ref=c_ref):
-            kept[:, rows, :] = spread_tile(x_ref[...], c_ref[0, 0], c_ref[1, 0], u_ref[...], e_ref[...], m_ref[...])
-
-    @pl.when(step == 1)
-    def _():
-        table = a_ref[0]
-        for z in range(est_ref.shape[0]):
-            out_ref[z] = part_ref[z] + est_ref[z] * along(table, kept[z])
-
-
-def edge_update(u, e, m, a, above, below, up, down, est, part):
+        def _(x_ref=x_ref):
+            table = a_ref[0]
+            for z in range(est_ref.shape[0]):
+                out_ref[z] = part_ref[z] + est_ref[z] * along(table, x_ref[z])
+
+
+def edge_update(a, up, down, est, part):
     depth, rows, cols = est.shape
-    step = rows // 16 - 1
-    tile = pl.BlockSpec((depth, 16, cols), lambda s, i: (0, s * step, 0))
-    fixed = lambda t: pl.BlockSpec(t.shape, lambda s, i: (0,) * t.ndim)
-    first, second = lambda s, i: jnp.maximum(i, s), lambda s, i: i * s
+    step, chunk = rows // 16 - 1, 16
+    last = depth // chunk - 1
+    tile = pl.BlockSpec((chunk, 16, cols), lambda s, i: (i, s * step, 0))
     return pl.pallas_call(
         edge_kernel,
-        grid=(2, 2),
-        in_specs=[fixed(u), fixed(e), fixed(m), pl.BlockSpec((1, 16, 48), lambda s, i: (s, 0, 0))]
-        + [pl.BlockSpec((2, 1, depth, 128), lambda s, i, at=at: (0, at(s, i), 0, 0)) for at in (first, second)]
-        + [pl.BlockSpec((8, depth, cols), lambda s, i, at=at: (at(s, i), 0, 0)) for at in (first, second)]
+        grid=(2, depth // chunk),
+        in_specs=[pl.BlockSpec((1, 16, 48), lambda s, i: (s, 0, 0))]
+        + [pl.BlockSpec((chunk, 16, cols), lambda s, i: (i + (last - i) * s, 0, 0))]
+        + [pl.BlockSpec((chunk, 16, cols), lambda s, i: (i * s, 0, 0))]
         + [tile, tile],
         out_specs=tile,
         out_shape=jax.ShapeDtypeStruct(est.shape, F32),
-        scratch_shapes=[pltpu.VMEM((depth, 16, cols), F32)],
-        input_output_aliases={9: 0},
-        **params(40, 6),
-    )(u, e, m, a, above, below, up, down, est, part)
+        input_output_aliases={4: 0},
+        **params(40, 3),
+    )(a, up, down, est, part)
 
 
 def send(x, axis, d):
@@ -362,7 +382,7 @@
     return pl.pallas_call(
         body,
         in_specs=[SMEM] + [ANY] * (len(inputs) - 1),
-        out_specs=[ANY] * len(shapes),
+        out_specs=[pl.BlockSpec(memory_space=pltpu.VMEM)] * len(shapes),
         out_shape=[jax.ShapeDtypeStruct(s, F32) for s in shapes],
         scratch_shapes=[pltpu.SemaphoreType.DMA((count,))],
         **params(56, us),
@@ -418,15 +438,13 @@
     return blur(tables[3], tables[4], tables[7], *column_edges(left, right), mixed)
 
 
-def backward(tables, ratio, top, bottom, left, right, estimate, column_edges, row_edges):
+def backward(tables, ratio, left, right, estimate, column_edges, row_edges):
     rb, re, ub, ube, zb = tables[1], tables[2], tables[5], tables[6], tables[8]
+    left, right = column_edges(left, right)
+    top, bottom = spread_ends(ub, ube, zb, left, right, ratio)
     up, down = row_edges(top, bottom)
-    left, right = column_edges(left, right)
-    groups = left.shape[0]
-    both = jnp.stack([left, right])
-    above, below = row_edges(both[:, :2], both[:, groups - 2 :])
-    part = own_update(ub, ube, zb, rb, left, right, ratio, estimate)
-    return edge_update(ub, ube, zb, re, above, below, up, down, estimate, part)
+    part = own_update(ub, ube, zb, rb, left, right, ratio, top, bottom, estimate)
+    return edge_update(re, up, down, estimate, part)
 
 
 def shards(estimate, measured, z_interp, r_interp, psf_z, psf_r, psf_u):
@@ -443,8 +461,8 @@
     pieces = ship(pieces_of(place, measured, far, rows, early, ()), early)
     blurred = forward(tables, up, estimate, down, column_edges, pieces[0])
     pieces += ship(pieces_of(place, measured, far, rows, late, (blurred,)), late)
-    ratio, top, bottom, left, right = ratio_of(place, blurred, pieces)
-    return backward(tables, ratio, top, bottom, left, right, estimate, column_edges, row_edges)
+    ratio, left, right = ratio_of(place, blurred, pieces)
+    return backward(tables, ratio, left, right, estimate, column_edges, row_edges)
 
 
 def solution(mesh):

time: 438 us -> 208 us (0.47)
  Pallas kernels: 300 us -> 52.6 us
  waiting for transfers between devices: 33.8 us -> 47 us
    pallas_call x4, Pallas kernels: 261 us -> 14.4 us  [copy_call(): pl.pallas_call(body, in_specs=[SMEM] + [ANY] * (len(inputs) - 1), out_spe...]
    ppermute x10 -> x8, waiting for transfers between devices: 8.5 us -> 32.6 us  [send(): return lax.ppermute(x, AXES, shift_perm(axis, d))]
    ppermute x10 -> x8, starting transfers between devices: 42.9 us -> 66.4 us  [send(): return lax.ppermute(x, AXES, shift_perm(axis, d))]
    ppermute x8, starting transfers between devices: 46.9 us -> 26.2 us  [shards(): lax.ppermute(p, AXES, piece_perm(k))]
    ppermute x8, waiting for transfers between devices: 25.2 us -> 14.4 us  [shards(): lax.ppermute(p, AXES, piece_perm(k))]
    pallas_call x2 -> x3, Pallas kernels: 17.7 us -> 17.6 us  [the longest x1 7.92 us: own_update(): pl.pallas_call(own_kernel, grid=(inner + depth // 8,), in_specs=[whole(u)...]
  transfers between devices with their start and end apart: 19 -> 17, of which waited for: 6 -> 8; matrix products, arithmetic and copies ran while one was open for 0% -> 1% of each run, Pallas kernels for 51% -> 16%
where the time goes in v4:
time: 208 us; the launch traced here: 204 us
  starting transfers between devices  93.3 us (45%)
  Pallas kernels  52.6 us (25%)
  waiting for transfers between devices  47 us (23%)
  local copies, waits for them, and re-layouts  9.03 us (4%)
  other arithmetic  2.11 us (1%)
    ppermute x8, starting transfers between devices, send(): return lax.ppermute(x, AXES, shift_perm(axis, d))  66.4 us
    ppermute x8, waiting for transfers between devices, send(): return lax.ppermute(x, AXES, shift_perm(axis, d))  32.6 us
    ppermute x8, starting transfers between devices, shards(): lax.ppermute(p, AXES, piece_perm(k))  26.2 us
    ppermute x8, waiting for transfers between devices, shards(): lax.ppermute(p, AXES, piece_perm(k))  14.4 us
    pallas_call x4, Pallas kernels, copy_call(): pl.pallas_call(body, in_specs=[SMEM] + [ANY] * (len(inputs) - 1), out_spe...  14.4 us
    unnamed x22, local copies, waits for them, and re-layouts  8.6 us
    pallas_call x1, Pallas kernels, own_update(): pl.pallas_call(own_kernel, grid=(inner + depth // 8,), in_specs=[whole(u)...  7.92 us
    pallas_call x1, Pallas kernels, blur(): pl.pallas_call(blur_kernel, grid=(rows // 8,), in_specs=[whole(u), whole(...  7.52 us
  transfers between devices with their start and end apart: 17, of which 8 were waited for; matrix products, arithmetic and copies ran while one was open for 1% of the time, Pallas kernels for 16%

profile of v4, /device:TPU:69, one launch (start us, length us, event | category | flops | bytes accessed | tf_op | source)
XLA Modules:
  0.0 204.5 jit_solution(3775481149098664499)
XLA Ops:
  0.6 3.6 %shard_map.75 = f32[8,8,64,128]{3,2,1,0:T(8,128)} custom-call(s32[4]{0:T(128)} %pad_add_fusion.place_ref, f32[8,8,2,64,128]{4,3,2,1,0:T(8,128)} %bitcast.14), custom_call_target="tpu_custom_call" | custom-call | bytes 6000000 | tf_op jit(solution)/shard_map/pallas_call | solution.py:382
  5.0 3.5 %shard_map.74 = (f32[64,16,256]{2,1,0:T(8,128)}, f32[64,16,256]{2,1,0:T(8,128)}) custom-call(s32[4]{0:T(128)} %pad_add_fusion.place_ref, f32[64,64,256]{2,1,0:T(8,128)} %est_ref.5), custom_call_target="tpu_custom_call" | custom-call | bytes 6000000 | tf_op jit(solution)/shard_map/pallas_call | solution.py:382
  8.6 3.3 %collective-permute-start = (f32[64,16,256]{2,1,0:T(8,128)}, f32[64,16,256]{2,1,0:T(8,128)S(1)}, u32[]{:S(2)}, u32[]{:S(2)}) collective-permute-start(f32[64,16,256]{2,1,0:T(8,128)} %get-tuple-element.40), channel_id=1, source_target_pairs={{0,8},{1,9},{2,10},{3,11},{4,12},{5,13},{6,14},{7,15},{8,16},{9,17... | collective-permute-start | bytes 3145736 | tf_op jit(solution)/shard_map/ppermute | solution.py:362
  11.9 4.2 %collective-permute-start.1 = (f32[64,16,256]{2,1,0:T(8,128)}, f32[64,16,256]{2,1,0:T(8,128)S(1)}, u32[]{:S(2)}, u32[]{:S(2)}) collective-permute-start(f32[64,16,256]{2,1,0:T(8,128)} %get-tuple-element.41), channel_id=1, source_target_pairs={{8,0},{9,1},{10,2},{11,3},{12,4},{13,5},{14,6},{15,7},{16,8},{17,9... | collective-permute-start | bytes 3145736 | tf_op jit(solution)/shard_map/ppermute | solution.py:362
  17.6 4.3 %shard_map.76 = (f32[2,8,64,128]{3,2,1,0:T(8,128)}, f32[2,8,64,128]{3,2,1,0:T(8,128)}, f32[2,8,64,128]{3,2,1,0:T(8,128)}, f32[2,8,64,128]{3,2,1,0:T(8,128)}, f32...) custom-call(s32[4]{0:T(128)} %pad_add_fusion.place_ref, f32[8,16,64,128]{3,2,1,0:T(8,128)} %bitcast.15, ...), custom_call_target="tpu_custom_call" | custom-call | bytes 9000000 | tf_op jit(solution)/shard_map/pallas_call | solution.py:382
  23.9 3.0 %collective-permute-start.6 = (f32[2,8,64,128]{3,2,1,0:T(8,128)}, f32[2,8,64,128]{3,2,1,0:T(8,128)S(1)}, u32[]{:S(2)}, u32[]{:S(2)}) collective-permute-start(f32[2,8,64,128]{3,2,1,0:T(8,128)} %get-tuple-element.46), channel_id=1, source_target_pairs={{0,16},{1,88},{2,48},{3,120},{4,80},{5,24},{6,112},{7,56},{8,0},{9... | collective-permute-start | bytes 1572872 | tf_op jit(solution)/shard_map/ppermute | solution.py:459
  26.9 5.8 %collective-permute-start.7 = (f32[2,8,64,128]{3,2,1,0:T(8,128)}, f32[2,8,64,128]{3,2,1,0:T(8,128)}, u32[]{:S(2)}, u32[]{:S(2)}) collective-permute-start(f32[2,8,64,128]{3,2,1,0:T(8,128)} %get-tuple-element.47), channel_id=1, source_target_pairs={{0,32},{1,104},{2,64},{3,8},{4,96},{5,40},{6,0},{7,72},{8,48},{9,1... | collective-permute-start | bytes 1572872 | tf_op jit(solution)/shard_map/ppermute | solution.py:459
  33.1 2.8 %shard_map.73 = (bf16[64,288]{1,0:T(8,128)(2,1)S(1)}, bf16[64,192]{1,0:T(8,128)(2,1)S(1)}, bf16[2,16,48]{2,1,0:T(8,128)(2,1)S(1)}, bf16[768,256]{1,0:T(8,128)(2,...) custom-call(f32[32]{0:T(128)S(1)} %copy-done.7, ...), custom_call_target="tpu_custom_call" | custom-call | bytes 9000000 | tf_op jit(solution)/shard_map/pallas_call | solution.py:125
  37.9 10.2 %collective-permute-done.1.down_ref = f32[64,16,256]{2,1,0:T(8,128)S(1)} collective-permute-done((f32[64,16,256]{2,1,0:T(8,128)}, f32[64,16,256]{2,1,0:T(8,128)S(1)}, u32[]{:S(2)}, u32[]{:S(2)}) %collective-permute-start.1) | collective-permute-done | bytes 1048608 | tf_op jit(solution)/shard_map/ppermute | solution.py:362
  50.2 3.8 %shard_map.77 = (f32[64,64,256]{2,1,0:T(8,128)S(1)}, f32[8,64,128]{2,1,0:T(8,128)S(1)}, f32[8,64,128]{2,1,0:T(8,128)S(1)}) custom-call(bf16[64,288]{1,0:T(8,128)(2,1)S(1)} %get-tuple-element.39.table_ref, f32[64,16,256]{2,1,0:T(8,128)S(1)} %collective-permute-done.up_ref, f32[64,64,256]{2,1,0:T(8,128)S(1)} %copy-done, ...), custom_call_target="tpu_custom_call" | custom-call | bytes 12000000 | tf_op jit(solution)/shard_map/pallas_call | solution.py:194
  54.0 25.8 %collective-permute-start.4 = (f32[8,64,128]{2,1,0:T(8,128)S(1)}, f32[8,64,128]{2,1,0:T(8,128)S(1)}, u32[]{:S(2)}, u32[]{:S(2)}) collective-permute-start(f32[8,64,128]{2,1,0:T(8,128)S(1)} %get-tuple-element.43), channel_id=1, source_target_pairs={{0,1},{1,2},{2,3},{3,4},{4,5},{5,6},{6,7},{8,9},{9,10},{10,11},{11... | collective-permute-start | bytes 786440 | tf_op jit(solution)/shard_map/ppermute | solution.py:362
  85.6 5.4 %collective-permute-done.5.right_ref = f32[8,64,128]{2,1,0:T(8,128)S(1)} collective-permute-done((f32[8,64,128]{2,1,0:T(8,128)S(1)}, f32[8,64,128]{2,1,0:T(8,128)S(1)}, u32[]{:S(2)}, u32[]{:S(2)}) %collective-permute-start.5) | collective-permute-done | bytes 262176 | tf_op jit(solution)/shard_map/ppermute | solution.py:362
  92.9 7.5 %shard_map.78.refs_0_.blur_ref = f32[64,64,256]{2,1,0:T(8,128)S(1)} custom-call(bf16[768,256]{1,0:T(8,128)(2,1)S(1)} %get-tuple-element.36.u_ref, bf16[768,256]{1,0:T(8,128)(2,1)S(1)} %get-tuple-element.37.e_ref, bf16[64,192]{1,0:T(8,128)(2,1)S(1)} %get-tuple-element.38.m_ref, f32[8,64,128]{2,1,0:T(8,128)S(1)} %collective-permute-done.4.left_ref, ...), custom_call_target="tpu_custom_call" | custom-call | bytes 24000000 | tf_op jit(solution)/shard_map/pallas_call | solution.py:222
  102.4 3.0 %shard_map.79 = (f32[2,8,64,128]{3,2,1,0:T(8,128)}, f32[2,8,64,128]{3,2,1,0:T(8,128)}) custom-call(s32[4]{0:T(128)} %pad_add_fusion.place_ref, f32[8,16,64,128]{3,2,1,0:T(8,128)} %bitcast.16, f32[8,8,64,128]{3,2,1,0:T(8,128)} %collective-permute-done.2.far_ref, f32[64,64,256]{2,1,0:T(8,128)} %copy-done.2), custom_call_target="tpu_custom_call" | custom-call | bytes 9000000 | tf_op jit(solution)/shard_map/pallas_call | solution.py:382
  107.4 7.8 %collective-permute-start.12 = (f32[2,8,64,128]{3,2,1,0:T(8,128)}, f32[2,8,64,128]{3,2,1,0:T(8,128)S(1)}, u32[]{:S(2)}, u32[]{:S(2)}) collective-permute-start(f32[2,8,64,128]{3,2,1,0:T(8,128)} %get-tuple-element.52), channel_id=1, source_target_pairs={{0,112},{1,56},{2,16},{3,88},{4,48},{5,120},{6,80},{7,24},{8,96},{... | collective-permute-start | bytes 1572872 | tf_op jit(solution)/shard_map/ppermute | solution.py:459
  115.2 14.4 %collective-permute-done.11.refs_6_ = f32[2,8,64,128]{3,2,1,0:T(8,128)S(1)} collective-permute-done((f32[2,8,64,128]{3,2,1,0:T(8,128)}, f32[2,8,64,128]{3,2,1,0:T(8,128)S(1)}, u32[]{:S(2)}, u32[]{:S(2)}) %collective-permute-start.11) | collective-permute-done | bytes 524320 | tf_op jit(solution)/shard_map/ppermute | solution.py:459
  129.6 6.6 %shard_map.80 = (f32[64,64,256]{2,1,0:T(8,128)}, f32[8,64,128]{2,1,0:T(8,128)S(1)}, f32[8,64,128]{2,1,0:T(8,128)S(1)}) custom-call(s32[4]{0:T(128)S(1)} %copy-done.6, f32[64,64,256]{2,1,0:T(8,128)} %copy-done.2, f32[2,8,64,128]{3,2,1,0:T(8,128)S(1)} %collective-permute-done.3.after_ref.refs_0_, f32[2,8,64,128]{3,2,1,0:T(8,128)S(1)} %collective-permute-done.6.refs_1_, ...), custom_call_target="tpu_custom_call" | custom-call | bytes 21000000 | tf_op jit(solution)/shard_map/pallas_call | solution.py:249
  136.2 21.8 %collective-permute-start.13 = (f32[8,64,128]{2,1,0:T(8,128)S(1)}, f32[8,64,128]{2,1,0:T(8,128)S(1)}, u32[]{:S(2)}, u32[]{:S(2)}) collective-permute-start(f32[8,64,128]{2,1,0:T(8,128)S(1)} %get-tuple-element.53), channel_id=1, source_target_pairs={{0,1},{1,2},{2,3},{3,4},{4,5},{5,6},{6,7},{8,9},{9,10},{10,11},{11... | collective-permute-start | bytes 786440 | tf_op jit(solution)/shard_map/ppermute | solution.py:362
  161.3 4.4 %collective-permute-done.14.right_ref = f32[8,64,128]{2,1,0:T(8,128)S(1)} collective-permute-done((f32[8,64,128]{2,1,0:T(8,128)S(1)}, f32[8,64,128]{2,1,0:T(8,128)S(1)}, u32[]{:S(2)}, u32[]{:S(2)}) %collective-permute-start.14) | collective-permute-done | bytes 262176 | tf_op jit(solution)/shard_map/ppermute | solution.py:362
  167.9 3.4 %shard_map.81 = (f32[64,16,256]{2,1,0:T(8,128)S(1)}, f32[64,16,256]{2,1,0:T(8,128)S(1)}) custom-call(bf16[768,256]{1,0:T(8,128)(2,1)S(1)} %get-tuple-element.33.u_ref, bf16[768,256]{1,0:T(8,128)(2,1)S(1)} %get-tuple-element.34.e_ref, bf16[64,192]{1,0:T(8,128)(2,1)S(1)} %get-tuple-element.35.m_ref, f32[8,64,128]{2,1,0:T(8,128)S(1)} %collective-permute-done.13.left_ref, ...), custom_call_target="tpu_custom_call" | custom-call | bytes 12000000 | tf_op jit(solution)/shard_map/pallas_call | solution.py:281
  173.2 5.5 %collective-permute-start.16 = (f32[64,16,256]{2,1,0:T(8,128)S(1)}, f32[64,16,256]{2,1,0:T(8,128)S(1)}, u32[]{:S(2)}, u32[]{:S(2)}) collective-permute-start(f32[64,16,256]{2,1,0:T(8,128)S(1)} %get-tuple-element.57.top_ref), channel_id=1, source_target_pairs={{8,0},{9,1},{10,2},{11,3},{12,4},{13,5},{14,6},{15,7},{16,8},{17,9... | collective-permute-start | bytes 3145736 | tf_op jit(solution)/shard_map/ppermute | solution.py:362
  180.9 7.9 %shard_map.82.part_ref = f32[64,64,256]{2,1,0:T(8,128)} custom-call(bf16[768,256]{1,0:T(8,128)(2,1)S(1)} %get-tuple-element.33.u_ref, bf16[768,256]{1,0:T(8,128)(2,1)S(1)} %get-tuple-element.34.e_ref, bf16[64,192]{1,0:T(8,128)(2,1)S(1)} %get-tuple-element.35.m_ref, bf16[64,192]{1,0:T(8,128)(2,1)S(1)} %get-tuple-element.58.a_ref, ...), custom_call_target="tpu_custom_call" | custom-call | bytes 24000000 | tf_op jit(solution)/shard_map/pallas_call | solution.py:316
  188.8 7.6 %collective-permute-done.15.up_ref = f32[64,16,256]{2,1,0:T(8,128)S(1)} collective-permute-done((f32[64,16,256]{2,1,0:T(8,128)S(1)}, f32[64,16,256]{2,1,0:T(8,128)S(1)}, u32[]{:S(2)}, u32[]{:S(2)}) %collective-permute-start.15) | collective-permute-done | bytes 1048608 | tf_op jit(solution)/shard_map/ppermute | solution.py:362
  198.2 6.3 %shard_map.83 = f32[64,64,256]{2,1,0:T(8,128)} custom-call(bf16[2,16,48]{2,1,0:T(8,128)(2,1)S(1)} %get-tuple-element.32.a_ref, f32[64,16,256]{2,1,0:T(8,128)S(1)} %collective-permute-done.15.up_ref, f32[64,16,256]{2,1,0:T(8,128)S(1)} %collective-permute-done.16.down_ref, f32[64,64,256]{2,1,0:T(8,128)S(1)} %copy-done.1, ...), custom_call_target="tpu_custom_call", output_to_operand_aliasing={{}: (4, {})} | custom-call | bytes 9000000 | tf_op jit(solution)/shard_map/pallas_call | solution.py:347
  (52 shorter events, 32.4 us)
Async XLA Ops:
  4.2 13.4 %collective-permute-start.2 = (f32[8,8,64,128]{3,2,1,0:T(8,128)}, f32[8,8,64,128]{3,2,1,0:T(8,128)}, u32[]{:S(2)}, u32[]{:S(2)}) collective-permute-start(f32[8,8,64,128]{3,2,1,0:T(8,128)} %shard_map.75), channel_id=1, source_target_pairs={{0,1},{1,0},{2,3},{3,2},{4,5},{5,4},{6,7},{7,6},{8,9},{9,8},{10,11... | collective-permute-start | bytes 6291464 | tf_op jit(solution)/shard_map/ppermute | solution.py:456
  8.5 24.5 %copy-start.5 = (f32[64,64]{1,0:T(8,128)S(1)}, f32[64,64]{1,0:T(8,128)}, u32[]{:S(2)}) copy-start(f32[64,64]{1,0:T(8,128)} %zi_ref.1) | copy-start | bytes 49156
  8.5 24.5 %copy-start.7 = (f32[32]{0:T(128)S(1)}, f32[32]{0:T(128)}, u32[]{:S(2)}) copy-start(f32[32]{0:T(128)} %pz_ref.1) | copy-start | bytes 388
  8.6 24.5 %copy-start.8 = (f32[32]{0:T(128)S(1)}, f32[32]{0:T(128)}, u32[]{:S(2)}) copy-start(f32[32]{0:T(128)} %pr_ref.1) | copy-start | bytes 388
  8.6 24.5 %copy-start.9 = (f32[32]{0:T(128)S(1)}, f32[32]{0:T(128)}, u32[]{:S(2)}) copy-start(f32[32]{0:T(128)} %pu_ref.1) | copy-start | bytes 388
  8.6 29.3 %collective-permute-start = (f32[64,16,256]{2,1,0:T(8,128)}, f32[64,16,256]{2,1,0:T(8,128)S(1)}, u32[]{:S(2)}, u32[]{:S(2)}) collective-permute-start(f32[64,16,256]{2,1,0:T(8,128)} %get-tuple-element.40), channel_id=1, source_target_pairs={{0,8},{1,9},{2,10},{3,11},{4,12},{5,13},{6,14},{7,15},{8,16},{9,17... | collective-permute-start | bytes 3145736 | tf_op jit(solution)/shard_map/ppermute | solution.py:362
  11.9 36.1 %collective-permute-start.1 = (f32[64,16,256]{2,1,0:T(8,128)}, f32[64,16,256]{2,1,0:T(8,128)S(1)}, u32[]{:S(2)}, u32[]{:S(2)}) collective-permute-start(f32[64,16,256]{2,1,0:T(8,128)} %get-tuple-element.41), channel_id=1, source_target_pairs={{8,0},{9,1},{10,2},{11,3},{12,4},{13,5},{14,6},{15,7},{16,8},{17,9... | collective-permute-start | bytes 3145736 | tf_op jit(solution)/shard_map/ppermute | solution.py:362
  21.9 26.1 %collective-permute-start.3 = (f32[2,8,64,128]{3,2,1,0:T(8,128)}, f32[2,8,64,128]{3,2,1,0:T(8,128)S(1)}, u32[]{:S(2)}, u32[]{:S(2)}) collective-permute-start(f32[2,8,64,128]{3,2,1,0:T(8,128)} %get-tuple-element.42), channel_id=1, source_target_pairs={{0,0},{1,72},{2,32},{3,104},{4,64},{5,8},{6,96},{7,40},{8,16},{9,8... | collective-permute-start | bytes 1572872 | tf_op jit(solution)/shard_map/ppermute | solution.py:459
  23.9 81.5 %collective-permute-start.6 = (f32[2,8,64,128]{3,2,1,0:T(8,128)}, f32[2,8,64,128]{3,2,1,0:T(8,128)S(1)}, u32[]{:S(2)}, u32[]{:S(2)}) collective-permute-start(f32[2,8,64,128]{3,2,1,0:T(8,128)} %get-tuple-element.46), channel_id=1, source_target_pairs={{0,16},{1,88},{2,48},{3,120},{4,80},{5,24},{6,112},{7,56},{8,0},{9... | collective-permute-start | bytes 1572872 | tf_op jit(solution)/shard_map/ppermute | solution.py:459
  26.9 80.5 %collective-permute-start.7 = (f32[2,8,64,128]{3,2,1,0:T(8,128)}, f32[2,8,64,128]{3,2,1,0:T(8,128)}, u32[]{:S(2)}, u32[]{:S(2)}) collective-permute-start(f32[2,8,64,128]{3,2,1,0:T(8,128)} %get-tuple-element.47), channel_id=1, source_target_pairs={{0,32},{1,104},{2,64},{3,8},{4,96},{5,40},{6,0},{7,72},{8,48},{9,1... | collective-permute-start | bytes 1572872 | tf_op jit(solution)/shard_map/ppermute | solution.py:459
  50.2 40.7 %copy-start.10 = (f32[2,8,64,128]{3,2,1,0:T(8,128)S(1)}, f32[2,8,64,128]{3,2,1,0:T(8,128)}, u32[]{:S(2)}) copy-start(f32[2,8,64,128]{3,2,1,0:T(8,128)} %get-tuple-element.50) | copy-start | bytes 1572868
  54.0 29.6 %collective-permute-start.4 = (f32[8,64,128]{2,1,0:T(8,128)S(1)}, f32[8,64,128]{2,1,0:T(8,128)S(1)}, u32[]{:S(2)}, u32[]{:S(2)}) collective-permute-start(f32[8,64,128]{2,1,0:T(8,128)S(1)} %get-tuple-element.43), channel_id=1, source_target_pairs={{0,1},{1,2},{2,3},{3,4},{4,5},{5,6},{6,7},{8,9},{9,10},{10,11},{11... | collective-permute-start | bytes 786440 | tf_op jit(solution)/shard_map/ppermute | solution.py:362
  79.8 11.1 %collective-permute-start.5 = (f32[8,64,128]{2,1,0:T(8,128)S(1)}, f32[8,64,128]{2,1,0:T(8,128)S(1)}, u32[]{:S(2)}, u32[]{:S(2)}) collective-permute-start(f32[8,64,128]{2,1,0:T(8,128)S(1)} %get-tuple-element.44), channel_id=1, source_target_pairs={{1,0},{2,1},{3,2},{4,3},{5,4},{6,5},{7,6},{9,8},{10,9},{11,10},{12... | collective-permute-start | bytes 786440 | tf_op jit(solution)/shard_map/ppermute | solution.py:362
  81.7 33.5 %collective-permute-start.8 = (f32[2,8,64,128]{3,2,1,0:T(8,128)}, f32[2,8,64,128]{3,2,1,0:T(8,128)S(1)}, u32[]{:S(2)}, u32[]{:S(2)}) collective-permute-start(f32[2,8,64,128]{3,2,1,0:T(8,128)} %get-tuple-element.48), channel_id=1, source_target_pairs={{0,48},{1,120},{2,80},{3,24},{4,112},{5,56},{6,16},{7,88},{8,32},{... | collective-permute-start | bytes 1572872 | tf_op jit(solution)/shard_map/ppermute | solution.py:459
  83.7 31.5 %collective-permute-start.9 = (f32[2,8,64,128]{3,2,1,0:T(8,128)}, f32[2,8,64,128]{3,2,1,0:T(8,128)S(1)}, u32[]{:S(2)}, u32[]{:S(2)}) collective-permute-start(f32[2,8,64,128]{3,2,1,0:T(8,128)} %get-tuple-element.49), channel_id=1, source_target_pairs={{0,64},{1,8},{2,96},{3,40},{4,0},{5,72},{6,32},{7,104},{8,80},{9,2... | collective-permute-start | bytes 1572872 | tf_op jit(solution)/shard_map/ppermute | solution.py:459
  90.9 24.3 %collective-permute-start.10 = (f32[2,8,64,128]{3,2,1,0:T(8,128)S(1)}, f32[2,8,64,128]{3,2,1,0:T(8,128)S(1)}, u32[]{:S(2)}, u32[]{:S(2)}) collective-permute-start(f32[2,8,64,128]{3,2,1,0:T(8,128)S(1)} %copy-done.10), channel_id=1, source_target_pairs={{0,80},{1,24},{2,112},{3,56},{4,16},{5,88},{6,48},{7,120},{8,64},{... | collective-permute-start | bytes 1572872 | tf_op jit(solution)/shard_map/ppermute | solution.py:459
  102.4 27.2 %copy-start.6 = (s32[4]{0:T(128)S(1)}, s32[4]{0:T(128)}, u32[]{:S(2)}) copy-start(s32[4]{0:T(128)} %pad_add_fusion.place_ref) | copy-start | bytes 52
  105.4 24.2 %collective-permute-start.11 = (f32[2,8,64,128]{3,2,1,0:T(8,128)}, f32[2,8,64,128]{3,2,1,0:T(8,128)S(1)}, u32[]{:S(2)}, u32[]{:S(2)}) collective-permute-start(f32[2,8,64,128]{3,2,1,0:T(8,128)} %get-tuple-element.51), channel_id=1, source_target_pairs={{0,96},{1,40},{2,0},{3,72},{4,32},{5,104},{6,64},{7,8},{8,112},{9,... | collective-permute-start | bytes 1572872 | tf_op jit(solution)/shard_map/ppermute | solution.py:459
  107.4 22.2 %collective-permute-start.12 = (f32[2,8,64,128]{3,2,1,0:T(8,128)}, f32[2,8,64,128]{3,2,1,0:T(8,128)S(1)}, u32[]{:S(2)}, u32[]{:S(2)}) collective-permute-start(f32[2,8,64,128]{3,2,1,0:T(8,128)} %get-tuple-element.52), channel_id=1, source_target_pairs={{0,112},{1,56},{2,16},{3,88},{4,48},{5,120},{6,80},{7,24},{8,96},{... | collective-permute-start | bytes 1572872 | tf_op jit(solution)/shard_map/ppermute | solution.py:459
  136.2 42.5 %copy-start.1 = (f32[64,64,256]{2,1,0:T(8,128)S(1)}, f32[64,64,256]{2,1,0:T(8,128)}, u32[]{:S(2)}) copy-start(f32[64,64,256]{2,1,0:T(8,128)} %est_ref.5) | copy-start | bytes 12582916
  136.2 25.1 %collective-permute-start.13 = (f32[8,64,128]{2,1,0:T(8,128)S(1)}, f32[8,64,128]{2,1,0:T(8,128)S(1)}, u32[]{:S(2)}, u32[]{:S(2)}) collective-permute-start(f32[8,64,128]{2,1,0:T(8,128)S(1)} %get-tuple-element.53), channel_id=1, source_target_pairs={{0,1},{1,2},{2,3},{3,4},{4,5},{5,6},{6,7},{8,9},{9,10},{10,11},{11... | collective-permute-start | bytes 786440 | tf_op jit(solution)/shard_map/ppermute | solution.py:362
  158.0 7.7 %collective-permute-start.14 = (f32[8,64,128]{2,1,0:T(8,128)S(1)}, f32[8,64,128]{2,1,0:T(8,128)S(1)}, u32[]{:S(2)}, u32[]{:S(2)}) collective-permute-start(f32[8,64,128]{2,1,0:T(8,128)S(1)} %get-tuple-element.54), channel_id=1, source_target_pairs={{1,0},{2,1},{3,2},{4,3},{5,4},{6,5},{7,6},{9,8},{10,9},{11,10},{12... | collective-permute-start | bytes 786440 | tf_op jit(solution)/shard_map/ppermute | solution.py:362
  171.3 25.1 %collective-permute-start.15 = (f32[64,16,256]{2,1,0:T(8,128)S(1)}, f32[64,16,256]{2,1,0:T(8,128)S(1)}, u32[]{:S(2)}, u32[]{:S(2)}) collective-permute-start(f32[64,16,256]{2,1,0:T(8,128)S(1)} %get-tuple-element.56.bottom_ref), channel_id=1, source_target_pairs={{0,8},{1,9},{2,10},{3,11},{4,12},{5,13},{6,14},{7,15},{8,16},{9,17... | collective-permute-start | bytes 3145736 | tf_op jit(solution)/shard_map/ppermute | solution.py:362
  173.2 24.9 %collective-permute-start.16 = (f32[64,16,256]{2,1,0:T(8,128)S(1)}, f32[64,16,256]{2,1,0:T(8,128)S(1)}, u32[]{:S(2)}, u32[]{:S(2)}) collective-permute-start(f32[64,16,256]{2,1,0:T(8,128)S(1)} %get-tuple-element.57.top_ref), channel_id=1, source_target_pairs={{8,0},{9,1},{10,2},{11,3},{12,4},{13,5},{14,6},{15,7},{16,8},{17,9... | collective-permute-start | bytes 3145736 | tf_op jit(solution)/shard_map/ppermute | solution.py:362
  (4 other events, 8.6 us)

commit v5 on v4

--- a/solution.py
+++ b/solution.py
@@ -46,14 +46,13 @@
 def target_of(x, y, z, c, k):
     k1, k2 = k // 2, k % 2
     side, half = y >> 1, y & 1
-    parity = c ^ (x & 1)
-    return (x + z + 2 * c + k1) & 3, 2 * (half ^ k2 ^ side) + parity
+    return (x + z + 2 * c + 2 * side + k1) & 3, 2 * (half ^ k2) + c
 
 
 def source_of(x, y, z, c, k):
     k1, k2 = k // 2, k % 2
-    core = (y & 1) ^ (z & 1)
-    return (x - z - 2 * core - k1) & 3, core, (y >> 1) ^ k2 ^ c
+    core = y & 1
+    return (x - z - 2 * core - 2 * c - k1) & 3, core, (y >> 1) ^ k2
 
 
 def piece_perm(k):
@@ -127,7 +126,7 @@
         in_specs=[smem] * 3 + [vmem] * 5,
         out_specs=[vmem] * len(shapes),
         out_shape=[jax.ShapeDtypeStruct(s, BF) for s in shapes],
-        **params(32, 3),
+        **params(8, 3),
     )(psf_z, psf_r, psf_u, z_interp, main[None], upper[None], main[own, None], upper[own, None])
 
 
@@ -166,7 +165,8 @@
     return dot(table, jnp.concatenate([h, l, h], axis=0))
 
 
-def row_kernel(table_ref, up_ref, own_ref, down_ref, after_ref, out_ref, left_ref, right_ref):
+def row_kernel(table_ref, up_ref, own_ref, down_ref, *refs):
+    out_ref, left_ref, right_ref = refs[-3:]
     table = table_ref[...]
     planes = []
     for z in range(8):
@@ -194,11 +194,11 @@
     return pl.pallas_call(
         row_kernel,
         grid=(depth // 8,),
-        in_specs=[whole(table), block(16), block(rows), block(16), ANY],
+        in_specs=[whole(table), block(16), block(rows), block(16)] + [ANY] * len(after),
         out_specs=[block(rows), edge, edge],
         out_shape=[jax.ShapeDtypeStruct(own.shape, F32), edge_shape, edge_shape],
-        **params(32, 4),
-    )(table, up, own, down, after)
+        **params(10, 4),
+    )(table, up, own, down, *after)
 
 
 def blur_kernel(u_ref, e_ref, m_ref, left_ref, right_ref, x_ref, out_ref):
@@ -225,14 +225,14 @@
         in_specs=[whole(u), whole(e), whole(m), block(depth // 8, 128), block(depth // 8, 128), block(depth, cols)],
         out_specs=pl.BlockSpec((8, depth, cols), lambda i: (i, 0, 0)),
         out_shape=jax.ShapeDtypeStruct((rows, depth, cols), F32),
-        **params(32, 8),
+        **params(14, 8),
     )(u, e, m, left, right, x)
 
 
-def ratio_kernel(place_ref, blur_ref, *refs):
+def ratio_kernel(blur_ref, *refs):
     pieces, (out_ref, left_ref, right_ref) = refs[:-3], refs[-3:]
     for k, piece in enumerate(pieces):
-        pair, core, half = source_of(*(place_ref[a] for a in range(4)), k)
+        pair, core, half = source_of(*place(), k)
         cols = pl.ds(pl.multiple_of(half * 128, 128), 128)
         for part in range(2):
             planes = pl.ds(pl.multiple_of((pair * 2 + (core ^ part)) * 8, 8), 8)
@@ -242,17 +242,17 @@
         left_ref[g], right_ref[g] = packed([out_ref[8 * g + q] for q in range(8)])
 
 
-def ratio_of(place, blurred, pieces):
+def ratio_of(blurred, pieces):
     rows, depth, cols = blurred.shape
     vmem = pl.BlockSpec(memory_space=pltpu.VMEM)
     shapes = [blurred.shape] + [(rows // 8, depth, 128)] * 2
     return pl.pallas_call(
         ratio_kernel,
-        in_specs=[pl.BlockSpec(memory_space=pltpu.SMEM), vmem] + [vmem] * len(pieces),
+        in_specs=[vmem] * (1 + len(pieces)),
         out_specs=[vmem] * 3,
         out_shape=[jax.ShapeDtypeStruct(s, F32) for s in shapes],
-        **params(48, 7),
-    )(place, blurred, *pieces)
+        **params(20, 7),
+    )(blurred, *pieces)
 
 
 def spread_tile(ratio, left, right, u, e, m):
@@ -286,7 +286,7 @@
         + [pl.BlockSpec((8, depth, cols), at)],
         out_specs=[end, end],
         out_shape=[jax.ShapeDtypeStruct((depth, 16, cols), F32)] * 2,
-        **params(40, 4),
+        **params(14, 4),
     )(u, e, m, left, right, ratio)
 
 
@@ -324,7 +324,7 @@
         out_specs=pl.BlockSpec((8, rows, cols), late),
         out_shape=jax.ShapeDtypeStruct(est.shape, F32),
         scratch_shapes=[pltpu.VMEM((depth, rows - 32, cols), F32)],
-        **params(40, 8),
+        **params(16, 8),
     )(u, e, m, a, left, right, ratio, top, bottom, est)
 
 
@@ -341,7 +341,7 @@
 
 def edge_update(a, up, down, est, part):
     depth, rows, cols = est.shape
-    step, chunk = rows // 16 - 1, 16
+    step, chunk = rows // 16 - 1, depth
     last = depth // chunk - 1
     tile = pl.BlockSpec((chunk, 16, cols), lambda s, i: (i, s * step, 0))
     return pl.pallas_call(
@@ -354,7 +354,7 @@
         out_specs=tile,
         out_shape=jax.ShapeDtypeStruct(est.shape, F32),
         input_output_aliases={4: 0},
-        **params(40, 3),
+        **params(20, 3),
     )(a, up, down, est, part)
 
 
@@ -366,8 +366,13 @@
     return send(right, "gy", 1), send(left, "gy", -1)
 
 
+def place():
+    gx, gy = lax.axis_index("gx"), lax.axis_index("gy")
+    return gx >> 2, gx & 3, gy >> 1, gy & 1
+
+
+HBM = pl.BlockSpec(memory_space=pltpu.HBM)
 ANY = pl.BlockSpec(memory_space=pl.ANY)
-SMEM = pl.BlockSpec(memory_space=pltpu.SMEM)
 
 
 def run_copies(pairs, sems):
@@ -381,44 +386,48 @@
 def copy_call(body, count, shapes, inputs, us):
     return pl.pallas_call(
         body,
-        in_specs=[SMEM] + [ANY] * (len(inputs) - 1),
+        in_specs=[HBM] * len(inputs),
         out_specs=[pl.BlockSpec(memory_space=pltpu.VMEM)] * len(shapes),
         out_shape=[jax.ShapeDtypeStruct(s, F32) for s in shapes],
         scratch_shapes=[pltpu.SemaphoreType.DMA((count,))],
-        **params(56, us),
+        **params(16, us),
     )(*inputs)
 
 
-def row_ends(place, est):
-    def body(place_ref, est_ref, top_ref, bottom_ref, sems):
-        rows = est_ref.shape[1]
-        pairs = [(est_ref.at[:, :16], top_ref), (est_ref.at[:, rows - 16 :], bottom_ref)]
+def row_ends(est):
+    def body(est_ref, top_ref, bottom_ref, sems):
+        depth, rows, _ = est_ref.shape
+        pairs = []
+        for d in range(0, depth, 16):
+            at = pl.ds(d, 16)
+            pairs.append((est_ref.at[at, :16], top_ref.at[at]))
+            pairs.append((est_ref.at[at, rows - 16 :], bottom_ref.at[at]))
         run_copies(pairs, sems)
 
     depth, _, cols = est.shape
-    return copy_call(body, 2, [(depth, 16, cols)] * 2, (place, est), 2)
-
-
-def far_half(place, measured, rows):
-    def body(place_ref, measured_ref, out_ref, sems):
-        other = 1 - (place_ref[3] ^ (place_ref[0] & 1))
-        run_copies([(measured_ref.at[:, :, other], out_ref)], sems)
-
-    return copy_call(body, 1, [(8, 8, rows, 128)], (place, measured.reshape(8, 8, 2, rows, 128)), 2)[0]
-
-
-def pieces_of(place, measured, far, rows, steps, after):
-    def body(place_ref, measured_ref, far_ref, *refs):
-        outs, sems = refs[len(after) : -1], refs[-1]
+    return copy_call(body, depth // 8, [(depth, 16, cols)] * 2, (est,), 2)
+
+
+def far_half(measured, rows):
+    def body(measured_ref, out_ref, sems):
+        _, _, _, c = place()
+        run_copies([(measured_ref.at[p, :, 1 - c], out_ref.at[p]) for p in range(8)], sems)
+
+    return copy_call(body, 8, [(8, 8, rows, 128)], (measured.reshape(8, 8, 2, rows, 128),), 2)[0]
+
+
+def pieces_of(measured, far, rows):
+    def body(measured_ref, far_ref, *refs):
+        outs, sems = refs[:-1], refs[-1]
         pairs = []
-        for k, out in zip(steps, outs):
-            tx, ty = target_of(*(place_ref[a] for a in range(4)), k)
+        for k, out in enumerate(outs):
+            tx, ty = target_of(*place(), k)
             pairs.append((measured_ref.at[:, tx * 4 + ty], out.at[0]))
             pairs.append((far_ref.at[:, tx * 2 + (ty >> 1)], out.at[1]))
         run_copies(pairs, sems)
 
-    inputs = (place, measured.reshape(8, 16, rows, 128), far, *after)
-    return copy_call(body, 2 * len(steps), [(2, 8, rows, 128)] * len(steps), inputs, 3)
+    inputs = (measured.reshape(8, 16, rows, 128), far)
+    return copy_call(body, 16, [(2, 8, rows, 128)] * 8, inputs, 3)
 
 
 def diagonal_windows(r_interp, gx, rows):
@@ -449,19 +458,15 @@
 
 def shards(estimate, measured, z_interp, r_interp, psf_z, psf_r, psf_u):
     depth, rows, width = estimate.shape
-    gx, gy = lax.axis_index("gx"), lax.axis_index("gy")
-    place = jnp.stack([gx // 4, gx % 4, gy // 2, gy % 2]).astype(jnp.int32)
+    gx = lax.axis_index("gx")
     row_edges = lambda top, bottom: (send(bottom, "gx", 1), send(top, "gx", -1))
-    up, down = row_edges(*row_ends(place, estimate))
-    far = lax.ppermute(far_half(place, measured, rows), AXES, core_swap())
+    up, down = row_edges(*row_ends(estimate))
+    far = lax.ppermute(far_half(measured, rows), AXES, core_swap())
     main, upper = diagonal_windows(r_interp, gx, rows)
     tables = make_tables(psf_z, psf_r, psf_u, z_interp, main, upper, rows, width)
-    ship = lambda parts, steps: [lax.ppermute(p, AXES, piece_perm(k)) for p, k in zip(parts, steps)]
-    early, late = range(6), range(6, 8)
-    pieces = ship(pieces_of(place, measured, far, rows, early, ()), early)
-    blurred = forward(tables, up, estimate, down, column_edges, pieces[0])
-    pieces += ship(pieces_of(place, measured, far, rows, late, (blurred,)), late)
-    ratio, left, right = ratio_of(place, blurred, pieces)
+    pieces = [lax.ppermute(p, AXES, piece_perm(k)) for k, p in enumerate(pieces_of(measured, far, rows))]
+    blurred = forward(tables, up, estimate, down, column_edges, pieces[:4])
+    ratio, left, right = ratio_of(blurred, pieces)
     return backward(tables, ratio, left, right, estimate, column_edges, row_edges)
 
 

time: 208 us -> 183 us (0.88)
  the two profiles are of different devices: /device:TPU:69 before, /device:TPU:75 now
where the time goes in v5:
time: 183 us; the launch traced here: 182 us
  starting transfers between devices  78.8 us (43%)
  waiting for transfers between devices  53.1 us (29%)
  Pallas kernels  37.9 us (21%)
  local copies, waits for them, and re-layouts  10.4 us (6%)
    ppermute x8, waiting for transfers between devices, send(): return lax.ppermute(x, AXES, shift_perm(axis, d))  48 us
    ppermute x8, starting transfers between devices, shards(): lax.ppermute(p, AXES, piece_perm(k))  46.1 us
    ppermute x8, starting transfers between devices, send(): return lax.ppermute(x, AXES, shift_perm(axis, d))  31.9 us
    unnamed x34, local copies, waits for them, and re-layouts  9.97 us
    pallas_call x1, Pallas kernels, own_update(): pl.pallas_call(own_kernel, grid=(inner + depth // 8,), in_specs=[whole(u)...  7.92 us
    pallas_call x1, Pallas kernels, blur(): pl.pallas_call(blur_kernel, grid=(rows // 8,), in_specs=[whole(u), whole(...  7.4 us
    pallas_call x1, Pallas kernels, row_mix(): pl.pallas_call(row_kernel, grid=(depth // 8,), in_specs=[whole(table), bl...  6.23 us
    ppermute x8, waiting for transfers between devices, shards(): lax.ppermute(p, AXES, piece_perm(k))  5.04 us
  transfers between devices with their start and end apart: 17, of which 9 were waited for; matrix products, arithmetic and copies ran while one was open for 1% of the time, Pallas kernels for 12%

profile of v5, /device:TPU:75, one launch (start us, length us, event | category | flops | bytes accessed | tf_op | source)
XLA Modules:
  0.0 182.0 jit_solution(14936522193642887538)
XLA Ops:
  0.0 2.3 %copy-done.3 = f32[8,1024,128]{2,1,0:T(8,128)S(1)} copy-done((f32[8,1024,128]{2,1,0:T(8,128)S(1)}, f32[8,1024,128]{2,1,0:T(8,128)}, u32[]{:S(2)}) %copy-start.3) | copy-done | bytes 4194328
  6.2 3.3 %collective-permute-start = (f32[64,16,256]{2,1,0:T(8,128)}, f32[64,16,256]{2,1,0:T(8,128)S(1)}, u32[]{:S(2)}, u32[]{:S(2)}) collective-permute-start(f32[64,16,256]{2,1,0:T(8,128)} %get-tuple-element.40), channel_id=1, source_target_pairs={{0,8},{1,9},{2,10},{3,11},{4,12},{5,13},{6,14},{7,15},{8,16},{9,17... | collective-permute-start | bytes 3145736 | tf_op jit(solution)/shard_map/ppermute | solution.py:362
  20.4 3.9 %collective-permute-start.3 = (f32[2,8,64,128]{3,2,1,0:T(8,128)}, f32[2,8,64,128]{3,2,1,0:T(8,128)S(1)}, u32[]{:S(2)}, u32[]{:S(2)}) collective-permute-start(f32[2,8,64,128]{3,2,1,0:T(8,128)} %get-tuple-element.42), channel_id=1, source_target_pairs={{0,0},{1,72},{2,32},{3,104},{4,64},{5,8},{6,96},{7,40},{8,16},{9,8... | collective-permute-start | bytes 1572872 | tf_op jit(solution)/shard_map/ppermute | solution.py:467
  25.2 5.3 %collective-permute-start.5 = (f32[2,8,64,128]{3,2,1,0:T(8,128)}, f32[2,8,64,128]{3,2,1,0:T(8,128)S(1)}, u32[]{:S(2)}, u32[]{:S(2)}) collective-permute-start(f32[2,8,64,128]{3,2,1,0:T(8,128)} %get-tuple-element.44), channel_id=1, source_target_pairs={{0,32},{1,104},{2,64},{3,8},{4,96},{5,40},{6,0},{7,72},{8,48},{9,1... | collective-permute-start | bytes 1572872 | tf_op jit(solution)/shard_map/ppermute | solution.py:467
  30.4 8.9 %collective-permute-done.up_ref = f32[64,16,256]{2,1,0:T(8,128)S(1)} collective-permute-done((f32[64,16,256]{2,1,0:T(8,128)}, f32[64,16,256]{2,1,0:T(8,128)S(1)}, u32[]{:S(2)}, u32[]{:S(2)}) %collective-permute-start) | collective-permute-done | bytes 1048608 | tf_op jit(solution)/shard_map/ppermute | solution.py:362
  39.3 11.4 %collective-permute-start.6 = (f32[2,8,64,128]{3,2,1,0:T(8,128)}, f32[2,8,64,128]{3,2,1,0:T(8,128)S(1)}, u32[]{:S(2)}, u32[]{:S(2)}) collective-permute-start(f32[2,8,64,128]{3,2,1,0:T(8,128)} %get-tuple-element.45), channel_id=1, source_target_pairs={{0,48},{1,120},{2,80},{3,24},{4,112},{5,56},{6,16},{7,88},{8,32},{... | collective-permute-start | bytes 1572872 | tf_op jit(solution)/shard_map/ppermute | solution.py:467
  51.2 2.8 %shard_map.73 = (bf16[64,288]{1,0:T(8,128)(2,1)S(1)}, bf16[64,192]{1,0:T(8,128)(2,1)S(1)}, bf16[2,16,48]{2,1,0:T(8,128)(2,1)S(1)}, bf16[768,256]{1,0:T(8,128)(2,...) custom-call(f32[32]{0:T(128)S(1)} %copy-done.6, ...), custom_call_target="tpu_custom_call" | custom-call | bytes 9000000 | tf_op jit(solution)/shard_map/pallas_call | solution.py:124
  54.0 4.7 %collective-permute-done.1.down_ref = f32[64,16,256]{2,1,0:T(8,128)} collective-permute-done((f32[64,16,256]{2,1,0:T(8,128)}, f32[64,16,256]{2,1,0:T(8,128)}, u32[]{:S(2)}, u32[]{:S(2)}) %collective-permute-start.1) | collective-permute-done | bytes 1048608 | tf_op jit(solution)/shard_map/ppermute | solution.py:362
  61.5 6.2 %shard_map.77 = (f32[64,64,256]{2,1,0:T(8,128)S(1)}, f32[8,64,128]{2,1,0:T(8,128)S(1)}, f32[8,64,128]{2,1,0:T(8,128)S(1)}) custom-call(bf16[64,288]{1,0:T(8,128)(2,1)S(1)} %get-tuple-element.39.table_ref, f32[64,16,256]{2,1,0:T(8,128)S(1)} %collective-permute-done.up_ref, f32[64,64,256]{2,1,0:T(8,128)S(1)} %copy-done.1, ...), custom_call_target="tpu_custom_call" | custom-call | bytes 12000000 | tf_op jit(solution)/shard_map/pallas_call | solution.py:194
  67.8 7.5 %collective-permute-start.7 = (f32[8,64,128]{2,1,0:T(8,128)S(1)}, f32[8,64,128]{2,1,0:T(8,128)S(1)}, u32[]{:S(2)}, u32[]{:S(2)}) collective-permute-start(f32[8,64,128]{2,1,0:T(8,128)S(1)} %get-tuple-element.46), channel_id=1, source_target_pairs={{0,1},{1,2},{2,3},{3,4},{4,5},{5,6},{6,7},{8,9},{9,10},{10,11},{11... | collective-permute-start | bytes 786440 | tf_op jit(solution)/shard_map/ppermute | solution.py:362
  75.2 21.1 %collective-permute-start.9 = (f32[2,8,64,128]{3,2,1,0:T(8,128)S(1)}, f32[2,8,64,128]{3,2,1,0:T(8,128)S(1)}, u32[]{:S(2)}, u32[]{:S(2)}) collective-permute-start(f32[2,8,64,128]{3,2,1,0:T(8,128)S(1)} %copy-done.16), channel_id=1, source_target_pairs={{0,64},{1,8},{2,96},{3,40},{4,0},{5,72},{6,32},{7,104},{8,80},{9,2... | collective-permute-start | bytes 1572872 | tf_op jit(solution)/shard_map/ppermute | solution.py:467
  99.9 3.5 %collective-permute-start.8 = (f32[8,64,128]{2,1,0:T(8,128)S(1)}, f32[8,64,128]{2,1,0:T(8,128)S(1)}, u32[]{:S(2)}, u32[]{:S(2)}) collective-permute-start(f32[8,64,128]{2,1,0:T(8,128)S(1)} %get-tuple-element.47), channel_id=1, source_target_pairs={{1,0},{2,1},{3,2},{4,3},{5,4},{6,5},{7,6},{9,8},{10,9},{11,10},{12... | collective-permute-start | bytes 786440 | tf_op jit(solution)/shard_map/ppermute | solution.py:362
  103.5 12.9 %collective-permute-done.8.right_ref = f32[8,64,128]{2,1,0:T(8,128)S(1)} collective-permute-done((f32[8,64,128]{2,1,0:T(8,128)S(1)}, f32[8,64,128]{2,1,0:T(8,128)S(1)}, u32[]{:S(2)}, u32[]{:S(2)}) %collective-permute-start.8) | collective-permute-done | bytes 262176 | tf_op jit(solution)/shard_map/ppermute | solution.py:362
  116.4 7.4 %shard_map.78.blur_ref = f32[64,64,256]{2,1,0:T(8,128)S(1)} custom-call(bf16[768,256]{1,0:T(8,128)(2,1)S(1)} %get-tuple-element.36.u_ref, bf16[768,256]{1,0:T(8,128)(2,1)S(1)} %get-tuple-element.37.e_ref, bf16[64,192]{1,0:T(8,128)(2,1)S(1)} %get-tuple-element.38.m_ref, f32[8,64,128]{2,1,0:T(8,128)S(1)} %collective-permute-done.7.left_ref, ...), custom_call_target="tpu_custom_call" | custom-call | bytes 24000000 | tf_op jit(solution)/shard_map/pallas_call | solution.py:222
  123.8 4.4 %collective-permute-done.12.refs_7_ = f32[2,8,64,128]{3,2,1,0:T(8,128)S(1)} collective-permute-done((f32[2,8,64,128]{3,2,1,0:T(8,128)S(1)}, f32[2,8,64,128]{3,2,1,0:T(8,128)S(1)}, u32[]{:S(2)}, u32[]{:S(2)}) %collective-permute-start.12) | collective-permute-done | bytes 524320 | tf_op jit(solution)/shard_map/ppermute | solution.py:467
  128.2 2.4 %shard_map.79 = (f32[64,64,256]{2,1,0:T(8,128)S(1)}, f32[8,64,128]{2,1,0:T(8,128)S(1)}, f32[8,64,128]{2,1,0:T(8,128)S(1)}) custom-call(f32[64,64,256]{2,1,0:T(8,128)S(1)} %shard_map.78.blur_ref, f32[2,8,64,128]{3,2,1,0:T(8,128)S(1)} %collective-permute-done.3.refs_0_, f32[2,8,64,128]{3,2,1,0:T(8,128)S(1)} %collective-permute-done.4.refs_1_, ...), custom_call_target="tpu_custom_call" | custom-call | bytes 21000000 | tf_op jit(solution)/shard_map/pallas_call | solution.py:249
  132.8 2.4 %collective-permute-start.14 = (f32[8,64,128]{2,1,0:T(8,128)S(1)}, f32[8,64,128]{2,1,0:T(8,128)S(1)}, u32[]{:S(2)}, u32[]{:S(2)}) collective-permute-start(f32[8,64,128]{2,1,0:T(8,128)S(1)} %get-tuple-element.54), channel_id=1, source_target_pairs={{1,0},{2,1},{3,2},{4,3},{5,4},{6,5},{7,6},{9,8},{10,9},{11,10},{12... | collective-permute-start | bytes 786440 | tf_op jit(solution)/shard_map/ppermute | solution.py:362
  136.1 4.4 %collective-permute-done.14.right_ref = f32[8,64,128]{2,1,0:T(8,128)S(1)} collective-permute-done((f32[8,64,128]{2,1,0:T(8,128)S(1)}, f32[8,64,128]{2,1,0:T(8,128)S(1)}, u32[]{:S(2)}, u32[]{:S(2)}) %collective-permute-start.14) | collective-permute-done | bytes 262176 | tf_op jit(solution)/shard_map/ppermute | solution.py:362
  140.5 3.3 %shard_map.80 = (f32[64,16,256]{2,1,0:T(8,128)S(1)}, f32[64,16,256]{2,1,0:T(8,128)S(1)}) custom-call(bf16[768,256]{1,0:T(8,128)(2,1)S(1)} %get-tuple-element.33.u_ref, bf16[768,256]{1,0:T(8,128)(2,1)S(1)} %get-tuple-element.34.e_ref, bf16[64,192]{1,0:T(8,128)(2,1)S(1)} %get-tuple-element.35.m_ref, f32[8,64,128]{2,1,0:T(8,128)S(1)} %collective-permute-done.13.left_ref, ...), custom_call_target="tpu_custom_call" | custom-call | bytes 12000000 | tf_op jit(solution)/shard_map/pallas_call | solution.py:281
  143.9 9.0 %collective-permute-start.15 = (f32[64,16,256]{2,1,0:T(8,128)S(1)}, f32[64,16,256]{2,1,0:T(8,128)S(1)}, u32[]{:S(2)}, u32[]{:S(2)}) collective-permute-start(f32[64,16,256]{2,1,0:T(8,128)S(1)} %get-tuple-element.56.bottom_ref), channel_id=1, source_target_pairs={{0,8},{1,9},{2,10},{3,11},{4,12},{5,13},{6,14},{7,15},{8,16},{9,17... | collective-permute-start | bytes 3145736 | tf_op jit(solution)/shard_map/ppermute | solution.py:362
  154.8 7.9 %shard_map.81.part_ref = f32[64,64,256]{2,1,0:T(8,128)} custom-call(bf16[768,256]{1,0:T(8,128)(2,1)S(1)} %get-tuple-element.33.u_ref, bf16[768,256]{1,0:T(8,128)(2,1)S(1)} %get-tuple-element.34.e_ref, bf16[64,192]{1,0:T(8,128)(2,1)S(1)} %get-tuple-element.35.m_ref, bf16[64,192]{1,0:T(8,128)(2,1)S(1)} %get-tuple-element.58.a_ref, ...), custom_call_target="tpu_custom_call" | custom-call | bytes 24000000 | tf_op jit(solution)/shard_map/pallas_call | solution.py:316
  162.7 12.2 %collective-permute-done.15.up_ref = f32[64,16,256]{2,1,0:T(8,128)S(1)} collective-permute-done((f32[64,16,256]{2,1,0:T(8,128)S(1)}, f32[64,16,256]{2,1,0:T(8,128)S(1)}, u32[]{:S(2)}, u32[]{:S(2)}) %collective-permute-start.15) | collective-permute-done | bytes 1048608 | tf_op jit(solution)/shard_map/ppermute | solution.py:362
  174.9 4.1 %collective-permute-done.16.down_ref = f32[64,16,256]{2,1,0:T(8,128)S(1)} collective-permute-done((f32[64,16,256]{2,1,0:T(8,128)S(1)}, f32[64,16,256]{2,1,0:T(8,128)S(1)}, u32[]{:S(2)}, u32[]{:S(2)}) %collective-permute-start.16) | collective-permute-done | bytes 1048608 | tf_op jit(solution)/shard_map/ppermute | solution.py:362
  179.0 3.0 %shard_map.82 = f32[64,64,256]{2,1,0:T(8,128)} custom-call(bf16[2,16,48]{2,1,0:T(8,128)(2,1)S(1)} %get-tuple-element.32.a_ref, f32[64,16,256]{2,1,0:T(8,128)S(1)} %collective-permute-done.15.up_ref, f32[64,16,256]{2,1,0:T(8,128)S(1)} %collective-permute-done.16.down_ref, f32[64,64,256]{2,1,0:T(8,128)S(1)} %copy-done.2, ...), custom_call_target="tpu_custom_call", output_to_operand_aliasing={{}: (4, {})} | custom-call | bytes 9000000 | tf_op jit(solution)/shard_map/pallas_call | solution.py:347
  (62 shorter events, 27.2 us)
Async XLA Ops:
  3.9 9.3 %collective-permute-start.2 = (f32[8,8,64,128]{3,2,1,0:T(8,128)}, f32[8,8,64,128]{3,2,1,0:T(8,128)S(1)}, u32[]{:S(2)}, u32[]{:S(2)}) collective-permute-start(f32[8,8,64,128]{3,2,1,0:T(8,128)} %shard_map.75), channel_id=1, source_target_pairs={{0,1},{1,0},{2,3},{3,2},{4,5},{5,4},{6,7},{7,6},{8,9},{9,8},{10,11... | collective-permute-start | bytes 6291464 | tf_op jit(solution)/shard_map/ppermute | solution.py:464
  6.2 45.0 %copy-start.5 = (f32[64,64]{1,0:T(8,128)S(1)}, f32[64,64]{1,0:T(8,128)}, u32[]{:S(2)}) copy-start(f32[64,64]{1,0:T(8,128)} %zi_ref.1) | copy-start | bytes 49156
  6.2 45.0 %copy-start.6 = (f32[32]{0:T(128)S(1)}, f32[32]{0:T(128)}, u32[]{:S(2)}) copy-start(f32[32]{0:T(128)} %pz_ref.1) | copy-start | bytes 388
  6.2 45.0 %copy-start.7 = (f32[32]{0:T(128)S(1)}, f32[32]{0:T(128)}, u32[]{:S(2)}) copy-start(f32[32]{0:T(128)} %pr_ref.1) | copy-start | bytes 388
  6.2 45.0 %copy-start.8 = (f32[32]{0:T(128)S(1)}, f32[32]{0:T(128)}, u32[]{:S(2)}) copy-start(f32[32]{0:T(128)} %pu_ref.1) | copy-start | bytes 388
  6.2 33.1 %collective-permute-start = (f32[64,16,256]{2,1,0:T(8,128)}, f32[64,16,256]{2,1,0:T(8,128)S(1)}, u32[]{:S(2)}, u32[]{:S(2)}) collective-permute-start(f32[64,16,256]{2,1,0:T(8,128)} %get-tuple-element.40), channel_id=1, source_target_pairs={{0,8},{1,9},{2,10},{3,11},{4,12},{5,13},{6,14},{7,15},{8,16},{9,17... | collective-permute-start | bytes 3145736 | tf_op jit(solution)/shard_map/ppermute | solution.py:362
  9.6 49.1 %collective-permute-start.1 = (f32[64,16,256]{2,1,0:T(8,128)}, f32[64,16,256]{2,1,0:T(8,128)}, u32[]{:S(2)}, u32[]{:S(2)}) collective-permute-start(f32[64,16,256]{2,1,0:T(8,128)} %get-tuple-element.41), channel_id=1, source_target_pairs={{8,0},{9,1},{10,2},{11,3},{12,4},{13,5},{14,6},{15,7},{16,8},{17,9... | collective-permute-start | bytes 3145736 | tf_op jit(solution)/shard_map/ppermute | solution.py:362
  20.4 38.9 %collective-permute-start.3 = (f32[2,8,64,128]{3,2,1,0:T(8,128)}, f32[2,8,64,128]{3,2,1,0:T(8,128)S(1)}, u32[]{:S(2)}, u32[]{:S(2)}) collective-permute-start(f32[2,8,64,128]{3,2,1,0:T(8,128)} %get-tuple-element.42), channel_id=1, source_target_pairs={{0,0},{1,72},{2,32},{3,104},{4,64},{5,8},{6,96},{7,40},{8,16},{9,8... | collective-permute-start | bytes 1572872 | tf_op jit(solution)/shard_map/ppermute | solution.py:467
  24.3 35.0 %collective-permute-start.4 = (f32[2,8,64,128]{3,2,1,0:T(8,128)}, f32[2,8,64,128]{3,2,1,0:T(8,128)S(1)}, u32[]{:S(2)}, u32[]{:S(2)}) collective-permute-start(f32[2,8,64,128]{3,2,1,0:T(8,128)} %get-tuple-element.43), channel_id=1, source_target_pairs={{0,16},{1,88},{2,48},{3,120},{4,80},{5,24},{6,112},{7,56},{8,0},{9... | collective-permute-start | bytes 1572872 | tf_op jit(solution)/shard_map/ppermute | solution.py:467
  25.2 34.1 %collective-permute-start.5 = (f32[2,8,64,128]{3,2,1,0:T(8,128)}, f32[2,8,64,128]{3,2,1,0:T(8,128)S(1)}, u32[]{:S(2)}, u32[]{:S(2)}) collective-permute-start(f32[2,8,64,128]{3,2,1,0:T(8,128)} %get-tuple-element.44), channel_id=1, source_target_pairs={{0,32},{1,104},{2,64},{3,8},{4,96},{5,40},{6,0},{7,72},{8,48},{9,1... | collective-permute-start | bytes 1572872 | tf_op jit(solution)/shard_map/ppermute | solution.py:467
  39.3 20.0 %collective-permute-start.6 = (f32[2,8,64,128]{3,2,1,0:T(8,128)}, f32[2,8,64,128]{3,2,1,0:T(8,128)S(1)}, u32[]{:S(2)}, u32[]{:S(2)}) collective-permute-start(f32[2,8,64,128]{3,2,1,0:T(8,128)} %get-tuple-element.45), channel_id=1, source_target_pairs={{0,48},{1,120},{2,80},{3,24},{4,112},{5,56},{6,16},{7,88},{8,32},{... | collective-permute-start | bytes 1572872 | tf_op jit(solution)/shard_map/ppermute | solution.py:467
  61.5 34.9 %copy-start.14 = (f32[2,8,64,128]{3,2,1,0:T(8,128)S(1)}, f32[2,8,64,128]{3,2,1,0:T(8,128)}, u32[]{:S(2)}) copy-start(f32[2,8,64,128]{3,2,1,0:T(8,128)} %copy-done.13) | copy-start | bytes 1572868
  61.5 34.9 %copy-start.12 = (f32[2,8,64,128]{3,2,1,0:T(8,128)S(1)}, f32[2,8,64,128]{3,2,1,0:T(8,128)}, u32[]{:S(2)}) copy-start(f32[2,8,64,128]{3,2,1,0:T(8,128)} %copy-done.11) | copy-start | bytes 1572868
  61.5 36.9 %copy-start.10 = (f32[2,8,64,128]{3,2,1,0:T(8,128)S(1)}, f32[2,8,64,128]{3,2,1,0:T(8,128)}, u32[]{:S(2)}) copy-start(f32[2,8,64,128]{3,2,1,0:T(8,128)} %copy-done.9) | copy-start | bytes 1572868
  67.8 32.2 %collective-permute-start.7 = (f32[8,64,128]{2,1,0:T(8,128)S(1)}, f32[8,64,128]{2,1,0:T(8,128)S(1)}, u32[]{:S(2)}, u32[]{:S(2)}) collective-permute-start(f32[8,64,128]{2,1,0:T(8,128)S(1)} %get-tuple-element.46), channel_id=1, source_target_pairs={{0,1},{1,2},{2,3},{3,4},{4,5},{5,6},{6,7},{8,9},{9,10},{10,11},{11... | collective-permute-start | bytes 786440 | tf_op jit(solution)/shard_map/ppermute | solution.py:362
  75.2 48.5 %collective-permute-start.9 = (f32[2,8,64,128]{3,2,1,0:T(8,128)S(1)}, f32[2,8,64,128]{3,2,1,0:T(8,128)S(1)}, u32[]{:S(2)}, u32[]{:S(2)}) collective-permute-start(f32[2,8,64,128]{3,2,1,0:T(8,128)S(1)} %copy-done.16), channel_id=1, source_target_pairs={{0,64},{1,8},{2,96},{3,40},{4,0},{5,72},{6,32},{7,104},{8,80},{9,2... | collective-permute-start | bytes 1572872 | tf_op jit(solution)/shard_map/ppermute | solution.py:467
  96.4 27.4 %collective-permute-start.10 = (f32[2,8,64,128]{3,2,1,0:T(8,128)S(1)}, f32[2,8,64,128]{3,2,1,0:T(8,128)S(1)}, u32[]{:S(2)}, u32[]{:S(2)}) collective-permute-start(f32[2,8,64,128]{3,2,1,0:T(8,128)S(1)} %copy-done.14), channel_id=1, source_target_pairs={{0,80},{1,24},{2,112},{3,56},{4,16},{5,88},{6,48},{7,120},{8,64},{... | collective-permute-start | bytes 1572872 | tf_op jit(solution)/shard_map/ppermute | solution.py:467
  96.5 27.3 %collective-permute-start.11 = (f32[2,8,64,128]{3,2,1,0:T(8,128)S(1)}, f32[2,8,64,128]{3,2,1,0:T(8,128)S(1)}, u32[]{:S(2)}, u32[]{:S(2)}) collective-permute-start(f32[2,8,64,128]{3,2,1,0:T(8,128)S(1)} %copy-done.12), channel_id=1, source_target_pairs={{0,96},{1,40},{2,0},{3,72},{4,32},{5,104},{6,64},{7,8},{8,112},{9,... | collective-permute-start | bytes 1572872 | tf_op jit(solution)/shard_map/ppermute | solution.py:467
  98.4 29.8 %collective-permute-start.12 = (f32[2,8,64,128]{3,2,1,0:T(8,128)S(1)}, f32[2,8,64,128]{3,2,1,0:T(8,128)S(1)}, u32[]{:S(2)}, u32[]{:S(2)}) collective-permute-start(f32[2,8,64,128]{3,2,1,0:T(8,128)S(1)} %copy-done.10), channel_id=1, source_target_pairs={{0,112},{1,56},{2,16},{3,88},{4,48},{5,120},{6,80},{7,24},{8,96},{... | collective-permute-start | bytes 1572872 | tf_op jit(solution)/shard_map/ppermute | solution.py:467
  99.9 16.4 %collective-permute-start.8 = (f32[8,64,128]{2,1,0:T(8,128)S(1)}, f32[8,64,128]{2,1,0:T(8,128)S(1)}, u32[]{:S(2)}, u32[]{:S(2)}) collective-permute-start(f32[8,64,128]{2,1,0:T(8,128)S(1)} %get-tuple-element.47), channel_id=1, source_target_pairs={{1,0},{2,1},{3,2},{4,3},{5,4},{6,5},{7,6},{9,8},{10,9},{11,10},{12... | collective-permute-start | bytes 786440 | tf_op jit(solution)/shard_map/ppermute | solution.py:362
  130.6 5.5 %collective-permute-start.13 = (f32[8,64,128]{2,1,0:T(8,128)S(1)}, f32[8,64,128]{2,1,0:T(8,128)S(1)}, u32[]{:S(2)}, u32[]{:S(2)}) collective-permute-start(f32[8,64,128]{2,1,0:T(8,128)S(1)} %get-tuple-element.53), channel_id=1, source_target_pairs={{0,1},{1,2},{2,3},{3,4},{4,5},{5,6},{6,7},{8,9},{9,10},{10,11},{11... | collective-permute-start | bytes 786440 | tf_op jit(solution)/shard_map/ppermute | solution.py:362
  132.8 7.7 %collective-permute-start.14 = (f32[8,64,128]{2,1,0:T(8,128)S(1)}, f32[8,64,128]{2,1,0:T(8,128)S(1)}, u32[]{:S(2)}, u32[]{:S(2)}) collective-permute-start(f32[8,64,128]{2,1,0:T(8,128)S(1)} %get-tuple-element.54), channel_id=1, source_target_pairs={{1,0},{2,1},{3,2},{4,3},{5,4},{6,5},{7,6},{9,8},{10,9},{11,10},{12... | collective-permute-start | bytes 786440 | tf_op jit(solution)/shard_map/ppermute | solution.py:362
  143.9 31.0 %collective-permute-start.15 = (f32[64,16,256]{2,1,0:T(8,128)S(1)}, f32[64,16,256]{2,1,0:T(8,128)S(1)}, u32[]{:S(2)}, u32[]{:S(2)}) collective-permute-start(f32[64,16,256]{2,1,0:T(8,128)S(1)} %get-tuple-element.56.bottom_ref), channel_id=1, source_target_pairs={{0,8},{1,9},{2,10},{3,11},{4,12},{5,13},{6,14},{7,15},{8,16},{9,17... | collective-permute-start | bytes 3145736 | tf_op jit(solution)/shard_map/ppermute | solution.py:362
  152.9 26.1 %collective-permute-start.16 = (f32[64,16,256]{2,1,0:T(8,128)S(1)}, f32[64,16,256]{2,1,0:T(8,128)S(1)}, u32[]{:S(2)}, u32[]{:S(2)}) collective-permute-start(f32[64,16,256]{2,1,0:T(8,128)S(1)} %get-tuple-element.57.top_ref), channel_id=1, source_target_pairs={{8,0},{9,1},{10,2},{11,3},{12,4},{13,5},{14,6},{15,7},{16,8},{17,9... | collective-permute-start | bytes 3145736 | tf_op jit(solution)/shard_map/ppermute | solution.py:362
  (10 other events, 52.5 us)

commit v6 on v5

--- a/solution.py
+++ b/solution.py
@@ -64,6 +64,13 @@
                     tx, ty = target_of(x, y, z, c, k)
                     pairs.append((position(x, y, z, c), position(tx, ty, x, y // 2)))
     return pairs
+
+
+def params(mib, us):
+    return dict(
+        compiler_params=pltpu.CompilerParams(vmem_limit_bytes=mib * MIB),
+        cost_estimate=pl.CostEstimate(flops=0, transcendentals=0, bytes_accessed=us * 3_000_000),
+    )
 
 
 def table_kernel(pz_ref, pr_ref, pu_ref, zi_ref, main_ref, upper_ref, mcol_ref, ucol_ref, *outs):
@@ -142,9 +149,8 @@
     return left, right
 
 
-def edge_sums(left, right, table):
-    h, l = split(jnp.concatenate([left, right], axis=1))
-    total = dot(jnp.concatenate([h, h, l], axis=1), table)
+def edge_sums(both, table):
+    total = across(both, table)
     return total[:, :128], total[:, 128:]
 
 
@@ -165,49 +171,41 @@
     return dot(table, jnp.concatenate([h, l, h], axis=0))
 
 
-def row_kernel(table_ref, up_ref, own_ref, down_ref, *refs):
-    out_ref, left_ref, right_ref = refs[-3:]
-    table = table_ref[...]
-    planes = []
-    for z in range(8):
-        planes.append(along(table, jnp.concatenate([up_ref[z], own_ref[z], down_ref[z]], axis=0)))
-        out_ref[z] = planes[-1]
-    left_ref[0], right_ref[0] = packed(planes)
-
-
-def params(mib, us):
-    return dict(
-        compiler_params=pltpu.CompilerParams(vmem_limit_bytes=mib * MIB),
-        cost_estimate=pl.CostEstimate(flops=0, transcendentals=0, bytes_accessed=us * 3_000_000),
-    )
-
-
 def whole(t):
     return pl.BlockSpec(t.shape, lambda i: (0,) * t.ndim)
 
 
-def row_mix(table, up, own, down, after):
+def row_kernel(table_ref, own_ref, left_ref, right_ref, *refs):
+    up_ref, down_ref, up_edge_ref, down_edge_ref = refs[:4]
+    out_ref, edge_ref = refs[-2:]
+    table = table_ref[...]
+    for z in range(8):
+        out_ref[z] = along(table, jnp.concatenate([up_ref[z], own_ref[z], down_ref[z]], axis=0))
+    both = jnp.concatenate([left_ref[0], right_ref[0]], axis=1)
+    edge_ref[0] = along(table, jnp.concatenate([up_edge_ref[0], both, down_edge_ref[0]], axis=0))
+
+
+def row_mix(table, up, own, down, left, right, after):
     depth, rows, cols = own.shape
+    groups = depth // 8
     block = lambda r: pl.BlockSpec((8, r, cols), lambda i: (i, 0, 0))
-    edge = pl.BlockSpec((1, rows, 128), lambda i: (i, 0, 0))
-    edge_shape = jax.ShapeDtypeStruct((depth // 8, rows, 128), F32)
+    packs = pl.BlockSpec((1, rows, 128), lambda i: (i, 0, 0))
+    extra = pl.BlockSpec((1, 16, cols), lambda i: (depth + i, 0, 0))
     return pl.pallas_call(
         row_kernel,
-        grid=(depth // 8,),
-        in_specs=[whole(table), block(16), block(rows), block(16)] + [ANY] * len(after),
-        out_specs=[block(rows), edge, edge],
-        out_shape=[jax.ShapeDtypeStruct(own.shape, F32), edge_shape, edge_shape],
+        grid=(groups,),
+        in_specs=[whole(table), block(rows), packs, packs, block(16), block(16), extra, extra] + [ANY] * len(after),
+        out_specs=[block(rows), pl.BlockSpec((1, rows, cols), lambda i: (i, 0, 0))],
+        out_shape=[jax.ShapeDtypeStruct(own.shape, F32), jax.ShapeDtypeStruct((groups, rows, cols), F32)],
         **params(10, 4),
-    )(table, up, own, down, *after)
-
-
-def blur_kernel(u_ref, e_ref, m_ref, left_ref, right_ref, x_ref, out_ref):
+    )(table, own, left, right, up, down, up, down, *after)
+
+
+def blur_kernel(u_ref, e_ref, m_ref, edge_ref, x_ref, out_ref):
     depth, rows, cols = x_ref.shape
     total = across(x_ref[...].reshape(depth * rows, cols), u_ref[...]).reshape(depth, rows, cols)
     groups = depth // 8
-    left, right = edge_sums(
-        left_ref[...].reshape(groups * rows, 128), right_ref[...].reshape(groups * rows, 128), e_ref[...]
-    )
+    left, right = edge_sums(edge_ref[...].reshape(groups * rows, cols), e_ref[...])
     left, right = left.reshape(groups, rows, 128), right.reshape(groups, rows, 128)
     extra = [unpacked(left[g], right[g], q) for g in range(groups) for q in range(8)]
     total = jnp.transpose(total + jnp.stack(extra), (1, 0, 2))
@@ -216,17 +214,17 @@
         out_ref[r] = along(table, total[r])
 
 
-def blur(u, e, m, left, right, x):
+def blur(u, e, m, edge, x):
     depth, rows, cols = x.shape
     block = lambda d, c: pl.BlockSpec((d, 8, c), lambda i: (0, i, 0))
     return pl.pallas_call(
         blur_kernel,
         grid=(rows // 8,),
-        in_specs=[whole(u), whole(e), whole(m), block(depth // 8, 128), block(depth // 8, 128), block(depth, cols)],
+        in_specs=[whole(u), whole(e), whole(m), block(depth // 8, cols), block(depth, cols)],
         out_specs=pl.BlockSpec((8, depth, cols), lambda i: (i, 0, 0)),
         out_shape=jax.ShapeDtypeStruct((rows, depth, cols), F32),
         **params(14, 8),
-    )(u, e, m, left, right, x)
+    )(u, e, m, edge, x)
 
 
 def ratio_kernel(blur_ref, *refs):
@@ -258,7 +256,7 @@
 def spread_tile(ratio, left, right, u, e, m):
     rows, depth, cols = ratio.shape
     total = across(ratio.reshape(rows * depth, cols), u).reshape(rows, depth, cols)
-    left, right = edge_sums(left, right, e)
+    left, right = edge_sums(jnp.concatenate([left, right], axis=1), e)
     planes = [along(m, total[q] + unpacked(left, right, q)) for q in range(rows)]
     return jnp.transpose(jnp.stack(planes), (1, 0, 2))
 
@@ -394,40 +392,62 @@
     )(*inputs)
 
 
-def row_ends(est):
-    def body(est_ref, top_ref, bottom_ref, sems):
+def column_ends(est):
+    def body(est_ref, left_ref, right_ref):
+        for g in range(left_ref.shape[0]):
+            left_ref[g], right_ref[g] = packed([est_ref[8 * g + q] for q in range(8)])
+
+    depth, rows, _ = est.shape
+    vmem = pl.BlockSpec(memory_space=pltpu.VMEM)
+    return pl.pallas_call(
+        body,
+        in_specs=[vmem],
+        out_specs=[vmem] * 2,
+        out_shape=[jax.ShapeDtypeStruct((depth // 8, rows, 128), F32)] * 2,
+        **params(14, 2),
+    )(est)
+
+
+def row_ends(est, left, right):
+    def body(est_ref, left_ref, right_ref, top_ref, bottom_ref, sems):
         depth, rows, _ = est_ref.shape
         pairs = []
-        for d in range(0, depth, 16):
-            at = pl.ds(d, 16)
-            pairs.append((est_ref.at[at, :16], top_ref.at[at]))
-            pairs.append((est_ref.at[at, rows - 16 :], bottom_ref.at[at]))
+        for out, r in ((top_ref, 0), (bottom_ref, rows - 16)):
+            at = pl.ds(r, 16)
+            for d in range(0, depth, 16):
+                pairs.append((est_ref.at[pl.ds(d, 16), at], out.at[pl.ds(d, 16)]))
+            tail = pl.ds(depth, depth // 8)
+            pairs.append((left_ref.at[:, at], out.at[tail, :, pl.ds(0, 128)]))
+            pairs.append((right_ref.at[:, at], out.at[tail, :, pl.ds(128, 128)]))
         run_copies(pairs, sems)
 
     depth, _, cols = est.shape
-    return copy_call(body, depth // 8, [(depth, 16, cols)] * 2, (est,), 2)
-
-
-def far_half(measured, rows):
-    def body(measured_ref, out_ref, sems):
-        _, _, _, c = place()
-        run_copies([(measured_ref.at[p, :, 1 - c], out_ref.at[p]) for p in range(8)], sems)
-
-    return copy_call(body, 8, [(8, 8, rows, 128)], (measured.reshape(8, 8, 2, rows, 128),), 2)[0]
-
-
-def pieces_of(measured, far, rows):
-    def body(measured_ref, far_ref, *refs):
+    return copy_call(body, depth // 8 + 4, [(depth + depth // 8, 16, cols)] * 2, (est, left, right), 2)
+
+
+def halves_of(measured, rows):
+    def body(measured_ref, near_ref, far_ref, sems):
+        x, y, z, c = place()
+        pairs = []
+        for out, core in ((near_ref, c), (far_ref, 1 - c)):
+            for k in range(8):
+                tx, ty = target_of(x, y, z, core, k)
+                pairs.append((measured_ref.at[:, tx * 4 + ty], out.at[k]))
+        run_copies(pairs, sems)
+
+    return copy_call(body, 16, [(8, 8, rows, 128)] * 2, (measured.reshape(8, 16, rows, 128),), 2)
+
+
+def pieces_of(near, far):
+    def body(near_ref, far_ref, *refs):
         outs, sems = refs[:-1], refs[-1]
         pairs = []
         for k, out in enumerate(outs):
-            tx, ty = target_of(*place(), k)
-            pairs.append((measured_ref.at[:, tx * 4 + ty], out.at[0]))
-            pairs.append((far_ref.at[:, tx * 2 + (ty >> 1)], out.at[1]))
+            pairs.append((near_ref.at[k], out.at[0]))
+            pairs.append((far_ref.at[k], out.at[1]))
         run_copies(pairs, sems)
 
-    inputs = (measured.reshape(8, 16, rows, 128), far)
-    return copy_call(body, 16, [(2, 8, rows, 128)] * 8, inputs, 3)
+    return copy_call(body, 16, [(2, *near.shape[1:])] * 8, (near, far), 2)
 
 
 def diagonal_windows(r_interp, gx, rows):
@@ -442,9 +462,9 @@
     return window(main), window(upper)
 
 
-def forward(tables, up, estimate, down, column_edges, after):
-    mixed, left, right = row_mix(tables[0], up, estimate, down, after)
-    return blur(tables[3], tables[4], tables[7], *column_edges(left, right), mixed)
+def forward(tables, up, estimate, down, left, right, after):
+    mixed, edge = row_mix(tables[0], up, estimate, down, left, right, after)
+    return blur(tables[3], tables[4], tables[7], edge, mixed)
 
 
 def backward(tables, ratio, left, right, estimate, column_edges, row_edges):
@@ -460,12 +480,14 @@
     depth, rows, width = estimate.shape
     gx = lax.axis_index("gx")
     row_edges = lambda top, bottom: (send(bottom, "gx", 1), send(top, "gx", -1))
-    up, down = row_edges(*row_ends(estimate))
-    far = lax.ppermute(far_half(measured, rows), AXES, core_swap())
+    left, right = column_edges(*column_ends(estimate))
+    near, far = halves_of(measured, rows)
+    far = lax.ppermute(far, AXES, core_swap())
+    up, down = row_edges(*row_ends(estimate, left, right))
     main, upper = diagonal_windows(r_interp, gx, rows)
     tables = make_tables(psf_z, psf_r, psf_u, z_interp, main, upper, rows, width)
-    pieces = [lax.ppermute(p, AXES, piece_perm(k)) for k, p in enumerate(pieces_of(measured, far, rows))]
-    blurred = forward(tables, up, estimate, down, column_edges, pieces[:4])
+    pieces = [lax.ppermute(p, AXES, piece_perm(k)) for k, p in enumerate(pieces_of(near, far))]
+    blurred = forward(tables, up, estimate, down, left, right, pieces[:3])
     ratio, left, right = ratio_of(blurred, pieces)
     return backward(tables, ratio, left, right, estimate, column_edges, row_edges)
 

time: 183 us -> 181 us (0.989)
  the two profiles are of different devices: /device:TPU:75 before, /device:TPU:1 now
where the time goes in v6:
time: 181 us; the launch traced here: 180 us
  starting transfers between devices  69.6 us (38%)
  waiting for transfers between devices  60.8 us (34%)
  Pallas kernels  36.9 us (20%)
  local copies, waits for them, and re-layouts  10.9 us (6%)
    ppermute x8, waiting for transfers between devices, send(): return lax.ppermute(x, AXES, shift_perm(axis, d))  51 us
    ppermute x8, starting transfers between devices, send(): return lax.ppermute(x, AXES, shift_perm(axis, d))  38.1 us
    ppermute x8, starting transfers between devices, shards(): lax.ppermute(p, AXES, piece_perm(k))  30 us
    unnamed x34, local copies, waits for them, and re-layouts  10.5 us
    ppermute x8, waiting for transfers between devices, shards(): lax.ppermute(p, AXES, piece_perm(k))  9.87 us
    pallas_call x1, Pallas kernels, own_update(): pl.pallas_call(own_kernel, grid=(inner + depth // 8,), in_specs=[whole(u)...  7.94 us
    pallas_call x1, Pallas kernels, blur(): pl.pallas_call(blur_kernel, grid=(rows // 8,), in_specs=[whole(u), whole(...  7.36 us
    pallas_call x1, Pallas kernels, ratio_of(): pl.pallas_call(ratio_kernel, in_specs=[vmem] * (1 + len(pieces)), out_spe...  4.25 us
  transfers between devices with their start and end apart: 17, of which 11 were waited for; matrix products, arithmetic and copies ran while one was open for 1% of the time, Pallas kernels for 14%

profile of v6, /device:TPU:1, one launch (start us, length us, event | category | flops | bytes accessed | tf_op | source)
XLA Modules:
  0.0 180.1 jit_solution(7934564336899165761)
XLA Ops:
  0.0 2.3 %copy-done.3 = f32[8,1024,128]{2,1,0:T(8,128)S(1)} copy-done((f32[8,1024,128]{2,1,0:T(8,128)S(1)}, f32[8,1024,128]{2,1,0:T(8,128)}, u32[]{:S(2)}) %copy-start.3) | copy-done | bytes 4194328
  5.4 4.0 %collective-permute-start = (f32[8,64,128]{2,1,0:T(8,128)S(1)}, f32[8,64,128]{2,1,0:T(8,128)S(1)}, u32[]{:S(2)}, u32[]{:S(2)}) collective-permute-start(f32[8,64,128]{2,1,0:T(8,128)S(1)} %get-tuple-element.43), channel_id=1, source_target_pairs={{0,1},{1,2},{2,3},{3,4},{4,5},{5,6},{6,7},{8,9},{9,10},{10,11},{11... | collective-permute-start | bytes 786440 | tf_op jit(solution)/shard_map/ppermute | solution.py:360
  12.7 4.6 %collective-permute-done.1.right_ref = f32[8,64,128]{2,1,0:T(8,128)S(1)} collective-permute-done((f32[8,64,128]{2,1,0:T(8,128)S(1)}, f32[8,64,128]{2,1,0:T(8,128)S(1)}, u32[]{:S(2)}, u32[]{:S(2)}) %collective-permute-start.1) | collective-permute-done | bytes 262176 | tf_op jit(solution)/shard_map/ppermute | solution.py:360
  19.0 3.3 %collective-permute-start.2 = (f32[72,16,256]{2,1,0:T(8,128)}, f32[72,16,256]{2,1,0:T(8,128)S(1)}, u32[]{:S(2)}, u32[]{:S(2)}) collective-permute-start(f32[72,16,256]{2,1,0:T(8,128)} %get-tuple-element.45), channel_id=1, source_target_pairs={{0,8},{1,9},{2,10},{3,11},{4,12},{5,13},{6,14},{7,15},{8,16},{9,17... | collective-permute-start | bytes 3538952 | tf_op jit(solution)/shard_map/ppermute | solution.py:360
  29.3 2.6 %collective-permute-start.5 = (f32[2,8,64,128]{3,2,1,0:T(8,128)}, f32[2,8,64,128]{3,2,1,0:T(8,128)S(1)}, u32[]{:S(2)}, u32[]{:S(2)}) collective-permute-start(f32[2,8,64,128]{3,2,1,0:T(8,128)} %get-tuple-element.49), channel_id=1, source_target_pairs={{0,0},{1,72},{2,32},{3,104},{4,64},{5,8},{6,96},{7,40},{8,16},{9,8... | collective-permute-start | bytes 1572872 | tf_op jit(solution)/shard_map/ppermute | solution.py:489
  31.8 9.0 %collective-permute-start.6 = (f32[2,8,64,128]{3,2,1,0:T(8,128)}, f32[2,8,64,128]{3,2,1,0:T(8,128)S(1)}, u32[]{:S(2)}, u32[]{:S(2)}) collective-permute-start(f32[2,8,64,128]{3,2,1,0:T(8,128)} %get-tuple-element.50), channel_id=1, source_target_pairs={{0,16},{1,88},{2,48},{3,120},{4,80},{5,24},{6,112},{7,56},{8,0},{9... | collective-permute-start | bytes 1572872 | tf_op jit(solution)/shard_map/ppermute | solution.py:489
  44.5 9.5 %collective-permute-done.2.refs_0_.refs_2_ = f32[72,16,256]{2,1,0:T(8,128)S(1)} collective-permute-done((f32[72,16,256]{2,1,0:T(8,128)}, f32[72,16,256]{2,1,0:T(8,128)S(1)}, u32[]{:S(2)}, u32[]{:S(2)}) %collective-permute-start.2) | collective-permute-done | bytes 1179680 | tf_op jit(solution)/shard_map/ppermute | solution.py:360
  54.0 15.4 %collective-permute-done.3.refs_1_.refs_3_ = f32[72,16,256]{2,1,0:T(8,128)S(1)} collective-permute-done((f32[72,16,256]{2,1,0:T(8,128)}, f32[72,16,256]{2,1,0:T(8,128)S(1)}, u32[]{:S(2)}, u32[]{:S(2)}) %collective-permute-start.3) | collective-permute-done | bytes 1179680 | tf_op jit(solution)/shard_map/ppermute | solution.py:360
  71.3 5.0 %collective-permute-done.5.refs_4_.refs_0_ = f32[2,8,64,128]{3,2,1,0:T(8,128)S(1)} collective-permute-done((f32[2,8,64,128]{3,2,1,0:T(8,128)}, f32[2,8,64,128]{3,2,1,0:T(8,128)S(1)}, u32[]{:S(2)}, u32[]{:S(2)}) %collective-permute-start.5) | collective-permute-done | bytes 524320 | tf_op jit(solution)/shard_map/ppermute | solution.py:489
  76.4 12.4 %collective-permute-start.10 = (f32[2,8,64,128]{3,2,1,0:T(8,128)}, f32[2,8,64,128]{3,2,1,0:T(8,128)}, u32[]{:S(2)}, u32[]{:S(2)}) collective-permute-start(f32[2,8,64,128]{3,2,1,0:T(8,128)} %copy-done.14), channel_id=1, source_target_pairs={{0,80},{1,24},{2,112},{3,56},{4,16},{5,88},{6,48},{7,120},{8,64},{... | collective-permute-start | bytes 1572872 | tf_op jit(solution)/shard_map/ppermute | solution.py:489
  91.3 2.8 %shard_map.73 = (bf16[64,288]{1,0:T(8,128)(2,1)S(1)}, bf16[64,192]{1,0:T(8,128)(2,1)S(1)}, bf16[2,16,48]{2,1,0:T(8,128)(2,1)S(1)}, bf16[768,256]{1,0:T(8,128)(2,...) custom-call(f32[32]{0:T(128)S(1)} %copy-done.9, ...), custom_call_target="tpu_custom_call" | custom-call | bytes 9000000 | tf_op jit(solution)/shard_map/pallas_call | solution.py:131
  94.1 2.2 %copy-done.1 = f32[64,64,256]{2,1,0:T(8,128)S(1)} copy-done((f32[64,64,256]{2,1,0:T(8,128)S(1)}, f32[64,64,256]{2,1,0:T(8,128)}, u32[]{:S(2)}) %copy-start.1) | copy-done | bytes 4194328
  98.2 3.3 %shard_map.78 = (f32[64,64,256]{2,1,0:T(8,128)S(1)}, f32[8,64,256]{2,1,0:T(8,128)S(1)}) custom-call(bf16[64,288]{1,0:T(8,128)(2,1)S(1)} %get-tuple-element.42.table_ref, f32[64,64,256]{2,1,0:T(8,128)S(1)} %copy-done.1, f32[8,64,128]{2,1,0:T(8,128)S(1)} %copy-done.5, f32[8,64,128]{2,1,0:T(8,128)S(1)} %copy-done.7, ...), custom_call_target="tpu_custom_call" | custom-call | bytes 12000000 | tf_op jit(solution)/shard_map/pallas_call | solution.py:194
  101.5 7.4 %shard_map.79.blur_ref = f32[64,64,256]{2,1,0:T(8,128)S(1)} custom-call(bf16[768,256]{1,0:T(8,128)(2,1)S(1)} %get-tuple-element.39.u_ref, bf16[768,256]{1,0:T(8,128)(2,1)S(1)} %get-tuple-element.40.e_ref, bf16[64,192]{1,0:T(8,128)(2,1)S(1)} %get-tuple-element.41.m_ref, f32[8,64,256]{2,1,0:T(8,128)S(1)} %get-tuple-element.52.edge_ref, ...), custom_call_target="tpu_custom_call" | custom-call | bytes 24000000 | tf_op jit(solution)/shard_map/pallas_call | solution.py:220
  108.9 2.8 %collective-permute-done.10.refs_5_ = f32[2,8,64,128]{3,2,1,0:T(8,128)} collective-permute-done((f32[2,8,64,128]{3,2,1,0:T(8,128)}, f32[2,8,64,128]{3,2,1,0:T(8,128)}, u32[]{:S(2)}, u32[]{:S(2)}) %collective-permute-start.10) | collective-permute-done | bytes 524320 | tf_op jit(solution)/shard_map/ppermute | solution.py:489
  113.7 4.2 %shard_map.80 = (f32[64,64,256]{2,1,0:T(8,128)S(1)}, f32[8,64,128]{2,1,0:T(8,128)S(1)}, f32[8,64,128]{2,1,0:T(8,128)S(1)}) custom-call(f32[64,64,256]{2,1,0:T(8,128)S(1)} %shard_map.79.blur_ref, f32[2,8,64,128]{3,2,1,0:T(8,128)S(1)} %collective-permute-done.5.refs_4_.refs_0_, f32[2,8,64,128]{3,2,1,0:T(8,128)S(1)} %collective-permute-done.6.refs_5_.refs_1_, ...), custom_call_target="tpu_custom_call" | custom-call | bytes 21000000 | tf_op jit(solution)/shard_map/pallas_call | solution.py:247
  118.0 21.8 %collective-permute-start.13 = (f32[8,64,128]{2,1,0:T(8,128)S(1)}, f32[8,64,128]{2,1,0:T(8,128)S(1)}, u32[]{:S(2)}, u32[]{:S(2)}) collective-permute-start(f32[8,64,128]{2,1,0:T(8,128)S(1)} %get-tuple-element.59), channel_id=1, source_target_pairs={{0,1},{1,2},{2,3},{3,4},{4,5},{5,6},{6,7},{8,9},{9,10},{10,11},{11... | collective-permute-start | bytes 786440 | tf_op jit(solution)/shard_map/ppermute | solution.py:360
  143.1 4.4 %collective-permute-done.14.right_ref = f32[8,64,128]{2,1,0:T(8,128)S(1)} collective-permute-done((f32[8,64,128]{2,1,0:T(8,128)S(1)}, f32[8,64,128]{2,1,0:T(8,128)S(1)}, u32[]{:S(2)}, u32[]{:S(2)}) %collective-permute-start.14) | collective-permute-done | bytes 262176 | tf_op jit(solution)/shard_map/ppermute | solution.py:360
  147.5 3.4 %shard_map.81 = (f32[64,16,256]{2,1,0:T(8,128)S(1)}, f32[64,16,256]{2,1,0:T(8,128)S(1)}) custom-call(bf16[768,256]{1,0:T(8,128)(2,1)S(1)} %get-tuple-element.36.u_ref, bf16[768,256]{1,0:T(8,128)(2,1)S(1)} %get-tuple-element.37.e_ref, bf16[64,192]{1,0:T(8,128)(2,1)S(1)} %get-tuple-element.38.m_ref, f32[8,64,128]{2,1,0:T(8,128)S(1)} %collective-permute-done.13.left_ref, ...), custom_call_target="tpu_custom_call" | custom-call | bytes 12000000 | tf_op jit(solution)/shard_map/pallas_call | solution.py:279
  150.9 2.4 %collective-permute-start.15 = (f32[64,16,256]{2,1,0:T(8,128)S(1)}, f32[64,16,256]{2,1,0:T(8,128)S(1)}, u32[]{:S(2)}, u32[]{:S(2)}) collective-permute-start(f32[64,16,256]{2,1,0:T(8,128)S(1)} %get-tuple-element.62.bottom_ref), channel_id=1, source_target_pairs={{0,8},{1,9},{2,10},{3,11},{4,12},{5,13},{6,14},{7,15},{8,16},{9,17... | collective-permute-start | bytes 3145736 | tf_op jit(solution)/shard_map/ppermute | solution.py:360
  154.6 7.9 %shard_map.82.part_ref = f32[64,64,256]{2,1,0:T(8,128)} custom-call(bf16[768,256]{1,0:T(8,128)(2,1)S(1)} %get-tuple-element.36.u_ref, bf16[768,256]{1,0:T(8,128)(2,1)S(1)} %get-tuple-element.37.e_ref, bf16[64,192]{1,0:T(8,128)(2,1)S(1)} %get-tuple-element.38.m_ref, bf16[64,192]{1,0:T(8,128)(2,1)S(1)} %get-tuple-element.64.a_ref, ...), custom_call_target="tpu_custom_call" | custom-call | bytes 24000000 | tf_op jit(solution)/shard_map/pallas_call | solution.py:314
  162.5 10.4 %collective-permute-done.15.up_ref = f32[64,16,256]{2,1,0:T(8,128)S(1)} collective-permute-done((f32[64,16,256]{2,1,0:T(8,128)S(1)}, f32[64,16,256]{2,1,0:T(8,128)S(1)}, u32[]{:S(2)}, u32[]{:S(2)}) %collective-permute-start.15) | collective-permute-done | bytes 1048608 | tf_op jit(solution)/shard_map/ppermute | solution.py:360
  172.9 4.2 %collective-permute-done.16.down_ref = f32[64,16,256]{2,1,0:T(8,128)S(1)} collective-permute-done((f32[64,16,256]{2,1,0:T(8,128)S(1)}, f32[64,16,256]{2,1,0:T(8,128)S(1)}, u32[]{:S(2)}, u32[]{:S(2)}) %collective-permute-start.16) | collective-permute-done | bytes 1048608 | tf_op jit(solution)/shard_map/ppermute | solution.py:360
  177.0 3.0 %shard_map.83 = f32[64,64,256]{2,1,0:T(8,128)} custom-call(bf16[2,16,48]{2,1,0:T(8,128)(2,1)S(1)} %get-tuple-element.35.a_ref, f32[64,16,256]{2,1,0:T(8,128)S(1)} %collective-permute-done.15.up_ref, f32[64,16,256]{2,1,0:T(8,128)S(1)} %collective-permute-done.16.down_ref, f32[64,64,256]{2,1,0:T(8,128)S(1)} %copy-done.2, ...), custom_call_target="tpu_custom_call", output_to_operand_aliasing={{}: (4, {})} | custom-call | bytes 9000000 | tf_op jit(solution)/shard_map/pallas_call | solution.py:345
  (63 shorter events, 31.3 us)
Async XLA Ops:
  2.8 20.8 %collective-permute-start.4 = (f32[8,8,64,128]{3,2,1,0:T(8,128)S(1)}, f32[8,8,64,128]{3,2,1,0:T(8,128)S(1)}, u32[]{:S(2)}, u32[]{:S(2)}) collective-permute-start(f32[8,8,64,128]{3,2,1,0:T(8,128)S(1)} %get-tuple-element.48), channel_id=1, source_target_pairs={{0,1},{1,0},{2,3},{3,2},{4,5},{5,4},{6,7},{7,6},{8,9},{9,8},{10,11... | collective-permute-start | bytes 6291464 | tf_op jit(solution)/shard_map/ppermute | solution.py:485
  5.4 7.3 %collective-permute-start = (f32[8,64,128]{2,1,0:T(8,128)S(1)}, f32[8,64,128]{2,1,0:T(8,128)S(1)}, u32[]{:S(2)}, u32[]{:S(2)}) collective-permute-start(f32[8,64,128]{2,1,0:T(8,128)S(1)} %get-tuple-element.43), channel_id=1, source_target_pairs={{0,1},{1,2},{2,3},{3,4},{4,5},{5,6},{6,7},{8,9},{9,10},{10,11},{11... | collective-permute-start | bytes 786440 | tf_op jit(solution)/shard_map/ppermute | solution.py:360
  9.4 81.9 %copy-start.8 = (f32[64,64]{1,0:T(8,128)S(1)}, f32[64,64]{1,0:T(8,128)}, u32[]{:S(2)}) copy-start(f32[64,64]{1,0:T(8,128)} %zi_ref.1) | copy-start | bytes 49156
  9.4 81.8 %copy-start.9 = (f32[32]{0:T(128)S(1)}, f32[32]{0:T(128)}, u32[]{:S(2)}) copy-start(f32[32]{0:T(128)} %pz_ref.1) | copy-start | bytes 388
  9.4 81.8 %copy-start.10 = (f32[32]{0:T(128)S(1)}, f32[32]{0:T(128)}, u32[]{:S(2)}) copy-start(f32[32]{0:T(128)} %pr_ref.1) | copy-start | bytes 388
  9.4 81.8 %copy-start.11 = (f32[32]{0:T(128)S(1)}, f32[32]{0:T(128)}, u32[]{:S(2)}) copy-start(f32[32]{0:T(128)} %pu_ref.1) | copy-start | bytes 388
  9.5 7.8 %collective-permute-start.1 = (f32[8,64,128]{2,1,0:T(8,128)S(1)}, f32[8,64,128]{2,1,0:T(8,128)S(1)}, u32[]{:S(2)}, u32[]{:S(2)}) collective-permute-start(f32[8,64,128]{2,1,0:T(8,128)S(1)} %get-tuple-element.44), channel_id=1, source_target_pairs={{1,0},{2,1},{3,2},{4,3},{5,4},{6,5},{7,6},{9,8},{10,9},{11,10},{12... | collective-permute-start | bytes 786440 | tf_op jit(solution)/shard_map/ppermute | solution.py:360
  12.7 10.9 %copy-start.4 = (f32[8,64,128]{2,1,0:T(8,128)}, f32[8,64,128]{2,1,0:T(8,128)S(1)}, u32[]{:S(2)}) copy-start(f32[8,64,128]{2,1,0:T(8,128)S(1)} %collective-permute-done.left_ref) | copy-start | bytes 786436
  17.3 6.3 %copy-start.6 = (f32[8,64,128]{2,1,0:T(8,128)}, f32[8,64,128]{2,1,0:T(8,128)S(1)}, u32[]{:S(2)}) copy-start(f32[8,64,128]{2,1,0:T(8,128)S(1)} %collective-permute-done.1.right_ref) | copy-start | bytes 786436
  19.0 35.0 %collective-permute-start.2 = (f32[72,16,256]{2,1,0:T(8,128)}, f32[72,16,256]{2,1,0:T(8,128)S(1)}, u32[]{:S(2)}, u32[]{:S(2)}) collective-permute-start(f32[72,16,256]{2,1,0:T(8,128)} %get-tuple-element.45), channel_id=1, source_target_pairs={{0,8},{1,9},{2,10},{3,11},{4,12},{5,13},{6,14},{7,15},{8,16},{9,17... | collective-permute-start | bytes 3538952 | tf_op jit(solution)/shard_map/ppermute | solution.py:360
  22.3 47.1 %collective-permute-start.3 = (f32[72,16,256]{2,1,0:T(8,128)}, f32[72,16,256]{2,1,0:T(8,128)S(1)}, u32[]{:S(2)}, u32[]{:S(2)}) collective-permute-start(f32[72,16,256]{2,1,0:T(8,128)} %get-tuple-element.46), channel_id=1, source_target_pairs={{8,0},{9,1},{10,2},{11,3},{12,4},{13,5},{14,6},{15,7},{16,8},{17,9... | collective-permute-start | bytes 3538952 | tf_op jit(solution)/shard_map/ppermute | solution.py:360
  29.3 47.1 %collective-permute-start.5 = (f32[2,8,64,128]{3,2,1,0:T(8,128)}, f32[2,8,64,128]{3,2,1,0:T(8,128)S(1)}, u32[]{:S(2)}, u32[]{:S(2)}) collective-permute-start(f32[2,8,64,128]{3,2,1,0:T(8,128)} %get-tuple-element.49), channel_id=1, source_target_pairs={{0,0},{1,72},{2,32},{3,104},{4,64},{5,8},{6,96},{7,40},{8,16},{9,8... | collective-permute-start | bytes 1572872 | tf_op jit(solution)/shard_map/ppermute | solution.py:489
  31.8 57.0 %collective-permute-start.6 = (f32[2,8,64,128]{3,2,1,0:T(8,128)}, f32[2,8,64,128]{3,2,1,0:T(8,128)S(1)}, u32[]{:S(2)}, u32[]{:S(2)}) collective-permute-start(f32[2,8,64,128]{3,2,1,0:T(8,128)} %get-tuple-element.50), channel_id=1, source_target_pairs={{0,16},{1,88},{2,48},{3,120},{4,80},{5,24},{6,112},{7,56},{8,0},{9... | collective-permute-start | bytes 1572872 | tf_op jit(solution)/shard_map/ppermute | solution.py:489
  40.9 49.9 %collective-permute-start.7 = (f32[2,8,64,128]{3,2,1,0:T(8,128)}, f32[2,8,64,128]{3,2,1,0:T(8,128)}, u32[]{:S(2)}, u32[]{:S(2)}) collective-permute-start(f32[2,8,64,128]{3,2,1,0:T(8,128)} %get-tuple-element.51), channel_id=1, source_target_pairs={{0,32},{1,104},{2,64},{3,8},{4,96},{5,40},{6,0},{7,72},{8,48},{9,1... | collective-permute-start | bytes 1572872 | tf_op jit(solution)/shard_map/ppermute | solution.py:489
  54.0 54.8 %collective-permute-start.8 = (f32[2,8,64,128]{3,2,1,0:T(8,128)}, f32[2,8,64,128]{3,2,1,0:T(8,128)}, u32[]{:S(2)}, u32[]{:S(2)}) collective-permute-start(f32[2,8,64,128]{3,2,1,0:T(8,128)} %copy-done.16), channel_id=1, source_target_pairs={{0,48},{1,120},{2,80},{3,24},{4,112},{5,56},{6,16},{7,88},{8,32},{... | collective-permute-start | bytes 1572872 | tf_op jit(solution)/shard_map/ppermute | solution.py:489
  69.4 39.4 %collective-permute-start.9 = (f32[2,8,64,128]{3,2,1,0:T(8,128)}, f32[2,8,64,128]{3,2,1,0:T(8,128)}, u32[]{:S(2)}, u32[]{:S(2)}) collective-permute-start(f32[2,8,64,128]{3,2,1,0:T(8,128)} %copy-done.15), channel_id=1, source_target_pairs={{0,64},{1,8},{2,96},{3,40},{4,0},{5,72},{6,32},{7,104},{8,80},{9,2... | collective-permute-start | bytes 1572872 | tf_op jit(solution)/shard_map/ppermute | solution.py:489
  76.4 35.3 %collective-permute-start.10 = (f32[2,8,64,128]{3,2,1,0:T(8,128)}, f32[2,8,64,128]{3,2,1,0:T(8,128)}, u32[]{:S(2)}, u32[]{:S(2)}) collective-permute-start(f32[2,8,64,128]{3,2,1,0:T(8,128)} %copy-done.14), channel_id=1, source_target_pairs={{0,80},{1,24},{2,112},{3,56},{4,16},{5,88},{6,48},{7,120},{8,64},{... | collective-permute-start | bytes 1572872 | tf_op jit(solution)/shard_map/ppermute | solution.py:489
  88.8 22.9 %collective-permute-start.11 = (f32[2,8,64,128]{3,2,1,0:T(8,128)}, f32[2,8,64,128]{3,2,1,0:T(8,128)}, u32[]{:S(2)}, u32[]{:S(2)}) collective-permute-start(f32[2,8,64,128]{3,2,1,0:T(8,128)} %copy-done.13), channel_id=1, source_target_pairs={{0,96},{1,40},{2,0},{3,72},{4,32},{5,104},{6,64},{7,8},{8,112},{9,... | collective-permute-start | bytes 1572872 | tf_op jit(solution)/shard_map/ppermute | solution.py:489
  90.7 23.0 %collective-permute-start.12 = (f32[2,8,64,128]{3,2,1,0:T(8,128)}, f32[2,8,64,128]{3,2,1,0:T(8,128)}, u32[]{:S(2)}, u32[]{:S(2)}) collective-permute-start(f32[2,8,64,128]{3,2,1,0:T(8,128)} %copy-done.12), channel_id=1, source_target_pairs={{0,112},{1,56},{2,16},{3,88},{4,48},{5,120},{6,80},{7,24},{8,96},{... | collective-permute-start | bytes 1572872 | tf_op jit(solution)/shard_map/ppermute | solution.py:489
  118.0 36.6 %copy-start.2 = (f32[64,64,256]{2,1,0:T(8,128)S(1)}, f32[64,64,256]{2,1,0:T(8,128)}, u32[]{:S(2)}) copy-start(f32[64,64,256]{2,1,0:T(8,128)} %est_ref.7) | copy-start | bytes 12582916
  118.0 25.1 %collective-permute-start.13 = (f32[8,64,128]{2,1,0:T(8,128)S(1)}, f32[8,64,128]{2,1,0:T(8,128)S(1)}, u32[]{:S(2)}, u32[]{:S(2)}) collective-permute-start(f32[8,64,128]{2,1,0:T(8,128)S(1)} %get-tuple-element.59), channel_id=1, source_target_pairs={{0,1},{1,2},{2,3},{3,4},{4,5},{5,6},{6,7},{8,9},{9,10},{10,11},{11... | collective-permute-start | bytes 786440 | tf_op jit(solution)/shard_map/ppermute | solution.py:360
  139.8 7.7 %collective-permute-start.14 = (f32[8,64,128]{2,1,0:T(8,128)S(1)}, f32[8,64,128]{2,1,0:T(8,128)S(1)}, u32[]{:S(2)}, u32[]{:S(2)}) collective-permute-start(f32[8,64,128]{2,1,0:T(8,128)S(1)} %get-tuple-element.60), channel_id=1, source_target_pairs={{1,0},{2,1},{3,2},{4,3},{5,4},{6,5},{7,6},{9,8},{10,9},{11,10},{12... | collective-permute-start | bytes 786440 | tf_op jit(solution)/shard_map/ppermute | solution.py:360
  150.9 22.0 %collective-permute-start.15 = (f32[64,16,256]{2,1,0:T(8,128)S(1)}, f32[64,16,256]{2,1,0:T(8,128)S(1)}, u32[]{:S(2)}, u32[]{:S(2)}) collective-permute-start(f32[64,16,256]{2,1,0:T(8,128)S(1)} %get-tuple-element.62.bottom_ref), channel_id=1, source_target_pairs={{0,8},{1,9},{2,10},{3,11},{4,12},{5,13},{6,14},{7,15},{8,16},{9,17... | collective-permute-start | bytes 3145736 | tf_op jit(solution)/shard_map/ppermute | solution.py:360
  153.3 23.8 %collective-permute-start.16 = (f32[64,16,256]{2,1,0:T(8,128)S(1)}, f32[64,16,256]{2,1,0:T(8,128)S(1)}, u32[]{:S(2)}, u32[]{:S(2)}) collective-permute-start(f32[64,16,256]{2,1,0:T(8,128)S(1)} %get-tuple-element.63.top_ref), channel_id=1, source_target_pairs={{8,0},{9,1},{10,2},{11,3},{12,4},{13,5},{14,6},{15,7},{16,8},{17,9... | collective-permute-start | bytes 3145736 | tf_op jit(solution)/shard_map/ppermute | solution.py:360
  (10 other events, 14.8 us)

commit v7 on v6

--- a/solution.py
+++ b/solution.py
@@ -175,9 +175,8 @@
     return pl.BlockSpec(t.shape, lambda i: (0,) * t.ndim)
 
 
-def row_kernel(table_ref, own_ref, left_ref, right_ref, *refs):
-    up_ref, down_ref, up_edge_ref, down_edge_ref = refs[:4]
-    out_ref, edge_ref = refs[-2:]
+def row_kernel(*refs):
+    (table_ref, own_ref, left_ref, right_ref, up_ref, down_ref, up_edge_ref, down_edge_ref, out_ref, edge_ref) = refs[-10:]
     table = table_ref[...]
     for z in range(8):
         out_ref[z] = along(table, jnp.concatenate([up_ref[z], own_ref[z], down_ref[z]], axis=0))
@@ -194,11 +193,11 @@
     return pl.pallas_call(
         row_kernel,
         grid=(groups,),
-        in_specs=[whole(table), block(rows), packs, packs, block(16), block(16), extra, extra] + [ANY] * len(after),
+        in_specs=[ANY] * len(after) + [whole(table), block(rows), packs, packs, block(16), block(16), extra, extra],
         out_specs=[block(rows), pl.BlockSpec((1, rows, cols), lambda i: (i, 0, 0))],
         out_shape=[jax.ShapeDtypeStruct(own.shape, F32), jax.ShapeDtypeStruct((groups, rows, cols), F32)],
         **params(10, 4),
-    )(table, own, left, right, up, down, up, down, *after)
+    )(*after, table, own, left, right, up, down, up, down)
 
 
 def blur_kernel(u_ref, e_ref, m_ref, edge_ref, x_ref, out_ref):
@@ -408,8 +407,9 @@
     )(est)
 
 
-def row_ends(est, left, right):
-    def body(est_ref, left_ref, right_ref, top_ref, bottom_ref, sems):
+def row_ends(est, left, right, after):
+    def body(*refs):
+        est_ref, left_ref, right_ref, top_ref, bottom_ref, sems = refs[-6:]
         depth, rows, _ = est_ref.shape
         pairs = []
         for out, r in ((top_ref, 0), (bottom_ref, rows - 16)):
@@ -422,7 +422,7 @@
         run_copies(pairs, sems)
 
     depth, _, cols = est.shape
-    return copy_call(body, depth // 8 + 4, [(depth + depth // 8, 16, cols)] * 2, (est, left, right), 2)
+    return copy_call(body, depth // 8 + 4, [(depth + depth // 8, 16, cols)] * 2, (*after, est, left, right), 2)
 
 
 def halves_of(measured, rows):
@@ -438,16 +438,18 @@
     return copy_call(body, 16, [(8, 8, rows, 128)] * 2, (measured.reshape(8, 16, rows, 128),), 2)
 
 
-def pieces_of(near, far):
-    def body(near_ref, far_ref, *refs):
-        outs, sems = refs[:-1], refs[-1]
+def pieces_of(near, far, steps, after):
+    def body(*refs):
+        near_ref, far_ref, *outs = refs[len(after) : -1]
+        sems = refs[-1]
         pairs = []
-        for k, out in enumerate(outs):
+        for k, out in zip(steps, outs):
             pairs.append((near_ref.at[k], out.at[0]))
             pairs.append((far_ref.at[k], out.at[1]))
         run_copies(pairs, sems)
 
-    return copy_call(body, 16, [(2, *near.shape[1:])] * 8, (near, far), 2)
+    shapes = [(2, *near.shape[1:])] * len(steps)
+    return copy_call(body, 2 * len(steps), shapes, (*after, near, far), 2)
 
 
 def diagonal_windows(r_interp, gx, rows):
@@ -483,10 +485,14 @@
     left, right = column_edges(*column_ends(estimate))
     near, far = halves_of(measured, rows)
     far = lax.ppermute(far, AXES, core_swap())
-    up, down = row_edges(*row_ends(estimate, left, right))
+    ship = lambda parts, steps: [lax.ppermute(p, AXES, piece_perm(k)) for p, k in zip(parts, steps)]
+    parts = pieces_of(near, far, range(3), ())
+    pieces = ship(parts, range(3))
+    top, bottom = row_ends(estimate, left, right, parts[:1])
+    up, down = row_edges(top, bottom)
     main, upper = diagonal_windows(r_interp, gx, rows)
     tables = make_tables(psf_z, psf_r, psf_u, z_interp, main, upper, rows, width)
-    pieces = [lax.ppermute(p, AXES, piece_perm(k)) for k, p in enumerate(pieces_of(near, far))]
+    pieces += ship(pieces_of(near, far, range(3, 8), (top, tables[0])), range(3, 8))
     blurred = forward(tables, up, estimate, down, left, right, pieces[:3])
     ratio, left, right = ratio_of(blurred, pieces)
     return backward(tables, ratio, left, right, estimate, column_edges, row_edges)

time: 181 us -> 193 us (1.066)
  the two profiles are of different devices: /device:TPU:1 before, /device:TPU:57 now
where the time goes in v7:
time: 193 us; the launch traced here: 192 us
  starting transfers between devices  81 us (42%)
  waiting for transfers between devices  57.5 us (30%)
  Pallas kernels  37.6 us (19%)
  local copies, waits for them, and re-layouts  14.1 us (7%)
    ppermute x8, starting transfers between devices, send(): return lax.ppermute(x, AXES, shift_perm(axis, d))  44.7 us
    ppermute x8, starting transfers between devices, shards(): lax.ppermute(p, AXES, piece_perm(k))  35.6 us
    ppermute x8, waiting for transfers between devices, shards(): lax.ppermute(p, AXES, piece_perm(k))  35.3 us
    ppermute x8, waiting for transfers between devices, send(): return lax.ppermute(x, AXES, shift_perm(axis, d))  22.2 us
    unnamed x32, local copies, waits for them, and re-layouts  10.2 us
    pallas_call x1, Pallas kernels, own_update(): pl.pallas_call(own_kernel, grid=(inner + depth // 8,), in_specs=[whole(u)...  7.93 us
    pallas_call x1, Pallas kernels, blur(): pl.pallas_call(blur_kernel, grid=(rows // 8,), in_specs=[whole(u), whole(...  7.36 us
    pallas_call x1, Pallas kernels, row_mix(): pl.pallas_call(row_kernel, grid=(groups,), in_specs=[ANY] * len(after) +...  5.79 us
  transfers between devices with their start and end apart: 17, of which 8 were waited for; matrix products, arithmetic and copies ran while one was open for 3% of the time, Pallas kernels for 13%

profile of v7, /device:TPU:57, one launch (start us, length us, event | category | flops | bytes accessed | tf_op | source)
XLA Modules:
  0.0 192.1 jit_solution(12146786147499763989)
XLA Ops:
  0.0 2.3 %copy-done.4 = f32[8,1024,128]{2,1,0:T(8,128)S(1)} copy-done((f32[8,1024,128]{2,1,0:T(8,128)S(1)}, f32[8,1024,128]{2,1,0:T(8,128)}, u32[]{:S(2)}) %copy-start.4) | copy-done | bytes 4194328
  4.6 4.0 %collective-permute-start.4 = (f32[8,64,128]{2,1,0:T(8,128)S(1)}, f32[8,64,128]{2,1,0:T(8,128)S(1)}, u32[]{:S(2)}, u32[]{:S(2)}) collective-permute-start(f32[8,64,128]{2,1,0:T(8,128)S(1)} %get-tuple-element.48), channel_id=1, source_target_pairs={{0,1},{1,2},{2,3},{3,4},{4,5},{5,6},{6,7},{8,9},{9,10},{10,11},{11... | collective-permute-start | bytes 786440 | tf_op jit(solution)/shard_map/ppermute | solution.py:359
  13.7 2.6 %collective-permute-done.5.refs_3_.refs_6_ = f32[8,64,128]{2,1,0:T(8,128)S(1)} collective-permute-done((f32[8,64,128]{2,1,0:T(8,128)S(1)}, f32[8,64,128]{2,1,0:T(8,128)S(1)}, u32[]{:S(2)}, u32[]{:S(2)}) %collective-permute-start.5) | collective-permute-done | bytes 262176 | tf_op jit(solution)/shard_map/ppermute | solution.py:359
  18.0 2.8 %collective-permute-start.6 = (f32[72,16,256]{2,1,0:T(8,128)}, f32[72,16,256]{2,1,0:T(8,128)S(1)}, u32[]{:S(2)}, u32[]{:S(2)}) collective-permute-start(f32[72,16,256]{2,1,0:T(8,128)} %get-tuple-element.50), channel_id=1, source_target_pairs={{0,8},{1,9},{2,10},{3,11},{4,12},{5,13},{6,14},{7,15},{8,16},{9,17... | collective-permute-start | bytes 3538952 | tf_op jit(solution)/shard_map/ppermute | solution.py:359
  20.8 2.5 %collective-permute-start.7 = (f32[72,16,256]{2,1,0:T(8,128)}, f32[72,16,256]{2,1,0:T(8,128)}, u32[]{:S(2)}, u32[]{:S(2)}) collective-permute-start(f32[72,16,256]{2,1,0:T(8,128)} %get-tuple-element.51.refs_0_), channel_id=1, source_target_pairs={{8,0},{9,1},{10,2},{11,3},{12,4},{13,5},{14,6},{15,7},{16,8},{17,9... | collective-permute-start | bytes 3538952 | tf_op jit(solution)/shard_map/ppermute | solution.py:359
  24.8 2.7 %collective-permute-start.1 = (f32[2,8,64,128]{3,2,1,0:T(8,128)}, f32[2,8,64,128]{3,2,1,0:T(8,128)}, u32[]{:S(2)}, u32[]{:S(2)}) collective-permute-start(f32[2,8,64,128]{3,2,1,0:T(8,128)} %copy-done.7), channel_id=1, source_target_pairs={{0,0},{1,72},{2,32},{3,104},{4,64},{5,8},{6,96},{7,40},{8,16},{9,8... | collective-permute-start | bytes 1572872 | tf_op jit(solution)/shard_map/ppermute | solution.py:488
  27.4 5.4 %collective-permute-start.2 = (f32[2,8,64,128]{3,2,1,0:T(8,128)}, f32[2,8,64,128]{3,2,1,0:T(8,128)}, u32[]{:S(2)}, u32[]{:S(2)}) collective-permute-start(f32[2,8,64,128]{3,2,1,0:T(8,128)} %copy-done.15), channel_id=1, source_target_pairs={{0,16},{1,88},{2,48},{3,120},{4,80},{5,24},{6,112},{7,56},{8,0},{9... | collective-permute-start | bytes 1572872 | tf_op jit(solution)/shard_map/ppermute | solution.py:488
  32.9 3.1 %collective-permute-start.3 = (f32[2,8,64,128]{3,2,1,0:T(8,128)}, f32[2,8,64,128]{3,2,1,0:T(8,128)}, u32[]{:S(2)}, u32[]{:S(2)}) collective-permute-start(f32[2,8,64,128]{3,2,1,0:T(8,128)} %copy-done.14), channel_id=1, source_target_pairs={{0,32},{1,104},{2,64},{3,8},{4,96},{5,40},{6,0},{7,72},{8,48},{9,1... | collective-permute-start | bytes 1572872 | tf_op jit(solution)/shard_map/ppermute | solution.py:488
  43.3 2.7 %shard_map.73 = (bf16[64,288]{1,0:T(8,128)(2,1)S(1)}, bf16[64,192]{1,0:T(8,128)(2,1)S(1)}, bf16[2,16,48]{2,1,0:T(8,128)(2,1)S(1)}, bf16[768,256]{1,0:T(8,128)(2,...) custom-call(f32[32]{0:T(128)S(1)} %copy-done.11, ...), custom_call_target="tpu_custom_call" | custom-call | bytes 9000000 | tf_op jit(solution)/shard_map/pallas_call | solution.py:131
  47.9 21.6 %collective-permute-done.2.refs_1_ = f32[2,8,64,128]{3,2,1,0:T(8,128)} collective-permute-done((f32[2,8,64,128]{3,2,1,0:T(8,128)}, f32[2,8,64,128]{3,2,1,0:T(8,128)}, u32[]{:S(2)}, u32[]{:S(2)}) %collective-permute-start.2) | collective-permute-done | bytes 524320 | tf_op jit(solution)/shard_map/ppermute | solution.py:488
  69.5 12.9 %collective-permute-start.8 = (f32[2,8,64,128]{3,2,1,0:T(8,128)S(1)}, f32[2,8,64,128]{3,2,1,0:T(8,128)S(1)}, u32[]{:S(2)}, u32[]{:S(2)}) collective-permute-start(f32[2,8,64,128]{3,2,1,0:T(8,128)S(1)} %get-tuple-element.54), channel_id=1, source_target_pairs={{0,48},{1,120},{2,80},{3,24},{4,112},{5,56},{6,16},{7,88},{8,32},{... | collective-permute-start | bytes 1572872 | tf_op jit(solution)/shard_map/ppermute | solution.py:488
  84.4 9.4 %collective-permute-start.11 = (f32[2,8,64,128]{3,2,1,0:T(8,128)S(1)}, f32[2,8,64,128]{3,2,1,0:T(8,128)S(1)}, u32[]{:S(2)}, u32[]{:S(2)}) collective-permute-start(f32[2,8,64,128]{3,2,1,0:T(8,128)S(1)} %get-tuple-element.57), channel_id=1, source_target_pairs={{0,96},{1,40},{2,0},{3,72},{4,32},{5,104},{6,64},{7,8},{8,112},{9,... | collective-permute-start | bytes 1572872 | tf_op jit(solution)/shard_map/ppermute | solution.py:488
  94.0 5.8 %shard_map.78 = (f32[64,64,256]{2,1,0:T(8,128)S(1)}, f32[8,64,256]{2,1,0:T(8,128)S(1)}) custom-call(f32[2,8,64,128]{3,2,1,0:T(8,128)} %collective-permute-done.1.refs_0_, f32[2,8,64,128]{3,2,1,0:T(8,128)} %collective-permute-done.2.refs_1_, f32[2,8,64,128]{3,2,1,0:T(8,128)} %collective-permute-done.3.refs_2_, ...), custom_call_target="tpu_custom_call" | custom-call | bytes 12000000 | tf_op jit(solution)/shard_map/pallas_call | solution.py:193
  99.8 7.4 %shard_map.79.blur_ref = f32[64,64,256]{2,1,0:T(8,128)S(1)} custom-call(bf16[768,256]{1,0:T(8,128)(2,1)S(1)} %get-tuple-element.39.u_ref, bf16[768,256]{1,0:T(8,128)(2,1)S(1)} %get-tuple-element.40.e_ref, bf16[64,192]{1,0:T(8,128)(2,1)S(1)} %get-tuple-element.41.m_ref, f32[8,64,256]{2,1,0:T(8,128)S(1)} %get-tuple-element.52.edge_ref, ...), custom_call_target="tpu_custom_call" | custom-call | bytes 24000000 | tf_op jit(solution)/shard_map/pallas_call | solution.py:219
  107.2 11.5 %collective-permute-done.11.refs_6_ = f32[2,8,64,128]{3,2,1,0:T(8,128)S(1)} collective-permute-done((f32[2,8,64,128]{3,2,1,0:T(8,128)S(1)}, f32[2,8,64,128]{3,2,1,0:T(8,128)S(1)}, u32[]{:S(2)}, u32[]{:S(2)}) %collective-permute-start.11) | collective-permute-done | bytes 524320 | tf_op jit(solution)/shard_map/ppermute | solution.py:488
  120.9 3.8 %shard_map.81 = (f32[64,64,256]{2,1,0:T(8,128)S(1)}, f32[8,64,128]{2,1,0:T(8,128)S(1)}, f32[8,64,128]{2,1,0:T(8,128)S(1)}) custom-call(f32[64,64,256]{2,1,0:T(8,128)S(1)} %shard_map.79.blur_ref, f32[2,8,64,128]{3,2,1,0:T(8,128)} %collective-permute-done.1.refs_0_, f32[2,8,64,128]{3,2,1,0:T(8,128)} %collective-permute-done.2.refs_1_, ...), custom_call_target="tpu_custom_call" | custom-call | bytes 21000000 | tf_op jit(solution)/shard_map/pallas_call | solution.py:246
  124.6 26.3 %collective-permute-start.13 = (f32[8,64,128]{2,1,0:T(8,128)S(1)}, f32[8,64,128]{2,1,0:T(8,128)S(1)}, u32[]{:S(2)}, u32[]{:S(2)}) collective-permute-start(f32[8,64,128]{2,1,0:T(8,128)S(1)} %get-tuple-element.59), channel_id=1, source_target_pairs={{0,1},{1,2},{2,3},{3,4},{4,5},{5,6},{6,7},{8,9},{9,10},{10,11},{11... | collective-permute-start | bytes 786440 | tf_op jit(solution)/shard_map/ppermute | solution.py:359
  154.3 4.4 %collective-permute-done.14.right_ref = f32[8,64,128]{2,1,0:T(8,128)S(1)} collective-permute-done((f32[8,64,128]{2,1,0:T(8,128)S(1)}, f32[8,64,128]{2,1,0:T(8,128)S(1)}, u32[]{:S(2)}, u32[]{:S(2)}) %collective-permute-start.14) | collective-permute-done | bytes 262176 | tf_op jit(solution)/shard_map/ppermute | solution.py:359
  158.6 3.4 %shard_map.82 = (f32[64,16,256]{2,1,0:T(8,128)S(1)}, f32[64,16,256]{2,1,0:T(8,128)S(1)}) custom-call(bf16[768,256]{1,0:T(8,128)(2,1)S(1)} %get-tuple-element.36.u_ref, bf16[768,256]{1,0:T(8,128)(2,1)S(1)} %get-tuple-element.37.e_ref, bf16[64,192]{1,0:T(8,128)(2,1)S(1)} %get-tuple-element.38.m_ref, f32[8,64,128]{2,1,0:T(8,128)S(1)} %collective-permute-done.13.left_ref, ...), custom_call_target="tpu_custom_call" | custom-call | bytes 12000000 | tf_op jit(solution)/shard_map/pallas_call | solution.py:278
  164.0 3.4 %collective-permute-start.16 = (f32[64,16,256]{2,1,0:T(8,128)S(1)}, f32[64,16,256]{2,1,0:T(8,128)S(1)}, u32[]{:S(2)}, u32[]{:S(2)}) collective-permute-start(f32[64,16,256]{2,1,0:T(8,128)S(1)} %get-tuple-element.63.top_ref), channel_id=1, source_target_pairs={{8,0},{9,1},{10,2},{11,3},{12,4},{13,5},{14,6},{15,7},{16,8},{17,9... | collective-permute-start | bytes 3145736 | tf_op jit(solution)/shard_map/ppermute | solution.py:359
  167.3 7.9 %shard_map.83.part_ref = f32[64,64,256]{2,1,0:T(8,128)} custom-call(bf16[768,256]{1,0:T(8,128)(2,1)S(1)} %get-tuple-element.36.u_ref, bf16[768,256]{1,0:T(8,128)(2,1)S(1)} %get-tuple-element.37.e_ref, bf16[64,192]{1,0:T(8,128)(2,1)S(1)} %get-tuple-element.38.m_ref, bf16[64,192]{1,0:T(8,128)(2,1)S(1)} %get-tuple-element.64.a_ref, ...), custom_call_target="tpu_custom_call" | custom-call | bytes 24000000 | tf_op jit(solution)/shard_map/pallas_call | solution.py:313
  175.3 10.1 %collective-permute-done.15.up_ref = f32[64,16,256]{2,1,0:T(8,128)S(1)} collective-permute-done((f32[64,16,256]{2,1,0:T(8,128)S(1)}, f32[64,16,256]{2,1,0:T(8,128)S(1)}, u32[]{:S(2)}, u32[]{:S(2)}) %collective-permute-start.15) | collective-permute-done | bytes 1048608 | tf_op jit(solution)/shard_map/ppermute | solution.py:359
  185.3 3.7 %collective-permute-done.16.down_ref = f32[64,16,256]{2,1,0:T(8,128)S(1)} collective-permute-done((f32[64,16,256]{2,1,0:T(8,128)S(1)}, f32[64,16,256]{2,1,0:T(8,128)S(1)}, u32[]{:S(2)}, u32[]{:S(2)}) %collective-permute-start.16) | collective-permute-done | bytes 1048608 | tf_op jit(solution)/shard_map/ppermute | solution.py:359
  189.1 3.0 %shard_map.84 = f32[64,64,256]{2,1,0:T(8,128)} custom-call(bf16[2,16,48]{2,1,0:T(8,128)(2,1)S(1)} %get-tuple-element.35.a_ref, f32[64,16,256]{2,1,0:T(8,128)S(1)} %collective-permute-done.15.up_ref, f32[64,16,256]{2,1,0:T(8,128)S(1)} %collective-permute-done.16.down_ref, f32[64,64,256]{2,1,0:T(8,128)S(1)} %copy-done.1, ...), custom_call_target="tpu_custom_call", output_to_operand_aliasing={{}: (4, {})} | custom-call | bytes 9000000 | tf_op jit(solution)/shard_map/pallas_call | solution.py:344
  (62 shorter events, 29.0 us)
Async XLA Ops:
  0.0 3.6 %copy-start = (f32[64,64,256]{2,1,0:T(8,128)S(1)}, f32[64,64,256]{2,1,0:T(8,128)}, u32[]{:S(2)}) copy-start(f32[64,64,256]{2,1,0:T(8,128)} %est_ref.5) | copy-start | bytes 12582916
  0.0 2.3 %copy-start.4 = (f32[8,1024,128]{2,1,0:T(8,128)S(1)}, f32[8,1024,128]{2,1,0:T(8,128)}, u32[]{:S(2)}) copy-start(f32[8,1024,128]{2,1,0:T(8,128)} %param.8) | copy-start | bytes 12582916
  2.8 7.7 %collective-permute-start = (f32[8,8,64,128]{3,2,1,0:T(8,128)S(1)}, f32[8,8,64,128]{3,2,1,0:T(8,128)S(1)}, u32[]{:S(2)}, u32[]{:S(2)}) collective-permute-start(f32[8,8,64,128]{3,2,1,0:T(8,128)S(1)} %get-tuple-element.43), channel_id=1, source_target_pairs={{0,1},{1,0},{2,3},{3,2},{4,5},{5,4},{6,7},{7,6},{8,9},{9,8},{10,11... | collective-permute-start | bytes 6291464 | tf_op jit(solution)/shard_map/ppermute | solution.py:487
  4.6 9.1 %collective-permute-start.4 = (f32[8,64,128]{2,1,0:T(8,128)S(1)}, f32[8,64,128]{2,1,0:T(8,128)S(1)}, u32[]{:S(2)}, u32[]{:S(2)}) collective-permute-start(f32[8,64,128]{2,1,0:T(8,128)S(1)} %get-tuple-element.48), channel_id=1, source_target_pairs={{0,1},{1,2},{2,3},{3,4},{4,5},{5,6},{6,7},{8,9},{9,10},{10,11},{11... | collective-permute-start | bytes 786440 | tf_op jit(solution)/shard_map/ppermute | solution.py:359
  8.6 7.7 %collective-permute-start.5 = (f32[8,64,128]{2,1,0:T(8,128)S(1)}, f32[8,64,128]{2,1,0:T(8,128)S(1)}, u32[]{:S(2)}, u32[]{:S(2)}) collective-permute-start(f32[8,64,128]{2,1,0:T(8,128)S(1)} %get-tuple-element.49), channel_id=1, source_target_pairs={{1,0},{2,1},{3,2},{4,3},{5,4},{6,5},{7,6},{9,8},{10,9},{11,10},{12... | collective-permute-start | bytes 786440 | tf_op jit(solution)/shard_map/ppermute | solution.py:359
  10.5 29.5 %copy-start.11 = (f32[32]{0:T(128)S(1)}, f32[32]{0:T(128)}, u32[]{:S(2)}) copy-start(f32[32]{0:T(128)} %pz_ref.1) | copy-start | bytes 388
  10.5 29.5 %copy-start.12 = (f32[32]{0:T(128)S(1)}, f32[32]{0:T(128)}, u32[]{:S(2)}) copy-start(f32[32]{0:T(128)} %pr_ref.1) | copy-start | bytes 388
  13.7 4.3 %copy-start.7 = (f32[2,8,64,128]{3,2,1,0:T(8,128)}, f32[2,8,64,128]{3,2,1,0:T(8,128)S(1)}, u32[]{:S(2)}) copy-start(f32[2,8,64,128]{3,2,1,0:T(8,128)S(1)} %get-tuple-element.44.refs_0_) | copy-start | bytes 1572868
  18.0 66.5 %collective-permute-start.6 = (f32[72,16,256]{2,1,0:T(8,128)}, f32[72,16,256]{2,1,0:T(8,128)S(1)}, u32[]{:S(2)}, u32[]{:S(2)}) collective-permute-start(f32[72,16,256]{2,1,0:T(8,128)} %get-tuple-element.50), channel_id=1, source_target_pairs={{0,8},{1,9},{2,10},{3,11},{4,12},{5,13},{6,14},{7,15},{8,16},{9,17... | collective-permute-start | bytes 3538952 | tf_op jit(solution)/shard_map/ppermute | solution.py:359
  20.8 73.1 %collective-permute-start.7 = (f32[72,16,256]{2,1,0:T(8,128)}, f32[72,16,256]{2,1,0:T(8,128)}, u32[]{:S(2)}, u32[]{:S(2)}) collective-permute-start(f32[72,16,256]{2,1,0:T(8,128)} %get-tuple-element.51.refs_0_), channel_id=1, source_target_pairs={{8,0},{9,1},{10,2},{11,3},{12,4},{13,5},{14,6},{15,7},{16,8},{17,9... | collective-permute-start | bytes 3538952 | tf_op jit(solution)/shard_map/ppermute | solution.py:359
  24.8 59.6 %collective-permute-start.1 = (f32[2,8,64,128]{3,2,1,0:T(8,128)}, f32[2,8,64,128]{3,2,1,0:T(8,128)}, u32[]{:S(2)}, u32[]{:S(2)}) collective-permute-start(f32[2,8,64,128]{3,2,1,0:T(8,128)} %copy-done.7), channel_id=1, source_target_pairs={{0,0},{1,72},{2,32},{3,104},{4,64},{5,8},{6,96},{7,40},{8,16},{9,8... | collective-permute-start | bytes 1572872 | tf_op jit(solution)/shard_map/ppermute | solution.py:488
  27.4 42.1 %collective-permute-start.2 = (f32[2,8,64,128]{3,2,1,0:T(8,128)}, f32[2,8,64,128]{3,2,1,0:T(8,128)}, u32[]{:S(2)}, u32[]{:S(2)}) collective-permute-start(f32[2,8,64,128]{3,2,1,0:T(8,128)} %copy-done.15), channel_id=1, source_target_pairs={{0,16},{1,88},{2,48},{3,120},{4,80},{5,24},{6,112},{7,56},{8,0},{9... | collective-permute-start | bytes 1572872 | tf_op jit(solution)/shard_map/ppermute | solution.py:488
  32.9 49.5 %collective-permute-start.3 = (f32[2,8,64,128]{3,2,1,0:T(8,128)}, f32[2,8,64,128]{3,2,1,0:T(8,128)}, u32[]{:S(2)}, u32[]{:S(2)}) collective-permute-start(f32[2,8,64,128]{3,2,1,0:T(8,128)} %copy-done.14), channel_id=1, source_target_pairs={{0,32},{1,104},{2,64},{3,8},{4,96},{5,40},{6,0},{7,72},{8,48},{9,1... | collective-permute-start | bytes 1572872 | tf_op jit(solution)/shard_map/ppermute | solution.py:488
  40.0 54.0 %copy-start.1 = (f32[64,64,256]{2,1,0:T(8,128)S(1)}, f32[64,64,256]{2,1,0:T(8,128)}, u32[]{:S(2)}) copy-start(f32[64,64,256]{2,1,0:T(8,128)} %est_ref.5) | copy-start | bytes 12582916
  47.6 46.4 %copy-start.6 = (f32[8,64,128]{2,1,0:T(8,128)S(1)}, f32[8,64,128]{2,1,0:T(8,128)}, u32[]{:S(2)}) copy-start(f32[8,64,128]{2,1,0:T(8,128)} %copy-done.5) | copy-start | bytes 786436
  69.5 37.6 %collective-permute-start.8 = (f32[2,8,64,128]{3,2,1,0:T(8,128)S(1)}, f32[2,8,64,128]{3,2,1,0:T(8,128)S(1)}, u32[]{:S(2)}, u32[]{:S(2)}) collective-permute-start(f32[2,8,64,128]{3,2,1,0:T(8,128)S(1)} %get-tuple-element.54), channel_id=1, source_target_pairs={{0,48},{1,120},{2,80},{3,24},{4,112},{5,56},{6,16},{7,88},{8,32},{... | collective-permute-start | bytes 1572872 | tf_op jit(solution)/shard_map/ppermute | solution.py:488
  82.4 24.8 %collective-permute-start.9 = (f32[2,8,64,128]{3,2,1,0:T(8,128)S(1)}, f32[2,8,64,128]{3,2,1,0:T(8,128)S(1)}, u32[]{:S(2)}, u32[]{:S(2)}) collective-permute-start(f32[2,8,64,128]{3,2,1,0:T(8,128)S(1)} %get-tuple-element.55), channel_id=1, source_target_pairs={{0,64},{1,8},{2,96},{3,40},{4,0},{5,72},{6,32},{7,104},{8,80},{9,2... | collective-permute-start | bytes 1572872 | tf_op jit(solution)/shard_map/ppermute | solution.py:488
  84.3 22.8 %collective-permute-start.10 = (f32[2,8,64,128]{3,2,1,0:T(8,128)S(1)}, f32[2,8,64,128]{3,2,1,0:T(8,128)S(1)}, u32[]{:S(2)}, u32[]{:S(2)}) collective-permute-start(f32[2,8,64,128]{3,2,1,0:T(8,128)S(1)} %get-tuple-element.56), channel_id=1, source_target_pairs={{0,80},{1,24},{2,112},{3,56},{4,16},{5,88},{6,48},{7,120},{8,64},{... | collective-permute-start | bytes 1572872 | tf_op jit(solution)/shard_map/ppermute | solution.py:488
  84.4 34.3 %collective-permute-start.11 = (f32[2,8,64,128]{3,2,1,0:T(8,128)S(1)}, f32[2,8,64,128]{3,2,1,0:T(8,128)S(1)}, u32[]{:S(2)}, u32[]{:S(2)}) collective-permute-start(f32[2,8,64,128]{3,2,1,0:T(8,128)S(1)} %get-tuple-element.57), channel_id=1, source_target_pairs={{0,96},{1,40},{2,0},{3,72},{4,32},{5,104},{6,64},{7,8},{8,112},{9,... | collective-permute-start | bytes 1572872 | tf_op jit(solution)/shard_map/ppermute | solution.py:488
  93.9 27.0 %collective-permute-start.12 = (f32[2,8,64,128]{3,2,1,0:T(8,128)S(1)}, f32[2,8,64,128]{3,2,1,0:T(8,128)S(1)}, u32[]{:S(2)}, u32[]{:S(2)}) collective-permute-start(f32[2,8,64,128]{3,2,1,0:T(8,128)S(1)} %get-tuple-element.58), channel_id=1, source_target_pairs={{0,112},{1,56},{2,16},{3,88},{4,48},{5,120},{6,80},{7,24},{8,96},{... | collective-permute-start | bytes 1572872 | tf_op jit(solution)/shard_map/ppermute | solution.py:488
  124.6 29.6 %collective-permute-start.13 = (f32[8,64,128]{2,1,0:T(8,128)S(1)}, f32[8,64,128]{2,1,0:T(8,128)S(1)}, u32[]{:S(2)}, u32[]{:S(2)}) collective-permute-start(f32[8,64,128]{2,1,0:T(8,128)S(1)} %get-tuple-element.59), channel_id=1, source_target_pairs={{0,1},{1,2},{2,3},{3,4},{4,5},{5,6},{6,7},{8,9},{9,10},{10,11},{11... | collective-permute-start | bytes 786440 | tf_op jit(solution)/shard_map/ppermute | solution.py:359
  151.0 7.7 %collective-permute-start.14 = (f32[8,64,128]{2,1,0:T(8,128)S(1)}, f32[8,64,128]{2,1,0:T(8,128)S(1)}, u32[]{:S(2)}, u32[]{:S(2)}) collective-permute-start(f32[8,64,128]{2,1,0:T(8,128)S(1)} %get-tuple-element.60), channel_id=1, source_target_pairs={{1,0},{2,1},{3,2},{4,3},{5,4},{6,5},{7,6},{9,8},{10,9},{11,10},{12... | collective-permute-start | bytes 786440 | tf_op jit(solution)/shard_map/ppermute | solution.py:359
  162.0 23.3 %collective-permute-start.15 = (f32[64,16,256]{2,1,0:T(8,128)S(1)}, f32[64,16,256]{2,1,0:T(8,128)S(1)}, u32[]{:S(2)}, u32[]{:S(2)}) collective-permute-start(f32[64,16,256]{2,1,0:T(8,128)S(1)} %get-tuple-element.62.bottom_ref), channel_id=1, source_target_pairs={{0,8},{1,9},{2,10},{3,11},{4,12},{5,13},{6,14},{7,15},{8,16},{9,17... | collective-permute-start | bytes 3145736 | tf_op jit(solution)/shard_map/ppermute | solution.py:359
  164.0 25.1 %collective-permute-start.16 = (f32[64,16,256]{2,1,0:T(8,128)S(1)}, f32[64,16,256]{2,1,0:T(8,128)S(1)}, u32[]{:S(2)}, u32[]{:S(2)}) collective-permute-start(f32[64,16,256]{2,1,0:T(8,128)S(1)} %get-tuple-element.63.top_ref), channel_id=1, source_target_pairs={{8,0},{9,1},{10,2},{11,3},{12,4},{13,5},{14,6},{15,7},{16,8},{17,9... | collective-permute-start | bytes 3145736 | tf_op jit(solution)/shard_map/ppermute | solution.py:359
  (9 other events, 9.5 us)

commit v8 on v6

--- a/solution.py
+++ b/solution.py
@@ -227,29 +227,35 @@
     )(u, e, m, edge, x)
 
 
-def ratio_kernel(blur_ref, *refs):
-    pieces, (out_ref, left_ref, right_ref) = refs[:-3], refs[-3:]
-    for k, piece in enumerate(pieces):
-        pair, core, half = source_of(*place(), k)
-        cols = pl.ds(pl.multiple_of(half * 128, 128), 128)
-        for part in range(2):
-            planes = pl.ds(pl.multiple_of((pair * 2 + (core ^ part)) * 8, 8), 8)
-            seen = jnp.transpose(piece[part], (1, 0, 2))
-            out_ref[:, planes, cols] = seen / (blur_ref[:, planes, cols] + background)
-    for g in range(left_ref.shape[0]):
-        left_ref[g], right_ref[g] = packed([out_ref[8 * g + q] for q in range(8)])
-
-
-def ratio_of(blurred, pieces):
-    rows, depth, cols = blurred.shape
+EARLY = 3
+ENDS = ((0, 0, 16), (48, 16, 16))
+INNER = ((16, 0, 32),)
+
+
+def ratio_of(blurred, pieces, segments):
+    def body(blur_ref, *refs):
+        pieces, (out_ref, left_ref, right_ref) = refs[:-3], refs[-3:]
+        for k, piece in enumerate(pieces):
+            pair, core, half = source_of(*place(), k)
+            cols = pl.ds(pl.multiple_of(half * 128, 128), 128)
+            for part in range(2):
+                planes = pl.ds(pl.multiple_of((pair * 2 + (core ^ part)) * 8, 8), 8)
+                seen = jnp.transpose(piece[part], (1, 0, 2))
+                for start, here, n in segments:
+                    below = blur_ref[start : start + n, planes, cols] + background
+                    out_ref[here : here + n, planes, cols] = seen[here : here + n] / below
+        for g in range(left_ref.shape[0]):
+            left_ref[g], right_ref[g] = packed([out_ref[8 * g + q] for q in range(8)])
+
+    _, depth, cols = blurred.shape
     vmem = pl.BlockSpec(memory_space=pltpu.VMEM)
-    shapes = [blurred.shape] + [(rows // 8, depth, 128)] * 2
-    return pl.pallas_call(
-        ratio_kernel,
+    shapes = [(32, depth, cols)] + [(4, depth, 128)] * 2
+    return pl.pallas_call(
+        body,
         in_specs=[vmem] * (1 + len(pieces)),
         out_specs=[vmem] * 3,
         out_shape=[jax.ShapeDtypeStruct(s, F32) for s in shapes],
-        **params(20, 7),
+        **params(14, 3),
     )(blurred, *pieces)
 
 
@@ -261,7 +267,8 @@
     return jnp.transpose(jnp.stack(planes), (1, 0, 2))
 
 
-def ends_kernel(u_ref, e_ref, m_ref, left_ref, right_ref, x_ref, top_ref, bottom_ref):
+def ends_kernel(*refs):
+    u_ref, e_ref, m_ref, left_ref, right_ref, x_ref, top_ref, bottom_ref = refs[-8:]
     step = pl.program_id(0)
     tile = spread_tile(x_ref[...], left_ref[0], right_ref[0], u_ref[...], e_ref[...], m_ref[...])
     for s, ref in ((0, top_ref), (2, bottom_ref)):
@@ -272,20 +279,21 @@
                 ref[:, 8 * t : 8 * t + 8, :] = tile
 
 
-def spread_ends(u, e, m, left, right, ratio):
-    rows, depth, cols = ratio.shape
-    at = lambda i: (jnp.where(i < 2, i, rows // 8 - 4 + i), 0, 0)
+def spread_ends(u, e, m, left, right, ratio, after):
+    _, depth, cols = ratio.shape
+    at = lambda i: (i, 0, 0)
     end = pl.BlockSpec((depth, 16, cols), lambda i: (0, 0, 0))
     return pl.pallas_call(
         ends_kernel,
         grid=(4,),
-        in_specs=[whole(u), whole(e), whole(m)]
+        in_specs=[ANY] * len(after)
+        + [whole(u), whole(e), whole(m)]
         + [pl.BlockSpec((1, depth, 128), at)] * 2
         + [pl.BlockSpec((8, depth, cols), at)],
         out_specs=[end, end],
         out_shape=[jax.ShapeDtypeStruct((depth, 16, cols), F32)] * 2,
         **params(14, 4),
-    )(u, e, m, left, right, ratio)
+    )(*after, u, e, m, left, right, ratio)
 
 
 def own_kernel(u_ref, e_ref, m_ref, a_ref, left_ref, right_ref, x_ref, top_ref, bottom_ref, est_ref, out_ref, kept):
@@ -307,9 +315,9 @@
 
 
 def own_update(u, e, m, a, left, right, ratio, top, bottom, est):
-    rows, depth, cols = ratio.shape
+    (_, depth, cols), rows = ratio.shape, est.shape[1]
     inner = rows // 8 - 4
-    early = lambda i: (jnp.minimum(i, inner - 1) + 2, 0, 0)
+    early = lambda i: (jnp.minimum(i, inner - 1), 0, 0)
     late = lambda i: (jnp.maximum(i - inner, 0), 0, 0)
     return pl.pallas_call(
         own_kernel,
@@ -438,16 +446,20 @@
     return copy_call(body, 16, [(8, 8, rows, 128)] * 2, (measured.reshape(8, 16, rows, 128),), 2)
 
 
-def pieces_of(near, far):
-    def body(near_ref, far_ref, *refs):
-        outs, sems = refs[:-1], refs[-1]
+def pieces_of(near, far, steps, segments, after):
+    def body(*refs):
+        near_ref, far_ref, *outs = refs[len(after) : -1]
+        sems = refs[-1]
         pairs = []
-        for k, out in enumerate(outs):
-            pairs.append((near_ref.at[k], out.at[0]))
-            pairs.append((far_ref.at[k], out.at[1]))
+        for k, out in zip(steps, outs):
+            for part, ref in enumerate((near_ref, far_ref)):
+                for start, here, n in segments:
+                    pairs.append((ref.at[k, :, pl.ds(start, n)], out.at[part, :, pl.ds(here, n)]))
         run_copies(pairs, sems)
 
-    return copy_call(body, 16, [(2, *near.shape[1:])] * 8, (near, far), 2)
+    _, planes, _, cols = near.shape
+    shapes = [(2, planes, 32, cols)] * len(steps)
+    return copy_call(body, 2 * len(steps) * len(segments), shapes, (*after, near, far), 2)
 
 
 def diagonal_windows(r_interp, gx, rows):
@@ -467,11 +479,14 @@
     return blur(tables[3], tables[4], tables[7], edge, mixed)
 
 
-def backward(tables, ratio, left, right, estimate, column_edges, row_edges):
+def backward(tables, ends, inner, estimate, column_edges, row_edges, after):
     rb, re, ub, ube, zb = tables[1], tables[2], tables[5], tables[6], tables[8]
+    ratio, left, right = ends
     left, right = column_edges(left, right)
-    top, bottom = spread_ends(ub, ube, zb, left, right, ratio)
+    top, bottom = spread_ends(ub, ube, zb, left, right, ratio, after)
     up, down = row_edges(top, bottom)
+    ratio, left, right = inner(top)
+    left, right = column_edges(left, right)
     part = own_update(ub, ube, zb, rb, left, right, ratio, top, bottom, estimate)
     return edge_update(re, up, down, estimate, part)
 
@@ -486,10 +501,18 @@
     up, down = row_edges(*row_ends(estimate, left, right))
     main, upper = diagonal_windows(r_interp, gx, rows)
     tables = make_tables(psf_z, psf_r, psf_u, z_interp, main, upper, rows, width)
-    pieces = [lax.ppermute(p, AXES, piece_perm(k)) for k, p in enumerate(pieces_of(near, far))]
+    every = range(8)
+    ship = lambda parts, steps: [lax.ppermute(p, AXES, piece_perm(k)) for p, k in zip(parts, steps)]
+    pieces = ship(pieces_of(near, far, every, ENDS, ()), every)
     blurred = forward(tables, up, estimate, down, left, right, pieces[:3])
-    ratio, left, right = ratio_of(blurred, pieces)
-    return backward(tables, ratio, left, right, estimate, column_edges, row_edges)
+    early, late = every[:EARLY], every[EARLY:]
+    rest = ship(pieces_of(near, far, early, INNER, (blurred,)), early)
+    ends = ratio_of(blurred, pieces, ENDS)
+
+    def inner(after):
+        return ratio_of(blurred, rest + ship(pieces_of(near, far, late, INNER, (after,)), late), INNER)
+
+    return backward(tables, ends, inner, estimate, column_edges, row_edges, rest[:1])
 
 
 def solution(mesh):

time: 181 us -> 220 us (1.22)
  the two profiles are of different devices: /device:TPU:1 before, /device:TPU:31 now
where the time goes in v8:
time: 220 us; the launch traced here: 219 us
  starting transfers between devices  118 us (54%)
  Pallas kernels  43.4 us (20%)
  waiting for transfers between devices  39.8 us (18%)
  local copies, waits for them, and re-layouts  15.7 us (7%)
    ppermute x16, starting transfers between devices, shards(): lax.ppermute(p, AXES, piece_perm(k))  79.9 us
    ppermute x10, starting transfers between devices, send(): return lax.ppermute(x, AXES, shift_perm(axis, d))  37.5 us
    ppermute x16, waiting for transfers between devices, shards(): lax.ppermute(p, AXES, piece_perm(k))  21.2 us
    ppermute x10, waiting for transfers between devices, send(): return lax.ppermute(x, AXES, shift_perm(axis, d))  18.6 us
    unnamed x32, local copies, waits for them, and re-layouts  11.5 us
    pallas_call x5, Pallas kernels, copy_call(): pl.pallas_call(body, in_specs=[HBM] * len(inputs), out_specs=[pl.BlockSpe...  8.47 us
    pallas_call x1, Pallas kernels, own_update(): pl.pallas_call(own_kernel, grid=(inner + depth // 8,), in_specs=[whole(u)...  7.92 us
    pallas_call x1, Pallas kernels, blur(): pl.pallas_call(blur_kernel, grid=(rows // 8,), in_specs=[whole(u), whole(...  7.36 us
  transfers between devices with their start and end apart: 27, of which 9 were waited for; matrix products, arithmetic and copies ran while one was open for 3% of the time, Pallas kernels for 16%

profile of v8, /device:TPU:31, one launch (start us, length us, event | category | flops | bytes accessed | tf_op | source)
XLA Modules:
  0.0 218.9 jit_solution(6980372650095442130)
XLA Ops:
  6.1 4.1 %collective-permute-start = (f32[8,64,128]{2,1,0:T(8,128)S(1)}, f32[8,64,128]{2,1,0:T(8,128)S(1)}, u32[]{:S(2)}, u32[]{:S(2)}) collective-permute-start(f32[8,64,128]{2,1,0:T(8,128)S(1)} %get-tuple-element.51), channel_id=1, source_target_pairs={{0,1},{1,2},{2,3},{3,4},{4,5},{5,6},{6,7},{8,9},{9,10},{10,11},{11... | collective-permute-start | bytes 786440 | tf_op jit(solution)/shard_map/ppermute | solution.py:368
  13.6 4.4 %collective-permute-done.1.right_ref = f32[8,64,128]{2,1,0:T(8,128)S(1)} collective-permute-done((f32[8,64,128]{2,1,0:T(8,128)S(1)}, f32[8,64,128]{2,1,0:T(8,128)S(1)}, u32[]{:S(2)}, u32[]{:S(2)}) %collective-permute-start.1) | collective-permute-done | bytes 262176 | tf_op jit(solution)/shard_map/ppermute | solution.py:368
  21.0 5.0 %collective-permute-start.3 = (f32[72,16,256]{2,1,0:T(8,128)}, f32[72,16,256]{2,1,0:T(8,128)}, u32[]{:S(2)}, u32[]{:S(2)}) collective-permute-start(f32[72,16,256]{2,1,0:T(8,128)} %get-tuple-element.54), channel_id=1, source_target_pairs={{8,0},{9,1},{10,2},{11,3},{12,4},{13,5},{14,6},{15,7},{16,8},{17,9... | collective-permute-start | bytes 3538952 | tf_op jit(solution)/shard_map/ppermute | solution.py:368
  34.9 4.2 %collective-permute-start.6 = (f32[2,8,32,128]{3,2,1,0:T(8,128)}, f32[2,8,32,128]{3,2,1,0:T(8,128)}, u32[]{:S(2)}, u32[]{:S(2)}) collective-permute-start(f32[2,8,32,128]{3,2,1,0:T(8,128)} %get-tuple-element.58), channel_id=1, source_target_pairs={{0,16},{1,88},{2,48},{3,120},{4,80},{5,24},{6,112},{7,56},{8,0},{9... | collective-permute-start | bytes 786440 | tf_op jit(solution)/shard_map/ppermute | solution.py:505
  39.1 7.3 %collective-permute-start.7 = (f32[2,8,32,128]{3,2,1,0:T(8,128)}, f32[2,8,32,128]{3,2,1,0:T(8,128)}, u32[]{:S(2)}, u32[]{:S(2)}) collective-permute-start(f32[2,8,32,128]{3,2,1,0:T(8,128)} %get-tuple-element.59), channel_id=1, source_target_pairs={{0,32},{1,104},{2,64},{3,8},{4,96},{5,40},{6,0},{7,72},{8,48},{9,1... | collective-permute-start | bytes 786440 | tf_op jit(solution)/shard_map/ppermute | solution.py:505
  53.2 12.5 %collective-permute-start.10 = (f32[2,8,32,128]{3,2,1,0:T(8,128)}, f32[2,8,32,128]{3,2,1,0:T(8,128)}, u32[]{:S(2)}, u32[]{:S(2)}) collective-permute-start(f32[2,8,32,128]{3,2,1,0:T(8,128)} %copy-done.15), channel_id=1, source_target_pairs={{0,64},{1,8},{2,96},{3,40},{4,0},{5,72},{6,32},{7,104},{8,80},{9,2... | collective-permute-start | bytes 786440 | tf_op jit(solution)/shard_map/ppermute | solution.py:505
  66.3 7.1 %collective-permute-start.12 = (f32[2,8,32,128]{3,2,1,0:T(8,128)}, f32[2,8,32,128]{3,2,1,0:T(8,128)}, u32[]{:S(2)}, u32[]{:S(2)}) collective-permute-start(f32[2,8,32,128]{3,2,1,0:T(8,128)} %copy-done.13), channel_id=1, source_target_pairs={{0,96},{1,40},{2,0},{3,72},{4,32},{5,104},{6,64},{7,8},{8,112},{9,... | collective-permute-start | bytes 786440 | tf_op jit(solution)/shard_map/ppermute | solution.py:505
  84.5 5.8 %shard_map.78 = (f32[64,64,256]{2,1,0:T(8,128)S(1)}, f32[8,64,256]{2,1,0:T(8,128)S(1)}) custom-call(bf16[64,288]{1,0:T(8,128)(2,1)S(1)} %get-tuple-element.50.table_ref, f32[64,64,256]{2,1,0:T(8,128)S(1)} %copy-done.1, f32[8,64,128]{2,1,0:T(8,128)S(1)} %collective-permute-done.left_ref, f32[8,64,128]{2,1,0:T(8,128)S(1)} %copy-done.5, ...), custom_call_target="tpu_custom_call" | custom-call | bytes 12000000 | tf_op jit(solution)/shard_map/pallas_call | solution.py:194
  90.2 7.4 %shard_map.79.refs_0_.blur_ref = f32[64,64,256]{2,1,0:T(8,128)S(1)} custom-call(bf16[768,256]{1,0:T(8,128)(2,1)S(1)} %get-tuple-element.47.u_ref, bf16[768,256]{1,0:T(8,128)(2,1)S(1)} %get-tuple-element.48.e_ref, bf16[64,192]{1,0:T(8,128)(2,1)S(1)} %get-tuple-element.49.m_ref, f32[8,64,256]{2,1,0:T(8,128)S(1)} %get-tuple-element.60.edge_ref, ...), custom_call_target="tpu_custom_call" | custom-call | bytes 24000000 | tf_op jit(solution)/shard_map/pallas_call | solution.py:220
  98.7 7.7 %collective-permute-start.8 = (f32[2,8,32,128]{3,2,1,0:T(8,128)S(1)}, f32[2,8,32,128]{3,2,1,0:T(8,128)S(1)}, u32[]{:S(2)}, u32[]{:S(2)}) collective-permute-start(f32[2,8,32,128]{3,2,1,0:T(8,128)S(1)} %get-tuple-element.62), channel_id=1, source_target_pairs={{0,0},{1,72},{2,32},{3,104},{4,64},{5,8},{6,96},{7,40},{8,16},{9,8... | collective-permute-start | bytes 786440 | tf_op jit(solution)/shard_map/ppermute | solution.py:505
  113.5 3.9 %collective-permute-done.15.refs_5_ = f32[4,64,128]{2,1,0:T(8,128)S(1)} collective-permute-done((f32[4,64,128]{2,1,0:T(8,128)S(1)}, f32[4,64,128]{2,1,0:T(8,128)S(1)}, u32[]{:S(2)}, u32[]{:S(2)}) %collective-permute-start.15) | collective-permute-done | bytes 131104 | tf_op jit(solution)/shard_map/ppermute | solution.py:368
  117.3 3.3 %shard_map.82 = (f32[64,16,256]{2,1,0:T(8,128)S(1)}, f32[64,16,256]{2,1,0:T(8,128)S(1)}) custom-call(f32[2,8,32,128]{3,2,1,0:T(8,128)S(1)} %collective-permute-done.8.refs_0_, bf16[768,256]{1,0:T(8,128)(2,1)S(1)} %get-tuple-element.63.refs_1_.u_ref, bf16[768,256]{1,0:T(8,128)(2,1)S(1)} %get-tuple-element.64.refs_2_.e_ref, ...), custom_call_target="tpu_custom_call" | custom-call | bytes 12000000 | tf_op jit(solution)/shard_map/pallas_call | solution.py:286
  122.0 4.1 %collective-permute-start.17 = (f32[64,16,256]{2,1,0:T(8,128)S(1)}, f32[64,16,256]{2,1,0:T(8,128)S(1)}, u32[]{:S(2)}, u32[]{:S(2)}) collective-permute-start(f32[64,16,256]{2,1,0:T(8,128)S(1)} %get-tuple-element.75.refs_0_.top_ref), channel_id=1, source_target_pairs={{8,0},{9,1},{10,2},{11,3},{12,4},{13,5},{14,6},{15,7},{16,8},{17,9... | collective-permute-start | bytes 3145736 | tf_op jit(solution)/shard_map/ppermute | solution.py:368
  126.1 10.3 %collective-permute-start.19 = (f32[2,8,32,128]{3,2,1,0:T(8,128)S(1)}, f32[2,8,32,128]{3,2,1,0:T(8,128)S(1)}, u32[]{:S(2)}, u32[]{:S(2)}) collective-permute-start(f32[2,8,32,128]{3,2,1,0:T(8,128)S(1)} %get-tuple-element.78), channel_id=1, source_target_pairs={{0,32},{1,104},{2,64},{3,8},{4,96},{5,40},{6,0},{7,72},{8,48},{9,1... | collective-permute-start | bytes 786440 | tf_op jit(solution)/shard_map/ppermute | solution.py:505
  137.8 6.4 %collective-permute-start.20 = (f32[2,8,32,128]{3,2,1,0:T(8,128)S(1)}, f32[2,8,32,128]{3,2,1,0:T(8,128)S(1)}, u32[]{:S(2)}, u32[]{:S(2)}) collective-permute-start(f32[2,8,32,128]{3,2,1,0:T(8,128)S(1)} %get-tuple-element.79), channel_id=1, source_target_pairs={{0,48},{1,120},{2,80},{3,24},{4,112},{5,56},{6,16},{7,88},{8,32},{... | collective-permute-start | bytes 786440 | tf_op jit(solution)/shard_map/ppermute | solution.py:505
  144.1 13.3 %collective-permute-done.18.refs_1_ = f32[2,8,32,128]{3,2,1,0:T(8,128)S(1)} collective-permute-done((f32[2,8,32,128]{3,2,1,0:T(8,128)S(1)}, f32[2,8,32,128]{3,2,1,0:T(8,128)S(1)}, u32[]{:S(2)}, u32[]{:S(2)}) %collective-permute-start.18) | collective-permute-done | bytes 262176 | tf_op jit(solution)/shard_map/ppermute | solution.py:505
  159.4 8.4 %collective-permute-start.22 = (f32[2,8,32,128]{3,2,1,0:T(8,128)S(1)}, f32[2,8,32,128]{3,2,1,0:T(8,128)S(1)}, u32[]{:S(2)}, u32[]{:S(2)}) collective-permute-start(f32[2,8,32,128]{3,2,1,0:T(8,128)S(1)} %get-tuple-element.81), channel_id=1, source_target_pairs={{0,80},{1,24},{2,112},{3,56},{4,16},{5,88},{6,48},{7,120},{8,64},{... | collective-permute-start | bytes 786440 | tf_op jit(solution)/shard_map/ppermute | solution.py:505
  167.8 11.2 %collective-permute-start.23 = (f32[2,8,32,128]{3,2,1,0:T(8,128)S(1)}, f32[2,8,32,128]{3,2,1,0:T(8,128)S(1)}, u32[]{:S(2)}, u32[]{:S(2)}) collective-permute-start(f32[2,8,32,128]{3,2,1,0:T(8,128)S(1)} %get-tuple-element.82), channel_id=1, source_target_pairs={{0,96},{1,40},{2,0},{3,72},{4,32},{5,104},{6,64},{7,8},{8,112},{9,... | collective-permute-start | bytes 786440 | tf_op jit(solution)/shard_map/ppermute | solution.py:505
  179.2 3.9 %collective-permute-done.23.refs_6_ = f32[2,8,32,128]{3,2,1,0:T(8,128)S(1)} collective-permute-done((f32[2,8,32,128]{3,2,1,0:T(8,128)S(1)}, f32[2,8,32,128]{3,2,1,0:T(8,128)S(1)}, u32[]{:S(2)}, u32[]{:S(2)}) %collective-permute-start.23) | collective-permute-done | bytes 262176 | tf_op jit(solution)/shard_map/ppermute | solution.py:505
  183.1 3.8 %collective-permute-done.24.refs_7_ = f32[2,8,32,128]{3,2,1,0:T(8,128)S(1)} collective-permute-done((f32[2,8,32,128]{3,2,1,0:T(8,128)S(1)}, f32[2,8,32,128]{3,2,1,0:T(8,128)S(1)}, u32[]{:S(2)}, u32[]{:S(2)}) %collective-permute-start.24) | collective-permute-done | bytes 262176 | tf_op jit(solution)/shard_map/ppermute | solution.py:505
  188.1 13.6 %collective-permute-start.25 = (f32[4,64,128]{2,1,0:T(8,128)S(1)}, f32[4,64,128]{2,1,0:T(8,128)S(1)}, u32[]{:S(2)}, u32[]{:S(2)}) collective-permute-start(f32[4,64,128]{2,1,0:T(8,128)S(1)} %get-tuple-element.84), channel_id=1, source_target_pairs={{0,1},{1,2},{2,3},{3,4},{4,5},{5,6},{6,7},{8,9},{9,10},{10,11},{11... | collective-permute-start | bytes 393224 | tf_op jit(solution)/shard_map/ppermute | solution.py:368
  203.6 4.3 %collective-permute-done.26.right_ref = f32[4,64,128]{2,1,0:T(8,128)S(1)} collective-permute-done((f32[4,64,128]{2,1,0:T(8,128)S(1)}, f32[4,64,128]{2,1,0:T(8,128)S(1)}, u32[]{:S(2)}, u32[]{:S(2)}) %collective-permute-start.26) | collective-permute-done | bytes 131104 | tf_op jit(solution)/shard_map/ppermute | solution.py:368
  208.0 7.9 %shard_map.85.part_ref = f32[64,64,256]{2,1,0:T(8,128)} custom-call(bf16[768,256]{1,0:T(8,128)(2,1)S(1)} %get-tuple-element.63.refs_1_.u_ref, bf16[768,256]{1,0:T(8,128)(2,1)S(1)} %get-tuple-element.64.refs_2_.e_ref, bf16[64,192]{1,0:T(8,128)(2,1)S(1)} %get-tuple-element.65.refs_3_.m_ref, bf16[64,192]{1,0:T(8,128)(2,1)S(1)} %get-tuple-element.76.a_ref, ...), custom_call_target="tpu_custom_call" | custom-call | bytes 24000000 | tf_op jit(solution)/shard_map/pallas_call | solution.py:322
  215.9 3.0 %shard_map.86 = f32[64,64,256]{2,1,0:T(8,128)} custom-call(bf16[2,16,48]{2,1,0:T(8,128)(2,1)S(1)} %get-tuple-element.46.a_ref, f32[64,16,256]{2,1,0:T(8,128)S(1)} %collective-permute-done.16.up_ref, f32[64,16,256]{2,1,0:T(8,128)S(1)} %collective-permute-done.17.down_ref, f32[64,64,256]{2,1,0:T(8,128)S(1)} %copy-done.2, ...), custom_call_target="tpu_custom_call", output_to_operand_aliasing={{}: (4, {})} | custom-call | bytes 9000000 | tf_op jit(solution)/shard_map/pallas_call | solution.py:353
  (84 shorter events, 55.4 us)
Async XLA Ops:
  4.0 23.4 %collective-permute-start.4 = (f32[8,8,64,128]{3,2,1,0:T(8,128)}, f32[8,8,64,128]{3,2,1,0:T(8,128)}, u32[]{:S(2)}, u32[]{:S(2)}) collective-permute-start(f32[8,8,64,128]{3,2,1,0:T(8,128)} %get-tuple-element.56), channel_id=1, source_target_pairs={{0,1},{1,0},{2,3},{3,2},{4,5},{5,4},{6,7},{7,6},{8,9},{9,8},{10,11... | collective-permute-start | bytes 6291464 | tf_op jit(solution)/shard_map/ppermute | solution.py:500
  6.1 7.4 %collective-permute-start = (f32[8,64,128]{2,1,0:T(8,128)S(1)}, f32[8,64,128]{2,1,0:T(8,128)S(1)}, u32[]{:S(2)}, u32[]{:S(2)}) collective-permute-start(f32[8,64,128]{2,1,0:T(8,128)S(1)} %get-tuple-element.51), channel_id=1, source_target_pairs={{0,1},{1,2},{2,3},{3,4},{4,5},{5,6},{6,7},{8,9},{9,10},{10,11},{11... | collective-permute-start | bytes 786440 | tf_op jit(solution)/shard_map/ppermute | solution.py:368
  10.3 7.7 %collective-permute-start.1 = (f32[8,64,128]{2,1,0:T(8,128)S(1)}, f32[8,64,128]{2,1,0:T(8,128)S(1)}, u32[]{:S(2)}, u32[]{:S(2)}) collective-permute-start(f32[8,64,128]{2,1,0:T(8,128)S(1)} %get-tuple-element.52), channel_id=1, source_target_pairs={{1,0},{2,1},{3,2},{4,3},{5,4},{6,5},{7,6},{9,8},{10,9},{11,10},{12... | collective-permute-start | bytes 786440 | tf_op jit(solution)/shard_map/ppermute | solution.py:368
  19.7 29.2 %collective-permute-start.2 = (f32[72,16,256]{2,1,0:T(8,128)}, f32[72,16,256]{2,1,0:T(8,128)S(1)}, u32[]{:S(2)}, u32[]{:S(2)}) collective-permute-start(f32[72,16,256]{2,1,0:T(8,128)} %get-tuple-element.53), channel_id=1, source_target_pairs={{0,8},{1,9},{2,10},{3,11},{4,12},{5,13},{6,14},{7,15},{8,16},{9,17... | collective-permute-start | bytes 3538952 | tf_op jit(solution)/shard_map/ppermute | solution.py:368
  21.0 32.2 %collective-permute-start.3 = (f32[72,16,256]{2,1,0:T(8,128)}, f32[72,16,256]{2,1,0:T(8,128)}, u32[]{:S(2)}, u32[]{:S(2)}) collective-permute-start(f32[72,16,256]{2,1,0:T(8,128)} %get-tuple-element.54), channel_id=1, source_target_pairs={{8,0},{9,1},{10,2},{11,3},{12,4},{13,5},{14,6},{15,7},{16,8},{17,9... | collective-permute-start | bytes 3538952 | tf_op jit(solution)/shard_map/ppermute | solution.py:368
  32.9 32.7 %collective-permute-start.5 = (f32[2,8,32,128]{3,2,1,0:T(8,128)}, f32[2,8,32,128]{3,2,1,0:T(8,128)}, u32[]{:S(2)}, u32[]{:S(2)}) collective-permute-start(f32[2,8,32,128]{3,2,1,0:T(8,128)} %get-tuple-element.57), channel_id=1, source_target_pairs={{0,0},{1,72},{2,32},{3,104},{4,64},{5,8},{6,96},{7,40},{8,16},{9,8... | collective-permute-start | bytes 786440 | tf_op jit(solution)/shard_map/ppermute | solution.py:505
  34.9 31.5 %collective-permute-start.6 = (f32[2,8,32,128]{3,2,1,0:T(8,128)}, f32[2,8,32,128]{3,2,1,0:T(8,128)}, u32[]{:S(2)}, u32[]{:S(2)}) collective-permute-start(f32[2,8,32,128]{3,2,1,0:T(8,128)} %get-tuple-element.58), channel_id=1, source_target_pairs={{0,16},{1,88},{2,48},{3,120},{4,80},{5,24},{6,112},{7,56},{8,0},{9... | collective-permute-start | bytes 786440 | tf_op jit(solution)/shard_map/ppermute | solution.py:505
  39.1 34.4 %collective-permute-start.7 = (f32[2,8,32,128]{3,2,1,0:T(8,128)}, f32[2,8,32,128]{3,2,1,0:T(8,128)}, u32[]{:S(2)}, u32[]{:S(2)}) collective-permute-start(f32[2,8,32,128]{3,2,1,0:T(8,128)} %get-tuple-element.59), channel_id=1, source_target_pairs={{0,32},{1,104},{2,64},{3,8},{4,96},{5,40},{6,0},{7,72},{8,48},{9,1... | collective-permute-start | bytes 786440 | tf_op jit(solution)/shard_map/ppermute | solution.py:505
  48.9 49.8 %collective-permute-start.9 = (f32[2,8,32,128]{3,2,1,0:T(8,128)}, f32[2,8,32,128]{3,2,1,0:T(8,128)}, u32[]{:S(2)}, u32[]{:S(2)}) collective-permute-start(f32[2,8,32,128]{3,2,1,0:T(8,128)} %get-tuple-element.66), channel_id=1, source_target_pairs={{0,48},{1,120},{2,80},{3,24},{4,112},{5,56},{6,16},{7,88},{8,32},{... | collective-permute-start | bytes 786440 | tf_op jit(solution)/shard_map/ppermute | solution.py:505
  53.2 53.3 %collective-permute-start.10 = (f32[2,8,32,128]{3,2,1,0:T(8,128)}, f32[2,8,32,128]{3,2,1,0:T(8,128)}, u32[]{:S(2)}, u32[]{:S(2)}) collective-permute-start(f32[2,8,32,128]{3,2,1,0:T(8,128)} %copy-done.15), channel_id=1, source_target_pairs={{0,64},{1,8},{2,96},{3,40},{4,0},{5,72},{6,32},{7,104},{8,80},{9,2... | collective-permute-start | bytes 786440 | tf_op jit(solution)/shard_map/ppermute | solution.py:505
  65.7 40.8 %collective-permute-start.11 = (f32[2,8,32,128]{3,2,1,0:T(8,128)}, f32[2,8,32,128]{3,2,1,0:T(8,128)}, u32[]{:S(2)}, u32[]{:S(2)}) collective-permute-start(f32[2,8,32,128]{3,2,1,0:T(8,128)} %copy-done.14), channel_id=1, source_target_pairs={{0,80},{1,24},{2,112},{3,56},{4,16},{5,88},{6,48},{7,120},{8,64},{... | collective-permute-start | bytes 786440 | tf_op jit(solution)/shard_map/ppermute | solution.py:505
  66.3 40.1 %collective-permute-start.12 = (f32[2,8,32,128]{3,2,1,0:T(8,128)}, f32[2,8,32,128]{3,2,1,0:T(8,128)}, u32[]{:S(2)}, u32[]{:S(2)}) collective-permute-start(f32[2,8,32,128]{3,2,1,0:T(8,128)} %copy-done.13), channel_id=1, source_target_pairs={{0,96},{1,40},{2,0},{3,72},{4,32},{5,104},{6,64},{7,8},{8,112},{9,... | collective-permute-start | bytes 786440 | tf_op jit(solution)/shard_map/ppermute | solution.py:505
  73.5 33.0 %collective-permute-start.13 = (f32[2,8,32,128]{3,2,1,0:T(8,128)}, f32[2,8,32,128]{3,2,1,0:T(8,128)}, u32[]{:S(2)}, u32[]{:S(2)}) collective-permute-start(f32[2,8,32,128]{3,2,1,0:T(8,128)} %copy-done.12), channel_id=1, source_target_pairs={{0,112},{1,56},{2,16},{3,88},{4,48},{5,120},{6,80},{7,24},{8,96},{... | collective-permute-start | bytes 786440 | tf_op jit(solution)/shard_map/ppermute | solution.py:505
  98.7 18.6 %collective-permute-start.8 = (f32[2,8,32,128]{3,2,1,0:T(8,128)S(1)}, f32[2,8,32,128]{3,2,1,0:T(8,128)S(1)}, u32[]{:S(2)}, u32[]{:S(2)}) collective-permute-start(f32[2,8,32,128]{3,2,1,0:T(8,128)S(1)} %get-tuple-element.62), channel_id=1, source_target_pairs={{0,0},{1,72},{2,32},{3,104},{4,64},{5,8},{6,96},{7,40},{8,16},{9,8... | collective-permute-start | bytes 786440 | tf_op jit(solution)/shard_map/ppermute | solution.py:505
  120.7 95.2 %collective-permute-start.16 = (f32[64,16,256]{2,1,0:T(8,128)S(1)}, f32[64,16,256]{2,1,0:T(8,128)S(1)}, u32[]{:S(2)}, u32[]{:S(2)}) collective-permute-start(f32[64,16,256]{2,1,0:T(8,128)S(1)} %get-tuple-element.74.bottom_ref), channel_id=1, source_target_pairs={{0,8},{1,9},{2,10},{3,11},{4,12},{5,13},{6,14},{7,15},{8,16},{9,17... | collective-permute-start | bytes 3145736 | tf_op jit(solution)/shard_map/ppermute | solution.py:368
  122.0 93.9 %collective-permute-start.17 = (f32[64,16,256]{2,1,0:T(8,128)S(1)}, f32[64,16,256]{2,1,0:T(8,128)S(1)}, u32[]{:S(2)}, u32[]{:S(2)}) collective-permute-start(f32[64,16,256]{2,1,0:T(8,128)S(1)} %get-tuple-element.75.refs_0_.top_ref), channel_id=1, source_target_pairs={{8,0},{9,1},{10,2},{11,3},{12,4},{13,5},{14,6},{15,7},{16,8},{17,9... | collective-permute-start | bytes 3145736 | tf_op jit(solution)/shard_map/ppermute | solution.py:368
  126.1 31.4 %collective-permute-start.18 = (f32[2,8,32,128]{3,2,1,0:T(8,128)S(1)}, f32[2,8,32,128]{3,2,1,0:T(8,128)S(1)}, u32[]{:S(2)}, u32[]{:S(2)}) collective-permute-start(f32[2,8,32,128]{3,2,1,0:T(8,128)S(1)} %get-tuple-element.77), channel_id=1, source_target_pairs={{0,16},{1,88},{2,48},{3,120},{4,80},{5,24},{6,112},{7,56},{8,0},{9... | collective-permute-start | bytes 786440 | tf_op jit(solution)/shard_map/ppermute | solution.py:505
  126.1 33.2 %collective-permute-start.19 = (f32[2,8,32,128]{3,2,1,0:T(8,128)S(1)}, f32[2,8,32,128]{3,2,1,0:T(8,128)S(1)}, u32[]{:S(2)}, u32[]{:S(2)}) collective-permute-start(f32[2,8,32,128]{3,2,1,0:T(8,128)S(1)} %get-tuple-element.78), channel_id=1, source_target_pairs={{0,32},{1,104},{2,64},{3,8},{4,96},{5,40},{6,0},{7,72},{8,48},{9,1... | collective-permute-start | bytes 786440 | tf_op jit(solution)/shard_map/ppermute | solution.py:505
  137.8 30.1 %collective-permute-start.20 = (f32[2,8,32,128]{3,2,1,0:T(8,128)S(1)}, f32[2,8,32,128]{3,2,1,0:T(8,128)S(1)}, u32[]{:S(2)}, u32[]{:S(2)}) collective-permute-start(f32[2,8,32,128]{3,2,1,0:T(8,128)S(1)} %get-tuple-element.79), channel_id=1, source_target_pairs={{0,48},{1,120},{2,80},{3,24},{4,112},{5,56},{6,16},{7,88},{8,32},{... | collective-permute-start | bytes 786440 | tf_op jit(solution)/shard_map/ppermute | solution.py:505
  157.5 21.6 %collective-permute-start.21 = (f32[2,8,32,128]{3,2,1,0:T(8,128)S(1)}, f32[2,8,32,128]{3,2,1,0:T(8,128)S(1)}, u32[]{:S(2)}, u32[]{:S(2)}) collective-permute-start(f32[2,8,32,128]{3,2,1,0:T(8,128)S(1)} %get-tuple-element.80), channel_id=1, source_target_pairs={{0,64},{1,8},{2,96},{3,40},{4,0},{5,72},{6,32},{7,104},{8,80},{9,2... | collective-permute-start | bytes 786440 | tf_op jit(solution)/shard_map/ppermute | solution.py:505
  159.4 19.8 %collective-permute-start.22 = (f32[2,8,32,128]{3,2,1,0:T(8,128)S(1)}, f32[2,8,32,128]{3,2,1,0:T(8,128)S(1)}, u32[]{:S(2)}, u32[]{:S(2)}) collective-permute-start(f32[2,8,32,128]{3,2,1,0:T(8,128)S(1)} %get-tuple-element.81), channel_id=1, source_target_pairs={{0,80},{1,24},{2,112},{3,56},{4,16},{5,88},{6,48},{7,120},{8,64},{... | collective-permute-start | bytes 786440 | tf_op jit(solution)/shard_map/ppermute | solution.py:505
  167.8 15.3 %collective-permute-start.23 = (f32[2,8,32,128]{3,2,1,0:T(8,128)S(1)}, f32[2,8,32,128]{3,2,1,0:T(8,128)S(1)}, u32[]{:S(2)}, u32[]{:S(2)}) collective-permute-start(f32[2,8,32,128]{3,2,1,0:T(8,128)S(1)} %get-tuple-element.82), channel_id=1, source_target_pairs={{0,96},{1,40},{2,0},{3,72},{4,32},{5,104},{6,64},{7,8},{8,112},{9,... | collective-permute-start | bytes 786440 | tf_op jit(solution)/shard_map/ppermute | solution.py:505
  179.1 7.9 %collective-permute-start.24 = (f32[2,8,32,128]{3,2,1,0:T(8,128)S(1)}, f32[2,8,32,128]{3,2,1,0:T(8,128)S(1)}, u32[]{:S(2)}, u32[]{:S(2)}) collective-permute-start(f32[2,8,32,128]{3,2,1,0:T(8,128)S(1)} %get-tuple-element.83), channel_id=1, source_target_pairs={{0,112},{1,56},{2,16},{3,88},{4,48},{5,120},{6,80},{7,24},{8,96},{... | collective-permute-start | bytes 786440 | tf_op jit(solution)/shard_map/ppermute | solution.py:505
  188.1 15.5 %collective-permute-start.25 = (f32[4,64,128]{2,1,0:T(8,128)S(1)}, f32[4,64,128]{2,1,0:T(8,128)S(1)}, u32[]{:S(2)}, u32[]{:S(2)}) collective-permute-start(f32[4,64,128]{2,1,0:T(8,128)S(1)} %get-tuple-element.84), channel_id=1, source_target_pairs={{0,1},{1,2},{2,3},{3,4},{4,5},{5,6},{6,7},{8,9},{9,10},{10,11},{11... | collective-permute-start | bytes 393224 | tf_op jit(solution)/shard_map/ppermute | solution.py:368
  (19 other events, 158.0 us)

commit v9 on v6

--- a/solution.py
+++ b/solution.py
@@ -73,7 +73,7 @@
     )
 
 
-def table_kernel(pz_ref, pr_ref, pu_ref, zi_ref, main_ref, upper_ref, mcol_ref, ucol_ref, *outs):
+def table_kernel(pz_ref, pr_ref, pu_ref, zi_ref, main_ref, upper_ref, *outs):
     ro_ref, rb_ref, re_ref, uo_ref, uoe_ref, ub_ref, ube_ref, zo_ref, zb_ref = outs
 
     def grid_of(rows, cols):
@@ -97,12 +97,15 @@
         return jnp.concatenate([h, l, h], axis=0)
 
     rows = rb_ref.shape[0]
-    i, j = grid_of(rows, rows + 32)
-    ro_ref[...] = left_table(taps(pr_ref, j - i) * main_ref[...] + taps(pr_ref, j - 1 - i) * upper_ref[...])
-    back = taps(pr_ref, i - j + 32) * mcol_ref[...] + taps(pr_ref, i - j + 31) * ucol_ref[...]
+    i, j = grid_of(rows, 128)
+    main, upper = main_ref[...], upper_ref[...]
+    out = taps(pr_ref, j - i) * main + taps(pr_ref, j - 1 - i) * upper
+    ro_ref[...] = left_table(out[:, : rows + 32])
+    i, j = grid_of(128, 128)
+    back = (taps(pr_ref, j - i + 16) * main + taps(pr_ref, j - i + 15) * upper).T[16 : 16 + rows]
     rb_ref[...] = left_table(back[:, 16 : 16 + rows])
     re_ref[0] = left_table(back[:16, :16])
-    re_ref[1] = left_table(back[rows - 16 :, rows + 16 :])
+    re_ref[1] = left_table(back[rows - 16 :, rows + 16 : rows + 32])
 
     width = uo_ref.shape[1]
     i, j = grid_of(width, width)
@@ -127,14 +130,13 @@
     shapes += [(depth, 3 * depth)] * 2
     smem = pl.BlockSpec(memory_space=pltpu.SMEM)
     vmem = pl.BlockSpec(memory_space=pltpu.VMEM)
-    own = slice(16, 16 + rows)
     return pl.pallas_call(
         table_kernel,
-        in_specs=[smem] * 3 + [vmem] * 5,
+        in_specs=[smem] * 3 + [vmem] * 3,
         out_specs=[vmem] * len(shapes),
         out_shape=[jax.ShapeDtypeStruct(s, BF) for s in shapes],
         **params(8, 3),
-    )(psf_z, psf_r, psf_u, z_interp, main[None], upper[None], main[own, None], upper[own, None])
+    )(psf_z, psf_r, psf_u, z_interp, main[None], upper[None])
 
 
 def packed(planes):
@@ -438,16 +440,18 @@
     return copy_call(body, 16, [(8, 8, rows, 128)] * 2, (measured.reshape(8, 16, rows, 128),), 2)
 
 
-def pieces_of(near, far):
-    def body(near_ref, far_ref, *refs):
-        outs, sems = refs[:-1], refs[-1]
+def pieces_of(near, far, steps, after):
+    def body(*refs):
+        near_ref, far_ref, *outs = refs[len(after) : -1]
+        sems = refs[-1]
         pairs = []
-        for k, out in enumerate(outs):
+        for k, out in zip(steps, outs):
             pairs.append((near_ref.at[k], out.at[0]))
             pairs.append((far_ref.at[k], out.at[1]))
         run_copies(pairs, sems)
 
-    return copy_call(body, 16, [(2, *near.shape[1:])] * 8, (near, far), 2)
+    shapes = [(2, *near.shape[1:])] * len(steps)
+    return copy_call(body, 2 * len(steps), shapes, (*after, near, far), 2)
 
 
 def diagonal_windows(r_interp, gx, rows):
@@ -458,7 +462,7 @@
     j = lax.broadcasted_iota(jnp.int32, (192, total), 1)
     main = jnp.sum(jnp.where(i == j, band, 0.0), axis=0)
     upper = jnp.sum(jnp.where(i + 1 == j, band, 0.0), axis=0)
-    window = lambda v: lax.dynamic_slice(jnp.pad(v, (16, 16)), (gx * rows,), (rows + 32,))
+    window = lambda v: lax.dynamic_slice(jnp.pad(v, (16, 48)), (gx * rows,), (128,))
     return window(main), window(upper)
 
 
@@ -486,7 +490,10 @@
     up, down = row_edges(*row_ends(estimate, left, right))
     main, upper = diagonal_windows(r_interp, gx, rows)
     tables = make_tables(psf_z, psf_r, psf_u, z_interp, main, upper, rows, width)
-    pieces = [lax.ppermute(p, AXES, piece_perm(k)) for k, p in enumerate(pieces_of(near, far))]
+    first, second = range(3), range(3, 8)
+    ship = lambda parts, steps: [lax.ppermute(p, AXES, piece_perm(k)) for p, k in zip(parts, steps)]
+    pieces = ship(pieces_of(near, far, first, ()), first)
+    pieces += ship(pieces_of(near, far, second, (tables[0],)), second)
     blurred = forward(tables, up, estimate, down, left, right, pieces[:3])
     ratio, left, right = ratio_of(blurred, pieces)
     return backward(tables, ratio, left, right, estimate, column_edges, row_edges)

time: 181 us -> 177 us (0.978)
  the two profiles are of different devices: /device:TPU:1 before, /device:TPU:57 now
where the time goes in v9:
time: 177 us
  waiting for transfers between devices  65.4 us (37%)
  starting transfers between devices  64.2 us (36%)
  Pallas kernels  38.9 us (22%)
  local copies, waits for them, and re-layouts  6.11 us (3%)
    ppermute x8, waiting for transfers between devices, send(): return lax.ppermute(x, AXES, shift_perm(axis, d))  41.5 us
    ppermute x8, starting transfers between devices, send(): return lax.ppermute(x, AXES, shift_perm(axis, d))  36 us
    ppermute x8, starting transfers between devices, shards(): lax.ppermute(p, AXES, piece_perm(k))  27.4 us
    ppermute x8, waiting for transfers between devices, shards(): lax.ppermute(p, AXES, piece_perm(k))  24 us
    pallas_call x1, Pallas kernels, own_update(): pl.pallas_call(own_kernel, grid=(inner + depth // 8,), in_specs=[whole(u)...  7.91 us
    pallas_call x1, Pallas kernels, blur(): pl.pallas_call(blur_kernel, grid=(rows // 8,), in_specs=[whole(u), whole(...  7.36 us
    unnamed x22, local copies, waits for them, and re-layouts  6.03 us
    pallas_call x1, Pallas kernels, row_mix(): pl.pallas_call(row_kernel, grid=(groups,), in_specs=[whole(table), block(...  5.78 us
  transfers between devices with their start and end apart: 17, of which 11 were waited for; matrix products, arithmetic and copies ran while one was open for 1% of the time, Pallas kernels for 16%

profile of v9, /device:TPU:57, one launch (start us, length us, event | category | flops | bytes accessed | tf_op | source)
XLA Modules:
  0.0 176.6 jit_solution(2832182737374044532)
XLA Ops:
  4.6 4.0 %collective-permute-start = (f32[8,64,128]{2,1,0:T(8,128)S(1)}, f32[8,64,128]{2,1,0:T(8,128)S(1)}, u32[]{:S(2)}, u32[]{:S(2)}) collective-permute-start(f32[8,64,128]{2,1,0:T(8,128)S(1)} %get-tuple-element.43), channel_id=1, source_target_pairs={{0,1},{1,2},{2,3},{3,4},{4,5},{5,6},{6,7},{8,9},{9,10},{10,11},{11... | collective-permute-start | bytes 786440 | tf_op jit(solution)/shard_map/ppermute | solution.py:362
  11.9 4.6 %collective-permute-done.1.right_ref = f32[8,64,128]{2,1,0:T(8,128)S(1)} collective-permute-done((f32[8,64,128]{2,1,0:T(8,128)S(1)}, f32[8,64,128]{2,1,0:T(8,128)S(1)}, u32[]{:S(2)}, u32[]{:S(2)}) %collective-permute-start.1) | collective-permute-done | bytes 262176 | tf_op jit(solution)/shard_map/ppermute | solution.py:362
  18.1 2.8 %collective-permute-start.2 = (f32[72,16,256]{2,1,0:T(8,128)}, f32[72,16,256]{2,1,0:T(8,128)S(1)}, u32[]{:S(2)}, u32[]{:S(2)}) collective-permute-start(f32[72,16,256]{2,1,0:T(8,128)} %get-tuple-element.45), channel_id=1, source_target_pairs={{0,8},{1,9},{2,10},{3,11},{4,12},{5,13},{6,14},{7,15},{8,16},{9,17... | collective-permute-start | bytes 3538952 | tf_op jit(solution)/shard_map/ppermute | solution.py:362
  20.9 2.5 %collective-permute-start.3 = (f32[72,16,256]{2,1,0:T(8,128)}, f32[72,16,256]{2,1,0:T(8,128)}, u32[]{:S(2)}, u32[]{:S(2)}) collective-permute-start(f32[72,16,256]{2,1,0:T(8,128)} %get-tuple-element.46), channel_id=1, source_target_pairs={{8,0},{9,1},{10,2},{11,3},{12,4},{13,5},{14,6},{15,7},{16,8},{17,9... | collective-permute-start | bytes 3538952 | tf_op jit(solution)/shard_map/ppermute | solution.py:362
  26.1 2.7 %collective-permute-start.5 = (f32[2,8,64,128]{3,2,1,0:T(8,128)}, f32[2,8,64,128]{3,2,1,0:T(8,128)}, u32[]{:S(2)}, u32[]{:S(2)}) collective-permute-start(f32[2,8,64,128]{3,2,1,0:T(8,128)} %get-tuple-element.49), channel_id=1, source_target_pairs={{0,0},{1,72},{2,32},{3,104},{4,64},{5,8},{6,96},{7,40},{8,16},{9,8... | collective-permute-start | bytes 1572872 | tf_op jit(solution)/shard_map/ppermute | solution.py:494
  28.8 5.5 %collective-permute-start.6 = (f32[2,8,64,128]{3,2,1,0:T(8,128)}, f32[2,8,64,128]{3,2,1,0:T(8,128)}, u32[]{:S(2)}, u32[]{:S(2)}) collective-permute-start(f32[2,8,64,128]{3,2,1,0:T(8,128)} %get-tuple-element.50), channel_id=1, source_target_pairs={{0,16},{1,88},{2,48},{3,120},{4,80},{5,24},{6,112},{7,56},{8,0},{9... | collective-permute-start | bytes 1572872 | tf_op jit(solution)/shard_map/ppermute | solution.py:494
  34.2 3.1 %collective-permute-start.7 = (f32[2,8,64,128]{3,2,1,0:T(8,128)}, f32[2,8,64,128]{3,2,1,0:T(8,128)}, u32[]{:S(2)}, u32[]{:S(2)}) collective-permute-start(f32[2,8,64,128]{3,2,1,0:T(8,128)} %get-tuple-element.51), channel_id=1, source_target_pairs={{0,32},{1,104},{2,64},{3,8},{4,96},{5,40},{6,0},{7,72},{8,48},{9,1... | collective-permute-start | bytes 1572872 | tf_op jit(solution)/shard_map/ppermute | solution.py:494
  39.8 2.9 %shard_map.73 = (bf16[64,288]{1,0:T(8,128)(2,1)S(1)}, bf16[64,192]{1,0:T(8,128)(2,1)S(1)}, bf16[2,16,48]{2,1,0:T(8,128)(2,1)S(1)}, bf16[768,256]{1,0:T(8,128)(2,...) custom-call(f32[32]{0:T(128)S(1)} %copy-done.8, ...), custom_call_target="tpu_custom_call" | custom-call | bytes 9000000 | tf_op jit(solution)/shard_map/pallas_call | solution.py:133
  44.6 15.0 %collective-permute-done.2.refs_0_.refs_2_ = f32[72,16,256]{2,1,0:T(8,128)S(1)} collective-permute-done((f32[72,16,256]{2,1,0:T(8,128)}, f32[72,16,256]{2,1,0:T(8,128)S(1)}, u32[]{:S(2)}, u32[]{:S(2)}) %collective-permute-start.2) | collective-permute-done | bytes 1179680 | tf_op jit(solution)/shard_map/ppermute | solution.py:362
  63.6 10.3 %collective-permute-start.10 = (f32[2,8,64,128]{3,2,1,0:T(8,128)S(1)}, f32[2,8,64,128]{3,2,1,0:T(8,128)S(1)}, u32[]{:S(2)}, u32[]{:S(2)}) collective-permute-start(f32[2,8,64,128]{3,2,1,0:T(8,128)S(1)} %get-tuple-element.56), channel_id=1, source_target_pairs={{0,80},{1,24},{2,112},{3,56},{4,16},{5,88},{6,48},{7,120},{8,64},{... | collective-permute-start | bytes 1572872 | tf_op jit(solution)/shard_map/ppermute | solution.py:494
  73.9 3.2 %collective-permute-done.6.refs_5_.refs_1_ = f32[2,8,64,128]{3,2,1,0:T(8,128)} collective-permute-done((f32[2,8,64,128]{3,2,1,0:T(8,128)}, f32[2,8,64,128]{3,2,1,0:T(8,128)}, u32[]{:S(2)}, u32[]{:S(2)}) %collective-permute-start.6) | collective-permute-done | bytes 524320 | tf_op jit(solution)/shard_map/ppermute | solution.py:494
  79.0 13.7 %collective-permute-done.7.refs_6_.refs_2_ = f32[2,8,64,128]{3,2,1,0:T(8,128)} collective-permute-done((f32[2,8,64,128]{3,2,1,0:T(8,128)}, f32[2,8,64,128]{3,2,1,0:T(8,128)}, u32[]{:S(2)}, u32[]{:S(2)}) %collective-permute-start.7) | collective-permute-done | bytes 524320 | tf_op jit(solution)/shard_map/ppermute | solution.py:494
  92.7 5.8 %shard_map.78 = (f32[64,64,256]{2,1,0:T(8,128)S(1)}, f32[8,64,256]{2,1,0:T(8,128)S(1)}) custom-call(bf16[64,288]{1,0:T(8,128)(2,1)S(1)} %get-tuple-element.42.table_ref.refs_0_, f32[64,64,256]{2,1,0:T(8,128)S(1)} %copy-done.1, f32[8,64,128]{2,1,0:T(8,128)S(1)} %collective-permute-done.left_ref, f32[8,64,128]{2,1,0:T(8,128)S(1)} %copy-done.6, ...), custom_call_target="tpu_custom_call" | custom-call | bytes 12000000 | tf_op jit(solution)/shard_map/pallas_call | solution.py:196
  98.5 7.4 %shard_map.79.blur_ref = f32[64,64,256]{2,1,0:T(8,128)S(1)} custom-call(bf16[768,256]{1,0:T(8,128)(2,1)S(1)} %get-tuple-element.39.u_ref, bf16[768,256]{1,0:T(8,128)(2,1)S(1)} %get-tuple-element.40.e_ref, bf16[64,192]{1,0:T(8,128)(2,1)S(1)} %get-tuple-element.41.m_ref, f32[8,64,256]{2,1,0:T(8,128)S(1)} %get-tuple-element.52.edge_ref, ...), custom_call_target="tpu_custom_call" | custom-call | bytes 24000000 | tf_op jit(solution)/shard_map/pallas_call | solution.py:222
  105.9 6.0 %collective-permute-done.11.refs_6_ = f32[2,8,64,128]{3,2,1,0:T(8,128)S(1)} collective-permute-done((f32[2,8,64,128]{3,2,1,0:T(8,128)S(1)}, f32[2,8,64,128]{3,2,1,0:T(8,128)S(1)}, u32[]{:S(2)}, u32[]{:S(2)}) %collective-permute-start.11) | collective-permute-done | bytes 524320 | tf_op jit(solution)/shard_map/ppermute | solution.py:494
  113.0 3.7 %shard_map.81 = (f32[64,64,256]{2,1,0:T(8,128)S(1)}, f32[8,64,128]{2,1,0:T(8,128)S(1)}, f32[8,64,128]{2,1,0:T(8,128)S(1)}) custom-call(f32[64,64,256]{2,1,0:T(8,128)S(1)} %shard_map.79.blur_ref, f32[2,8,64,128]{3,2,1,0:T(8,128)} %collective-permute-done.5.refs_4_.refs_0_, f32[2,8,64,128]{3,2,1,0:T(8,128)} %collective-permute-done.6.refs_5_.refs_1_, ...), custom_call_target="tpu_custom_call" | custom-call | bytes 21000000 | tf_op jit(solution)/shard_map/pallas_call | solution.py:249
  116.8 6.9 %collective-permute-start.13 = (f32[8,64,128]{2,1,0:T(8,128)S(1)}, f32[8,64,128]{2,1,0:T(8,128)S(1)}, u32[]{:S(2)}, u32[]{:S(2)}) collective-permute-start(f32[8,64,128]{2,1,0:T(8,128)S(1)} %get-tuple-element.59), channel_id=1, source_target_pairs={{0,1},{1,2},{2,3},{3,4},{4,5},{5,6},{6,7},{8,9},{9,10},{10,11},{11... | collective-permute-start | bytes 786440 | tf_op jit(solution)/shard_map/ppermute | solution.py:362
  127.0 4.4 %collective-permute-done.14.right_ref = f32[8,64,128]{2,1,0:T(8,128)S(1)} collective-permute-done((f32[8,64,128]{2,1,0:T(8,128)S(1)}, f32[8,64,128]{2,1,0:T(8,128)S(1)}, u32[]{:S(2)}, u32[]{:S(2)}) %collective-permute-start.14) | collective-permute-done | bytes 262176 | tf_op jit(solution)/shard_map/ppermute | solution.py:362
  131.4 3.3 %shard_map.82 = (f32[64,16,256]{2,1,0:T(8,128)S(1)}, f32[64,16,256]{2,1,0:T(8,128)S(1)}) custom-call(bf16[768,256]{1,0:T(8,128)(2,1)S(1)} %get-tuple-element.36.u_ref, bf16[768,256]{1,0:T(8,128)(2,1)S(1)} %get-tuple-element.37.e_ref, bf16[64,192]{1,0:T(8,128)(2,1)S(1)} %get-tuple-element.38.m_ref, f32[8,64,128]{2,1,0:T(8,128)S(1)} %collective-permute-done.13.left_ref, ...), custom_call_target="tpu_custom_call" | custom-call | bytes 12000000 | tf_op jit(solution)/shard_map/pallas_call | solution.py:281
  134.7 13.4 %collective-permute-start.15 = (f32[64,16,256]{2,1,0:T(8,128)S(1)}, f32[64,16,256]{2,1,0:T(8,128)S(1)}, u32[]{:S(2)}, u32[]{:S(2)}) collective-permute-start(f32[64,16,256]{2,1,0:T(8,128)S(1)} %get-tuple-element.62.bottom_ref), channel_id=1, source_target_pairs={{0,8},{1,9},{2,10},{3,11},{4,12},{5,13},{6,14},{7,15},{8,16},{9,17... | collective-permute-start | bytes 3145736 | tf_op jit(solution)/shard_map/ppermute | solution.py:362
  150.1 7.9 %shard_map.83.part_ref = f32[64,64,256]{2,1,0:T(8,128)} custom-call(bf16[768,256]{1,0:T(8,128)(2,1)S(1)} %get-tuple-element.36.u_ref, bf16[768,256]{1,0:T(8,128)(2,1)S(1)} %get-tuple-element.37.e_ref, bf16[64,192]{1,0:T(8,128)(2,1)S(1)} %get-tuple-element.38.m_ref, bf16[64,192]{1,0:T(8,128)(2,1)S(1)} %get-tuple-element.64.a_ref, ...), custom_call_target="tpu_custom_call" | custom-call | bytes 24000000 | tf_op jit(solution)/shard_map/pallas_call | solution.py:316
  158.0 9.3 %collective-permute-done.15.up_ref = f32[64,16,256]{2,1,0:T(8,128)S(1)} collective-permute-done((f32[64,16,256]{2,1,0:T(8,128)S(1)}, f32[64,16,256]{2,1,0:T(8,128)S(1)}, u32[]{:S(2)}, u32[]{:S(2)}) %collective-permute-start.15) | collective-permute-done | bytes 1048608 | tf_op jit(solution)/shard_map/ppermute | solution.py:362
  167.3 6.2 %collective-permute-done.16.down_ref = f32[64,16,256]{2,1,0:T(8,128)S(1)} collective-permute-done((f32[64,16,256]{2,1,0:T(8,128)S(1)}, f32[64,16,256]{2,1,0:T(8,128)S(1)}, u32[]{:S(2)}, u32[]{:S(2)}) %collective-permute-start.16) | collective-permute-done | bytes 1048608 | tf_op jit(solution)/shard_map/ppermute | solution.py:362
  173.6 3.0 %shard_map.84 = f32[64,64,256]{2,1,0:T(8,128)} custom-call(bf16[2,16,48]{2,1,0:T(8,128)(2,1)S(1)} %get-tuple-element.35.a_ref, f32[64,16,256]{2,1,0:T(8,128)S(1)} %collective-permute-done.15.up_ref, f32[64,16,256]{2,1,0:T(8,128)S(1)} %collective-permute-done.16.down_ref, f32[64,64,256]{2,1,0:T(8,128)S(1)} %copy-done.1, ...), custom_call_target="tpu_custom_call", output_to_operand_aliasing={{}: (4, {})} | custom-call | bytes 9000000 | tf_op jit(solution)/shard_map/pallas_call | solution.py:347
  (48 shorter events, 28.7 us)
Async XLA Ops:
  0.0 3.6 %copy-start = (f32[64,64,256]{2,1,0:T(8,128)S(1)}, f32[64,64,256]{2,1,0:T(8,128)}, u32[]{:S(2)}) copy-start(f32[64,64,256]{2,1,0:T(8,128)} %est_ref.7) | copy-start | bytes 12582916
  0.0 2.3 %copy-start.4 = (f32[8,1024,128]{2,1,0:T(8,128)S(1)}, f32[8,1024,128]{2,1,0:T(8,128)}, u32[]{:S(2)}) copy-start(f32[8,1024,128]{2,1,0:T(8,128)} %param.8) | copy-start | bytes 12582916
  2.8 20.6 %collective-permute-start.4 = (f32[8,8,64,128]{3,2,1,0:T(8,128)S(1)}, f32[8,8,64,128]{3,2,1,0:T(8,128)S(1)}, u32[]{:S(2)}, u32[]{:S(2)}) collective-permute-start(f32[8,8,64,128]{3,2,1,0:T(8,128)S(1)} %get-tuple-element.48), channel_id=1, source_target_pairs={{0,1},{1,0},{2,3},{3,2},{4,5},{5,4},{6,7},{7,6},{8,9},{9,8},{10,11... | collective-permute-start | bytes 6291464 | tf_op jit(solution)/shard_map/ppermute | solution.py:489
  4.6 7.3 %collective-permute-start = (f32[8,64,128]{2,1,0:T(8,128)S(1)}, f32[8,64,128]{2,1,0:T(8,128)S(1)}, u32[]{:S(2)}, u32[]{:S(2)}) collective-permute-start(f32[8,64,128]{2,1,0:T(8,128)S(1)} %get-tuple-element.43), channel_id=1, source_target_pairs={{0,1},{1,2},{2,3},{3,4},{4,5},{5,6},{6,7},{8,9},{9,10},{10,11},{11... | collective-permute-start | bytes 786440 | tf_op jit(solution)/shard_map/ppermute | solution.py:362
  8.6 30.5 %copy-start.8 = (f32[32]{0:T(128)S(1)}, f32[32]{0:T(128)}, u32[]{:S(2)}) copy-start(f32[32]{0:T(128)} %pz_ref.1) | copy-start | bytes 388
  8.6 30.5 %copy-start.9 = (f32[32]{0:T(128)S(1)}, f32[32]{0:T(128)}, u32[]{:S(2)}) copy-start(f32[32]{0:T(128)} %pr_ref.1) | copy-start | bytes 388
  8.6 30.5 %copy-start.10 = (f32[32]{0:T(128)S(1)}, f32[32]{0:T(128)}, u32[]{:S(2)}) copy-start(f32[32]{0:T(128)} %pu_ref.1) | copy-start | bytes 388
  8.6 7.8 %collective-permute-start.1 = (f32[8,64,128]{2,1,0:T(8,128)S(1)}, f32[8,64,128]{2,1,0:T(8,128)S(1)}, u32[]{:S(2)}, u32[]{:S(2)}) collective-permute-start(f32[8,64,128]{2,1,0:T(8,128)S(1)} %get-tuple-element.44), channel_id=1, source_target_pairs={{1,0},{2,1},{3,2},{4,3},{5,4},{6,5},{7,6},{9,8},{10,9},{11,10},{12... | collective-permute-start | bytes 786440 | tf_op jit(solution)/shard_map/ppermute | solution.py:362
  18.1 41.5 %collective-permute-start.2 = (f32[72,16,256]{2,1,0:T(8,128)}, f32[72,16,256]{2,1,0:T(8,128)S(1)}, u32[]{:S(2)}, u32[]{:S(2)}) collective-permute-start(f32[72,16,256]{2,1,0:T(8,128)} %get-tuple-element.45), channel_id=1, source_target_pairs={{0,8},{1,9},{2,10},{3,11},{4,12},{5,13},{6,14},{7,15},{8,16},{9,17... | collective-permute-start | bytes 3538952 | tf_op jit(solution)/shard_map/ppermute | solution.py:362
  20.9 40.8 %collective-permute-start.3 = (f32[72,16,256]{2,1,0:T(8,128)}, f32[72,16,256]{2,1,0:T(8,128)}, u32[]{:S(2)}, u32[]{:S(2)}) collective-permute-start(f32[72,16,256]{2,1,0:T(8,128)} %get-tuple-element.46), channel_id=1, source_target_pairs={{8,0},{9,1},{10,2},{11,3},{12,4},{13,5},{14,6},{15,7},{16,8},{17,9... | collective-permute-start | bytes 3538952 | tf_op jit(solution)/shard_map/ppermute | solution.py:362
  26.1 37.5 %collective-permute-start.5 = (f32[2,8,64,128]{3,2,1,0:T(8,128)}, f32[2,8,64,128]{3,2,1,0:T(8,128)}, u32[]{:S(2)}, u32[]{:S(2)}) collective-permute-start(f32[2,8,64,128]{3,2,1,0:T(8,128)} %get-tuple-element.49), channel_id=1, source_target_pairs={{0,0},{1,72},{2,32},{3,104},{4,64},{5,8},{6,96},{7,40},{8,16},{9,8... | collective-permute-start | bytes 1572872 | tf_op jit(solution)/shard_map/ppermute | solution.py:494
  28.8 48.4 %collective-permute-start.6 = (f32[2,8,64,128]{3,2,1,0:T(8,128)}, f32[2,8,64,128]{3,2,1,0:T(8,128)}, u32[]{:S(2)}, u32[]{:S(2)}) collective-permute-start(f32[2,8,64,128]{3,2,1,0:T(8,128)} %get-tuple-element.50), channel_id=1, source_target_pairs={{0,16},{1,88},{2,48},{3,120},{4,80},{5,24},{6,112},{7,56},{8,0},{9... | collective-permute-start | bytes 1572872 | tf_op jit(solution)/shard_map/ppermute | solution.py:494
  34.2 58.5 %collective-permute-start.7 = (f32[2,8,64,128]{3,2,1,0:T(8,128)}, f32[2,8,64,128]{3,2,1,0:T(8,128)}, u32[]{:S(2)}, u32[]{:S(2)}) collective-permute-start(f32[2,8,64,128]{3,2,1,0:T(8,128)} %get-tuple-element.51), channel_id=1, source_target_pairs={{0,32},{1,104},{2,64},{3,8},{4,96},{5,40},{6,0},{7,72},{8,48},{9,1... | collective-permute-start | bytes 1572872 | tf_op jit(solution)/shard_map/ppermute | solution.py:494
  37.3 55.4 %copy-start.1 = (f32[64,64,256]{2,1,0:T(8,128)S(1)}, f32[64,64,256]{2,1,0:T(8,128)}, u32[]{:S(2)}) copy-start(f32[64,64,256]{2,1,0:T(8,128)} %est_ref.7) | copy-start | bytes 12582916
  44.3 48.4 %copy-start.6 = (f32[8,64,128]{2,1,0:T(8,128)S(1)}, f32[8,64,128]{2,1,0:T(8,128)}, u32[]{:S(2)}) copy-start(f32[8,64,128]{2,1,0:T(8,128)} %copy-done.5) | copy-start | bytes 786436
  59.6 46.3 %collective-permute-start.8 = (f32[2,8,64,128]{3,2,1,0:T(8,128)S(1)}, f32[2,8,64,128]{3,2,1,0:T(8,128)S(1)}, u32[]{:S(2)}, u32[]{:S(2)}) collective-permute-start(f32[2,8,64,128]{3,2,1,0:T(8,128)S(1)} %get-tuple-element.54), channel_id=1, source_target_pairs={{0,48},{1,120},{2,80},{3,24},{4,112},{5,56},{6,16},{7,88},{8,32},{... | collective-permute-start | bytes 1572872 | tf_op jit(solution)/shard_map/ppermute | solution.py:494
  61.7 44.2 %collective-permute-start.9 = (f32[2,8,64,128]{3,2,1,0:T(8,128)S(1)}, f32[2,8,64,128]{3,2,1,0:T(8,128)S(1)}, u32[]{:S(2)}, u32[]{:S(2)}) collective-permute-start(f32[2,8,64,128]{3,2,1,0:T(8,128)S(1)} %get-tuple-element.55), channel_id=1, source_target_pairs={{0,64},{1,8},{2,96},{3,40},{4,0},{5,72},{6,32},{7,104},{8,80},{9,2... | collective-permute-start | bytes 1572872 | tf_op jit(solution)/shard_map/ppermute | solution.py:494
  63.6 42.3 %collective-permute-start.10 = (f32[2,8,64,128]{3,2,1,0:T(8,128)S(1)}, f32[2,8,64,128]{3,2,1,0:T(8,128)S(1)}, u32[]{:S(2)}, u32[]{:S(2)}) collective-permute-start(f32[2,8,64,128]{3,2,1,0:T(8,128)S(1)} %get-tuple-element.56), channel_id=1, source_target_pairs={{0,80},{1,24},{2,112},{3,56},{4,16},{5,88},{6,48},{7,120},{8,64},{... | collective-permute-start | bytes 1572872 | tf_op jit(solution)/shard_map/ppermute | solution.py:494
  77.1 34.8 %collective-permute-start.11 = (f32[2,8,64,128]{3,2,1,0:T(8,128)S(1)}, f32[2,8,64,128]{3,2,1,0:T(8,128)S(1)}, u32[]{:S(2)}, u32[]{:S(2)}) collective-permute-start(f32[2,8,64,128]{3,2,1,0:T(8,128)S(1)} %get-tuple-element.57), channel_id=1, source_target_pairs={{0,96},{1,40},{2,0},{3,72},{4,32},{5,104},{6,64},{7,8},{8,112},{9,... | collective-permute-start | bytes 1572872 | tf_op jit(solution)/shard_map/ppermute | solution.py:494
  92.7 20.3 %collective-permute-start.12 = (f32[2,8,64,128]{3,2,1,0:T(8,128)S(1)}, f32[2,8,64,128]{3,2,1,0:T(8,128)S(1)}, u32[]{:S(2)}, u32[]{:S(2)}) collective-permute-start(f32[2,8,64,128]{3,2,1,0:T(8,128)S(1)} %get-tuple-element.58), channel_id=1, source_target_pairs={{0,112},{1,56},{2,16},{3,88},{4,48},{5,120},{6,80},{7,24},{8,96},{... | collective-permute-start | bytes 1572872 | tf_op jit(solution)/shard_map/ppermute | solution.py:494
  116.8 10.2 %collective-permute-start.13 = (f32[8,64,128]{2,1,0:T(8,128)S(1)}, f32[8,64,128]{2,1,0:T(8,128)S(1)}, u32[]{:S(2)}, u32[]{:S(2)}) collective-permute-start(f32[8,64,128]{2,1,0:T(8,128)S(1)} %get-tuple-element.59), channel_id=1, source_target_pairs={{0,1},{1,2},{2,3},{3,4},{4,5},{5,6},{6,7},{8,9},{9,10},{10,11},{11... | collective-permute-start | bytes 786440 | tf_op jit(solution)/shard_map/ppermute | solution.py:362
  123.7 7.7 %collective-permute-start.14 = (f32[8,64,128]{2,1,0:T(8,128)S(1)}, f32[8,64,128]{2,1,0:T(8,128)S(1)}, u32[]{:S(2)}, u32[]{:S(2)}) collective-permute-start(f32[8,64,128]{2,1,0:T(8,128)S(1)} %get-tuple-element.60), channel_id=1, source_target_pairs={{1,0},{2,1},{3,2},{4,3},{5,4},{6,5},{7,6},{9,8},{10,9},{11,10},{12... | collective-permute-start | bytes 786440 | tf_op jit(solution)/shard_map/ppermute | solution.py:362
  134.7 32.6 %collective-permute-start.15 = (f32[64,16,256]{2,1,0:T(8,128)S(1)}, f32[64,16,256]{2,1,0:T(8,128)S(1)}, u32[]{:S(2)}, u32[]{:S(2)}) collective-permute-start(f32[64,16,256]{2,1,0:T(8,128)S(1)} %get-tuple-element.62.bottom_ref), channel_id=1, source_target_pairs={{0,8},{1,9},{2,10},{3,11},{4,12},{5,13},{6,14},{7,15},{8,16},{9,17... | collective-permute-start | bytes 3145736 | tf_op jit(solution)/shard_map/ppermute | solution.py:362
  148.2 25.4 %collective-permute-start.16 = (f32[64,16,256]{2,1,0:T(8,128)S(1)}, f32[64,16,256]{2,1,0:T(8,128)S(1)}, u32[]{:S(2)}, u32[]{:S(2)}) collective-permute-start(f32[64,16,256]{2,1,0:T(8,128)S(1)} %get-tuple-element.63.top_ref), channel_id=1, source_target_pairs={{8,0},{9,1},{10,2},{11,3},{12,4},{13,5},{14,6},{15,7},{16,8},{17,9... | collective-permute-start | bytes 3145736 | tf_op jit(solution)/shard_map/ppermute | solution.py:362
  (4 other events, 5.4 us)

commit v10 on v9

--- a/solution.py
+++ b/solution.py
@@ -187,20 +187,20 @@
     edge_ref[0] = along(table, jnp.concatenate([up_edge_ref[0], both, down_edge_ref[0]], axis=0))
 
 
-def row_mix(table, up, own, down, left, right, after):
+def row_mix(table, up, own, down, left, right, above, below, after):
     depth, rows, cols = own.shape
     groups = depth // 8
-    block = lambda r: pl.BlockSpec((8, r, cols), lambda i: (i, 0, 0))
+    block = lambda d, r: pl.BlockSpec((d, r, cols), lambda i: (i, 0, 0))
     packs = pl.BlockSpec((1, rows, 128), lambda i: (i, 0, 0))
-    extra = pl.BlockSpec((1, 16, cols), lambda i: (depth + i, 0, 0))
     return pl.pallas_call(
         row_kernel,
         grid=(groups,),
-        in_specs=[whole(table), block(rows), packs, packs, block(16), block(16), extra, extra] + [ANY] * len(after),
-        out_specs=[block(rows), pl.BlockSpec((1, rows, cols), lambda i: (i, 0, 0))],
+        in_specs=[whole(table), block(8, rows), packs, packs, block(8, 16), block(8, 16), block(1, 16), block(1, 16)]
+        + [ANY] * len(after),
+        out_specs=[block(8, rows), block(1, rows)],
         out_shape=[jax.ShapeDtypeStruct(own.shape, F32), jax.ShapeDtypeStruct((groups, rows, cols), F32)],
         **params(10, 4),
-    )(table, own, left, right, up, down, up, down, *after)
+    )(table, own, left, right, up, down, above, below, *after)
 
 
 def blur_kernel(u_ref, e_ref, m_ref, edge_ref, x_ref, out_ref):
@@ -394,8 +394,9 @@
     )(*inputs)
 
 
-def column_ends(est):
-    def body(est_ref, left_ref, right_ref):
+def column_ends(est, after):
+    def body(*refs):
+        est_ref, left_ref, right_ref = refs[-3:]
         for g in range(left_ref.shape[0]):
             left_ref[g], right_ref[g] = packed([est_ref[8 * g + q] for q in range(8)])
 
@@ -403,32 +404,29 @@
     vmem = pl.BlockSpec(memory_space=pltpu.VMEM)
     return pl.pallas_call(
         body,
-        in_specs=[vmem],
+        in_specs=[ANY] * len(after) + [vmem],
         out_specs=[vmem] * 2,
         out_shape=[jax.ShapeDtypeStruct((depth // 8, rows, 128), F32)] * 2,
         **params(14, 2),
-    )(est)
-
-
-def row_ends(est, left, right):
-    def body(est_ref, left_ref, right_ref, top_ref, bottom_ref, sems):
+    )(*after, est)
+
+
+def row_ends(est):
+    def body(est_ref, top_ref, bottom_ref, sems):
         depth, rows, _ = est_ref.shape
         pairs = []
         for out, r in ((top_ref, 0), (bottom_ref, rows - 16)):
-            at = pl.ds(r, 16)
             for d in range(0, depth, 16):
-                pairs.append((est_ref.at[pl.ds(d, 16), at], out.at[pl.ds(d, 16)]))
-            tail = pl.ds(depth, depth // 8)
-            pairs.append((left_ref.at[:, at], out.at[tail, :, pl.ds(0, 128)]))
-            pairs.append((right_ref.at[:, at], out.at[tail, :, pl.ds(128, 128)]))
+                pairs.append((est_ref.at[pl.ds(d, 16), pl.ds(r, 16)], out.at[pl.ds(d, 16)]))
         run_copies(pairs, sems)
 
     depth, _, cols = est.shape
-    return copy_call(body, depth // 8 + 4, [(depth + depth // 8, 16, cols)] * 2, (est, left, right), 2)
-
-
-def halves_of(measured, rows):
-    def body(measured_ref, near_ref, far_ref, sems):
+    return copy_call(body, depth // 8, [(depth, 16, cols)] * 2, (est,), 2)
+
+
+def halves_of(measured, rows, after):
+    def body(*refs):
+        measured_ref, near_ref, far_ref, sems = refs[-4:]
         x, y, z, c = place()
         pairs = []
         for out, core in ((near_ref, c), (far_ref, 1 - c)):
@@ -437,7 +435,7 @@
                 pairs.append((measured_ref.at[:, tx * 4 + ty], out.at[k]))
         run_copies(pairs, sems)
 
-    return copy_call(body, 16, [(8, 8, rows, 128)] * 2, (measured.reshape(8, 16, rows, 128),), 2)
+    return copy_call(body, 16, [(8, 8, rows, 128)] * 2, (*after, measured.reshape(8, 16, rows, 128)), 2)
 
 
 def pieces_of(near, far, steps, after):
@@ -466,8 +464,8 @@
     return window(main), window(upper)
 
 
-def forward(tables, up, estimate, down, left, right, after):
-    mixed, edge = row_mix(tables[0], up, estimate, down, left, right, after)
+def forward(tables, up, estimate, down, left, right, above, below, after):
+    mixed, edge = row_mix(tables[0], up, estimate, down, left, right, above, below, after)
     return blur(tables[3], tables[4], tables[7], edge, mixed)
 
 
@@ -484,17 +482,21 @@
     depth, rows, width = estimate.shape
     gx = lax.axis_index("gx")
     row_edges = lambda top, bottom: (send(bottom, "gx", 1), send(top, "gx", -1))
-    left, right = column_edges(*column_ends(estimate))
-    near, far = halves_of(measured, rows)
+    top, bottom = row_ends(estimate)
+    up, down = row_edges(top, bottom)
+    ends = column_ends(estimate, (top,))
+    left, right = column_edges(*ends)
+    near, far = halves_of(measured, rows, ends[:1])
     far = lax.ppermute(far, AXES, core_swap())
-    up, down = row_edges(*row_ends(estimate, left, right))
+    both = jnp.concatenate([left, right], axis=2)
+    above, below = row_edges(both[:, :16], both[:, rows - 16 :])
     main, upper = diagonal_windows(r_interp, gx, rows)
     tables = make_tables(psf_z, psf_r, psf_u, z_interp, main, upper, rows, width)
     first, second = range(3), range(3, 8)
     ship = lambda parts, steps: [lax.ppermute(p, AXES, piece_perm(k)) for p, k in zip(parts, steps)]
-    pieces = ship(pieces_of(near, far, first, ()), first)
+    pieces = ship(pieces_of(near, far, first, (above, below, tables[0], up, down)), first)
     pieces += ship(pieces_of(near, far, second, (tables[0],)), second)
-    blurred = forward(tables, up, estimate, down, left, right, pieces[:3])
+    blurred = forward(tables, up, estimate, down, left, right, above, below, pieces[:3])
     ratio, left, right = ratio_of(blurred, pieces)
     return backward(tables, ratio, left, right, estimate, column_edges, row_edges)
 

time: 177 us -> 163 us (0.921)
  the two profiles are of different devices: /device:TPU:57 before, /device:TPU:69 now
where the time goes in v10:
time: 163 us; the launch traced here: 160 us
  starting transfers between devices  79.7 us (49%)
  Pallas kernels  40.6 us (25%)
  waiting for transfers between devices  30.3 us (19%)
  local copies, waits for them, and re-layouts  6.8 us (4%)
  other arithmetic  2.05 us (1%)
    ppermute x8, starting transfers between devices, shards(): lax.ppermute(p, AXES, piece_perm(k))  41 us
    ppermute x10, starting transfers between devices, send(): return lax.ppermute(x, AXES, shift_perm(axis, d))  38 us
    ppermute x10, waiting for transfers between devices, send(): return lax.ppermute(x, AXES, shift_perm(axis, d))  23.6 us
    pallas_call x1, Pallas kernels, own_update(): pl.pallas_call(own_kernel, grid=(inner + depth // 8,), in_specs=[whole(u)...  7.9 us
    pallas_call x1, Pallas kernels, blur(): pl.pallas_call(blur_kernel, grid=(rows // 8,), in_specs=[whole(u), whole(...  7.36 us
    ppermute x8, waiting for transfers between devices, shards(): lax.ppermute(p, AXES, piece_perm(k))  6.63 us
    pallas_call x4, Pallas kernels, copy_call(): pl.pallas_call(body, in_specs=[HBM] * len(inputs), out_specs=[pl.BlockSpe...  6.1 us
    pallas_call x1, Pallas kernels, row_mix(): pl.pallas_call(row_kernel, grid=(groups,), in_specs=[whole(table), block(...  5.81 us
  transfers between devices with their start and end apart: 19, of which 8 were waited for; matrix products, arithmetic and copies ran while one was open for 3% of the time, Pallas kernels for 16%

profile of v10, /device:TPU:69, one launch (start us, length us, event | category | flops | bytes accessed | tf_op | source)
XLA Modules:
  0.0 159.8 jit_solution(15268046579549889931)
XLA Ops:
  9.6 3.2 %collective-permute-start.2 = (f32[64,16,256]{2,1,0:T(8,128)}, f32[64,16,256]{2,1,0:T(8,128)S(1)}, u32[]{:S(2)}, u32[]{:S(2)}) collective-permute-start(f32[64,16,256]{2,1,0:T(8,128)} %get-tuple-element.46), channel_id=1, source_target_pairs={{0,8},{1,9},{2,10},{3,11},{4,12},{5,13},{6,14},{7,15},{8,16},{9,17... | collective-permute-start | bytes 3145736 | tf_op jit(solution)/shard_map/ppermute | solution.py:362
  12.8 4.2 %collective-permute-start.3 = (f32[64,16,256]{2,1,0:T(8,128)}, f32[64,16,256]{2,1,0:T(8,128)}, u32[]{:S(2)}, u32[]{:S(2)}) collective-permute-start(f32[64,16,256]{2,1,0:T(8,128)} %get-tuple-element.43.refs_0_), channel_id=1, source_target_pairs={{8,0},{9,1},{10,2},{11,3},{12,4},{13,5},{14,6},{15,7},{16,8},{17,9... | collective-permute-start | bytes 3145736 | tf_op jit(solution)/shard_map/ppermute | solution.py:362
  17.0 3.7 %collective-permute-start = (f32[8,64,128]{2,1,0:T(8,128)}, f32[8,64,128]{2,1,0:T(8,128)S(1)}, u32[]{:S(2)}, u32[]{:S(2)}) collective-permute-start(f32[8,64,128]{2,1,0:T(8,128)} %get-tuple-element.44), channel_id=1, source_target_pairs={{0,1},{1,2},{2,3},{3,4},{4,5},{5,6},{6,7},{8,9},{9,10},{10,11},{11... | collective-permute-start | bytes 786440 | tf_op jit(solution)/shard_map/ppermute | solution.py:362
  24.3 4.7 %collective-permute-done.1.right_ref = f32[8,64,128]{2,1,0:T(8,128)} collective-permute-done((f32[8,64,128]{2,1,0:T(8,128)}, f32[8,64,128]{2,1,0:T(8,128)}, u32[]{:S(2)}, u32[]{:S(2)}) %collective-permute-start.1) | collective-permute-done | bytes 262176 | tf_op jit(solution)/shard_map/ppermute | solution.py:362
  33.2 2.8 %collective-permute-start.4 = (f32[8,16,256]{2,1,0:T(8,128)}, f32[8,16,256]{2,1,0:T(8,128)}, u32[]{:S(2)}, u32[]{:S(2)}) collective-permute-start(f32[8,16,256]{2,1,0:T(8,128)} %get-tuple-element.68), channel_id=1, source_target_pairs={{0,8},{1,9},{2,10},{3,11},{4,12},{5,13},{6,14},{7,15},{8,16},{9,17... | collective-permute-start | bytes 393224 | tf_op jit(solution)/shard_map/ppermute | solution.py:362
  39.5 2.9 %shard_map.73 = (bf16[64,288]{1,0:T(8,128)(2,1)S(1)}, bf16[64,192]{1,0:T(8,128)(2,1)S(1)}, bf16[2,16,48]{2,1,0:T(8,128)(2,1)S(1)}, bf16[768,256]{1,0:T(8,128)(2,...) custom-call(f32[32]{0:T(128)S(1)} %copy-done.5, ...), custom_call_target="tpu_custom_call" | custom-call | bytes 9000000 | tf_op jit(solution)/shard_map/pallas_call | solution.py:133
  43.8 4.0 %collective-permute-start.7 = (f32[2,8,64,128]{3,2,1,0:T(8,128)S(1)}, f32[2,8,64,128]{3,2,1,0:T(8,128)S(1)}, u32[]{:S(2)}, u32[]{:S(2)}) collective-permute-start(f32[2,8,64,128]{3,2,1,0:T(8,128)S(1)} %get-tuple-element.49), channel_id=1, source_target_pairs={{0,0},{1,72},{2,32},{3,104},{4,64},{5,8},{6,96},{7,40},{8,16},{9,8... | collective-permute-start | bytes 1572872 | tf_op jit(solution)/shard_map/ppermute | solution.py:496
  47.9 2.9 %collective-permute-start.8 = (f32[2,8,64,128]{3,2,1,0:T(8,128)S(1)}, f32[2,8,64,128]{3,2,1,0:T(8,128)S(1)}, u32[]{:S(2)}, u32[]{:S(2)}) collective-permute-start(f32[2,8,64,128]{3,2,1,0:T(8,128)S(1)} %get-tuple-element.50), channel_id=1, source_target_pairs={{0,16},{1,88},{2,48},{3,120},{4,80},{5,24},{6,112},{7,56},{8,0},{9... | collective-permute-start | bytes 1572872 | tf_op jit(solution)/shard_map/ppermute | solution.py:496
  50.8 2.9 %collective-permute-start.9 = (f32[2,8,64,128]{3,2,1,0:T(8,128)S(1)}, f32[2,8,64,128]{3,2,1,0:T(8,128)S(1)}, u32[]{:S(2)}, u32[]{:S(2)}) collective-permute-start(f32[2,8,64,128]{3,2,1,0:T(8,128)S(1)} %get-tuple-element.51), channel_id=1, source_target_pairs={{0,32},{1,104},{2,64},{3,8},{4,96},{5,40},{6,0},{7,72},{8,48},{9,1... | collective-permute-start | bytes 1572872 | tf_op jit(solution)/shard_map/ppermute | solution.py:496
  57.7 8.9 %collective-permute-start.11 = (f32[2,8,64,128]{3,2,1,0:T(8,128)S(1)}, f32[2,8,64,128]{3,2,1,0:T(8,128)S(1)}, u32[]{:S(2)}, u32[]{:S(2)}) collective-permute-start(f32[2,8,64,128]{3,2,1,0:T(8,128)S(1)} %get-tuple-element.55), channel_id=1, source_target_pairs={{0,64},{1,8},{2,96},{3,40},{4,0},{5,72},{6,32},{7,104},{8,80},{9,2... | collective-permute-start | bytes 1572872 | tf_op jit(solution)/shard_map/ppermute | solution.py:496
  66.7 8.0 %collective-permute-start.12 = (f32[2,8,64,128]{3,2,1,0:T(8,128)S(1)}, f32[2,8,64,128]{3,2,1,0:T(8,128)S(1)}, u32[]{:S(2)}, u32[]{:S(2)}) collective-permute-start(f32[2,8,64,128]{3,2,1,0:T(8,128)S(1)} %get-tuple-element.56), channel_id=1, source_target_pairs={{0,80},{1,24},{2,112},{3,56},{4,16},{5,88},{6,48},{7,120},{8,64},{... | collective-permute-start | bytes 1572872 | tf_op jit(solution)/shard_map/ppermute | solution.py:496
  74.7 11.5 %collective-permute-start.13 = (f32[2,8,64,128]{3,2,1,0:T(8,128)S(1)}, f32[2,8,64,128]{3,2,1,0:T(8,128)S(1)}, u32[]{:S(2)}, u32[]{:S(2)}) collective-permute-start(f32[2,8,64,128]{3,2,1,0:T(8,128)S(1)} %get-tuple-element.57), channel_id=1, source_target_pairs={{0,96},{1,40},{2,0},{3,72},{4,32},{5,104},{6,64},{7,8},{8,112},{9,... | collective-permute-start | bytes 1572872 | tf_op jit(solution)/shard_map/ppermute | solution.py:496
  86.3 5.8 %shard_map.78 = (f32[64,64,256]{2,1,0:T(8,128)S(1)}, f32[8,64,256]{2,1,0:T(8,128)S(1)}) custom-call(bf16[64,288]{1,0:T(8,128)(2,1)S(1)} %get-tuple-element.42.refs_2_.table_ref.refs_0_, f32[64,64,256]{2,1,0:T(8,128)S(1)} %copy-done.2, f32[8,64,128]{2,1,0:T(8,128)S(1)} %collective-permute-done.left_ref, f32[8,64,128]{2,1,0:T(8,128)} %collective-permute-done.1.right_ref, ...), custom_call_target="tpu_custom_call" | custom-call | bytes 12000000 | tf_op jit(solution)/shard_map/pallas_call | solution.py:195
  92.1 7.4 %shard_map.79.blur_ref = f32[64,64,256]{2,1,0:T(8,128)S(1)} custom-call(bf16[768,256]{1,0:T(8,128)(2,1)S(1)} %get-tuple-element.39.u_ref, bf16[768,256]{1,0:T(8,128)(2,1)S(1)} %get-tuple-element.40.e_ref, bf16[64,192]{1,0:T(8,128)(2,1)S(1)} %get-tuple-element.41.m_ref, f32[8,64,256]{2,1,0:T(8,128)S(1)} %get-tuple-element.52.edge_ref, ...), custom_call_target="tpu_custom_call" | custom-call | bytes 24000000 | tf_op jit(solution)/shard_map/pallas_call | solution.py:222
  99.5 3.9 %collective-permute-done.12.refs_5_ = f32[2,8,64,128]{3,2,1,0:T(8,128)S(1)} collective-permute-done((f32[2,8,64,128]{3,2,1,0:T(8,128)S(1)}, f32[2,8,64,128]{3,2,1,0:T(8,128)S(1)}, u32[]{:S(2)}, u32[]{:S(2)}) %collective-permute-start.12) | collective-permute-done | bytes 524320 | tf_op jit(solution)/shard_map/ppermute | solution.py:496
  103.4 2.7 %collective-permute-done.14.refs_7_ = f32[2,8,64,128]{3,2,1,0:T(8,128)S(1)} collective-permute-done((f32[2,8,64,128]{3,2,1,0:T(8,128)S(1)}, f32[2,8,64,128]{3,2,1,0:T(8,128)S(1)}, u32[]{:S(2)}, u32[]{:S(2)}) %collective-permute-start.14) | collective-permute-done | bytes 524320 | tf_op jit(solution)/shard_map/ppermute | solution.py:496
  108.5 10.4 %collective-permute-start.15 = (f32[8,64,128]{2,1,0:T(8,128)S(1)}, f32[8,64,128]{2,1,0:T(8,128)S(1)}, u32[]{:S(2)}, u32[]{:S(2)}) collective-permute-start(f32[8,64,128]{2,1,0:T(8,128)S(1)} %get-tuple-element.59), channel_id=1, source_target_pairs={{0,1},{1,2},{2,3},{3,4},{4,5},{5,6},{6,7},{8,9},{9,10},{10,11},{11... | collective-permute-start | bytes 786440 | tf_op jit(solution)/shard_map/ppermute | solution.py:362
  122.2 4.4 %collective-permute-done.16.right_ref = f32[8,64,128]{2,1,0:T(8,128)S(1)} collective-permute-done((f32[8,64,128]{2,1,0:T(8,128)S(1)}, f32[8,64,128]{2,1,0:T(8,128)S(1)}, u32[]{:S(2)}, u32[]{:S(2)}) %collective-permute-start.16) | collective-permute-done | bytes 262176 | tf_op jit(solution)/shard_map/ppermute | solution.py:362
  126.6 3.3 %shard_map.82 = (f32[64,16,256]{2,1,0:T(8,128)S(1)}, f32[64,16,256]{2,1,0:T(8,128)S(1)}) custom-call(bf16[768,256]{1,0:T(8,128)(2,1)S(1)} %get-tuple-element.36.u_ref, bf16[768,256]{1,0:T(8,128)(2,1)S(1)} %get-tuple-element.37.e_ref, bf16[64,192]{1,0:T(8,128)(2,1)S(1)} %get-tuple-element.38.m_ref, f32[8,64,128]{2,1,0:T(8,128)S(1)} %collective-permute-done.15.left_ref, ...), custom_call_target="tpu_custom_call" | custom-call | bytes 12000000 | tf_op jit(solution)/shard_map/pallas_call | solution.py:281
  130.0 2.7 %collective-permute-start.17 = (f32[64,16,256]{2,1,0:T(8,128)S(1)}, f32[64,16,256]{2,1,0:T(8,128)S(1)}, u32[]{:S(2)}, u32[]{:S(2)}) collective-permute-start(f32[64,16,256]{2,1,0:T(8,128)S(1)} %get-tuple-element.62.bottom_ref), channel_id=1, source_target_pairs={{0,8},{1,9},{2,10},{3,11},{4,12},{5,13},{6,14},{7,15},{8,16},{9,17... | collective-permute-start | bytes 3145736 | tf_op jit(solution)/shard_map/ppermute | solution.py:362
  132.7 4.7 %collective-permute-start.18 = (f32[64,16,256]{2,1,0:T(8,128)S(1)}, f32[64,16,256]{2,1,0:T(8,128)S(1)}, u32[]{:S(2)}, u32[]{:S(2)}) collective-permute-start(f32[64,16,256]{2,1,0:T(8,128)S(1)} %get-tuple-element.63.top_ref), channel_id=1, source_target_pairs={{8,0},{9,1},{10,2},{11,3},{12,4},{13,5},{14,6},{15,7},{16,8},{17,9... | collective-permute-start | bytes 3145736 | tf_op jit(solution)/shard_map/ppermute | solution.py:362
  137.4 7.9 %shard_map.83.part_ref = f32[64,64,256]{2,1,0:T(8,128)} custom-call(bf16[768,256]{1,0:T(8,128)(2,1)S(1)} %get-tuple-element.36.u_ref, bf16[768,256]{1,0:T(8,128)(2,1)S(1)} %get-tuple-element.37.e_ref, bf16[64,192]{1,0:T(8,128)(2,1)S(1)} %get-tuple-element.38.m_ref, bf16[64,192]{1,0:T(8,128)(2,1)S(1)} %get-tuple-element.64.a_ref, ...), custom_call_target="tpu_custom_call" | custom-call | bytes 24000000 | tf_op jit(solution)/shard_map/pallas_call | solution.py:316
  145.3 9.8 %collective-permute-done.17.up_ref = f32[64,16,256]{2,1,0:T(8,128)S(1)} collective-permute-done((f32[64,16,256]{2,1,0:T(8,128)S(1)}, f32[64,16,256]{2,1,0:T(8,128)S(1)}, u32[]{:S(2)}, u32[]{:S(2)}) %collective-permute-start.17) | collective-permute-done | bytes 1048608 | tf_op jit(solution)/shard_map/ppermute | solution.py:362
  156.8 3.0 %shard_map.84 = f32[64,64,256]{2,1,0:T(8,128)} custom-call(bf16[2,16,48]{2,1,0:T(8,128)(2,1)S(1)} %get-tuple-element.35.a_ref, f32[64,16,256]{2,1,0:T(8,128)S(1)} %collective-permute-done.17.up_ref, f32[64,16,256]{2,1,0:T(8,128)S(1)} %collective-permute-done.18.down_ref, f32[64,64,256]{2,1,0:T(8,128)S(1)} %copy-done.2, ...), custom_call_target="tpu_custom_call", output_to_operand_aliasing={{}: (4, {})} | custom-call | bytes 9000000 | tf_op jit(solution)/shard_map/pallas_call | solution.py:347
  (49 shorter events, 33.8 us)
Async XLA Ops:
  2.2 4.8 %copy-start.3 = (f32[8,1024,128]{2,1,0:T(8,128)S(1)}, f32[8,1024,128]{2,1,0:T(8,128)}, u32[]{:S(2)}) copy-start(f32[8,1024,128]{2,1,0:T(8,128)} %param.8) | copy-start | bytes 12582916
  7.0 31.8 %copy-start.5 = (f32[32]{0:T(128)S(1)}, f32[32]{0:T(128)}, u32[]{:S(2)}) copy-start(f32[32]{0:T(128)} %pz_ref.1) | copy-start | bytes 388
  7.0 31.8 %copy-start.6 = (f32[32]{0:T(128)S(1)}, f32[32]{0:T(128)}, u32[]{:S(2)}) copy-start(f32[32]{0:T(128)} %pr_ref.1) | copy-start | bytes 388
  7.0 31.8 %copy-start.7 = (f32[32]{0:T(128)S(1)}, f32[32]{0:T(128)}, u32[]{:S(2)}) copy-start(f32[32]{0:T(128)} %pu_ref.1) | copy-start | bytes 388
  8.8 33.7 %collective-permute-start.6 = (f32[8,8,64,128]{3,2,1,0:T(8,128)}, f32[8,8,64,128]{3,2,1,0:T(8,128)}, u32[]{:S(2)}, u32[]{:S(2)}) collective-permute-start(f32[8,8,64,128]{3,2,1,0:T(8,128)} %get-tuple-element.48), channel_id=1, source_target_pairs={{0,1},{1,0},{2,3},{3,2},{4,5},{5,4},{6,7},{7,6},{8,9},{9,8},{10,11... | collective-permute-start | bytes 6291464 | tf_op jit(solution)/shard_map/ppermute | solution.py:490
  9.6 32.9 %collective-permute-start.2 = (f32[64,16,256]{2,1,0:T(8,128)}, f32[64,16,256]{2,1,0:T(8,128)S(1)}, u32[]{:S(2)}, u32[]{:S(2)}) collective-permute-start(f32[64,16,256]{2,1,0:T(8,128)} %get-tuple-element.46), channel_id=1, source_target_pairs={{0,8},{1,9},{2,10},{3,11},{4,12},{5,13},{6,14},{7,15},{8,16},{9,17... | collective-permute-start | bytes 3145736 | tf_op jit(solution)/shard_map/ppermute | solution.py:362
  12.8 29.7 %collective-permute-start.3 = (f32[64,16,256]{2,1,0:T(8,128)}, f32[64,16,256]{2,1,0:T(8,128)}, u32[]{:S(2)}, u32[]{:S(2)}) collective-permute-start(f32[64,16,256]{2,1,0:T(8,128)} %get-tuple-element.43.refs_0_), channel_id=1, source_target_pairs={{8,0},{9,1},{10,2},{11,3},{12,4},{13,5},{14,6},{15,7},{16,8},{17,9... | collective-permute-start | bytes 3145736 | tf_op jit(solution)/shard_map/ppermute | solution.py:362
  17.0 7.3 %collective-permute-start = (f32[8,64,128]{2,1,0:T(8,128)}, f32[8,64,128]{2,1,0:T(8,128)S(1)}, u32[]{:S(2)}, u32[]{:S(2)}) collective-permute-start(f32[8,64,128]{2,1,0:T(8,128)} %get-tuple-element.44), channel_id=1, source_target_pairs={{0,1},{1,2},{2,3},{3,4},{4,5},{5,6},{6,7},{8,9},{9,10},{10,11},{11... | collective-permute-start | bytes 786440 | tf_op jit(solution)/shard_map/ppermute | solution.py:362
  20.7 8.3 %collective-permute-start.1 = (f32[8,64,128]{2,1,0:T(8,128)}, f32[8,64,128]{2,1,0:T(8,128)}, u32[]{:S(2)}, u32[]{:S(2)}) collective-permute-start(f32[8,64,128]{2,1,0:T(8,128)} %get-tuple-element.45.refs_0_), channel_id=1, source_target_pairs={{1,0},{2,1},{3,2},{4,3},{5,4},{6,5},{7,6},{9,8},{10,9},{11,10},{12... | collective-permute-start | bytes 786440 | tf_op jit(solution)/shard_map/ppermute | solution.py:362
  30.7 11.8 %collective-permute-start.5 = (f32[8,16,256]{2,1,0:T(8,128)}, f32[8,16,256]{2,1,0:T(8,128)S(1)}, u32[]{:S(2)}, u32[]{:S(2)}) collective-permute-start(f32[8,16,256]{2,1,0:T(8,128)} %get-tuple-element.67), channel_id=1, source_target_pairs={{8,0},{9,1},{10,2},{11,3},{12,4},{13,5},{14,6},{15,7},{16,8},{17,9... | collective-permute-start | bytes 393224 | tf_op jit(solution)/shard_map/ppermute | solution.py:362
  33.2 9.3 %collective-permute-start.4 = (f32[8,16,256]{2,1,0:T(8,128)}, f32[8,16,256]{2,1,0:T(8,128)}, u32[]{:S(2)}, u32[]{:S(2)}) collective-permute-start(f32[8,16,256]{2,1,0:T(8,128)} %get-tuple-element.68), channel_id=1, source_target_pairs={{0,8},{1,9},{2,10},{3,11},{4,12},{5,13},{6,14},{7,15},{8,16},{9,17... | collective-permute-start | bytes 393224 | tf_op jit(solution)/shard_map/ppermute | solution.py:362
  42.5 43.8 %copy-start.2 = (f32[64,64,256]{2,1,0:T(8,128)S(1)}, f32[64,64,256]{2,1,0:T(8,128)}, u32[]{:S(2)}) copy-start(f32[64,64,256]{2,1,0:T(8,128)} %est_ref.5) | copy-start | bytes 12582916
  43.8 22.8 %collective-permute-start.7 = (f32[2,8,64,128]{3,2,1,0:T(8,128)S(1)}, f32[2,8,64,128]{3,2,1,0:T(8,128)S(1)}, u32[]{:S(2)}, u32[]{:S(2)}) collective-permute-start(f32[2,8,64,128]{3,2,1,0:T(8,128)S(1)} %get-tuple-element.49), channel_id=1, source_target_pairs={{0,0},{1,72},{2,32},{3,104},{4,64},{5,8},{6,96},{7,40},{8,16},{9,8... | collective-permute-start | bytes 1572872 | tf_op jit(solution)/shard_map/ppermute | solution.py:496
  47.9 26.8 %collective-permute-start.8 = (f32[2,8,64,128]{3,2,1,0:T(8,128)S(1)}, f32[2,8,64,128]{3,2,1,0:T(8,128)S(1)}, u32[]{:S(2)}, u32[]{:S(2)}) collective-permute-start(f32[2,8,64,128]{3,2,1,0:T(8,128)S(1)} %get-tuple-element.50), channel_id=1, source_target_pairs={{0,16},{1,88},{2,48},{3,120},{4,80},{5,24},{6,112},{7,56},{8,0},{9... | collective-permute-start | bytes 1572872 | tf_op jit(solution)/shard_map/ppermute | solution.py:496
  50.8 35.4 %collective-permute-start.9 = (f32[2,8,64,128]{3,2,1,0:T(8,128)S(1)}, f32[2,8,64,128]{3,2,1,0:T(8,128)S(1)}, u32[]{:S(2)}, u32[]{:S(2)}) collective-permute-start(f32[2,8,64,128]{3,2,1,0:T(8,128)S(1)} %get-tuple-element.51), channel_id=1, source_target_pairs={{0,32},{1,104},{2,64},{3,8},{4,96},{5,40},{6,0},{7,72},{8,48},{9,1... | collective-permute-start | bytes 1572872 | tf_op jit(solution)/shard_map/ppermute | solution.py:496
  55.1 44.4 %collective-permute-start.10 = (f32[2,8,64,128]{3,2,1,0:T(8,128)S(1)}, f32[2,8,64,128]{3,2,1,0:T(8,128)S(1)}, u32[]{:S(2)}, u32[]{:S(2)}) collective-permute-start(f32[2,8,64,128]{3,2,1,0:T(8,128)S(1)} %get-tuple-element.54), channel_id=1, source_target_pairs={{0,48},{1,120},{2,80},{3,24},{4,112},{5,56},{6,16},{7,88},{8,32},{... | collective-permute-start | bytes 1572872 | tf_op jit(solution)/shard_map/ppermute | solution.py:496
  57.7 41.7 %collective-permute-start.11 = (f32[2,8,64,128]{3,2,1,0:T(8,128)S(1)}, f32[2,8,64,128]{3,2,1,0:T(8,128)S(1)}, u32[]{:S(2)}, u32[]{:S(2)}) collective-permute-start(f32[2,8,64,128]{3,2,1,0:T(8,128)S(1)} %get-tuple-element.55), channel_id=1, source_target_pairs={{0,64},{1,8},{2,96},{3,40},{4,0},{5,72},{6,32},{7,104},{8,80},{9,2... | collective-permute-start | bytes 1572872 | tf_op jit(solution)/shard_map/ppermute | solution.py:496
  66.7 36.7 %collective-permute-start.12 = (f32[2,8,64,128]{3,2,1,0:T(8,128)S(1)}, f32[2,8,64,128]{3,2,1,0:T(8,128)S(1)}, u32[]{:S(2)}, u32[]{:S(2)}) collective-permute-start(f32[2,8,64,128]{3,2,1,0:T(8,128)S(1)} %get-tuple-element.56), channel_id=1, source_target_pairs={{0,80},{1,24},{2,112},{3,56},{4,16},{5,88},{6,48},{7,120},{8,64},{... | collective-permute-start | bytes 1572872 | tf_op jit(solution)/shard_map/ppermute | solution.py:496
  74.7 28.7 %collective-permute-start.13 = (f32[2,8,64,128]{3,2,1,0:T(8,128)S(1)}, f32[2,8,64,128]{3,2,1,0:T(8,128)S(1)}, u32[]{:S(2)}, u32[]{:S(2)}) collective-permute-start(f32[2,8,64,128]{3,2,1,0:T(8,128)S(1)} %get-tuple-element.57), channel_id=1, source_target_pairs={{0,96},{1,40},{2,0},{3,72},{4,32},{5,104},{6,64},{7,8},{8,112},{9,... | collective-permute-start | bytes 1572872 | tf_op jit(solution)/shard_map/ppermute | solution.py:496
  86.2 19.9 %collective-permute-start.14 = (f32[2,8,64,128]{3,2,1,0:T(8,128)S(1)}, f32[2,8,64,128]{3,2,1,0:T(8,128)S(1)}, u32[]{:S(2)}, u32[]{:S(2)}) collective-permute-start(f32[2,8,64,128]{3,2,1,0:T(8,128)S(1)} %get-tuple-element.58), channel_id=1, source_target_pairs={{0,112},{1,56},{2,16},{3,88},{4,48},{5,120},{6,80},{7,24},{8,96},{... | collective-permute-start | bytes 1572872 | tf_op jit(solution)/shard_map/ppermute | solution.py:496
  108.5 13.7 %collective-permute-start.15 = (f32[8,64,128]{2,1,0:T(8,128)S(1)}, f32[8,64,128]{2,1,0:T(8,128)S(1)}, u32[]{:S(2)}, u32[]{:S(2)}) collective-permute-start(f32[8,64,128]{2,1,0:T(8,128)S(1)} %get-tuple-element.59), channel_id=1, source_target_pairs={{0,1},{1,2},{2,3},{3,4},{4,5},{5,6},{6,7},{8,9},{9,10},{10,11},{11... | collective-permute-start | bytes 786440 | tf_op jit(solution)/shard_map/ppermute | solution.py:362
  118.9 7.7 %collective-permute-start.16 = (f32[8,64,128]{2,1,0:T(8,128)S(1)}, f32[8,64,128]{2,1,0:T(8,128)S(1)}, u32[]{:S(2)}, u32[]{:S(2)}) collective-permute-start(f32[8,64,128]{2,1,0:T(8,128)S(1)} %get-tuple-element.60), channel_id=1, source_target_pairs={{1,0},{2,1},{3,2},{4,3},{5,4},{6,5},{7,6},{9,8},{10,9},{11,10},{12... | collective-permute-start | bytes 786440 | tf_op jit(solution)/shard_map/ppermute | solution.py:362
  130.0 25.1 %collective-permute-start.17 = (f32[64,16,256]{2,1,0:T(8,128)S(1)}, f32[64,16,256]{2,1,0:T(8,128)S(1)}, u32[]{:S(2)}, u32[]{:S(2)}) collective-permute-start(f32[64,16,256]{2,1,0:T(8,128)S(1)} %get-tuple-element.62.bottom_ref), channel_id=1, source_target_pairs={{0,8},{1,9},{2,10},{3,11},{4,12},{5,13},{6,14},{7,15},{8,16},{9,17... | collective-permute-start | bytes 3145736 | tf_op jit(solution)/shard_map/ppermute | solution.py:362
  132.7 24.1 %collective-permute-start.18 = (f32[64,16,256]{2,1,0:T(8,128)S(1)}, f32[64,16,256]{2,1,0:T(8,128)S(1)}, u32[]{:S(2)}, u32[]{:S(2)}) collective-permute-start(f32[64,16,256]{2,1,0:T(8,128)S(1)} %get-tuple-element.63.top_ref), channel_id=1, source_target_pairs={{8,0},{9,1},{10,2},{11,3},{12,4},{13,5},{14,6},{15,7},{16,8},{17,9... | collective-permute-start | bytes 3145736 | tf_op jit(solution)/shard_map/ppermute | solution.py:362
  (3 other events, 5.9 us)

commit v11 on v10

--- a/solution.py
+++ b/solution.py
@@ -230,7 +230,7 @@
 
 
 def ratio_kernel(blur_ref, *refs):
-    pieces, (out_ref, left_ref, right_ref) = refs[:-3], refs[-3:]
+    pieces, (out_ref, top_ref, bottom_ref, left_ref, right_ref) = refs[:-5], refs[-5:]
     for k, piece in enumerate(pieces):
         pair, core, half = source_of(*place(), k)
         cols = pl.ds(pl.multiple_of(half * 128, 128), 128)
@@ -238,6 +238,8 @@
             planes = pl.ds(pl.multiple_of((pair * 2 + (core ^ part)) * 8, 8), 8)
             seen = jnp.transpose(piece[part], (1, 0, 2))
             out_ref[:, planes, cols] = seen / (blur_ref[:, planes, cols] + background)
+    top_ref[...] = out_ref[:16]
+    bottom_ref[...] = out_ref[out_ref.shape[0] - 16 :]
     for g in range(left_ref.shape[0]):
         left_ref[g], right_ref[g] = packed([out_ref[8 * g + q] for q in range(8)])
 
@@ -245,117 +247,94 @@
 def ratio_of(blurred, pieces):
     rows, depth, cols = blurred.shape
     vmem = pl.BlockSpec(memory_space=pltpu.VMEM)
-    shapes = [blurred.shape] + [(rows // 8, depth, 128)] * 2
+    shapes = [blurred.shape] + [(16, depth, cols)] * 2 + [(rows // 8, depth, 128)] * 2
     return pl.pallas_call(
         ratio_kernel,
         in_specs=[vmem] * (1 + len(pieces)),
-        out_specs=[vmem] * 3,
+        out_specs=[vmem] * 5,
         out_shape=[jax.ShapeDtypeStruct(s, F32) for s in shapes],
         **params(20, 7),
     )(blurred, *pieces)
 
 
-def spread_tile(ratio, left, right, u, e, m):
+def spread_tile(ratio, both, u, e, m):
     rows, depth, cols = ratio.shape
     total = across(ratio.reshape(rows * depth, cols), u).reshape(rows, depth, cols)
-    left, right = edge_sums(jnp.concatenate([left, right], axis=1), e)
+    left, right = edge_sums(both, e)
     planes = [along(m, total[q] + unpacked(left, right, q)) for q in range(rows)]
     return jnp.transpose(jnp.stack(planes), (1, 0, 2))
 
 
-def ends_kernel(u_ref, e_ref, m_ref, left_ref, right_ref, x_ref, top_ref, bottom_ref):
+def own_kernel(u_ref, e_ref, m_ref, a_ref, both_ref, x_ref, est_ref, out_ref, kept):
     step = pl.program_id(0)
-    tile = spread_tile(x_ref[...], left_ref[0], right_ref[0], u_ref[...], e_ref[...], m_ref[...])
-    for s, ref in ((0, top_ref), (2, bottom_ref)):
-        for t in range(2):
-
-            @pl.when(step == s + t)
-            def _(ref=ref, t=t):
-                ref[:, 8 * t : 8 * t + 8, :] = tile
-
-
-def spread_ends(u, e, m, left, right, ratio):
-    rows, depth, cols = ratio.shape
-    at = lambda i: (jnp.where(i < 2, i, rows // 8 - 4 + i), 0, 0)
-    end = pl.BlockSpec((depth, 16, cols), lambda i: (0, 0, 0))
-    return pl.pallas_call(
-        ends_kernel,
-        grid=(4,),
-        in_specs=[whole(u), whole(e), whole(m)]
-        + [pl.BlockSpec((1, depth, 128), at)] * 2
-        + [pl.BlockSpec((8, depth, cols), at)],
-        out_specs=[end, end],
-        out_shape=[jax.ShapeDtypeStruct((depth, 16, cols), F32)] * 2,
-        **params(14, 4),
-    )(u, e, m, left, right, ratio)
-
-
-def own_kernel(u_ref, e_ref, m_ref, a_ref, left_ref, right_ref, x_ref, top_ref, bottom_ref, est_ref, out_ref, kept):
-    step = pl.program_id(0)
-    inner = kept.shape[1] // 8
-
-    @pl.when(step < inner)
+    half = kept.shape[1] // 8
+
+    @pl.when(step < half)
     def _():
         rows = pl.ds(pl.multiple_of(step * 8, 8), 8)
-        kept[:, rows, :] = spread_tile(x_ref[...], left_ref[0], right_ref[0], u_ref[...], e_ref[...], m_ref[...])
-
-    @pl.when(step >= inner)
+        kept[:, rows, :] = spread_tile(x_ref[...], both_ref[0], u_ref[...], e_ref[...], m_ref[...])
+
+    @pl.when(step >= half)
     def _():
-        first = pl.multiple_of((step - inner) * 8, 8)
+        first = pl.multiple_of((step - half) * 16, 16)
         table = a_ref[...]
-        for z in range(8):
-            x = jnp.concatenate([top_ref[z], kept[first + z], bottom_ref[z]], axis=0)
-            out_ref[z] = est_ref[z] * along(table, x)
-
-
-def own_update(u, e, m, a, left, right, ratio, top, bottom, est):
+        for z in range(16):
+            out_ref[z] = est_ref[z] * along(table, kept[first + z])
+
+
+def own_update(u, e, m, a, both, ratio, est):
     rows, depth, cols = ratio.shape
-    inner = rows // 8 - 4
-    early = lambda i: (jnp.minimum(i, inner - 1) + 2, 0, 0)
-    late = lambda i: (jnp.maximum(i - inner, 0), 0, 0)
+    half = rows // 8
+    early = lambda i: (jnp.minimum(i, half - 1), 0, 0)
+    late = lambda i: (jnp.maximum(i - half, 0), 0, 0)
     return pl.pallas_call(
         own_kernel,
-        grid=(inner + depth // 8,),
+        grid=(half + depth // 16,),
         in_specs=[whole(u), whole(e), whole(m), whole(a)]
-        + [pl.BlockSpec((1, depth, 128), early)] * 2
-        + [pl.BlockSpec((8, depth, cols), early)]
-        + [pl.BlockSpec((8, 16, cols), late)] * 2
-        + [pl.BlockSpec((8, rows, cols), late)],
-        out_specs=pl.BlockSpec((8, rows, cols), late),
+        + [pl.BlockSpec((1, depth, cols), early), pl.BlockSpec((8, depth, cols), early)]
+        + [pl.BlockSpec((16, rows, cols), late)],
+        out_specs=pl.BlockSpec((16, rows, cols), late),
         out_shape=jax.ShapeDtypeStruct(est.shape, F32),
-        scratch_shapes=[pltpu.VMEM((depth, rows - 32, cols), F32)],
-        **params(16, 8),
-    )(u, e, m, a, left, right, ratio, top, bottom, est)
-
-
-def edge_kernel(a_ref, up_ref, down_ref, est_ref, part_ref, out_ref):
-    side = pl.program_id(0)
-    for s, x_ref in ((0, up_ref), (1, down_ref)):
+        scratch_shapes=[pltpu.VMEM(est.shape, F32)],
+        **params(18, 10),
+    )(u, e, m, a, both, ratio, est)
+
+
+def edge_kernel(u_ref, e_ref, m_ref, a_ref, above_ref, below_ref, up_ref, down_ref, est_ref, part_ref, out_ref, kept):
+    side, step = pl.program_id(0), pl.program_id(1)
+    rows = pl.ds(pl.multiple_of(step * 8, 8), 8)
+    for s, x_ref, c_ref in ((0, up_ref, above_ref), (1, down_ref, below_ref)):
 
         @pl.when(side == s)
-        def _(x_ref=x_ref):
-            table = a_ref[0]
-            for z in range(est_ref.shape[0]):
-                out_ref[z] = part_ref[z] + est_ref[z] * along(table, x_ref[z])
-
-
-def edge_update(a, up, down, est, part):
+        def _(x_ref=x_ref, c_ref=c_ref):
+            kept[:, rows, :] = spread_tile(x_ref[...], c_ref[0], u_ref[...], e_ref[...], m_ref[...])
+
+    @pl.when(step == 1)
+    def _():
+        table = a_ref[0]
+        for z in range(est_ref.shape[0]):
+            out_ref[z] = part_ref[z] + est_ref[z] * along(table, kept[z])
+
+
+def edge_update(u, e, m, a, above, below, up, down, est, part):
     depth, rows, cols = est.shape
-    step, chunk = rows // 16 - 1, depth
-    last = depth // chunk - 1
-    tile = pl.BlockSpec((chunk, 16, cols), lambda s, i: (i, s * step, 0))
+    far = rows // 16 - 1
+    tile = pl.BlockSpec((depth, 16, cols), lambda s, i: (0, s * far, 0))
+    fixed = lambda t: pl.BlockSpec(t.shape, lambda s, i: (0,) * t.ndim)
+    order = (lambda s, i: (jnp.maximum(i, s), 0, 0), lambda s, i: (i * s, 0, 0))
     return pl.pallas_call(
         edge_kernel,
-        grid=(2, depth // chunk),
-        in_specs=[pl.BlockSpec((1, 16, 48), lambda s, i: (s, 0, 0))]
-        + [pl.BlockSpec((chunk, 16, cols), lambda s, i: (i + (last - i) * s, 0, 0))]
-        + [pl.BlockSpec((chunk, 16, cols), lambda s, i: (i * s, 0, 0))]
+        grid=(2, 2),
+        in_specs=[fixed(u), fixed(e), fixed(m), pl.BlockSpec((1, 16, 48), lambda s, i: (s, 0, 0))]
+        + [pl.BlockSpec((1, depth, cols), at) for at in order]
+        + [pl.BlockSpec((8, depth, cols), at) for at in order]
         + [tile, tile],
         out_specs=tile,
         out_shape=jax.ShapeDtypeStruct(est.shape, F32),
-        input_output_aliases={4: 0},
-        **params(20, 3),
-    )(a, up, down, est, part)
+        scratch_shapes=[pltpu.VMEM((depth, 16, cols), F32)],
+        input_output_aliases={9: 0},
+        **params(20, 6),
+    )(u, e, m, a, above, below, up, down, est, part)
 
 
 def send(x, axis, d):
@@ -469,13 +448,13 @@
     return blur(tables[3], tables[4], tables[7], edge, mixed)
 
 
-def backward(tables, ratio, left, right, estimate, column_edges, row_edges):
+def backward(tables, ratio, top, bottom, left, right, estimate, column_edges, row_edges):
     rb, re, ub, ube, zb = tables[1], tables[2], tables[5], tables[6], tables[8]
-    left, right = column_edges(left, right)
-    top, bottom = spread_ends(ub, ube, zb, left, right, ratio)
     up, down = row_edges(top, bottom)
-    part = own_update(ub, ube, zb, rb, left, right, ratio, top, bottom, estimate)
-    return edge_update(re, up, down, estimate, part)
+    both = jnp.concatenate(column_edges(left, right), axis=2)
+    above, below = row_edges(both[:2], both[both.shape[0] - 2 :])
+    part = own_update(ub, ube, zb, rb, both, ratio, estimate)
+    return edge_update(ub, ube, zb, re, above, below, up, down, estimate, part)
 
 
 def shards(estimate, measured, z_interp, r_interp, psf_z, psf_r, psf_u):
@@ -497,8 +476,7 @@
     pieces = ship(pieces_of(near, far, first, (above, below, tables[0], up, down)), first)
     pieces += ship(pieces_of(near, far, second, (tables[0],)), second)
     blurred = forward(tables, up, estimate, down, left, right, above, below, pieces[:3])
-    ratio, left, right = ratio_of(blurred, pieces)
-    return backward(tables, ratio, left, right, estimate, column_edges, row_edges)
+    return backward(tables, *ratio_of(blurred, pieces), estimate, column_edges, row_edges)
 
 
 def solution(mesh):

time: 163 us -> 158 us (0.969); the launches traced: 160 us -> 157 us
  waiting for transfers between devices: 30.3 us -> 18.9 us
  starting transfers between devices: 79.7 us -> 85.7 us
  Pallas kernels: 40.6 us -> 43.1 us
    ppermute x10 -> x12, waiting for transfers between devices: 23.6 us -> 12.4 us  [send(): return lax.ppermute(x, AXES, shift_perm(axis, d))]
    ppermute x10 -> x12, starting transfers between devices: 38 us -> 44 us  [send(): return lax.ppermute(x, AXES, shift_perm(axis, d))]
    pallas_call x3 -> x2, Pallas kernels: 14.3 us -> 16.6 us  [the longest x1 10 us: own_update(): pl.pallas_call(own_kernel, grid=(half + depth // 16,), in_specs=[whole(u)...]
    unnamed x17 -> x18, local copies, waits for them, and re-layouts: 4.37 us -> 4.38 us
  transfers between devices with their start and end apart: 19 -> 21, of which waited for: 8 -> 6; matrix products, arithmetic and copies ran while one was open for 3% -> 3% of each run, Pallas kernels for 16% -> 18%
where the time goes in v11:
time: 158 us; the launch traced here: 157 us
  starting transfers between devices  85.7 us (54%)
  Pallas kernels  43.1 us (27%)
  waiting for transfers between devices  18.9 us (12%)
  local copies, waits for them, and re-layouts  6.85 us (4%)
  other arithmetic  2.06 us (1%)
    ppermute x12, starting transfers between devices, send(): return lax.ppermute(x, AXES, shift_perm(axis, d))  44 us
    ppermute x8, starting transfers between devices, shards(): lax.ppermute(p, AXES, piece_perm(k))  41 us
    ppermute x12, waiting for transfers between devices, send(): return lax.ppermute(x, AXES, shift_perm(axis, d))  12.4 us
    pallas_call x1, Pallas kernels, own_update(): pl.pallas_call(own_kernel, grid=(half + depth // 16,), in_specs=[whole(u)...  10 us
    pallas_call x1, Pallas kernels, blur(): pl.pallas_call(blur_kernel, grid=(rows // 8,), in_specs=[whole(u), whole(...  7.36 us
    ppermute x8, waiting for transfers between devices, shards(): lax.ppermute(p, AXES, piece_perm(k))  6.54 us
    pallas_call x1, Pallas kernels, edge_update(): pl.pallas_call(edge_kernel, grid=(2, 2), in_specs=[fixed(u), fixed(e), fi...  6.54 us
    pallas_call x4, Pallas kernels, copy_call(): pl.pallas_call(body, in_specs=[HBM] * len(inputs), out_specs=[pl.BlockSpe...  6.11 us
  transfers between devices with their start and end apart: 21, of which 6 were waited for; matrix products, arithmetic and copies ran while one was open for 3% of the time, Pallas kernels for 18%

profile of v11, /device:TPU:69, one launch (start us, length us, event | category | flops | bytes accessed | tf_op | source)
XLA Modules:
  0.0 157.0 jit_solution(10110250217099514596)
XLA Ops:
  9.6 3.2 %collective-permute-start.2 = (f32[64,16,256]{2,1,0:T(8,128)}, f32[64,16,256]{2,1,0:T(8,128)S(1)}, u32[]{:S(2)}, u32[]{:S(2)}) collective-permute-start(f32[64,16,256]{2,1,0:T(8,128)} %get-tuple-element.46), channel_id=1, source_target_pairs={{0,8},{1,9},{2,10},{3,11},{4,12},{5,13},{6,14},{7,15},{8,16},{9,17... | collective-permute-start | bytes 3145736 | tf_op jit(solution)/shard_map/ppermute | solution.py:341
  12.8 4.2 %collective-permute-start.3 = (f32[64,16,256]{2,1,0:T(8,128)}, f32[64,16,256]{2,1,0:T(8,128)}, u32[]{:S(2)}, u32[]{:S(2)}) collective-permute-start(f32[64,16,256]{2,1,0:T(8,128)} %get-tuple-element.43.refs_0_), channel_id=1, source_target_pairs={{8,0},{9,1},{10,2},{11,3},{12,4},{13,5},{14,6},{15,7},{16,8},{17,9... | collective-permute-start | bytes 3145736 | tf_op jit(solution)/shard_map/ppermute | solution.py:341
  17.0 3.7 %collective-permute-start = (f32[8,64,128]{2,1,0:T(8,128)}, f32[8,64,128]{2,1,0:T(8,128)S(1)}, u32[]{:S(2)}, u32[]{:S(2)}) collective-permute-start(f32[8,64,128]{2,1,0:T(8,128)} %get-tuple-element.44), channel_id=1, source_target_pairs={{0,1},{1,2},{2,3},{3,4},{4,5},{5,6},{6,7},{8,9},{9,10},{10,11},{11... | collective-permute-start | bytes 786440 | tf_op jit(solution)/shard_map/ppermute | solution.py:341
  24.3 4.7 %collective-permute-done.1.right_ref = f32[8,64,128]{2,1,0:T(8,128)} collective-permute-done((f32[8,64,128]{2,1,0:T(8,128)}, f32[8,64,128]{2,1,0:T(8,128)}, u32[]{:S(2)}, u32[]{:S(2)}) %collective-permute-start.1) | collective-permute-done | bytes 262176 | tf_op jit(solution)/shard_map/ppermute | solution.py:341
  33.2 2.8 %collective-permute-start.4 = (f32[8,16,256]{2,1,0:T(8,128)}, f32[8,16,256]{2,1,0:T(8,128)}, u32[]{:S(2)}, u32[]{:S(2)}) collective-permute-start(f32[8,16,256]{2,1,0:T(8,128)} %get-tuple-element.70), channel_id=1, source_target_pairs={{0,8},{1,9},{2,10},{3,11},{4,12},{5,13},{6,14},{7,15},{8,16},{9,17... | collective-permute-start | bytes 393224 | tf_op jit(solution)/shard_map/ppermute | solution.py:341
  39.5 2.9 %shard_map.73 = (bf16[64,288]{1,0:T(8,128)(2,1)S(1)}, bf16[64,192]{1,0:T(8,128)(2,1)S(1)}, bf16[2,16,48]{2,1,0:T(8,128)(2,1)S(1)}, bf16[768,256]{1,0:T(8,128)(2,...) custom-call(f32[32]{0:T(128)S(1)} %copy-done.5, ...), custom_call_target="tpu_custom_call" | custom-call | bytes 9000000 | tf_op jit(solution)/shard_map/pallas_call | solution.py:133
  43.9 4.0 %collective-permute-start.7 = (f32[2,8,64,128]{3,2,1,0:T(8,128)S(1)}, f32[2,8,64,128]{3,2,1,0:T(8,128)S(1)}, u32[]{:S(2)}, u32[]{:S(2)}) collective-permute-start(f32[2,8,64,128]{3,2,1,0:T(8,128)S(1)} %get-tuple-element.49), channel_id=1, source_target_pairs={{0,0},{1,72},{2,32},{3,104},{4,64},{5,8},{6,96},{7,40},{8,16},{9,8... | collective-permute-start | bytes 1572872 | tf_op jit(solution)/shard_map/ppermute | solution.py:475
  47.8 2.9 %collective-permute-start.8 = (f32[2,8,64,128]{3,2,1,0:T(8,128)S(1)}, f32[2,8,64,128]{3,2,1,0:T(8,128)S(1)}, u32[]{:S(2)}, u32[]{:S(2)}) collective-permute-start(f32[2,8,64,128]{3,2,1,0:T(8,128)S(1)} %get-tuple-element.50), channel_id=1, source_target_pairs={{0,16},{1,88},{2,48},{3,120},{4,80},{5,24},{6,112},{7,56},{8,0},{9... | collective-permute-start | bytes 1572872 | tf_op jit(solution)/shard_map/ppermute | solution.py:475
  50.8 2.9 %collective-permute-start.9 = (f32[2,8,64,128]{3,2,1,0:T(8,128)S(1)}, f32[2,8,64,128]{3,2,1,0:T(8,128)S(1)}, u32[]{:S(2)}, u32[]{:S(2)}) collective-permute-start(f32[2,8,64,128]{3,2,1,0:T(8,128)S(1)} %get-tuple-element.51), channel_id=1, source_target_pairs={{0,32},{1,104},{2,64},{3,8},{4,96},{5,40},{6,0},{7,72},{8,48},{9,1... | collective-permute-start | bytes 1572872 | tf_op jit(solution)/shard_map/ppermute | solution.py:475
  55.1 2.7 %collective-permute-start.10 = (f32[2,8,64,128]{3,2,1,0:T(8,128)S(1)}, f32[2,8,64,128]{3,2,1,0:T(8,128)S(1)}, u32[]{:S(2)}, u32[]{:S(2)}) collective-permute-start(f32[2,8,64,128]{3,2,1,0:T(8,128)S(1)} %get-tuple-element.54), channel_id=1, source_target_pairs={{0,48},{1,120},{2,80},{3,24},{4,112},{5,56},{6,16},{7,88},{8,32},{... | collective-permute-start | bytes 1572872 | tf_op jit(solution)/shard_map/ppermute | solution.py:475
  57.7 8.9 %collective-permute-start.11 = (f32[2,8,64,128]{3,2,1,0:T(8,128)S(1)}, f32[2,8,64,128]{3,2,1,0:T(8,128)S(1)}, u32[]{:S(2)}, u32[]{:S(2)}) collective-permute-start(f32[2,8,64,128]{3,2,1,0:T(8,128)S(1)} %get-tuple-element.55), channel_id=1, source_target_pairs={{0,64},{1,8},{2,96},{3,40},{4,0},{5,72},{6,32},{7,104},{8,80},{9,2... | collective-permute-start | bytes 1572872 | tf_op jit(solution)/shard_map/ppermute | solution.py:475
  66.7 8.0 %collective-permute-start.12 = (f32[2,8,64,128]{3,2,1,0:T(8,128)S(1)}, f32[2,8,64,128]{3,2,1,0:T(8,128)S(1)}, u32[]{:S(2)}, u32[]{:S(2)}) collective-permute-start(f32[2,8,64,128]{3,2,1,0:T(8,128)S(1)} %get-tuple-element.56), channel_id=1, source_target_pairs={{0,80},{1,24},{2,112},{3,56},{4,16},{5,88},{6,48},{7,120},{8,64},{... | collective-permute-start | bytes 1572872 | tf_op jit(solution)/shard_map/ppermute | solution.py:475
  74.7 11.5 %collective-permute-start.13 = (f32[2,8,64,128]{3,2,1,0:T(8,128)S(1)}, f32[2,8,64,128]{3,2,1,0:T(8,128)S(1)}, u32[]{:S(2)}, u32[]{:S(2)}) collective-permute-start(f32[2,8,64,128]{3,2,1,0:T(8,128)S(1)} %get-tuple-element.57), channel_id=1, source_target_pairs={{0,96},{1,40},{2,0},{3,72},{4,32},{5,104},{6,64},{7,8},{8,112},{9,... | collective-permute-start | bytes 1572872 | tf_op jit(solution)/shard_map/ppermute | solution.py:475
  86.3 5.9 %shard_map.78 = (f32[64,64,256]{2,1,0:T(8,128)S(1)}, f32[8,64,256]{2,1,0:T(8,128)S(1)}) custom-call(bf16[64,288]{1,0:T(8,128)(2,1)S(1)} %get-tuple-element.42.refs_2_.table_ref.refs_0_, f32[64,64,256]{2,1,0:T(8,128)S(1)} %copy-done.2, f32[8,64,128]{2,1,0:T(8,128)S(1)} %collective-permute-done.left_ref, f32[8,64,128]{2,1,0:T(8,128)} %collective-permute-done.1.right_ref, ...), custom_call_target="tpu_custom_call" | custom-call | bytes 12000000 | tf_op jit(solution)/shard_map/pallas_call | solution.py:195
  92.2 7.4 %shard_map.79.blur_ref = f32[64,64,256]{2,1,0:T(8,128)S(1)} custom-call(bf16[768,256]{1,0:T(8,128)(2,1)S(1)} %get-tuple-element.39.u_ref, bf16[768,256]{1,0:T(8,128)(2,1)S(1)} %get-tuple-element.40.e_ref, bf16[64,192]{1,0:T(8,128)(2,1)S(1)} %get-tuple-element.41.m_ref, f32[8,64,256]{2,1,0:T(8,128)S(1)} %get-tuple-element.52.edge_ref, ...), custom_call_target="tpu_custom_call" | custom-call | bytes 24000000 | tf_op jit(solution)/shard_map/pallas_call | solution.py:222
  99.6 3.8 %collective-permute-done.12.refs_5_ = f32[2,8,64,128]{3,2,1,0:T(8,128)S(1)} collective-permute-done((f32[2,8,64,128]{3,2,1,0:T(8,128)S(1)}, f32[2,8,64,128]{3,2,1,0:T(8,128)S(1)}, u32[]{:S(2)}, u32[]{:S(2)}) %collective-permute-start.12) | collective-permute-done | bytes 524320 | tf_op jit(solution)/shard_map/ppermute | solution.py:475
  103.3 2.8 %collective-permute-done.14.refs_7_ = f32[2,8,64,128]{3,2,1,0:T(8,128)S(1)} collective-permute-done((f32[2,8,64,128]{3,2,1,0:T(8,128)S(1)}, f32[2,8,64,128]{3,2,1,0:T(8,128)S(1)}, u32[]{:S(2)}, u32[]{:S(2)}) %collective-permute-start.14) | collective-permute-done | bytes 524320 | tf_op jit(solution)/shard_map/ppermute | solution.py:475
  108.6 3.8 %collective-permute-start.19 = (f32[16,64,256]{2,1,0:T(8,128)S(1)}, f32[16,64,256]{2,1,0:T(8,128)S(1)}, u32[]{:S(2)}, u32[]{:S(2)}) collective-permute-start(f32[16,64,256]{2,1,0:T(8,128)S(1)} %get-tuple-element.61), channel_id=1, source_target_pairs={{0,8},{1,9},{2,10},{3,11},{4,12},{5,13},{6,14},{7,15},{8,16},{9,17... | collective-permute-start | bytes 3145736 | tf_op jit(solution)/shard_map/ppermute | solution.py:341
  112.4 3.6 %collective-permute-start.20 = (f32[16,64,256]{2,1,0:T(8,128)S(1)}, f32[16,64,256]{2,1,0:T(8,128)S(1)}, u32[]{:S(2)}, u32[]{:S(2)}) collective-permute-start(f32[16,64,256]{2,1,0:T(8,128)S(1)} %get-tuple-element.62), channel_id=1, source_target_pairs={{8,0},{9,1},{10,2},{11,3},{12,4},{13,5},{14,6},{15,7},{16,8},{17,9... | collective-permute-start | bytes 3145736 | tf_op jit(solution)/shard_map/ppermute | solution.py:341
  116.0 11.0 %collective-permute-start.15 = (f32[8,64,128]{2,1,0:T(8,128)S(1)}, f32[8,64,128]{2,1,0:T(8,128)S(1)}, u32[]{:S(2)}, u32[]{:S(2)}) collective-permute-start(f32[8,64,128]{2,1,0:T(8,128)S(1)} %get-tuple-element.59), channel_id=1, source_target_pairs={{0,1},{1,2},{2,3},{3,4},{4,5},{5,6},{6,7},{8,9},{9,10},{10,11},{11... | collective-permute-start | bytes 786440 | tf_op jit(solution)/shard_map/ppermute | solution.py:341
  130.3 4.7 %collective-permute-done.16 = f32[8,64,128]{2,1,0:T(8,128)S(1)} collective-permute-done((f32[8,64,128]{2,1,0:T(8,128)S(1)}, f32[8,64,128]{2,1,0:T(8,128)S(1)}, u32[]{:S(2)}, u32[]{:S(2)}) %collective-permute-start.16) | collective-permute-done | bytes 262176 | tf_op jit(solution)/shard_map/ppermute | solution.py:341
  136.9 3.5 %collective-permute-start.17 = (f32[2,64,256]{2,1,0:T(8,128)S(1)}, f32[2,64,256]{2,1,0:T(8,128)S(1)}, u32[]{:S(2)}, u32[]{:S(2)}) collective-permute-start(f32[2,64,256]{2,1,0:T(8,128)S(1)} %get-tuple-element.68), channel_id=1, source_target_pairs={{0,8},{1,9},{2,10},{3,11},{4,12},{5,13},{6,14},{7,15},{8,16},{9,17... | collective-permute-start | bytes 393224 | tf_op jit(solution)/shard_map/ppermute | solution.py:341
  140.5 10.0 %shard_map.82.part_ref = f32[64,64,256]{2,1,0:T(8,128)} custom-call(bf16[768,256]{1,0:T(8,128)(2,1)S(1)} %get-tuple-element.35.u_ref, bf16[768,256]{1,0:T(8,128)(2,1)S(1)} %get-tuple-element.36.e_ref, bf16[64,192]{1,0:T(8,128)(2,1)S(1)} %get-tuple-element.37.m_ref, bf16[64,192]{1,0:T(8,128)(2,1)S(1)} %get-tuple-element.63.a_ref, ...), custom_call_target="tpu_custom_call" | custom-call | bytes 30000000 | tf_op jit(solution)/shard_map/pallas_call | solution.py:290
  150.5 6.5 %shard_map.83 = f32[64,64,256]{2,1,0:T(8,128)} custom-call(bf16[768,256]{1,0:T(8,128)(2,1)S(1)} %get-tuple-element.35.u_ref, bf16[768,256]{1,0:T(8,128)(2,1)S(1)} %get-tuple-element.36.e_ref, bf16[64,192]{1,0:T(8,128)(2,1)S(1)} %get-tuple-element.37.m_ref, bf16[2,16,48]{2,1,0:T(8,128)(2,1)S(1)} %get-tuple-element.38.a_ref, ...), custom_call_target="tpu_custom_call", output_to_operand_aliasing={{}: (9, {})} | custom-call | bytes 18000000 | tf_op jit(solution)/shard_map/pallas_call | solution.py:325
  (55 shorter events, 31.5 us)
Async XLA Ops:
  6.9 31.8 %copy-start.6 = (f32[32]{0:T(128)S(1)}, f32[32]{0:T(128)}, u32[]{:S(2)}) copy-start(f32[32]{0:T(128)} %pr_ref.1) | copy-start | bytes 388
  7.0 31.8 %copy-start.7 = (f32[32]{0:T(128)S(1)}, f32[32]{0:T(128)}, u32[]{:S(2)}) copy-start(f32[32]{0:T(128)} %pu_ref.1) | copy-start | bytes 388
  8.8 33.7 %collective-permute-start.6 = (f32[8,8,64,128]{3,2,1,0:T(8,128)}, f32[8,8,64,128]{3,2,1,0:T(8,128)}, u32[]{:S(2)}, u32[]{:S(2)}) collective-permute-start(f32[8,8,64,128]{3,2,1,0:T(8,128)} %get-tuple-element.48), channel_id=1, source_target_pairs={{0,1},{1,0},{2,3},{3,2},{4,5},{5,4},{6,7},{7,6},{8,9},{9,8},{10,11... | collective-permute-start | bytes 6291464 | tf_op jit(solution)/shard_map/ppermute | solution.py:469
  9.6 32.9 %collective-permute-start.2 = (f32[64,16,256]{2,1,0:T(8,128)}, f32[64,16,256]{2,1,0:T(8,128)S(1)}, u32[]{:S(2)}, u32[]{:S(2)}) collective-permute-start(f32[64,16,256]{2,1,0:T(8,128)} %get-tuple-element.46), channel_id=1, source_target_pairs={{0,8},{1,9},{2,10},{3,11},{4,12},{5,13},{6,14},{7,15},{8,16},{9,17... | collective-permute-start | bytes 3145736 | tf_op jit(solution)/shard_map/ppermute | solution.py:341
  12.8 29.7 %collective-permute-start.3 = (f32[64,16,256]{2,1,0:T(8,128)}, f32[64,16,256]{2,1,0:T(8,128)}, u32[]{:S(2)}, u32[]{:S(2)}) collective-permute-start(f32[64,16,256]{2,1,0:T(8,128)} %get-tuple-element.43.refs_0_), channel_id=1, source_target_pairs={{8,0},{9,1},{10,2},{11,3},{12,4},{13,5},{14,6},{15,7},{16,8},{17,9... | collective-permute-start | bytes 3145736 | tf_op jit(solution)/shard_map/ppermute | solution.py:341
  17.0 7.3 %collective-permute-start = (f32[8,64,128]{2,1,0:T(8,128)}, f32[8,64,128]{2,1,0:T(8,128)S(1)}, u32[]{:S(2)}, u32[]{:S(2)}) collective-permute-start(f32[8,64,128]{2,1,0:T(8,128)} %get-tuple-element.44), channel_id=1, source_target_pairs={{0,1},{1,2},{2,3},{3,4},{4,5},{5,6},{6,7},{8,9},{9,10},{10,11},{11... | collective-permute-start | bytes 786440 | tf_op jit(solution)/shard_map/ppermute | solution.py:341
  20.7 8.3 %collective-permute-start.1 = (f32[8,64,128]{2,1,0:T(8,128)}, f32[8,64,128]{2,1,0:T(8,128)}, u32[]{:S(2)}, u32[]{:S(2)}) collective-permute-start(f32[8,64,128]{2,1,0:T(8,128)} %get-tuple-element.45.refs_0_), channel_id=1, source_target_pairs={{1,0},{2,1},{3,2},{4,3},{5,4},{6,5},{7,6},{9,8},{10,9},{11,10},{12... | collective-permute-start | bytes 786440 | tf_op jit(solution)/shard_map/ppermute | solution.py:341
  30.7 11.8 %collective-permute-start.5 = (f32[8,16,256]{2,1,0:T(8,128)}, f32[8,16,256]{2,1,0:T(8,128)S(1)}, u32[]{:S(2)}, u32[]{:S(2)}) collective-permute-start(f32[8,16,256]{2,1,0:T(8,128)} %get-tuple-element.69), channel_id=1, source_target_pairs={{8,0},{9,1},{10,2},{11,3},{12,4},{13,5},{14,6},{15,7},{16,8},{17,9... | collective-permute-start | bytes 393224 | tf_op jit(solution)/shard_map/ppermute | solution.py:341
  33.2 9.3 %collective-permute-start.4 = (f32[8,16,256]{2,1,0:T(8,128)}, f32[8,16,256]{2,1,0:T(8,128)}, u32[]{:S(2)}, u32[]{:S(2)}) collective-permute-start(f32[8,16,256]{2,1,0:T(8,128)} %get-tuple-element.70), channel_id=1, source_target_pairs={{0,8},{1,9},{2,10},{3,11},{4,12},{5,13},{6,14},{7,15},{8,16},{9,17... | collective-permute-start | bytes 393224 | tf_op jit(solution)/shard_map/ppermute | solution.py:341
  42.5 43.8 %copy-start.2 = (f32[64,64,256]{2,1,0:T(8,128)S(1)}, f32[64,64,256]{2,1,0:T(8,128)}, u32[]{:S(2)}) copy-start(f32[64,64,256]{2,1,0:T(8,128)} %est_ref.5) | copy-start | bytes 12582916
  43.9 22.8 %collective-permute-start.7 = (f32[2,8,64,128]{3,2,1,0:T(8,128)S(1)}, f32[2,8,64,128]{3,2,1,0:T(8,128)S(1)}, u32[]{:S(2)}, u32[]{:S(2)}) collective-permute-start(f32[2,8,64,128]{3,2,1,0:T(8,128)S(1)} %get-tuple-element.49), channel_id=1, source_target_pairs={{0,0},{1,72},{2,32},{3,104},{4,64},{5,8},{6,96},{7,40},{8,16},{9,8... | collective-permute-start | bytes 1572872 | tf_op jit(solution)/shard_map/ppermute | solution.py:475
  47.8 26.9 %collective-permute-start.8 = (f32[2,8,64,128]{3,2,1,0:T(8,128)S(1)}, f32[2,8,64,128]{3,2,1,0:T(8,128)S(1)}, u32[]{:S(2)}, u32[]{:S(2)}) collective-permute-start(f32[2,8,64,128]{3,2,1,0:T(8,128)S(1)} %get-tuple-element.50), channel_id=1, source_target_pairs={{0,16},{1,88},{2,48},{3,120},{4,80},{5,24},{6,112},{7,56},{8,0},{9... | collective-permute-start | bytes 1572872 | tf_op jit(solution)/shard_map/ppermute | solution.py:475
  50.8 35.4 %collective-permute-start.9 = (f32[2,8,64,128]{3,2,1,0:T(8,128)S(1)}, f32[2,8,64,128]{3,2,1,0:T(8,128)S(1)}, u32[]{:S(2)}, u32[]{:S(2)}) collective-permute-start(f32[2,8,64,128]{3,2,1,0:T(8,128)S(1)} %get-tuple-element.51), channel_id=1, source_target_pairs={{0,32},{1,104},{2,64},{3,8},{4,96},{5,40},{6,0},{7,72},{8,48},{9,1... | collective-permute-start | bytes 1572872 | tf_op jit(solution)/shard_map/ppermute | solution.py:475
  55.1 44.5 %collective-permute-start.10 = (f32[2,8,64,128]{3,2,1,0:T(8,128)S(1)}, f32[2,8,64,128]{3,2,1,0:T(8,128)S(1)}, u32[]{:S(2)}, u32[]{:S(2)}) collective-permute-start(f32[2,8,64,128]{3,2,1,0:T(8,128)S(1)} %get-tuple-element.54), channel_id=1, source_target_pairs={{0,48},{1,120},{2,80},{3,24},{4,112},{5,56},{6,16},{7,88},{8,32},{... | collective-permute-start | bytes 1572872 | tf_op jit(solution)/shard_map/ppermute | solution.py:475
  57.7 41.8 %collective-permute-start.11 = (f32[2,8,64,128]{3,2,1,0:T(8,128)S(1)}, f32[2,8,64,128]{3,2,1,0:T(8,128)S(1)}, u32[]{:S(2)}, u32[]{:S(2)}) collective-permute-start(f32[2,8,64,128]{3,2,1,0:T(8,128)S(1)} %get-tuple-element.55), channel_id=1, source_target_pairs={{0,64},{1,8},{2,96},{3,40},{4,0},{5,72},{6,32},{7,104},{8,80},{9,2... | collective-permute-start | bytes 1572872 | tf_op jit(solution)/shard_map/ppermute | solution.py:475
  66.7 36.6 %collective-permute-start.12 = (f32[2,8,64,128]{3,2,1,0:T(8,128)S(1)}, f32[2,8,64,128]{3,2,1,0:T(8,128)S(1)}, u32[]{:S(2)}, u32[]{:S(2)}) collective-permute-start(f32[2,8,64,128]{3,2,1,0:T(8,128)S(1)} %get-tuple-element.56), channel_id=1, source_target_pairs={{0,80},{1,24},{2,112},{3,56},{4,16},{5,88},{6,48},{7,120},{8,64},{... | collective-permute-start | bytes 1572872 | tf_op jit(solution)/shard_map/ppermute | solution.py:475
  74.7 28.6 %collective-permute-start.13 = (f32[2,8,64,128]{3,2,1,0:T(8,128)S(1)}, f32[2,8,64,128]{3,2,1,0:T(8,128)S(1)}, u32[]{:S(2)}, u32[]{:S(2)}) collective-permute-start(f32[2,8,64,128]{3,2,1,0:T(8,128)S(1)} %get-tuple-element.57), channel_id=1, source_target_pairs={{0,96},{1,40},{2,0},{3,72},{4,32},{5,104},{6,64},{7,8},{8,112},{9,... | collective-permute-start | bytes 1572872 | tf_op jit(solution)/shard_map/ppermute | solution.py:475
  86.2 19.9 %collective-permute-start.14 = (f32[2,8,64,128]{3,2,1,0:T(8,128)S(1)}, f32[2,8,64,128]{3,2,1,0:T(8,128)S(1)}, u32[]{:S(2)}, u32[]{:S(2)}) collective-permute-start(f32[2,8,64,128]{3,2,1,0:T(8,128)S(1)} %get-tuple-element.58), channel_id=1, source_target_pairs={{0,112},{1,56},{2,16},{3,88},{4,48},{5,120},{6,80},{7,24},{8,96},{... | collective-permute-start | bytes 1572872 | tf_op jit(solution)/shard_map/ppermute | solution.py:475
  108.6 41.9 %collective-permute-start.19 = (f32[16,64,256]{2,1,0:T(8,128)S(1)}, f32[16,64,256]{2,1,0:T(8,128)S(1)}, u32[]{:S(2)}, u32[]{:S(2)}) collective-permute-start(f32[16,64,256]{2,1,0:T(8,128)S(1)} %get-tuple-element.61), channel_id=1, source_target_pairs={{0,8},{1,9},{2,10},{3,11},{4,12},{5,13},{6,14},{7,15},{8,16},{9,17... | collective-permute-start | bytes 3145736 | tf_op jit(solution)/shard_map/ppermute | solution.py:341
  112.4 38.1 %collective-permute-start.20 = (f32[16,64,256]{2,1,0:T(8,128)S(1)}, f32[16,64,256]{2,1,0:T(8,128)S(1)}, u32[]{:S(2)}, u32[]{:S(2)}) collective-permute-start(f32[16,64,256]{2,1,0:T(8,128)S(1)} %get-tuple-element.62), channel_id=1, source_target_pairs={{8,0},{9,1},{10,2},{11,3},{12,4},{13,5},{14,6},{15,7},{16,8},{17,9... | collective-permute-start | bytes 3145736 | tf_op jit(solution)/shard_map/ppermute | solution.py:341
  116.0 14.3 %collective-permute-start.15 = (f32[8,64,128]{2,1,0:T(8,128)S(1)}, f32[8,64,128]{2,1,0:T(8,128)S(1)}, u32[]{:S(2)}, u32[]{:S(2)}) collective-permute-start(f32[8,64,128]{2,1,0:T(8,128)S(1)} %get-tuple-element.59), channel_id=1, source_target_pairs={{0,1},{1,2},{2,3},{3,4},{4,5},{5,6},{6,7},{8,9},{9,10},{10,11},{11... | collective-permute-start | bytes 786440 | tf_op jit(solution)/shard_map/ppermute | solution.py:341
  126.9 8.0 %collective-permute-start.16 = (f32[8,64,128]{2,1,0:T(8,128)S(1)}, f32[8,64,128]{2,1,0:T(8,128)S(1)}, u32[]{:S(2)}, u32[]{:S(2)}) collective-permute-start(f32[8,64,128]{2,1,0:T(8,128)S(1)} %get-tuple-element.60), channel_id=1, source_target_pairs={{1,0},{2,1},{3,2},{4,3},{5,4},{6,5},{7,6},{9,8},{10,9},{11,10},{12... | collective-permute-start | bytes 786440 | tf_op jit(solution)/shard_map/ppermute | solution.py:341
  135.0 15.5 %collective-permute-start.18 = (f32[2,64,256]{2,1,0:T(8,128)S(1)}, f32[2,64,256]{2,1,0:T(8,128)S(1)}, u32[]{:S(2)}, u32[]{:S(2)}) collective-permute-start(f32[2,64,256]{2,1,0:T(8,128)S(1)} %get-tuple-element.67), channel_id=1, source_target_pairs={{8,0},{9,1},{10,2},{11,3},{12,4},{13,5},{14,6},{15,7},{16,8},{17,9... | collective-permute-start | bytes 393224 | tf_op jit(solution)/shard_map/ppermute | solution.py:341
  136.9 13.6 %collective-permute-start.17 = (f32[2,64,256]{2,1,0:T(8,128)S(1)}, f32[2,64,256]{2,1,0:T(8,128)S(1)}, u32[]{:S(2)}, u32[]{:S(2)}) collective-permute-start(f32[2,64,256]{2,1,0:T(8,128)S(1)} %get-tuple-element.68), channel_id=1, source_target_pairs={{0,8},{1,9},{2,10},{3,11},{4,12},{5,13},{6,14},{7,15},{8,16},{9,17... | collective-permute-start | bytes 393224 | tf_op jit(solution)/shard_map/ppermute | solution.py:341
  (5 other events, 42.5 us)

commit v12 on v11

--- a/solution.py
+++ b/solution.py
@@ -177,30 +177,28 @@
     return pl.BlockSpec(t.shape, lambda i: (0,) * t.ndim)
 
 
-def row_kernel(table_ref, own_ref, left_ref, right_ref, *refs):
+def row_kernel(table_ref, own_ref, both_ref, *refs):
     up_ref, down_ref, up_edge_ref, down_edge_ref = refs[:4]
     out_ref, edge_ref = refs[-2:]
     table = table_ref[...]
     for z in range(8):
         out_ref[z] = along(table, jnp.concatenate([up_ref[z], own_ref[z], down_ref[z]], axis=0))
-    both = jnp.concatenate([left_ref[0], right_ref[0]], axis=1)
-    edge_ref[0] = along(table, jnp.concatenate([up_edge_ref[0], both, down_edge_ref[0]], axis=0))
-
-
-def row_mix(table, up, own, down, left, right, above, below, after):
+    edge_ref[0] = along(table, jnp.concatenate([up_edge_ref[0], both_ref[0], down_edge_ref[0]], axis=0))
+
+
+def row_mix(table, up, own, down, both, above, below, after):
     depth, rows, cols = own.shape
     groups = depth // 8
     block = lambda d, r: pl.BlockSpec((d, r, cols), lambda i: (i, 0, 0))
-    packs = pl.BlockSpec((1, rows, 128), lambda i: (i, 0, 0))
     return pl.pallas_call(
         row_kernel,
         grid=(groups,),
-        in_specs=[whole(table), block(8, rows), packs, packs, block(8, 16), block(8, 16), block(1, 16), block(1, 16)]
+        in_specs=[whole(table), block(8, rows), block(1, rows), block(8, 16), block(8, 16), block(1, 16), block(1, 16)]
         + [ANY] * len(after),
         out_specs=[block(8, rows), block(1, rows)],
         out_shape=[jax.ShapeDtypeStruct(own.shape, F32), jax.ShapeDtypeStruct((groups, rows, cols), F32)],
         **params(10, 4),
-    )(table, own, left, right, up, down, above, below, *after)
+    )(table, own, both, up, down, above, below, *after)
 
 
 def blur_kernel(u_ref, e_ref, m_ref, edge_ref, x_ref, out_ref):
@@ -362,14 +360,14 @@
         copy.wait()
 
 
-def copy_call(body, count, shapes, inputs, us):
+def copy_call(body, count, shapes, inputs, us, mib=16):
     return pl.pallas_call(
         body,
         in_specs=[HBM] * len(inputs),
         out_specs=[pl.BlockSpec(memory_space=pltpu.VMEM)] * len(shapes),
         out_shape=[jax.ShapeDtypeStruct(s, F32) for s in shapes],
         scratch_shapes=[pltpu.SemaphoreType.DMA((count,))],
-        **params(16, us),
+        **params(mib, us),
     )(*inputs)
 
 
@@ -400,7 +398,28 @@
         run_copies(pairs, sems)
 
     depth, _, cols = est.shape
-    return copy_call(body, depth // 8, [(depth, 16, cols)] * 2, (est,), 2)
+    return copy_call(body, depth // 8, [(depth, 16, cols)] * 2, (est,), 2, 50)
+
+
+def join_edges(left, right, dim, n):
+    def body(left_ref, right_ref, both_ref, first_ref, last_ref):
+        both_ref[:, :, :128] = left_ref[...]
+        both_ref[:, :, 128:] = right_ref[...]
+        size = both_ref.shape[dim]
+        for ref, start in ((first_ref, 0), (last_ref, size - n)):
+            at = tuple(pl.ds(start, n) if d == dim else slice(None) for d in range(3))
+            ref[...] = both_ref[at]
+
+    shape = (*left.shape[:2], 256)
+    part = tuple(n if d == dim else size for d, size in enumerate(shape))
+    vmem = pl.BlockSpec(memory_space=pltpu.VMEM)
+    return pl.pallas_call(
+        body,
+        in_specs=[vmem] * 2,
+        out_specs=[vmem] * 3,
+        out_shape=[jax.ShapeDtypeStruct(t, F32) for t in (shape, part, part)],
+        **params(8, 1),
+    )(left, right)
 
 
 def halves_of(measured, rows, after):
@@ -443,16 +462,16 @@
     return window(main), window(upper)
 
 
-def forward(tables, up, estimate, down, left, right, above, below, after):
-    mixed, edge = row_mix(tables[0], up, estimate, down, left, right, above, below, after)
+def forward(tables, up, estimate, down, both, above, below, after):
+    mixed, edge = row_mix(tables[0], up, estimate, down, both, above, below, after)
     return blur(tables[3], tables[4], tables[7], edge, mixed)
 
 
 def backward(tables, ratio, top, bottom, left, right, estimate, column_edges, row_edges):
     rb, re, ub, ube, zb = tables[1], tables[2], tables[5], tables[6], tables[8]
     up, down = row_edges(top, bottom)
-    both = jnp.concatenate(column_edges(left, right), axis=2)
-    above, below = row_edges(both[:2], both[both.shape[0] - 2 :])
+    both, first, last = join_edges(*column_edges(left, right), 0, 2)
+    above, below = row_edges(first, last)
     part = own_update(ub, ube, zb, rb, both, ratio, estimate)
     return edge_update(ub, ube, zb, re, above, below, up, down, estimate, part)
 
@@ -467,15 +486,15 @@
     left, right = column_edges(*ends)
     near, far = halves_of(measured, rows, ends[:1])
     far = lax.ppermute(far, AXES, core_swap())
-    both = jnp.concatenate([left, right], axis=2)
-    above, below = row_edges(both[:, :16], both[:, rows - 16 :])
+    both, first, last = join_edges(left, right, 1, 16)
+    above, below = row_edges(first, last)
     main, upper = diagonal_windows(r_interp, gx, rows)
     tables = make_tables(psf_z, psf_r, psf_u, z_interp, main, upper, rows, width)
     first, second = range(3), range(3, 8)
     ship = lambda parts, steps: [lax.ppermute(p, AXES, piece_perm(k)) for p, k in zip(parts, steps)]
     pieces = ship(pieces_of(near, far, first, (above, below, tables[0], up, down)), first)
     pieces += ship(pieces_of(near, far, second, (tables[0],)), second)
-    blurred = forward(tables, up, estimate, down, left, right, above, below, pieces[:3])
+    blurred = forward(tables, up, estimate, down, both, above, below, pieces[:3])
     return backward(tables, *ratio_of(blurred, pieces), estimate, column_edges, row_edges)
 
 

time: 158 us -> 159 us (level)
  local copies, waits for them, and re-layouts: 6.85 us -> 1.22 us
  starting transfers between devices: 85.7 us -> 91 us
  Pallas kernels: 43.1 us -> 46 us
    ppermute x12, starting transfers between devices: 44 us -> 50 us  [send(): return lax.ppermute(x, AXES, shift_perm(axis, d))]
    unnamed x18, local copies, waits for them, and re-layouts: 4.38 us -> 1.13 us
    pallas_call x0 -> x2, Pallas kernels: none -> 1.86 us  [join_edges(): pl.pallas_call(body, in_specs=[vmem] * 2, out_specs=[vmem] * 3, out_shape...]
  transfers between devices with their start and end apart: 21 -> 21, of which waited for: 6 -> 6; matrix products, arithmetic and copies ran while one was open for 3% -> 1% of each run, Pallas kernels for 18% -> 18%
where the time goes in v12:
time: 159 us; the launch traced here: 158 us
  starting transfers between devices  91 us (57%)
  Pallas kernels  46 us (29%)
  waiting for transfers between devices  18.1 us (11%)
    ppermute x12, starting transfers between devices, send(): return lax.ppermute(x, AXES, shift_perm(axis, d))  50 us
    ppermute x8, starting transfers between devices, shards(): lax.ppermute(p, AXES, piece_perm(k))  40.3 us
    ppermute x12, waiting for transfers between devices, send(): return lax.ppermute(x, AXES, shift_perm(axis, d))  12.2 us
    pallas_call x1, Pallas kernels, own_update(): pl.pallas_call(own_kernel, grid=(half + depth // 16,), in_specs=[whole(u)...  9.84 us
    pallas_call x4, Pallas kernels, copy_call(): pl.pallas_call(body, in_specs=[HBM] * len(inputs), out_specs=[pl.BlockSpe...  7.61 us
    pallas_call x1, Pallas kernels, blur(): pl.pallas_call(blur_kernel, grid=(rows // 8,), in_specs=[whole(u), whole(...  7.36 us
    pallas_call x1, Pallas kernels, edge_update(): pl.pallas_call(edge_kernel, grid=(2, 2), in_specs=[fixed(u), fixed(e), fi...  6.51 us
    ppermute x8, waiting for transfers between devices, shards(): lax.ppermute(p, AXES, piece_perm(k))  5.92 us
  transfers between devices with their start and end apart: 21, of which 6 were waited for; matrix products, arithmetic and copies ran while one was open for 1% of the time, Pallas kernels for 18%

profile of v12, /device:TPU:69, one launch (start us, length us, event | category | flops | bytes accessed | tf_op | source)
XLA Modules:
  0.0 158.2 jit_solution(5142746449515378214)
XLA Ops:
  0.0 3.0 %shard_map.74 = (f32[64,16,256]{2,1,0:T(8,128)}, f32[64,16,256]{2,1,0:T(8,128)}) custom-call(f32[64,64,256]{2,1,0:T(8,128)} %est_ref.5), custom_call_target="tpu_custom_call" | custom-call | bytes 6000000 | tf_op jit(solution)/shard_map/pallas_call | solution.py:364
  7.7 3.2 %collective-permute-start.2 = (f32[64,16,256]{2,1,0:T(8,128)}, f32[64,16,256]{2,1,0:T(8,128)S(1)}, u32[]{:S(2)}, u32[]{:S(2)}) collective-permute-start(f32[64,16,256]{2,1,0:T(8,128)} %get-tuple-element.53), channel_id=1, source_target_pairs={{0,8},{1,9},{2,10},{3,11},{4,12},{5,13},{6,14},{7,15},{8,16},{9,17... | collective-permute-start | bytes 3145736 | tf_op jit(solution)/shard_map/ppermute | solution.py:339
  10.9 4.2 %collective-permute-start.3 = (f32[64,16,256]{2,1,0:T(8,128)}, f32[64,16,256]{2,1,0:T(8,128)}, u32[]{:S(2)}, u32[]{:S(2)}) collective-permute-start(f32[64,16,256]{2,1,0:T(8,128)} %get-tuple-element.49.refs_0_), channel_id=1, source_target_pairs={{8,0},{9,1},{10,2},{11,3},{12,4},{13,5},{14,6},{15,7},{16,8},{17,9... | collective-permute-start | bytes 3145736 | tf_op jit(solution)/shard_map/ppermute | solution.py:339
  15.1 3.7 %collective-permute-start = (f32[8,64,128]{2,1,0:T(8,128)}, f32[8,64,128]{2,1,0:T(8,128)}, u32[]{:S(2)}, u32[]{:S(2)}) collective-permute-start(f32[8,64,128]{2,1,0:T(8,128)} %get-tuple-element.50), channel_id=1, source_target_pairs={{0,1},{1,2},{2,3},{3,4},{4,5},{5,6},{6,7},{8,9},{9,10},{10,11},{11... | collective-permute-start | bytes 786440 | tf_op jit(solution)/shard_map/ppermute | solution.py:339
  22.4 4.5 %collective-permute-done.1.right_ref = f32[8,64,128]{2,1,0:T(8,128)} collective-permute-done((f32[8,64,128]{2,1,0:T(8,128)S(1)}, f32[8,64,128]{2,1,0:T(8,128)}, u32[]{:S(2)}, u32[]{:S(2)}) %collective-permute-start.1) | collective-permute-done | bytes 262176 | tf_op jit(solution)/shard_map/ppermute | solution.py:339
  31.4 5.5 %collective-permute-start.5 = (f32[8,16,256]{2,1,0:T(8,128)}, f32[8,16,256]{2,1,0:T(8,128)S(1)}, u32[]{:S(2)}, u32[]{:S(2)}) collective-permute-start(f32[8,16,256]{2,1,0:T(8,128)} %get-tuple-element.55), channel_id=1, source_target_pairs={{8,0},{9,1},{10,2},{11,3},{12,4},{13,5},{14,6},{15,7},{16,8},{17,9... | collective-permute-start | bytes 393224 | tf_op jit(solution)/shard_map/ppermute | solution.py:339
  38.5 2.9 %shard_map.73 = (bf16[64,288]{1,0:T(8,128)(2,1)S(1)}, bf16[64,192]{1,0:T(8,128)(2,1)S(1)}, bf16[2,16,48]{2,1,0:T(8,128)(2,1)S(1)}, bf16[768,256]{1,0:T(8,128)(2,...) custom-call(f32[32]{0:T(128)S(1)} %copy-done.6, ...), custom_call_target="tpu_custom_call" | custom-call | bytes 9000000 | tf_op jit(solution)/shard_map/pallas_call | solution.py:133
  42.8 3.2 %collective-permute-start.7 = (f32[2,8,64,128]{3,2,1,0:T(8,128)S(1)}, f32[2,8,64,128]{3,2,1,0:T(8,128)S(1)}, u32[]{:S(2)}, u32[]{:S(2)}) collective-permute-start(f32[2,8,64,128]{3,2,1,0:T(8,128)S(1)} %get-tuple-element.58), channel_id=1, source_target_pairs={{0,0},{1,72},{2,32},{3,104},{4,64},{5,8},{6,96},{7,40},{8,16},{9,8... | collective-permute-start | bytes 1572872 | tf_op jit(solution)/shard_map/ppermute | solution.py:494
  46.0 2.9 %collective-permute-start.8 = (f32[2,8,64,128]{3,2,1,0:T(8,128)S(1)}, f32[2,8,64,128]{3,2,1,0:T(8,128)S(1)}, u32[]{:S(2)}, u32[]{:S(2)}) collective-permute-start(f32[2,8,64,128]{3,2,1,0:T(8,128)S(1)} %get-tuple-element.59), channel_id=1, source_target_pairs={{0,16},{1,88},{2,48},{3,120},{4,80},{5,24},{6,112},{7,56},{8,0},{9... | collective-permute-start | bytes 1572872 | tf_op jit(solution)/shard_map/ppermute | solution.py:494
  48.9 2.9 %collective-permute-start.9 = (f32[2,8,64,128]{3,2,1,0:T(8,128)S(1)}, f32[2,8,64,128]{3,2,1,0:T(8,128)S(1)}, u32[]{:S(2)}, u32[]{:S(2)}) collective-permute-start(f32[2,8,64,128]{3,2,1,0:T(8,128)S(1)} %get-tuple-element.60), channel_id=1, source_target_pairs={{0,32},{1,104},{2,64},{3,8},{4,96},{5,40},{6,0},{7,72},{8,48},{9,1... | collective-permute-start | bytes 1572872 | tf_op jit(solution)/shard_map/ppermute | solution.py:494
  53.2 2.7 %collective-permute-start.10 = (f32[2,8,64,128]{3,2,1,0:T(8,128)S(1)}, f32[2,8,64,128]{3,2,1,0:T(8,128)S(1)}, u32[]{:S(2)}, u32[]{:S(2)}) collective-permute-start(f32[2,8,64,128]{3,2,1,0:T(8,128)S(1)} %get-tuple-element.63), channel_id=1, source_target_pairs={{0,48},{1,120},{2,80},{3,24},{4,112},{5,56},{6,16},{7,88},{8,32},{... | collective-permute-start | bytes 1572872 | tf_op jit(solution)/shard_map/ppermute | solution.py:494
  55.9 8.9 %collective-permute-start.11 = (f32[2,8,64,128]{3,2,1,0:T(8,128)S(1)}, f32[2,8,64,128]{3,2,1,0:T(8,128)S(1)}, u32[]{:S(2)}, u32[]{:S(2)}) collective-permute-start(f32[2,8,64,128]{3,2,1,0:T(8,128)S(1)} %get-tuple-element.64), channel_id=1, source_target_pairs={{0,64},{1,8},{2,96},{3,40},{4,0},{5,72},{6,32},{7,104},{8,80},{9,2... | collective-permute-start | bytes 1572872 | tf_op jit(solution)/shard_map/ppermute | solution.py:494
  64.8 8.6 %collective-permute-start.12 = (f32[2,8,64,128]{3,2,1,0:T(8,128)S(1)}, f32[2,8,64,128]{3,2,1,0:T(8,128)S(1)}, u32[]{:S(2)}, u32[]{:S(2)}) collective-permute-start(f32[2,8,64,128]{3,2,1,0:T(8,128)S(1)} %get-tuple-element.65), channel_id=1, source_target_pairs={{0,80},{1,24},{2,112},{3,56},{4,16},{5,88},{6,48},{7,120},{8,64},{... | collective-permute-start | bytes 1572872 | tf_op jit(solution)/shard_map/ppermute | solution.py:494
  73.4 11.1 %collective-permute-start.13 = (f32[2,8,64,128]{3,2,1,0:T(8,128)S(1)}, f32[2,8,64,128]{3,2,1,0:T(8,128)S(1)}, u32[]{:S(2)}, u32[]{:S(2)}) collective-permute-start(f32[2,8,64,128]{3,2,1,0:T(8,128)S(1)} %get-tuple-element.66), channel_id=1, source_target_pairs={{0,96},{1,40},{2,0},{3,72},{4,32},{5,104},{6,64},{7,8},{8,112},{9,... | collective-permute-start | bytes 1572872 | tf_op jit(solution)/shard_map/ppermute | solution.py:494
  84.6 5.7 %shard_map.79 = (f32[64,64,256]{2,1,0:T(8,128)S(1)}, f32[8,64,256]{2,1,0:T(8,128)S(1)}) custom-call(bf16[64,288]{1,0:T(8,128)(2,1)S(1)} %get-tuple-element.48.refs_2_.table_ref.refs_0_, f32[64,64,256]{2,1,0:T(8,128)S(1)} %copy-done.1, f32[8,64,256]{2,1,0:T(8,128)S(1)} %copy-done.4, f32[64,16,256]{2,1,0:T(8,128)S(1)} %collective-permute-done.2.refs_3_.refs_0_, ...), custom_call_target="tpu_custom_call" | custom-call | bytes 12000000 | tf_op jit(solution)/shard_map/pallas_call | solution.py:193
  90.3 7.4 %shard_map.80.blur_ref = f32[64,64,256]{2,1,0:T(8,128)S(1)} custom-call(bf16[768,256]{1,0:T(8,128)(2,1)S(1)} %get-tuple-element.45.u_ref, bf16[768,256]{1,0:T(8,128)(2,1)S(1)} %get-tuple-element.46.e_ref, bf16[64,192]{1,0:T(8,128)(2,1)S(1)} %get-tuple-element.47.m_ref, f32[8,64,256]{2,1,0:T(8,128)S(1)} %get-tuple-element.61.edge_ref, ...), custom_call_target="tpu_custom_call" | custom-call | bytes 24000000 | tf_op jit(solution)/shard_map/pallas_call | solution.py:220
  97.7 3.5 %collective-permute-done.12.refs_5_ = f32[2,8,64,128]{3,2,1,0:T(8,128)S(1)} collective-permute-done((f32[2,8,64,128]{3,2,1,0:T(8,128)S(1)}, f32[2,8,64,128]{3,2,1,0:T(8,128)S(1)}, u32[]{:S(2)}, u32[]{:S(2)}) %collective-permute-start.12) | collective-permute-done | bytes 524320 | tf_op jit(solution)/shard_map/ppermute | solution.py:494
  103.6 2.4 %shard_map.82 = (f32[64,64,256]{2,1,0:T(8,128)S(1)}, f32[16,64,256]{2,1,0:T(8,128)S(1)}, f32[16,64,256]{2,1,0:T(8,128)S(1)}, f32[8,64,128]{2,1,0:T(8,128)S(1)}, f32[8,64,128]{2,1,0:T(8,128)S(1)}) custom-call(f32[64,64,256]{2,1,0:T(8,128)S(1)} %shard_map.80.blur_ref, f32[2,8,64,128]{3,2,1,0:T(8,128)S(1)} %collective-permute-done.7.refs_4_.refs_0_, ...), custom_call_target="tpu_custom_call" | custom-call | bytes 21000000 | tf_op jit(solution)/shard_map/pallas_call | solution.py:249
  106.1 6.3 %collective-permute-start.19 = (f32[16,64,256]{2,1,0:T(8,128)S(1)}, f32[16,64,256]{2,1,0:T(8,128)S(1)}, u32[]{:S(2)}, u32[]{:S(2)}) collective-permute-start(f32[16,64,256]{2,1,0:T(8,128)S(1)} %get-tuple-element.72), channel_id=1, source_target_pairs={{0,8},{1,9},{2,10},{3,11},{4,12},{5,13},{6,14},{7,15},{8,16},{9,17... | collective-permute-start | bytes 3145736 | tf_op jit(solution)/shard_map/ppermute | solution.py:339
  114.3 11.8 %collective-permute-start.15 = (f32[8,64,128]{2,1,0:T(8,128)S(1)}, f32[8,64,128]{2,1,0:T(8,128)S(1)}, u32[]{:S(2)}, u32[]{:S(2)}) collective-permute-start(f32[8,64,128]{2,1,0:T(8,128)S(1)} %get-tuple-element.68), channel_id=1, source_target_pairs={{0,1},{1,2},{2,3},{3,4},{4,5},{5,6},{6,7},{8,9},{9,10},{10,11},{11... | collective-permute-start | bytes 786440 | tf_op jit(solution)/shard_map/ppermute | solution.py:339
  129.5 4.7 %collective-permute-done.16.right_ref = f32[8,64,128]{2,1,0:T(8,128)S(1)} collective-permute-done((f32[8,64,128]{2,1,0:T(8,128)S(1)}, f32[8,64,128]{2,1,0:T(8,128)S(1)}, u32[]{:S(2)}, u32[]{:S(2)}) %collective-permute-start.16) | collective-permute-done | bytes 262176 | tf_op jit(solution)/shard_map/ppermute | solution.py:339
  136.2 5.7 %collective-permute-start.18 = (f32[2,64,256]{2,1,0:T(8,128)S(1)}, f32[2,64,256]{2,1,0:T(8,128)S(1)}, u32[]{:S(2)}, u32[]{:S(2)}) collective-permute-start(f32[2,64,256]{2,1,0:T(8,128)S(1)} %get-tuple-element.71), channel_id=1, source_target_pairs={{8,0},{9,1},{10,2},{11,3},{12,4},{13,5},{14,6},{15,7},{16,8},{17,9... | collective-permute-start | bytes 393224 | tf_op jit(solution)/shard_map/ppermute | solution.py:339
  141.8 9.8 %shard_map.84.part_ref = f32[64,64,256]{2,1,0:T(8,128)} custom-call(bf16[768,256]{1,0:T(8,128)(2,1)S(1)} %get-tuple-element.41.u_ref, bf16[768,256]{1,0:T(8,128)(2,1)S(1)} %get-tuple-element.42.e_ref, bf16[64,192]{1,0:T(8,128)(2,1)S(1)} %get-tuple-element.43.m_ref, bf16[64,192]{1,0:T(8,128)(2,1)S(1)} %get-tuple-element.74.a_ref, ...), custom_call_target="tpu_custom_call" | custom-call | bytes 30000000 | tf_op jit(solution)/shard_map/pallas_call | solution.py:288
  151.7 6.5 %shard_map.85 = f32[64,64,256]{2,1,0:T(8,128)} custom-call(bf16[768,256]{1,0:T(8,128)(2,1)S(1)} %get-tuple-element.41.u_ref, bf16[768,256]{1,0:T(8,128)(2,1)S(1)} %get-tuple-element.42.e_ref, bf16[64,192]{1,0:T(8,128)(2,1)S(1)} %get-tuple-element.43.m_ref, bf16[2,16,48]{2,1,0:T(8,128)(2,1)S(1)} %get-tuple-element.44.a_ref, ...), custom_call_target="tpu_custom_call", output_to_operand_aliasing={{}: (9, {})} | custom-call | bytes 18000000 | tf_op jit(solution)/shard_map/pallas_call | solution.py:323
  (53 shorter events, 26.7 us)
Async XLA Ops:
  5.1 33.4 %copy-start.8 = (f32[32]{0:T(128)S(1)}, f32[32]{0:T(128)}, u32[]{:S(2)}) copy-start(f32[32]{0:T(128)} %pu_ref.1) | copy-start | bytes 388
  6.9 34.5 %collective-permute-start.6 = (f32[8,8,64,128]{3,2,1,0:T(8,128)}, f32[8,8,64,128]{3,2,1,0:T(8,128)}, u32[]{:S(2)}, u32[]{:S(2)}) collective-permute-start(f32[8,8,64,128]{3,2,1,0:T(8,128)} %get-tuple-element.57), channel_id=1, source_target_pairs={{0,1},{1,0},{2,3},{3,2},{4,5},{5,4},{6,7},{7,6},{8,9},{9,8},{10,11... | collective-permute-start | bytes 6291464 | tf_op jit(solution)/shard_map/ppermute | solution.py:488
  7.7 33.7 %collective-permute-start.2 = (f32[64,16,256]{2,1,0:T(8,128)}, f32[64,16,256]{2,1,0:T(8,128)S(1)}, u32[]{:S(2)}, u32[]{:S(2)}) collective-permute-start(f32[64,16,256]{2,1,0:T(8,128)} %get-tuple-element.53), channel_id=1, source_target_pairs={{0,8},{1,9},{2,10},{3,11},{4,12},{5,13},{6,14},{7,15},{8,16},{9,17... | collective-permute-start | bytes 3145736 | tf_op jit(solution)/shard_map/ppermute | solution.py:339
  10.9 30.5 %collective-permute-start.3 = (f32[64,16,256]{2,1,0:T(8,128)}, f32[64,16,256]{2,1,0:T(8,128)}, u32[]{:S(2)}, u32[]{:S(2)}) collective-permute-start(f32[64,16,256]{2,1,0:T(8,128)} %get-tuple-element.49.refs_0_), channel_id=1, source_target_pairs={{8,0},{9,1},{10,2},{11,3},{12,4},{13,5},{14,6},{15,7},{16,8},{17,9... | collective-permute-start | bytes 3145736 | tf_op jit(solution)/shard_map/ppermute | solution.py:339
  15.1 7.3 %collective-permute-start = (f32[8,64,128]{2,1,0:T(8,128)}, f32[8,64,128]{2,1,0:T(8,128)}, u32[]{:S(2)}, u32[]{:S(2)}) collective-permute-start(f32[8,64,128]{2,1,0:T(8,128)} %get-tuple-element.50), channel_id=1, source_target_pairs={{0,1},{1,2},{2,3},{3,4},{4,5},{5,6},{6,7},{8,9},{9,10},{10,11},{11... | collective-permute-start | bytes 786440 | tf_op jit(solution)/shard_map/ppermute | solution.py:339
  18.8 8.1 %collective-permute-start.1 = (f32[8,64,128]{2,1,0:T(8,128)S(1)}, f32[8,64,128]{2,1,0:T(8,128)}, u32[]{:S(2)}, u32[]{:S(2)}) collective-permute-start(f32[8,64,128]{2,1,0:T(8,128)S(1)} %get-tuple-element.51.refs_0_), channel_id=1, source_target_pairs={{1,0},{2,1},{3,2},{4,3},{5,4},{6,5},{7,6},{9,8},{10,9},{11,10},{12... | collective-permute-start | bytes 786440 | tf_op jit(solution)/shard_map/ppermute | solution.py:339
  29.5 11.9 %collective-permute-start.4 = (f32[8,16,256]{2,1,0:T(8,128)}, f32[8,16,256]{2,1,0:T(8,128)S(1)}, u32[]{:S(2)}, u32[]{:S(2)}) collective-permute-start(f32[8,16,256]{2,1,0:T(8,128)} %get-tuple-element.54), channel_id=1, source_target_pairs={{0,8},{1,9},{2,10},{3,11},{4,12},{5,13},{6,14},{7,15},{8,16},{9,17... | collective-permute-start | bytes 393224 | tf_op jit(solution)/shard_map/ppermute | solution.py:339
  31.4 10.0 %collective-permute-start.5 = (f32[8,16,256]{2,1,0:T(8,128)}, f32[8,16,256]{2,1,0:T(8,128)S(1)}, u32[]{:S(2)}, u32[]{:S(2)}) collective-permute-start(f32[8,16,256]{2,1,0:T(8,128)} %get-tuple-element.55), channel_id=1, source_target_pairs={{8,0},{9,1},{10,2},{11,3},{12,4},{13,5},{14,6},{15,7},{16,8},{17,9... | collective-permute-start | bytes 393224 | tf_op jit(solution)/shard_map/ppermute | solution.py:339
  41.4 43.1 %copy-start.1 = (f32[64,64,256]{2,1,0:T(8,128)S(1)}, f32[64,64,256]{2,1,0:T(8,128)}, u32[]{:S(2)}) copy-start(f32[64,64,256]{2,1,0:T(8,128)} %est_ref.5) | copy-start | bytes 12582916
  41.5 43.1 %copy-start.4 = (f32[8,64,256]{2,1,0:T(8,128)S(1)}, f32[8,64,256]{2,1,0:T(8,128)}, u32[]{:S(2)}) copy-start(f32[8,64,256]{2,1,0:T(8,128)} %copy-done.3) | copy-start | bytes 1572868
  42.8 22.0 %collective-permute-start.7 = (f32[2,8,64,128]{3,2,1,0:T(8,128)S(1)}, f32[2,8,64,128]{3,2,1,0:T(8,128)S(1)}, u32[]{:S(2)}, u32[]{:S(2)}) collective-permute-start(f32[2,8,64,128]{3,2,1,0:T(8,128)S(1)} %get-tuple-element.58), channel_id=1, source_target_pairs={{0,0},{1,72},{2,32},{3,104},{4,64},{5,8},{6,96},{7,40},{8,16},{9,8... | collective-permute-start | bytes 1572872 | tf_op jit(solution)/shard_map/ppermute | solution.py:494
  46.0 27.4 %collective-permute-start.8 = (f32[2,8,64,128]{3,2,1,0:T(8,128)S(1)}, f32[2,8,64,128]{3,2,1,0:T(8,128)S(1)}, u32[]{:S(2)}, u32[]{:S(2)}) collective-permute-start(f32[2,8,64,128]{3,2,1,0:T(8,128)S(1)} %get-tuple-element.59), channel_id=1, source_target_pairs={{0,16},{1,88},{2,48},{3,120},{4,80},{5,24},{6,112},{7,56},{8,0},{9... | collective-permute-start | bytes 1572872 | tf_op jit(solution)/shard_map/ppermute | solution.py:494
  48.9 35.6 %collective-permute-start.9 = (f32[2,8,64,128]{3,2,1,0:T(8,128)S(1)}, f32[2,8,64,128]{3,2,1,0:T(8,128)S(1)}, u32[]{:S(2)}, u32[]{:S(2)}) collective-permute-start(f32[2,8,64,128]{3,2,1,0:T(8,128)S(1)} %get-tuple-element.60), channel_id=1, source_target_pairs={{0,32},{1,104},{2,64},{3,8},{4,96},{5,40},{6,0},{7,72},{8,48},{9,1... | collective-permute-start | bytes 1572872 | tf_op jit(solution)/shard_map/ppermute | solution.py:494
  53.2 44.5 %collective-permute-start.10 = (f32[2,8,64,128]{3,2,1,0:T(8,128)S(1)}, f32[2,8,64,128]{3,2,1,0:T(8,128)S(1)}, u32[]{:S(2)}, u32[]{:S(2)}) collective-permute-start(f32[2,8,64,128]{3,2,1,0:T(8,128)S(1)} %get-tuple-element.63), channel_id=1, source_target_pairs={{0,48},{1,120},{2,80},{3,24},{4,112},{5,56},{6,16},{7,88},{8,32},{... | collective-permute-start | bytes 1572872 | tf_op jit(solution)/shard_map/ppermute | solution.py:494
  55.9 41.8 %collective-permute-start.11 = (f32[2,8,64,128]{3,2,1,0:T(8,128)S(1)}, f32[2,8,64,128]{3,2,1,0:T(8,128)S(1)}, u32[]{:S(2)}, u32[]{:S(2)}) collective-permute-start(f32[2,8,64,128]{3,2,1,0:T(8,128)S(1)} %get-tuple-element.64), channel_id=1, source_target_pairs={{0,64},{1,8},{2,96},{3,40},{4,0},{5,72},{6,32},{7,104},{8,80},{9,2... | collective-permute-start | bytes 1572872 | tf_op jit(solution)/shard_map/ppermute | solution.py:494
  64.8 36.4 %collective-permute-start.12 = (f32[2,8,64,128]{3,2,1,0:T(8,128)S(1)}, f32[2,8,64,128]{3,2,1,0:T(8,128)S(1)}, u32[]{:S(2)}, u32[]{:S(2)}) collective-permute-start(f32[2,8,64,128]{3,2,1,0:T(8,128)S(1)} %get-tuple-element.65), channel_id=1, source_target_pairs={{0,80},{1,24},{2,112},{3,56},{4,16},{5,88},{6,48},{7,120},{8,64},{... | collective-permute-start | bytes 1572872 | tf_op jit(solution)/shard_map/ppermute | solution.py:494
  73.4 27.8 %collective-permute-start.13 = (f32[2,8,64,128]{3,2,1,0:T(8,128)S(1)}, f32[2,8,64,128]{3,2,1,0:T(8,128)S(1)}, u32[]{:S(2)}, u32[]{:S(2)}) collective-permute-start(f32[2,8,64,128]{3,2,1,0:T(8,128)S(1)} %get-tuple-element.66), channel_id=1, source_target_pairs={{0,96},{1,40},{2,0},{3,72},{4,32},{5,104},{6,64},{7,8},{8,112},{9,... | collective-permute-start | bytes 1572872 | tf_op jit(solution)/shard_map/ppermute | solution.py:494
  84.5 19.2 %collective-permute-start.14 = (f32[2,8,64,128]{3,2,1,0:T(8,128)S(1)}, f32[2,8,64,128]{3,2,1,0:T(8,128)S(1)}, u32[]{:S(2)}, u32[]{:S(2)}) collective-permute-start(f32[2,8,64,128]{3,2,1,0:T(8,128)S(1)} %get-tuple-element.67), channel_id=1, source_target_pairs={{0,112},{1,56},{2,16},{3,88},{4,48},{5,120},{6,80},{7,24},{8,96},{... | collective-permute-start | bytes 1572872 | tf_op jit(solution)/shard_map/ppermute | solution.py:494
  106.1 45.6 %collective-permute-start.19 = (f32[16,64,256]{2,1,0:T(8,128)S(1)}, f32[16,64,256]{2,1,0:T(8,128)S(1)}, u32[]{:S(2)}, u32[]{:S(2)}) collective-permute-start(f32[16,64,256]{2,1,0:T(8,128)S(1)} %get-tuple-element.72), channel_id=1, source_target_pairs={{0,8},{1,9},{2,10},{3,11},{4,12},{5,13},{6,14},{7,15},{8,16},{9,17... | collective-permute-start | bytes 3145736 | tf_op jit(solution)/shard_map/ppermute | solution.py:339
  112.4 39.3 %collective-permute-start.20 = (f32[16,64,256]{2,1,0:T(8,128)S(1)}, f32[16,64,256]{2,1,0:T(8,128)S(1)}, u32[]{:S(2)}, u32[]{:S(2)}) collective-permute-start(f32[16,64,256]{2,1,0:T(8,128)S(1)} %get-tuple-element.73), channel_id=1, source_target_pairs={{8,0},{9,1},{10,2},{11,3},{12,4},{13,5},{14,6},{15,7},{16,8},{17,9... | collective-permute-start | bytes 3145736 | tf_op jit(solution)/shard_map/ppermute | solution.py:339
  114.3 15.1 %collective-permute-start.15 = (f32[8,64,128]{2,1,0:T(8,128)S(1)}, f32[8,64,128]{2,1,0:T(8,128)S(1)}, u32[]{:S(2)}, u32[]{:S(2)}) collective-permute-start(f32[8,64,128]{2,1,0:T(8,128)S(1)} %get-tuple-element.68), channel_id=1, source_target_pairs={{0,1},{1,2},{2,3},{3,4},{4,5},{5,6},{6,7},{8,9},{9,10},{10,11},{11... | collective-permute-start | bytes 786440 | tf_op jit(solution)/shard_map/ppermute | solution.py:339
  126.2 8.0 %collective-permute-start.16 = (f32[8,64,128]{2,1,0:T(8,128)S(1)}, f32[8,64,128]{2,1,0:T(8,128)S(1)}, u32[]{:S(2)}, u32[]{:S(2)}) collective-permute-start(f32[8,64,128]{2,1,0:T(8,128)S(1)} %get-tuple-element.69), channel_id=1, source_target_pairs={{1,0},{2,1},{3,2},{4,3},{5,4},{6,5},{7,6},{9,8},{10,9},{11,10},{12... | collective-permute-start | bytes 786440 | tf_op jit(solution)/shard_map/ppermute | solution.py:339
  134.2 17.4 %collective-permute-start.17 = (f32[2,64,256]{2,1,0:T(8,128)S(1)}, f32[2,64,256]{2,1,0:T(8,128)S(1)}, u32[]{:S(2)}, u32[]{:S(2)}) collective-permute-start(f32[2,64,256]{2,1,0:T(8,128)S(1)} %get-tuple-element.70), channel_id=1, source_target_pairs={{0,8},{1,9},{2,10},{3,11},{4,12},{5,13},{6,14},{7,15},{8,16},{9,17... | collective-permute-start | bytes 393224 | tf_op jit(solution)/shard_map/ppermute | solution.py:339
  136.2 15.5 %collective-permute-start.18 = (f32[2,64,256]{2,1,0:T(8,128)S(1)}, f32[2,64,256]{2,1,0:T(8,128)S(1)}, u32[]{:S(2)}, u32[]{:S(2)}) collective-permute-start(f32[2,64,256]{2,1,0:T(8,128)S(1)} %get-tuple-element.71), channel_id=1, source_target_pairs={{8,0},{9,1},{10,2},{11,3},{12,4},{13,5},{14,6},{15,7},{16,8},{17,9... | collective-permute-start | bytes 393224 | tf_op jit(solution)/shard_map/ppermute | solution.py:339
  (6 other events, 109.4 us)

commit v13 on v12

--- a/solution.py
+++ b/solution.py
@@ -490,11 +490,11 @@
     above, below = row_edges(first, last)
     main, upper = diagonal_windows(r_interp, gx, rows)
     tables = make_tables(psf_z, psf_r, psf_u, z_interp, main, upper, rows, width)
-    first, second = range(3), range(3, 8)
+    first, second = range(5), range(5, 8)
     ship = lambda parts, steps: [lax.ppermute(p, AXES, piece_perm(k)) for p, k in zip(parts, steps)]
     pieces = ship(pieces_of(near, far, first, (above, below, tables[0], up, down)), first)
-    pieces += ship(pieces_of(near, far, second, (tables[0],)), second)
-    blurred = forward(tables, up, estimate, down, both, above, below, pieces[:3])
+    blurred = forward(tables, up, estimate, down, both, above, below, pieces[:1])
+    pieces += ship(pieces_of(near, far, second, (blurred,)), second)
     return backward(tables, *ratio_of(blurred, pieces), estimate, column_edges, row_edges)
 
 

time: 159 us -> 161 us (1.013)
  the two profiles are of different devices: /device:TPU:69 before, /device:TPU:5 now
where the time goes in v13:
time: 161 us; the launch traced here: 160 us
  starting transfers between devices  80.5 us (50%)
  Pallas kernels  45.8 us (28%)
  waiting for transfers between devices  30.4 us (19%)
    ppermute x12, starting transfers between devices, send(): return lax.ppermute(x, AXES, shift_perm(axis, d))  43.9 us
    ppermute x8, starting transfers between devices, shards(): lax.ppermute(p, AXES, piece_perm(k))  35.8 us
    ppermute x8, waiting for transfers between devices, shards(): lax.ppermute(p, AXES, piece_perm(k))  18.7 us
    ppermute x12, waiting for transfers between devices, send(): return lax.ppermute(x, AXES, shift_perm(axis, d))  11.7 us
    pallas_call x1, Pallas kernels, own_update(): pl.pallas_call(own_kernel, grid=(half + depth // 16,), in_specs=[whole(u)...  9.84 us
    pallas_call x4, Pallas kernels, copy_call(): pl.pallas_call(body, in_specs=[HBM] * len(inputs), out_specs=[pl.BlockSpe...  7.47 us
    pallas_call x1, Pallas kernels, blur(): pl.pallas_call(blur_kernel, grid=(rows // 8,), in_specs=[whole(u), whole(...  7.36 us
    pallas_call x1, Pallas kernels, edge_update(): pl.pallas_call(edge_kernel, grid=(2, 2), in_specs=[fixed(u), fixed(e), fi...  6.51 us
  transfers between devices with their start and end apart: 21, of which 8 were waited for; matrix products, arithmetic and copies ran while one was open for 1% of the time, Pallas kernels for 18%

profile of v13, /device:TPU:5, one launch (start us, length us, event | category | flops | bytes accessed | tf_op | source)
XLA Modules:
  0.0 159.8 jit_solution(6792747175099504315)
XLA Ops:
  0.0 3.0 %shard_map.74 = (f32[64,16,256]{2,1,0:T(8,128)}, f32[64,16,256]{2,1,0:T(8,128)}) custom-call(f32[64,64,256]{2,1,0:T(8,128)} %est_ref.5), custom_call_target="tpu_custom_call" | custom-call | bytes 6000000 | tf_op jit(solution)/shard_map/pallas_call | solution.py:364
  7.7 3.2 %collective-permute-start.2 = (f32[64,16,256]{2,1,0:T(8,128)}, f32[64,16,256]{2,1,0:T(8,128)S(1)}, u32[]{:S(2)}, u32[]{:S(2)}) collective-permute-start(f32[64,16,256]{2,1,0:T(8,128)} %get-tuple-element.53), channel_id=1, source_target_pairs={{0,8},{1,9},{2,10},{3,11},{4,12},{5,13},{6,14},{7,15},{8,16},{9,17... | collective-permute-start | bytes 3145736 | tf_op jit(solution)/shard_map/ppermute | solution.py:339
  10.9 4.2 %collective-permute-start.3 = (f32[64,16,256]{2,1,0:T(8,128)}, f32[64,16,256]{2,1,0:T(8,128)}, u32[]{:S(2)}, u32[]{:S(2)}) collective-permute-start(f32[64,16,256]{2,1,0:T(8,128)} %get-tuple-element.49.refs_0_), channel_id=1, source_target_pairs={{8,0},{9,1},{10,2},{11,3},{12,4},{13,5},{14,6},{15,7},{16,8},{17,9... | collective-permute-start | bytes 3145736 | tf_op jit(solution)/shard_map/ppermute | solution.py:339
  15.1 4.0 %collective-permute-start = (f32[8,64,128]{2,1,0:T(8,128)}, f32[8,64,128]{2,1,0:T(8,128)}, u32[]{:S(2)}, u32[]{:S(2)}) collective-permute-start(f32[8,64,128]{2,1,0:T(8,128)} %get-tuple-element.50), channel_id=1, source_target_pairs={{0,1},{1,2},{2,3},{3,4},{4,5},{5,6},{6,7},{8,9},{9,10},{10,11},{11... | collective-permute-start | bytes 786440 | tf_op jit(solution)/shard_map/ppermute | solution.py:339
  22.7 4.5 %collective-permute-done.1.right_ref = f32[8,64,128]{2,1,0:T(8,128)} collective-permute-done((f32[8,64,128]{2,1,0:T(8,128)S(1)}, f32[8,64,128]{2,1,0:T(8,128)}, u32[]{:S(2)}, u32[]{:S(2)}) %collective-permute-start.1) | collective-permute-done | bytes 262176 | tf_op jit(solution)/shard_map/ppermute | solution.py:339
  31.7 5.5 %collective-permute-start.5 = (f32[8,16,256]{2,1,0:T(8,128)}, f32[8,16,256]{2,1,0:T(8,128)S(1)}, u32[]{:S(2)}, u32[]{:S(2)}) collective-permute-start(f32[8,16,256]{2,1,0:T(8,128)} %get-tuple-element.55), channel_id=1, source_target_pairs={{8,0},{9,1},{10,2},{11,3},{12,4},{13,5},{14,6},{15,7},{16,8},{17,9... | collective-permute-start | bytes 393224 | tf_op jit(solution)/shard_map/ppermute | solution.py:339
  38.8 2.9 %shard_map.73 = (bf16[64,288]{1,0:T(8,128)(2,1)S(1)}, bf16[64,192]{1,0:T(8,128)(2,1)S(1)}, bf16[2,16,48]{2,1,0:T(8,128)(2,1)S(1)}, bf16[768,256]{1,0:T(8,128)(2,...) custom-call(f32[32]{0:T(128)S(1)} %copy-done.6, ...), custom_call_target="tpu_custom_call" | custom-call | bytes 9000000 | tf_op jit(solution)/shard_map/pallas_call | solution.py:133
  43.2 6.0 %collective-permute-start.7 = (f32[2,8,64,128]{3,2,1,0:T(8,128)S(1)}, f32[2,8,64,128]{3,2,1,0:T(8,128)S(1)}, u32[]{:S(2)}, u32[]{:S(2)}) collective-permute-start(f32[2,8,64,128]{3,2,1,0:T(8,128)S(1)} %get-tuple-element.58), channel_id=1, source_target_pairs={{0,0},{1,72},{2,32},{3,104},{4,64},{5,8},{6,96},{7,40},{8,16},{9,8... | collective-permute-start | bytes 1572872 | tf_op jit(solution)/shard_map/ppermute | solution.py:494
  49.1 3.2 %collective-permute-start.8 = (f32[2,8,64,128]{3,2,1,0:T(8,128)S(1)}, f32[2,8,64,128]{3,2,1,0:T(8,128)S(1)}, u32[]{:S(2)}, u32[]{:S(2)}) collective-permute-start(f32[2,8,64,128]{3,2,1,0:T(8,128)S(1)} %get-tuple-element.61), channel_id=1, source_target_pairs={{0,16},{1,88},{2,48},{3,120},{4,80},{5,24},{6,112},{7,56},{8,0},{9... | collective-permute-start | bytes 1572872 | tf_op jit(solution)/shard_map/ppermute | solution.py:494
  52.4 3.3 %collective-permute-start.9 = (f32[2,8,64,128]{3,2,1,0:T(8,128)S(1)}, f32[2,8,64,128]{3,2,1,0:T(8,128)S(1)}, u32[]{:S(2)}, u32[]{:S(2)}) collective-permute-start(f32[2,8,64,128]{3,2,1,0:T(8,128)S(1)} %get-tuple-element.62), channel_id=1, source_target_pairs={{0,32},{1,104},{2,64},{3,8},{4,96},{5,40},{6,0},{7,72},{8,48},{9,1... | collective-permute-start | bytes 1572872 | tf_op jit(solution)/shard_map/ppermute | solution.py:494
  55.7 4.1 %collective-permute-start.10 = (f32[2,8,64,128]{3,2,1,0:T(8,128)S(1)}, f32[2,8,64,128]{3,2,1,0:T(8,128)S(1)}, u32[]{:S(2)}, u32[]{:S(2)}) collective-permute-start(f32[2,8,64,128]{3,2,1,0:T(8,128)S(1)} %get-tuple-element.63), channel_id=1, source_target_pairs={{0,48},{1,120},{2,80},{3,24},{4,112},{5,56},{6,16},{7,88},{8,32},{... | collective-permute-start | bytes 1572872 | tf_op jit(solution)/shard_map/ppermute | solution.py:494
  61.7 5.7 %shard_map.79 = (f32[64,64,256]{2,1,0:T(8,128)S(1)}, f32[8,64,256]{2,1,0:T(8,128)S(1)}) custom-call(bf16[64,288]{1,0:T(8,128)(2,1)S(1)} %get-tuple-element.48.refs_2_.table_ref, f32[64,64,256]{2,1,0:T(8,128)S(1)} %copy-done.1, f32[8,64,256]{2,1,0:T(8,128)S(1)} %copy-done.4, f32[64,16,256]{2,1,0:T(8,128)S(1)} %collective-permute-done.2.refs_3_.refs_0_, ...), custom_call_target="tpu_custom_call" | custom-call | bytes 12000000 | tf_op jit(solution)/shard_map/pallas_call | solution.py:193
  67.4 7.4 %shard_map.80.refs_0_.blur_ref = f32[64,64,256]{2,1,0:T(8,128)S(1)} custom-call(bf16[768,256]{1,0:T(8,128)(2,1)S(1)} %get-tuple-element.45.u_ref, bf16[768,256]{1,0:T(8,128)(2,1)S(1)} %get-tuple-element.46.e_ref, bf16[64,192]{1,0:T(8,128)(2,1)S(1)} %get-tuple-element.47.m_ref, f32[8,64,256]{2,1,0:T(8,128)S(1)} %get-tuple-element.59.edge_ref, ...), custom_call_target="tpu_custom_call" | custom-call | bytes 24000000 | tf_op jit(solution)/shard_map/pallas_call | solution.py:220
  76.0 15.4 %collective-permute-start.12 = (f32[2,8,64,128]{3,2,1,0:T(8,128)S(1)}, f32[2,8,64,128]{3,2,1,0:T(8,128)S(1)}, u32[]{:S(2)}, u32[]{:S(2)}) collective-permute-start(f32[2,8,64,128]{3,2,1,0:T(8,128)S(1)} %get-tuple-element.65), channel_id=1, source_target_pairs={{0,80},{1,24},{2,112},{3,56},{4,16},{5,88},{6,48},{7,120},{8,64},{... | collective-permute-start | bytes 1572872 | tf_op jit(solution)/shard_map/ppermute | solution.py:494
  93.5 4.3 %collective-permute-done.11.refs_4_ = f32[2,8,64,128]{3,2,1,0:T(8,128)S(1)} collective-permute-done((f32[2,8,64,128]{3,2,1,0:T(8,128)S(1)}, f32[2,8,64,128]{3,2,1,0:T(8,128)S(1)}, u32[]{:S(2)}, u32[]{:S(2)}) %collective-permute-start.11) | collective-permute-done | bytes 524320 | tf_op jit(solution)/shard_map/ppermute | solution.py:494
  97.8 12.3 %collective-permute-done.12.refs_5_ = f32[2,8,64,128]{3,2,1,0:T(8,128)S(1)} collective-permute-done((f32[2,8,64,128]{3,2,1,0:T(8,128)S(1)}, f32[2,8,64,128]{3,2,1,0:T(8,128)S(1)}, u32[]{:S(2)}, u32[]{:S(2)}) %collective-permute-start.12) | collective-permute-done | bytes 524320 | tf_op jit(solution)/shard_map/ppermute | solution.py:494
  112.1 2.4 %shard_map.82 = (f32[64,64,256]{2,1,0:T(8,128)S(1)}, f32[16,64,256]{2,1,0:T(8,128)S(1)}, f32[16,64,256]{2,1,0:T(8,128)S(1)}, f32[8,64,128]{2,1,0:T(8,128)S(1)}, f32[8,64,128]{2,1,0:T(8,128)S(1)}) custom-call(f32[64,64,256]{2,1,0:T(8,128)S(1)} %shard_map.80.refs_0_.blur_ref, f32[2,8,64,128]{3,2,1,0:T(8,128)S(1)} %collective-permute-done.7.refs_4_.refs_0_, ...), custom_call_target="tpu_custom_call" | custom-call | bytes 21000000 | tf_op jit(solution)/shard_map/pallas_call | solution.py:249
  114.6 9.4 %collective-permute-start.19 = (f32[16,64,256]{2,1,0:T(8,128)S(1)}, f32[16,64,256]{2,1,0:T(8,128)S(1)}, u32[]{:S(2)}, u32[]{:S(2)}) collective-permute-start(f32[16,64,256]{2,1,0:T(8,128)S(1)} %get-tuple-element.72), channel_id=1, source_target_pairs={{0,8},{1,9},{2,10},{3,11},{4,12},{5,13},{6,14},{7,15},{8,16},{9,17... | collective-permute-start | bytes 3145736 | tf_op jit(solution)/shard_map/ppermute | solution.py:339
  127.8 2.4 %collective-permute-start.16 = (f32[8,64,128]{2,1,0:T(8,128)S(1)}, f32[8,64,128]{2,1,0:T(8,128)S(1)}, u32[]{:S(2)}, u32[]{:S(2)}) collective-permute-start(f32[8,64,128]{2,1,0:T(8,128)S(1)} %get-tuple-element.69), channel_id=1, source_target_pairs={{1,0},{2,1},{3,2},{4,3},{5,4},{6,5},{7,6},{9,8},{10,9},{11,10},{12... | collective-permute-start | bytes 786440 | tf_op jit(solution)/shard_map/ppermute | solution.py:339
  131.1 4.7 %collective-permute-done.16.right_ref = f32[8,64,128]{2,1,0:T(8,128)S(1)} collective-permute-done((f32[8,64,128]{2,1,0:T(8,128)S(1)}, f32[8,64,128]{2,1,0:T(8,128)S(1)}, u32[]{:S(2)}, u32[]{:S(2)}) %collective-permute-start.16) | collective-permute-done | bytes 262176 | tf_op jit(solution)/shard_map/ppermute | solution.py:339
  135.9 3.4 %collective-permute-start.17 = (f32[2,64,256]{2,1,0:T(8,128)S(1)}, f32[2,64,256]{2,1,0:T(8,128)S(1)}, u32[]{:S(2)}, u32[]{:S(2)}) collective-permute-start(f32[2,64,256]{2,1,0:T(8,128)S(1)} %get-tuple-element.70), channel_id=1, source_target_pairs={{0,8},{1,9},{2,10},{3,11},{4,12},{5,13},{6,14},{7,15},{8,16},{9,17... | collective-permute-start | bytes 393224 | tf_op jit(solution)/shard_map/ppermute | solution.py:339
  139.2 4.2 %collective-permute-start.18 = (f32[2,64,256]{2,1,0:T(8,128)S(1)}, f32[2,64,256]{2,1,0:T(8,128)S(1)}, u32[]{:S(2)}, u32[]{:S(2)}) collective-permute-start(f32[2,64,256]{2,1,0:T(8,128)S(1)} %get-tuple-element.71), channel_id=1, source_target_pairs={{8,0},{9,1},{10,2},{11,3},{12,4},{13,5},{14,6},{15,7},{16,8},{17,9... | collective-permute-start | bytes 393224 | tf_op jit(solution)/shard_map/ppermute | solution.py:339
  143.5 9.8 %shard_map.84.part_ref = f32[64,64,256]{2,1,0:T(8,128)} custom-call(bf16[768,256]{1,0:T(8,128)(2,1)S(1)} %get-tuple-element.41.u_ref, bf16[768,256]{1,0:T(8,128)(2,1)S(1)} %get-tuple-element.42.e_ref, bf16[64,192]{1,0:T(8,128)(2,1)S(1)} %get-tuple-element.43.m_ref, bf16[64,192]{1,0:T(8,128)(2,1)S(1)} %get-tuple-element.74.a_ref, ...), custom_call_target="tpu_custom_call" | custom-call | bytes 30000000 | tf_op jit(solution)/shard_map/pallas_call | solution.py:288
  153.3 6.5 %shard_map.85 = f32[64,64,256]{2,1,0:T(8,128)} custom-call(bf16[768,256]{1,0:T(8,128)(2,1)S(1)} %get-tuple-element.41.u_ref, bf16[768,256]{1,0:T(8,128)(2,1)S(1)} %get-tuple-element.42.e_ref, bf16[64,192]{1,0:T(8,128)(2,1)S(1)} %get-tuple-element.43.m_ref, bf16[2,16,48]{2,1,0:T(8,128)(2,1)S(1)} %get-tuple-element.44.a_ref, ...), custom_call_target="tpu_custom_call", output_to_operand_aliasing={{}: (9, {})} | custom-call | bytes 18000000 | tf_op jit(solution)/shard_map/pallas_call | solution.py:323
  (53 shorter events, 27.7 us)
Async XLA Ops:
  5.1 33.7 %copy-start.6 = (f32[32]{0:T(128)S(1)}, f32[32]{0:T(128)}, u32[]{:S(2)}) copy-start(f32[32]{0:T(128)} %pz_ref.1) | copy-start | bytes 388
  5.1 33.7 %copy-start.7 = (f32[32]{0:T(128)S(1)}, f32[32]{0:T(128)}, u32[]{:S(2)}) copy-start(f32[32]{0:T(128)} %pr_ref.1) | copy-start | bytes 388
  5.1 33.7 %copy-start.8 = (f32[32]{0:T(128)S(1)}, f32[32]{0:T(128)}, u32[]{:S(2)}) copy-start(f32[32]{0:T(128)} %pu_ref.1) | copy-start | bytes 388
  6.9 34.8 %collective-permute-start.6 = (f32[8,8,64,128]{3,2,1,0:T(8,128)}, f32[8,8,64,128]{3,2,1,0:T(8,128)}, u32[]{:S(2)}, u32[]{:S(2)}) collective-permute-start(f32[8,8,64,128]{3,2,1,0:T(8,128)} %get-tuple-element.57), channel_id=1, source_target_pairs={{0,1},{1,0},{2,3},{3,2},{4,5},{5,4},{6,7},{7,6},{8,9},{9,8},{10,11... | collective-permute-start | bytes 6291464 | tf_op jit(solution)/shard_map/ppermute | solution.py:488
  7.7 34.0 %collective-permute-start.2 = (f32[64,16,256]{2,1,0:T(8,128)}, f32[64,16,256]{2,1,0:T(8,128)S(1)}, u32[]{:S(2)}, u32[]{:S(2)}) collective-permute-start(f32[64,16,256]{2,1,0:T(8,128)} %get-tuple-element.53), channel_id=1, source_target_pairs={{0,8},{1,9},{2,10},{3,11},{4,12},{5,13},{6,14},{7,15},{8,16},{9,17... | collective-permute-start | bytes 3145736 | tf_op jit(solution)/shard_map/ppermute | solution.py:339
  10.9 30.9 %collective-permute-start.3 = (f32[64,16,256]{2,1,0:T(8,128)}, f32[64,16,256]{2,1,0:T(8,128)}, u32[]{:S(2)}, u32[]{:S(2)}) collective-permute-start(f32[64,16,256]{2,1,0:T(8,128)} %get-tuple-element.49.refs_0_), channel_id=1, source_target_pairs={{8,0},{9,1},{10,2},{11,3},{12,4},{13,5},{14,6},{15,7},{16,8},{17,9... | collective-permute-start | bytes 3145736 | tf_op jit(solution)/shard_map/ppermute | solution.py:339
  15.1 7.6 %collective-permute-start = (f32[8,64,128]{2,1,0:T(8,128)}, f32[8,64,128]{2,1,0:T(8,128)}, u32[]{:S(2)}, u32[]{:S(2)}) collective-permute-start(f32[8,64,128]{2,1,0:T(8,128)} %get-tuple-element.50), channel_id=1, source_target_pairs={{0,1},{1,2},{2,3},{3,4},{4,5},{5,6},{6,7},{8,9},{9,10},{10,11},{11... | collective-permute-start | bytes 786440 | tf_op jit(solution)/shard_map/ppermute | solution.py:339
  19.1 8.1 %collective-permute-start.1 = (f32[8,64,128]{2,1,0:T(8,128)S(1)}, f32[8,64,128]{2,1,0:T(8,128)}, u32[]{:S(2)}, u32[]{:S(2)}) collective-permute-start(f32[8,64,128]{2,1,0:T(8,128)S(1)} %get-tuple-element.51.refs_0_), channel_id=1, source_target_pairs={{1,0},{2,1},{3,2},{4,3},{5,4},{6,5},{7,6},{9,8},{10,9},{11,10},{12... | collective-permute-start | bytes 786440 | tf_op jit(solution)/shard_map/ppermute | solution.py:339
  29.8 11.9 %collective-permute-start.4 = (f32[8,16,256]{2,1,0:T(8,128)}, f32[8,16,256]{2,1,0:T(8,128)S(1)}, u32[]{:S(2)}, u32[]{:S(2)}) collective-permute-start(f32[8,16,256]{2,1,0:T(8,128)} %get-tuple-element.54), channel_id=1, source_target_pairs={{0,8},{1,9},{2,10},{3,11},{4,12},{5,13},{6,14},{7,15},{8,16},{9,17... | collective-permute-start | bytes 393224 | tf_op jit(solution)/shard_map/ppermute | solution.py:339
  31.7 10.0 %collective-permute-start.5 = (f32[8,16,256]{2,1,0:T(8,128)}, f32[8,16,256]{2,1,0:T(8,128)S(1)}, u32[]{:S(2)}, u32[]{:S(2)}) collective-permute-start(f32[8,16,256]{2,1,0:T(8,128)} %get-tuple-element.55), channel_id=1, source_target_pairs={{8,0},{9,1},{10,2},{11,3},{12,4},{13,5},{14,6},{15,7},{16,8},{17,9... | collective-permute-start | bytes 393224 | tf_op jit(solution)/shard_map/ppermute | solution.py:339
  43.2 18.5 %collective-permute-start.7 = (f32[2,8,64,128]{3,2,1,0:T(8,128)S(1)}, f32[2,8,64,128]{3,2,1,0:T(8,128)S(1)}, u32[]{:S(2)}, u32[]{:S(2)}) collective-permute-start(f32[2,8,64,128]{3,2,1,0:T(8,128)S(1)} %get-tuple-element.58), channel_id=1, source_target_pairs={{0,0},{1,72},{2,32},{3,104},{4,64},{5,8},{6,96},{7,40},{8,16},{9,8... | collective-permute-start | bytes 1572872 | tf_op jit(solution)/shard_map/ppermute | solution.py:494
  49.1 42.2 %collective-permute-start.8 = (f32[2,8,64,128]{3,2,1,0:T(8,128)S(1)}, f32[2,8,64,128]{3,2,1,0:T(8,128)S(1)}, u32[]{:S(2)}, u32[]{:S(2)}) collective-permute-start(f32[2,8,64,128]{3,2,1,0:T(8,128)S(1)} %get-tuple-element.61), channel_id=1, source_target_pairs={{0,16},{1,88},{2,48},{3,120},{4,80},{5,24},{6,112},{7,56},{8,0},{9... | collective-permute-start | bytes 1572872 | tf_op jit(solution)/shard_map/ppermute | solution.py:494
  52.4 41.0 %collective-permute-start.9 = (f32[2,8,64,128]{3,2,1,0:T(8,128)S(1)}, f32[2,8,64,128]{3,2,1,0:T(8,128)S(1)}, u32[]{:S(2)}, u32[]{:S(2)}) collective-permute-start(f32[2,8,64,128]{3,2,1,0:T(8,128)S(1)} %get-tuple-element.62), channel_id=1, source_target_pairs={{0,32},{1,104},{2,64},{3,8},{4,96},{5,40},{6,0},{7,72},{8,48},{9,1... | collective-permute-start | bytes 1572872 | tf_op jit(solution)/shard_map/ppermute | solution.py:494
  55.7 37.8 %collective-permute-start.10 = (f32[2,8,64,128]{3,2,1,0:T(8,128)S(1)}, f32[2,8,64,128]{3,2,1,0:T(8,128)S(1)}, u32[]{:S(2)}, u32[]{:S(2)}) collective-permute-start(f32[2,8,64,128]{3,2,1,0:T(8,128)S(1)} %get-tuple-element.63), channel_id=1, source_target_pairs={{0,48},{1,120},{2,80},{3,24},{4,112},{5,56},{6,16},{7,88},{8,32},{... | collective-permute-start | bytes 1572872 | tf_op jit(solution)/shard_map/ppermute | solution.py:494
  59.7 38.1 %collective-permute-start.11 = (f32[2,8,64,128]{3,2,1,0:T(8,128)S(1)}, f32[2,8,64,128]{3,2,1,0:T(8,128)S(1)}, u32[]{:S(2)}, u32[]{:S(2)}) collective-permute-start(f32[2,8,64,128]{3,2,1,0:T(8,128)S(1)} %get-tuple-element.64), channel_id=1, source_target_pairs={{0,64},{1,8},{2,96},{3,40},{4,0},{5,72},{6,32},{7,104},{8,80},{9,2... | collective-permute-start | bytes 1572872 | tf_op jit(solution)/shard_map/ppermute | solution.py:494
  76.0 34.1 %collective-permute-start.12 = (f32[2,8,64,128]{3,2,1,0:T(8,128)S(1)}, f32[2,8,64,128]{3,2,1,0:T(8,128)S(1)}, u32[]{:S(2)}, u32[]{:S(2)}) collective-permute-start(f32[2,8,64,128]{3,2,1,0:T(8,128)S(1)} %get-tuple-element.65), channel_id=1, source_target_pairs={{0,80},{1,24},{2,112},{3,56},{4,16},{5,88},{6,48},{7,120},{8,64},{... | collective-permute-start | bytes 1572872 | tf_op jit(solution)/shard_map/ppermute | solution.py:494
  91.4 20.7 %collective-permute-start.13 = (f32[2,8,64,128]{3,2,1,0:T(8,128)S(1)}, f32[2,8,64,128]{3,2,1,0:T(8,128)S(1)}, u32[]{:S(2)}, u32[]{:S(2)}) collective-permute-start(f32[2,8,64,128]{3,2,1,0:T(8,128)S(1)} %get-tuple-element.66), channel_id=1, source_target_pairs={{0,96},{1,40},{2,0},{3,72},{4,32},{5,104},{6,64},{7,8},{8,112},{9,... | collective-permute-start | bytes 1572872 | tf_op jit(solution)/shard_map/ppermute | solution.py:494
  93.3 18.8 %collective-permute-start.14 = (f32[2,8,64,128]{3,2,1,0:T(8,128)S(1)}, f32[2,8,64,128]{3,2,1,0:T(8,128)S(1)}, u32[]{:S(2)}, u32[]{:S(2)}) collective-permute-start(f32[2,8,64,128]{3,2,1,0:T(8,128)S(1)} %get-tuple-element.67), channel_id=1, source_target_pairs={{0,112},{1,56},{2,16},{3,88},{4,48},{5,120},{6,80},{7,24},{8,96},{... | collective-permute-start | bytes 1572872 | tf_op jit(solution)/shard_map/ppermute | solution.py:494
  114.6 38.7 %collective-permute-start.19 = (f32[16,64,256]{2,1,0:T(8,128)S(1)}, f32[16,64,256]{2,1,0:T(8,128)S(1)}, u32[]{:S(2)}, u32[]{:S(2)}) collective-permute-start(f32[16,64,256]{2,1,0:T(8,128)S(1)} %get-tuple-element.72), channel_id=1, source_target_pairs={{0,8},{1,9},{2,10},{3,11},{4,12},{5,13},{6,14},{7,15},{8,16},{9,17... | collective-permute-start | bytes 3145736 | tf_op jit(solution)/shard_map/ppermute | solution.py:339
  124.0 29.4 %collective-permute-start.20 = (f32[16,64,256]{2,1,0:T(8,128)S(1)}, f32[16,64,256]{2,1,0:T(8,128)S(1)}, u32[]{:S(2)}, u32[]{:S(2)}) collective-permute-start(f32[16,64,256]{2,1,0:T(8,128)S(1)} %get-tuple-element.73), channel_id=1, source_target_pairs={{8,0},{9,1},{10,2},{11,3},{12,4},{13,5},{14,6},{15,7},{16,8},{17,9... | collective-permute-start | bytes 3145736 | tf_op jit(solution)/shard_map/ppermute | solution.py:339
  125.9 5.2 %collective-permute-start.15 = (f32[8,64,128]{2,1,0:T(8,128)S(1)}, f32[8,64,128]{2,1,0:T(8,128)S(1)}, u32[]{:S(2)}, u32[]{:S(2)}) collective-permute-start(f32[8,64,128]{2,1,0:T(8,128)S(1)} %get-tuple-element.68), channel_id=1, source_target_pairs={{0,1},{1,2},{2,3},{3,4},{4,5},{5,6},{6,7},{8,9},{9,10},{10,11},{11... | collective-permute-start | bytes 786440 | tf_op jit(solution)/shard_map/ppermute | solution.py:339
  127.8 8.0 %collective-permute-start.16 = (f32[8,64,128]{2,1,0:T(8,128)S(1)}, f32[8,64,128]{2,1,0:T(8,128)S(1)}, u32[]{:S(2)}, u32[]{:S(2)}) collective-permute-start(f32[8,64,128]{2,1,0:T(8,128)S(1)} %get-tuple-element.69), channel_id=1, source_target_pairs={{1,0},{2,1},{3,2},{4,3},{5,4},{6,5},{7,6},{9,8},{10,9},{11,10},{12... | collective-permute-start | bytes 786440 | tf_op jit(solution)/shard_map/ppermute | solution.py:339
  135.9 17.4 %collective-permute-start.17 = (f32[2,64,256]{2,1,0:T(8,128)S(1)}, f32[2,64,256]{2,1,0:T(8,128)S(1)}, u32[]{:S(2)}, u32[]{:S(2)}) collective-permute-start(f32[2,64,256]{2,1,0:T(8,128)S(1)} %get-tuple-element.70), channel_id=1, source_target_pairs={{0,8},{1,9},{2,10},{3,11},{4,12},{5,13},{6,14},{7,15},{8,16},{9,17... | collective-permute-start | bytes 393224 | tf_op jit(solution)/shard_map/ppermute | solution.py:339
  139.2 14.1 %collective-permute-start.18 = (f32[2,64,256]{2,1,0:T(8,128)S(1)}, f32[2,64,256]{2,1,0:T(8,128)S(1)}, u32[]{:S(2)}, u32[]{:S(2)}) collective-permute-start(f32[2,64,256]{2,1,0:T(8,128)S(1)} %get-tuple-element.71), channel_id=1, source_target_pairs={{8,0},{9,1},{10,2},{11,3},{12,4},{13,5},{14,6},{15,7},{16,8},{17,9... | collective-permute-start | bytes 393224 | tf_op jit(solution)/shard_map/ppermute | solution.py:339
  (6 other events, 88.9 us)

commit v14 on v12

--- a/solution.py
+++ b/solution.py
@@ -46,13 +46,14 @@
 def target_of(x, y, z, c, k):
     k1, k2 = k // 2, k % 2
     side, half = y >> 1, y & 1
-    return (x + z + 2 * c + 2 * side + k1) & 3, 2 * (half ^ k2) + c
+    return (x + z + 2 * c + 2 * side + k1) & 3, 2 * (half ^ k2 ^ (z & 1)) + c
 
 
 def source_of(x, y, z, c, k):
     k1, k2 = k // 2, k % 2
     core = y & 1
-    return (x - z - 2 * core - 2 * c - k1) & 3, core, (y >> 1) ^ k2
+    pair = (x - z - 2 * core - 2 * c - k1) & 3
+    return pair, core, (y >> 1) ^ k2 ^ (pair & 1)
 
 
 def piece_perm(k):

time: 159 us -> 165 us (1.038)
  waiting for transfers between devices: 18.1 us -> 28.6 us
  starting transfers between devices: 91 us -> 86.4 us
    ppermute x8, waiting for transfers between devices: 5.92 us -> 16.7 us  [shards(): lax.ppermute(p, AXES, piece_perm(k))]
    ppermute x8, starting transfers between devices: 40.3 us -> 34.2 us  [shards(): lax.ppermute(p, AXES, piece_perm(k))]
  transfers between devices with their start and end apart: 21 -> 21, of which waited for: 6 -> 7; matrix products, arithmetic and copies ran while one was open for 1% -> 1% of each run, Pallas kernels for 18% -> 18%
where the time goes in v14:
time: 165 us; the launch traced here: 164 us
  starting transfers between devices  86.4 us (52%)
  Pallas kernels  46 us (28%)
  waiting for transfers between devices  28.6 us (17%)
    ppermute x12, starting transfers between devices, send(): return lax.ppermute(x, AXES, shift_perm(axis, d))  51.4 us
    ppermute x8, starting transfers between devices, shards(): lax.ppermute(p, AXES, piece_perm(k))  34.2 us
    ppermute x8, waiting for transfers between devices, shards(): lax.ppermute(p, AXES, piece_perm(k))  16.7 us
    ppermute x12, waiting for transfers between devices, send(): return lax.ppermute(x, AXES, shift_perm(axis, d))  11.9 us
    pallas_call x1, Pallas kernels, own_update(): pl.pallas_call(own_kernel, grid=(half + depth // 16,), in_specs=[whole(u)...  9.85 us
    pallas_call x4, Pallas kernels, copy_call(): pl.pallas_call(body, in_specs=[HBM] * len(inputs), out_specs=[pl.BlockSpe...  7.6 us
    pallas_call x1, Pallas kernels, blur(): pl.pallas_call(blur_kernel, grid=(rows // 8,), in_specs=[whole(u), whole(...  7.36 us
    pallas_call x1, Pallas kernels, edge_update(): pl.pallas_call(edge_kernel, grid=(2, 2), in_specs=[fixed(u), fixed(e), fi...  6.51 us
  transfers between devices with their start and end apart: 21, of which 7 were waited for; matrix products, arithmetic and copies ran while one was open for 1% of the time, Pallas kernels for 18%

profile of v14, /device:TPU:69, one launch (start us, length us, event | category | flops | bytes accessed | tf_op | source)
XLA Modules:
  0.0 164.0 jit_solution(14536216432204730051)
XLA Ops:
  0.0 3.0 %shard_map.74 = (f32[64,16,256]{2,1,0:T(8,128)}, f32[64,16,256]{2,1,0:T(8,128)}) custom-call(f32[64,64,256]{2,1,0:T(8,128)} %est_ref.5), custom_call_target="tpu_custom_call" | custom-call | bytes 6000000 | tf_op jit(solution)/shard_map/pallas_call | solution.py:365
  7.7 3.2 %collective-permute-start.2 = (f32[64,16,256]{2,1,0:T(8,128)}, f32[64,16,256]{2,1,0:T(8,128)S(1)}, u32[]{:S(2)}, u32[]{:S(2)}) collective-permute-start(f32[64,16,256]{2,1,0:T(8,128)} %get-tuple-element.53), channel_id=1, source_target_pairs={{0,8},{1,9},{2,10},{3,11},{4,12},{5,13},{6,14},{7,15},{8,16},{9,17... | collective-permute-start | bytes 3145736 | tf_op jit(solution)/shard_map/ppermute | solution.py:340
  10.9 4.2 %collective-permute-start.3 = (f32[64,16,256]{2,1,0:T(8,128)}, f32[64,16,256]{2,1,0:T(8,128)}, u32[]{:S(2)}, u32[]{:S(2)}) collective-permute-start(f32[64,16,256]{2,1,0:T(8,128)} %get-tuple-element.49.refs_0_), channel_id=1, source_target_pairs={{8,0},{9,1},{10,2},{11,3},{12,4},{13,5},{14,6},{15,7},{16,8},{17,9... | collective-permute-start | bytes 3145736 | tf_op jit(solution)/shard_map/ppermute | solution.py:340
  15.1 3.7 %collective-permute-start = (f32[8,64,128]{2,1,0:T(8,128)}, f32[8,64,128]{2,1,0:T(8,128)}, u32[]{:S(2)}, u32[]{:S(2)}) collective-permute-start(f32[8,64,128]{2,1,0:T(8,128)} %get-tuple-element.50), channel_id=1, source_target_pairs={{0,1},{1,2},{2,3},{3,4},{4,5},{5,6},{6,7},{8,9},{9,10},{10,11},{11... | collective-permute-start | bytes 786440 | tf_op jit(solution)/shard_map/ppermute | solution.py:340
  22.4 4.5 %collective-permute-done.1.right_ref = f32[8,64,128]{2,1,0:T(8,128)} collective-permute-done((f32[8,64,128]{2,1,0:T(8,128)S(1)}, f32[8,64,128]{2,1,0:T(8,128)}, u32[]{:S(2)}, u32[]{:S(2)}) %collective-permute-start.1) | collective-permute-done | bytes 262176 | tf_op jit(solution)/shard_map/ppermute | solution.py:340
  31.4 5.5 %collective-permute-start.5 = (f32[8,16,256]{2,1,0:T(8,128)}, f32[8,16,256]{2,1,0:T(8,128)S(1)}, u32[]{:S(2)}, u32[]{:S(2)}) collective-permute-start(f32[8,16,256]{2,1,0:T(8,128)} %get-tuple-element.55), channel_id=1, source_target_pairs={{8,0},{9,1},{10,2},{11,3},{12,4},{13,5},{14,6},{15,7},{16,8},{17,9... | collective-permute-start | bytes 393224 | tf_op jit(solution)/shard_map/ppermute | solution.py:340
  38.5 2.9 %shard_map.73 = (bf16[64,288]{1,0:T(8,128)(2,1)S(1)}, bf16[64,192]{1,0:T(8,128)(2,1)S(1)}, bf16[2,16,48]{2,1,0:T(8,128)(2,1)S(1)}, bf16[768,256]{1,0:T(8,128)(2,...) custom-call(f32[32]{0:T(128)S(1)} %copy-done.6, ...), custom_call_target="tpu_custom_call" | custom-call | bytes 9000000 | tf_op jit(solution)/shard_map/pallas_call | solution.py:134
  42.8 3.2 %collective-permute-start.7 = (f32[2,8,64,128]{3,2,1,0:T(8,128)S(1)}, f32[2,8,64,128]{3,2,1,0:T(8,128)S(1)}, u32[]{:S(2)}, u32[]{:S(2)}) collective-permute-start(f32[2,8,64,128]{3,2,1,0:T(8,128)S(1)} %get-tuple-element.58), channel_id=1, source_target_pairs={{0,0},{1,72},{2,48},{3,120},{4,64},{5,8},{6,112},{7,56},{8,16},{9,... | collective-permute-start | bytes 1572872 | tf_op jit(solution)/shard_map/ppermute | solution.py:495
  46.0 2.9 %collective-permute-start.8 = (f32[2,8,64,128]{3,2,1,0:T(8,128)S(1)}, f32[2,8,64,128]{3,2,1,0:T(8,128)S(1)}, u32[]{:S(2)}, u32[]{:S(2)}) collective-permute-start(f32[2,8,64,128]{3,2,1,0:T(8,128)S(1)} %get-tuple-element.59), channel_id=1, source_target_pairs={{0,16},{1,88},{2,32},{3,104},{4,80},{5,24},{6,96},{7,40},{8,0},{9,... | collective-permute-start | bytes 1572872 | tf_op jit(solution)/shard_map/ppermute | solution.py:495
  48.9 3.0 %collective-permute-start.9 = (f32[2,8,64,128]{3,2,1,0:T(8,128)S(1)}, f32[2,8,64,128]{3,2,1,0:T(8,128)S(1)}, u32[]{:S(2)}, u32[]{:S(2)}) collective-permute-start(f32[2,8,64,128]{3,2,1,0:T(8,128)S(1)} %get-tuple-element.60), channel_id=1, source_target_pairs={{0,32},{1,104},{2,80},{3,24},{4,96},{5,40},{6,16},{7,88},{8,48},{9... | collective-permute-start | bytes 1572872 | tf_op jit(solution)/shard_map/ppermute | solution.py:495
  53.3 8.9 %collective-permute-start.10 = (f32[2,8,64,128]{3,2,1,0:T(8,128)S(1)}, f32[2,8,64,128]{3,2,1,0:T(8,128)S(1)}, u32[]{:S(2)}, u32[]{:S(2)}) collective-permute-start(f32[2,8,64,128]{3,2,1,0:T(8,128)S(1)} %get-tuple-element.63), channel_id=1, source_target_pairs={{0,48},{1,120},{2,64},{3,8},{4,112},{5,56},{6,0},{7,72},{8,32},{9,... | collective-permute-start | bytes 1572872 | tf_op jit(solution)/shard_map/ppermute | solution.py:495
  64.1 3.2 %collective-permute-start.12 = (f32[2,8,64,128]{3,2,1,0:T(8,128)S(1)}, f32[2,8,64,128]{3,2,1,0:T(8,128)S(1)}, u32[]{:S(2)}, u32[]{:S(2)}) collective-permute-start(f32[2,8,64,128]{3,2,1,0:T(8,128)S(1)} %get-tuple-element.65), channel_id=1, source_target_pairs={{0,80},{1,24},{2,96},{3,40},{4,16},{5,88},{6,32},{7,104},{8,64},{9... | collective-permute-start | bytes 1572872 | tf_op jit(solution)/shard_map/ppermute | solution.py:495
  67.3 9.0 %collective-permute-start.13 = (f32[2,8,64,128]{3,2,1,0:T(8,128)S(1)}, f32[2,8,64,128]{3,2,1,0:T(8,128)S(1)}, u32[]{:S(2)}, u32[]{:S(2)}) collective-permute-start(f32[2,8,64,128]{3,2,1,0:T(8,128)S(1)} %get-tuple-element.66), channel_id=1, source_target_pairs={{0,96},{1,40},{2,16},{3,88},{4,32},{5,104},{6,80},{7,24},{8,112},{... | collective-permute-start | bytes 1572872 | tf_op jit(solution)/shard_map/ppermute | solution.py:495
  76.2 8.2 %collective-permute-done.9.refs_6_.refs_2_ = f32[2,8,64,128]{3,2,1,0:T(8,128)S(1)} collective-permute-done((f32[2,8,64,128]{3,2,1,0:T(8,128)S(1)}, f32[2,8,64,128]{3,2,1,0:T(8,128)S(1)}, u32[]{:S(2)}, u32[]{:S(2)}) %collective-permute-start.9) | collective-permute-done | bytes 524320 | tf_op jit(solution)/shard_map/ppermute | solution.py:495
  86.7 5.7 %shard_map.79 = (f32[64,64,256]{2,1,0:T(8,128)S(1)}, f32[8,64,256]{2,1,0:T(8,128)S(1)}) custom-call(bf16[64,288]{1,0:T(8,128)(2,1)S(1)} %get-tuple-element.48.refs_2_.table_ref.refs_0_, f32[64,64,256]{2,1,0:T(8,128)S(1)} %copy-done.1, f32[8,64,256]{2,1,0:T(8,128)S(1)} %copy-done.4, f32[64,16,256]{2,1,0:T(8,128)S(1)} %collective-permute-done.2.refs_3_.refs_0_, ...), custom_call_target="tpu_custom_call" | custom-call | bytes 12000000 | tf_op jit(solution)/shard_map/pallas_call | solution.py:194
  92.5 7.4 %shard_map.80.blur_ref = f32[64,64,256]{2,1,0:T(8,128)S(1)} custom-call(bf16[768,256]{1,0:T(8,128)(2,1)S(1)} %get-tuple-element.45.u_ref, bf16[768,256]{1,0:T(8,128)(2,1)S(1)} %get-tuple-element.46.e_ref, bf16[64,192]{1,0:T(8,128)(2,1)S(1)} %get-tuple-element.47.m_ref, f32[8,64,256]{2,1,0:T(8,128)S(1)} %get-tuple-element.61.edge_ref, ...), custom_call_target="tpu_custom_call" | custom-call | bytes 24000000 | tf_op jit(solution)/shard_map/pallas_call | solution.py:221
  102.4 5.8 %collective-permute-done.14.refs_7_ = f32[2,8,64,128]{3,2,1,0:T(8,128)S(1)} collective-permute-done((f32[2,8,64,128]{3,2,1,0:T(8,128)S(1)}, f32[2,8,64,128]{3,2,1,0:T(8,128)S(1)}, u32[]{:S(2)}, u32[]{:S(2)}) %collective-permute-start.14) | collective-permute-done | bytes 524320 | tf_op jit(solution)/shard_map/ppermute | solution.py:495
  110.7 3.2 %collective-permute-start.19 = (f32[16,64,256]{2,1,0:T(8,128)S(1)}, f32[16,64,256]{2,1,0:T(8,128)S(1)}, u32[]{:S(2)}, u32[]{:S(2)}) collective-permute-start(f32[16,64,256]{2,1,0:T(8,128)S(1)} %get-tuple-element.72), channel_id=1, source_target_pairs={{0,8},{1,9},{2,10},{3,11},{4,12},{5,13},{6,14},{7,15},{8,16},{9,17... | collective-permute-start | bytes 3145736 | tf_op jit(solution)/shard_map/ppermute | solution.py:340
  113.9 4.2 %collective-permute-start.20 = (f32[16,64,256]{2,1,0:T(8,128)S(1)}, f32[16,64,256]{2,1,0:T(8,128)S(1)}, u32[]{:S(2)}, u32[]{:S(2)}) collective-permute-start(f32[16,64,256]{2,1,0:T(8,128)S(1)} %get-tuple-element.73), channel_id=1, source_target_pairs={{8,0},{9,1},{10,2},{11,3},{12,4},{13,5},{14,6},{15,7},{16,8},{17,9... | collective-permute-start | bytes 3145736 | tf_op jit(solution)/shard_map/ppermute | solution.py:340
  118.1 14.1 %collective-permute-start.15 = (f32[8,64,128]{2,1,0:T(8,128)S(1)}, f32[8,64,128]{2,1,0:T(8,128)S(1)}, u32[]{:S(2)}, u32[]{:S(2)}) collective-permute-start(f32[8,64,128]{2,1,0:T(8,128)S(1)} %get-tuple-element.68), channel_id=1, source_target_pairs={{0,1},{1,2},{2,3},{3,4},{4,5},{5,6},{6,7},{8,9},{9,10},{10,11},{11... | collective-permute-start | bytes 786440 | tf_op jit(solution)/shard_map/ppermute | solution.py:340
  135.5 4.4 %collective-permute-done.16.right_ref = f32[8,64,128]{2,1,0:T(8,128)S(1)} collective-permute-done((f32[8,64,128]{2,1,0:T(8,128)S(1)}, f32[8,64,128]{2,1,0:T(8,128)S(1)}, u32[]{:S(2)}, u32[]{:S(2)}) %collective-permute-start.16) | collective-permute-done | bytes 262176 | tf_op jit(solution)/shard_map/ppermute | solution.py:340
  141.9 5.7 %collective-permute-start.18 = (f32[2,64,256]{2,1,0:T(8,128)S(1)}, f32[2,64,256]{2,1,0:T(8,128)S(1)}, u32[]{:S(2)}, u32[]{:S(2)}) collective-permute-start(f32[2,64,256]{2,1,0:T(8,128)S(1)} %get-tuple-element.71), channel_id=1, source_target_pairs={{8,0},{9,1},{10,2},{11,3},{12,4},{13,5},{14,6},{15,7},{16,8},{17,9... | collective-permute-start | bytes 393224 | tf_op jit(solution)/shard_map/ppermute | solution.py:340
  147.6 9.9 %shard_map.84.part_ref = f32[64,64,256]{2,1,0:T(8,128)} custom-call(bf16[768,256]{1,0:T(8,128)(2,1)S(1)} %get-tuple-element.41.u_ref, bf16[768,256]{1,0:T(8,128)(2,1)S(1)} %get-tuple-element.42.e_ref, bf16[64,192]{1,0:T(8,128)(2,1)S(1)} %get-tuple-element.43.m_ref, bf16[64,192]{1,0:T(8,128)(2,1)S(1)} %get-tuple-element.74.a_ref, ...), custom_call_target="tpu_custom_call" | custom-call | bytes 30000000 | tf_op jit(solution)/shard_map/pallas_call | solution.py:289
  157.5 6.5 %shard_map.85 = f32[64,64,256]{2,1,0:T(8,128)} custom-call(bf16[768,256]{1,0:T(8,128)(2,1)S(1)} %get-tuple-element.41.u_ref, bf16[768,256]{1,0:T(8,128)(2,1)S(1)} %get-tuple-element.42.e_ref, bf16[64,192]{1,0:T(8,128)(2,1)S(1)} %get-tuple-element.43.m_ref, bf16[2,16,48]{2,1,0:T(8,128)(2,1)S(1)} %get-tuple-element.44.a_ref, ...), custom_call_target="tpu_custom_call", output_to_operand_aliasing={{}: (9, {})} | custom-call | bytes 18000000 | tf_op jit(solution)/shard_map/pallas_call | solution.py:324
  (53 shorter events, 31.4 us)
Async XLA Ops:
  5.1 33.4 %copy-start.8 = (f32[32]{0:T(128)S(1)}, f32[32]{0:T(128)}, u32[]{:S(2)}) copy-start(f32[32]{0:T(128)} %pu_ref.1) | copy-start | bytes 388
  6.9 34.5 %collective-permute-start.6 = (f32[8,8,64,128]{3,2,1,0:T(8,128)}, f32[8,8,64,128]{3,2,1,0:T(8,128)}, u32[]{:S(2)}, u32[]{:S(2)}) collective-permute-start(f32[8,8,64,128]{3,2,1,0:T(8,128)} %get-tuple-element.57), channel_id=1, source_target_pairs={{0,1},{1,0},{2,3},{3,2},{4,5},{5,4},{6,7},{7,6},{8,9},{9,8},{10,11... | collective-permute-start | bytes 6291464 | tf_op jit(solution)/shard_map/ppermute | solution.py:489
  7.7 33.7 %collective-permute-start.2 = (f32[64,16,256]{2,1,0:T(8,128)}, f32[64,16,256]{2,1,0:T(8,128)S(1)}, u32[]{:S(2)}, u32[]{:S(2)}) collective-permute-start(f32[64,16,256]{2,1,0:T(8,128)} %get-tuple-element.53), channel_id=1, source_target_pairs={{0,8},{1,9},{2,10},{3,11},{4,12},{5,13},{6,14},{7,15},{8,16},{9,17... | collective-permute-start | bytes 3145736 | tf_op jit(solution)/shard_map/ppermute | solution.py:340
  10.9 30.5 %collective-permute-start.3 = (f32[64,16,256]{2,1,0:T(8,128)}, f32[64,16,256]{2,1,0:T(8,128)}, u32[]{:S(2)}, u32[]{:S(2)}) collective-permute-start(f32[64,16,256]{2,1,0:T(8,128)} %get-tuple-element.49.refs_0_), channel_id=1, source_target_pairs={{8,0},{9,1},{10,2},{11,3},{12,4},{13,5},{14,6},{15,7},{16,8},{17,9... | collective-permute-start | bytes 3145736 | tf_op jit(solution)/shard_map/ppermute | solution.py:340
  15.1 7.3 %collective-permute-start = (f32[8,64,128]{2,1,0:T(8,128)}, f32[8,64,128]{2,1,0:T(8,128)}, u32[]{:S(2)}, u32[]{:S(2)}) collective-permute-start(f32[8,64,128]{2,1,0:T(8,128)} %get-tuple-element.50), channel_id=1, source_target_pairs={{0,1},{1,2},{2,3},{3,4},{4,5},{5,6},{6,7},{8,9},{9,10},{10,11},{11... | collective-permute-start | bytes 786440 | tf_op jit(solution)/shard_map/ppermute | solution.py:340
  18.8 8.1 %collective-permute-start.1 = (f32[8,64,128]{2,1,0:T(8,128)S(1)}, f32[8,64,128]{2,1,0:T(8,128)}, u32[]{:S(2)}, u32[]{:S(2)}) collective-permute-start(f32[8,64,128]{2,1,0:T(8,128)S(1)} %get-tuple-element.51.refs_0_), channel_id=1, source_target_pairs={{1,0},{2,1},{3,2},{4,3},{5,4},{6,5},{7,6},{9,8},{10,9},{11,10},{12... | collective-permute-start | bytes 786440 | tf_op jit(solution)/shard_map/ppermute | solution.py:340
  29.5 11.9 %collective-permute-start.4 = (f32[8,16,256]{2,1,0:T(8,128)}, f32[8,16,256]{2,1,0:T(8,128)S(1)}, u32[]{:S(2)}, u32[]{:S(2)}) collective-permute-start(f32[8,16,256]{2,1,0:T(8,128)} %get-tuple-element.54), channel_id=1, source_target_pairs={{0,8},{1,9},{2,10},{3,11},{4,12},{5,13},{6,14},{7,15},{8,16},{9,17... | collective-permute-start | bytes 393224 | tf_op jit(solution)/shard_map/ppermute | solution.py:340
  31.4 10.0 %collective-permute-start.5 = (f32[8,16,256]{2,1,0:T(8,128)}, f32[8,16,256]{2,1,0:T(8,128)S(1)}, u32[]{:S(2)}, u32[]{:S(2)}) collective-permute-start(f32[8,16,256]{2,1,0:T(8,128)} %get-tuple-element.55), channel_id=1, source_target_pairs={{8,0},{9,1},{10,2},{11,3},{12,4},{13,5},{14,6},{15,7},{16,8},{17,9... | collective-permute-start | bytes 393224 | tf_op jit(solution)/shard_map/ppermute | solution.py:340
  41.4 45.2 %copy-start.1 = (f32[64,64,256]{2,1,0:T(8,128)S(1)}, f32[64,64,256]{2,1,0:T(8,128)}, u32[]{:S(2)}) copy-start(f32[64,64,256]{2,1,0:T(8,128)} %est_ref.5) | copy-start | bytes 12582916
  41.5 45.2 %copy-start.4 = (f32[8,64,256]{2,1,0:T(8,128)S(1)}, f32[8,64,256]{2,1,0:T(8,128)}, u32[]{:S(2)}) copy-start(f32[8,64,256]{2,1,0:T(8,128)} %copy-done.3) | copy-start | bytes 1572868
  42.8 21.3 %collective-permute-start.7 = (f32[2,8,64,128]{3,2,1,0:T(8,128)S(1)}, f32[2,8,64,128]{3,2,1,0:T(8,128)S(1)}, u32[]{:S(2)}, u32[]{:S(2)}) collective-permute-start(f32[2,8,64,128]{3,2,1,0:T(8,128)S(1)} %get-tuple-element.58), channel_id=1, source_target_pairs={{0,0},{1,72},{2,48},{3,120},{4,64},{5,8},{6,112},{7,56},{8,16},{9,... | collective-permute-start | bytes 1572872 | tf_op jit(solution)/shard_map/ppermute | solution.py:495
  46.0 21.3 %collective-permute-start.8 = (f32[2,8,64,128]{3,2,1,0:T(8,128)S(1)}, f32[2,8,64,128]{3,2,1,0:T(8,128)S(1)}, u32[]{:S(2)}, u32[]{:S(2)}) collective-permute-start(f32[2,8,64,128]{3,2,1,0:T(8,128)S(1)} %get-tuple-element.59), channel_id=1, source_target_pairs={{0,16},{1,88},{2,32},{3,104},{4,80},{5,24},{6,96},{7,40},{8,0},{9,... | collective-permute-start | bytes 1572872 | tf_op jit(solution)/shard_map/ppermute | solution.py:495
  48.9 35.6 %collective-permute-start.9 = (f32[2,8,64,128]{3,2,1,0:T(8,128)S(1)}, f32[2,8,64,128]{3,2,1,0:T(8,128)S(1)}, u32[]{:S(2)}, u32[]{:S(2)}) collective-permute-start(f32[2,8,64,128]{3,2,1,0:T(8,128)S(1)} %get-tuple-element.60), channel_id=1, source_target_pairs={{0,32},{1,104},{2,80},{3,24},{4,96},{5,40},{6,16},{7,88},{8,48},{9... | collective-permute-start | bytes 1572872 | tf_op jit(solution)/shard_map/ppermute | solution.py:495
  53.3 46.5 %collective-permute-start.10 = (f32[2,8,64,128]{3,2,1,0:T(8,128)S(1)}, f32[2,8,64,128]{3,2,1,0:T(8,128)S(1)}, u32[]{:S(2)}, u32[]{:S(2)}) collective-permute-start(f32[2,8,64,128]{3,2,1,0:T(8,128)S(1)} %get-tuple-element.63), channel_id=1, source_target_pairs={{0,48},{1,120},{2,64},{3,8},{4,112},{5,56},{6,0},{7,72},{8,32},{9,... | collective-permute-start | bytes 1572872 | tf_op jit(solution)/shard_map/ppermute | solution.py:495
  62.2 37.7 %collective-permute-start.11 = (f32[2,8,64,128]{3,2,1,0:T(8,128)S(1)}, f32[2,8,64,128]{3,2,1,0:T(8,128)S(1)}, u32[]{:S(2)}, u32[]{:S(2)}) collective-permute-start(f32[2,8,64,128]{3,2,1,0:T(8,128)S(1)} %get-tuple-element.64), channel_id=1, source_target_pairs={{0,64},{1,8},{2,112},{3,56},{4,0},{5,72},{6,48},{7,120},{8,80},{9,... | collective-permute-start | bytes 1572872 | tf_op jit(solution)/shard_map/ppermute | solution.py:495
  64.1 38.3 %collective-permute-start.12 = (f32[2,8,64,128]{3,2,1,0:T(8,128)S(1)}, f32[2,8,64,128]{3,2,1,0:T(8,128)S(1)}, u32[]{:S(2)}, u32[]{:S(2)}) collective-permute-start(f32[2,8,64,128]{3,2,1,0:T(8,128)S(1)} %get-tuple-element.65), channel_id=1, source_target_pairs={{0,80},{1,24},{2,96},{3,40},{4,16},{5,88},{6,32},{7,104},{8,64},{9... | collective-permute-start | bytes 1572872 | tf_op jit(solution)/shard_map/ppermute | solution.py:495
  67.3 35.1 %collective-permute-start.13 = (f32[2,8,64,128]{3,2,1,0:T(8,128)S(1)}, f32[2,8,64,128]{3,2,1,0:T(8,128)S(1)}, u32[]{:S(2)}, u32[]{:S(2)}) collective-permute-start(f32[2,8,64,128]{3,2,1,0:T(8,128)S(1)} %get-tuple-element.66), channel_id=1, source_target_pairs={{0,96},{1,40},{2,16},{3,88},{4,32},{5,104},{6,80},{7,24},{8,112},{... | collective-permute-start | bytes 1572872 | tf_op jit(solution)/shard_map/ppermute | solution.py:495
  84.5 23.8 %collective-permute-start.14 = (f32[2,8,64,128]{3,2,1,0:T(8,128)S(1)}, f32[2,8,64,128]{3,2,1,0:T(8,128)S(1)}, u32[]{:S(2)}, u32[]{:S(2)}) collective-permute-start(f32[2,8,64,128]{3,2,1,0:T(8,128)S(1)} %get-tuple-element.67), channel_id=1, source_target_pairs={{0,112},{1,56},{2,0},{3,72},{4,48},{5,120},{6,64},{7,8},{8,96},{9,... | collective-permute-start | bytes 1572872 | tf_op jit(solution)/shard_map/ppermute | solution.py:495
  110.7 46.8 %collective-permute-start.19 = (f32[16,64,256]{2,1,0:T(8,128)S(1)}, f32[16,64,256]{2,1,0:T(8,128)S(1)}, u32[]{:S(2)}, u32[]{:S(2)}) collective-permute-start(f32[16,64,256]{2,1,0:T(8,128)S(1)} %get-tuple-element.72), channel_id=1, source_target_pairs={{0,8},{1,9},{2,10},{3,11},{4,12},{5,13},{6,14},{7,15},{8,16},{9,17... | collective-permute-start | bytes 3145736 | tf_op jit(solution)/shard_map/ppermute | solution.py:340
  113.9 43.5 %collective-permute-start.20 = (f32[16,64,256]{2,1,0:T(8,128)S(1)}, f32[16,64,256]{2,1,0:T(8,128)S(1)}, u32[]{:S(2)}, u32[]{:S(2)}) collective-permute-start(f32[16,64,256]{2,1,0:T(8,128)S(1)} %get-tuple-element.73), channel_id=1, source_target_pairs={{8,0},{9,1},{10,2},{11,3},{12,4},{13,5},{14,6},{15,7},{16,8},{17,9... | collective-permute-start | bytes 3145736 | tf_op jit(solution)/shard_map/ppermute | solution.py:340
  118.1 17.4 %collective-permute-start.15 = (f32[8,64,128]{2,1,0:T(8,128)S(1)}, f32[8,64,128]{2,1,0:T(8,128)S(1)}, u32[]{:S(2)}, u32[]{:S(2)}) collective-permute-start(f32[8,64,128]{2,1,0:T(8,128)S(1)} %get-tuple-element.68), channel_id=1, source_target_pairs={{0,1},{1,2},{2,3},{3,4},{4,5},{5,6},{6,7},{8,9},{9,10},{10,11},{11... | collective-permute-start | bytes 786440 | tf_op jit(solution)/shard_map/ppermute | solution.py:340
  132.2 7.7 %collective-permute-start.16 = (f32[8,64,128]{2,1,0:T(8,128)S(1)}, f32[8,64,128]{2,1,0:T(8,128)S(1)}, u32[]{:S(2)}, u32[]{:S(2)}) collective-permute-start(f32[8,64,128]{2,1,0:T(8,128)S(1)} %get-tuple-element.69), channel_id=1, source_target_pairs={{1,0},{2,1},{3,2},{4,3},{5,4},{6,5},{7,6},{9,8},{10,9},{11,10},{12... | collective-permute-start | bytes 786440 | tf_op jit(solution)/shard_map/ppermute | solution.py:340
  140.0 17.4 %collective-permute-start.17 = (f32[2,64,256]{2,1,0:T(8,128)S(1)}, f32[2,64,256]{2,1,0:T(8,128)S(1)}, u32[]{:S(2)}, u32[]{:S(2)}) collective-permute-start(f32[2,64,256]{2,1,0:T(8,128)S(1)} %get-tuple-element.70), channel_id=1, source_target_pairs={{0,8},{1,9},{2,10},{3,11},{4,12},{5,13},{6,14},{7,15},{8,16},{9,17... | collective-permute-start | bytes 393224 | tf_op jit(solution)/shard_map/ppermute | solution.py:340
  141.9 15.5 %collective-permute-start.18 = (f32[2,64,256]{2,1,0:T(8,128)S(1)}, f32[2,64,256]{2,1,0:T(8,128)S(1)}, u32[]{:S(2)}, u32[]{:S(2)}) collective-permute-start(f32[2,64,256]{2,1,0:T(8,128)S(1)} %get-tuple-element.71), channel_id=1, source_target_pairs={{8,0},{9,1},{10,2},{11,3},{12,4},{13,5},{14,6},{15,7},{16,8},{17,9... | collective-permute-start | bytes 393224 | tf_op jit(solution)/shard_map/ppermute | solution.py:340
  (6 other events, 109.4 us)

commit v15 on v11

--- a/solution.py
+++ b/solution.py
@@ -267,12 +267,14 @@
 
 def own_kernel(u_ref, e_ref, m_ref, a_ref, both_ref, x_ref, est_ref, out_ref, kept):
     step = pl.program_id(0)
-    half = kept.shape[1] // 8
+    half = kept.shape[1] // 16
 
     @pl.when(step < half)
     def _():
-        rows = pl.ds(pl.multiple_of(step * 8, 8), 8)
-        kept[:, rows, :] = spread_tile(x_ref[...], both_ref[0], u_ref[...], e_ref[...], m_ref[...])
+        for t in range(2):
+            rows = pl.ds(pl.multiple_of(step * 16 + t * 8, 8), 8)
+            x = x_ref[8 * t : 8 * t + 8]
+            kept[:, rows, :] = spread_tile(x, both_ref[t], u_ref[...], e_ref[...], m_ref[...])
 
     @pl.when(step >= half)
     def _():
@@ -284,14 +286,14 @@
 
 def own_update(u, e, m, a, both, ratio, est):
     rows, depth, cols = ratio.shape
-    half = rows // 8
+    half = rows // 16
     early = lambda i: (jnp.minimum(i, half - 1), 0, 0)
     late = lambda i: (jnp.maximum(i - half, 0), 0, 0)
     return pl.pallas_call(
         own_kernel,
         grid=(half + depth // 16,),
         in_specs=[whole(u), whole(e), whole(m), whole(a)]
-        + [pl.BlockSpec((1, depth, cols), early), pl.BlockSpec((8, depth, cols), early)]
+        + [pl.BlockSpec((2, depth, cols), early), pl.BlockSpec((16, depth, cols), early)]
         + [pl.BlockSpec((16, rows, cols), late)],
         out_specs=pl.BlockSpec((16, rows, cols), late),
         out_shape=jax.ShapeDtypeStruct(est.shape, F32),
@@ -301,33 +303,30 @@
 
 
 def edge_kernel(u_ref, e_ref, m_ref, a_ref, above_ref, below_ref, up_ref, down_ref, est_ref, part_ref, out_ref, kept):
-    side, step = pl.program_id(0), pl.program_id(1)
-    rows = pl.ds(pl.multiple_of(step * 8, 8), 8)
+    side = pl.program_id(0)
     for s, x_ref, c_ref in ((0, up_ref, above_ref), (1, down_ref, below_ref)):
 
         @pl.when(side == s)
         def _(x_ref=x_ref, c_ref=c_ref):
-            kept[:, rows, :] = spread_tile(x_ref[...], c_ref[0], u_ref[...], e_ref[...], m_ref[...])
-
-    @pl.when(step == 1)
-    def _():
-        table = a_ref[0]
-        for z in range(est_ref.shape[0]):
-            out_ref[z] = part_ref[z] + est_ref[z] * along(table, kept[z])
+            for t in range(2):
+                x = x_ref[8 * t : 8 * t + 8]
+                tile = spread_tile(x, c_ref[t], u_ref[...], e_ref[...], m_ref[...])
+                kept[:, 8 * t : 8 * t + 8, :] = tile
+
+    table = a_ref[0]
+    for z in range(est_ref.shape[0]):
+        out_ref[z] = part_ref[z] + est_ref[z] * along(table, kept[z])
 
 
 def edge_update(u, e, m, a, above, below, up, down, est, part):
     depth, rows, cols = est.shape
     far = rows // 16 - 1
-    tile = pl.BlockSpec((depth, 16, cols), lambda s, i: (0, s * far, 0))
-    fixed = lambda t: pl.BlockSpec(t.shape, lambda s, i: (0,) * t.ndim)
-    order = (lambda s, i: (jnp.maximum(i, s), 0, 0), lambda s, i: (i * s, 0, 0))
+    tile = pl.BlockSpec((depth, 16, cols), lambda s: (0, s * far, 0))
     return pl.pallas_call(
         edge_kernel,
-        grid=(2, 2),
-        in_specs=[fixed(u), fixed(e), fixed(m), pl.BlockSpec((1, 16, 48), lambda s, i: (s, 0, 0))]
-        + [pl.BlockSpec((1, depth, cols), at) for at in order]
-        + [pl.BlockSpec((8, depth, cols), at) for at in order]
+        grid=(2,),
+        in_specs=[whole(u), whole(e), whole(m), pl.BlockSpec((1, 16, 48), lambda s: (s, 0, 0))]
+        + [whole(t) for t in (above, below, up, down)]
         + [tile, tile],
         out_specs=tile,
         out_shape=jax.ShapeDtypeStruct(est.shape, F32),

time: 158 us -> 158 us (level)
  transfers between devices with their start and end apart: 21 -> 21, of which waited for: 6 -> 6; matrix products, arithmetic and copies ran while one was open for 3% -> 3% of each run, Pallas kernels for 18% -> 17%
where the time goes in v15:
time: 158 us; the launch traced here: 156 us
  starting transfers between devices  85.7 us (54%)
  Pallas kernels  42 us (27%)
  waiting for transfers between devices  18.9 us (12%)
  local copies, waits for them, and re-layouts  6.85 us (4%)
  other arithmetic  2.06 us (1%)
    ppermute x12, starting transfers between devices, send(): return lax.ppermute(x, AXES, shift_perm(axis, d))  44 us
    ppermute x8, starting transfers between devices, shards(): lax.ppermute(p, AXES, piece_perm(k))  41 us
    ppermute x12, waiting for transfers between devices, send(): return lax.ppermute(x, AXES, shift_perm(axis, d))  12.4 us
    pallas_call x1, Pallas kernels, own_update(): pl.pallas_call(own_kernel, grid=(half + depth // 16,), in_specs=[whole(u)...  9.44 us
    pallas_call x1, Pallas kernels, blur(): pl.pallas_call(blur_kernel, grid=(rows // 8,), in_specs=[whole(u), whole(...  7.36 us
    ppermute x8, waiting for transfers between devices, shards(): lax.ppermute(p, AXES, piece_perm(k))  6.54 us
    pallas_call x4, Pallas kernels, copy_call(): pl.pallas_call(body, in_specs=[HBM] * len(inputs), out_specs=[pl.BlockSpe...  6.11 us
    pallas_call x1, Pallas kernels, edge_update(): pl.pallas_call(edge_kernel, grid=(2,), in_specs=[whole(u), whole(e), whol...  6.06 us
  transfers between devices with their start and end apart: 21, of which 6 were waited for; matrix products, arithmetic and copies ran while one was open for 3% of the time, Pallas kernels for 17%

profile of v15, /device:TPU:69, one launch (start us, length us, event | category | flops | bytes accessed | tf_op | source)
XLA Modules:
  0.0 156.0 jit_solution(12079487585604551031)
XLA Ops:
  9.6 3.2 %collective-permute-start.2 = (f32[64,16,256]{2,1,0:T(8,128)}, f32[64,16,256]{2,1,0:T(8,128)S(1)}, u32[]{:S(2)}, u32[]{:S(2)}) collective-permute-start(f32[64,16,256]{2,1,0:T(8,128)} %get-tuple-element.46), channel_id=1, source_target_pairs={{0,8},{1,9},{2,10},{3,11},{4,12},{5,13},{6,14},{7,15},{8,16},{9,17... | collective-permute-start | bytes 3145736 | tf_op jit(solution)/shard_map/ppermute | solution.py:340
  12.8 4.2 %collective-permute-start.3 = (f32[64,16,256]{2,1,0:T(8,128)}, f32[64,16,256]{2,1,0:T(8,128)}, u32[]{:S(2)}, u32[]{:S(2)}) collective-permute-start(f32[64,16,256]{2,1,0:T(8,128)} %get-tuple-element.43.refs_0_), channel_id=1, source_target_pairs={{8,0},{9,1},{10,2},{11,3},{12,4},{13,5},{14,6},{15,7},{16,8},{17,9... | collective-permute-start | bytes 3145736 | tf_op jit(solution)/shard_map/ppermute | solution.py:340
  17.0 3.7 %collective-permute-start = (f32[8,64,128]{2,1,0:T(8,128)}, f32[8,64,128]{2,1,0:T(8,128)S(1)}, u32[]{:S(2)}, u32[]{:S(2)}) collective-permute-start(f32[8,64,128]{2,1,0:T(8,128)} %get-tuple-element.44), channel_id=1, source_target_pairs={{0,1},{1,2},{2,3},{3,4},{4,5},{5,6},{6,7},{8,9},{9,10},{10,11},{11... | collective-permute-start | bytes 786440 | tf_op jit(solution)/shard_map/ppermute | solution.py:340
  24.3 4.7 %collective-permute-done.1.right_ref = f32[8,64,128]{2,1,0:T(8,128)} collective-permute-done((f32[8,64,128]{2,1,0:T(8,128)}, f32[8,64,128]{2,1,0:T(8,128)}, u32[]{:S(2)}, u32[]{:S(2)}) %collective-permute-start.1) | collective-permute-done | bytes 262176 | tf_op jit(solution)/shard_map/ppermute | solution.py:340
  33.2 2.8 %collective-permute-start.4 = (f32[8,16,256]{2,1,0:T(8,128)}, f32[8,16,256]{2,1,0:T(8,128)}, u32[]{:S(2)}, u32[]{:S(2)}) collective-permute-start(f32[8,16,256]{2,1,0:T(8,128)} %get-tuple-element.70), channel_id=1, source_target_pairs={{0,8},{1,9},{2,10},{3,11},{4,12},{5,13},{6,14},{7,15},{8,16},{9,17... | collective-permute-start | bytes 393224 | tf_op jit(solution)/shard_map/ppermute | solution.py:340
  39.5 2.9 %shard_map.73 = (bf16[64,288]{1,0:T(8,128)(2,1)S(1)}, bf16[64,192]{1,0:T(8,128)(2,1)S(1)}, bf16[2,16,48]{2,1,0:T(8,128)(2,1)S(1)}, bf16[768,256]{1,0:T(8,128)(2,...) custom-call(f32[32]{0:T(128)S(1)} %copy-done.5, ...), custom_call_target="tpu_custom_call" | custom-call | bytes 9000000 | tf_op jit(solution)/shard_map/pallas_call | solution.py:133
  43.9 4.0 %collective-permute-start.7 = (f32[2,8,64,128]{3,2,1,0:T(8,128)S(1)}, f32[2,8,64,128]{3,2,1,0:T(8,128)S(1)}, u32[]{:S(2)}, u32[]{:S(2)}) collective-permute-start(f32[2,8,64,128]{3,2,1,0:T(8,128)S(1)} %get-tuple-element.49), channel_id=1, source_target_pairs={{0,0},{1,72},{2,32},{3,104},{4,64},{5,8},{6,96},{7,40},{8,16},{9,8... | collective-permute-start | bytes 1572872 | tf_op jit(solution)/shard_map/ppermute | solution.py:474
  47.8 2.9 %collective-permute-start.8 = (f32[2,8,64,128]{3,2,1,0:T(8,128)S(1)}, f32[2,8,64,128]{3,2,1,0:T(8,128)S(1)}, u32[]{:S(2)}, u32[]{:S(2)}) collective-permute-start(f32[2,8,64,128]{3,2,1,0:T(8,128)S(1)} %get-tuple-element.50), channel_id=1, source_target_pairs={{0,16},{1,88},{2,48},{3,120},{4,80},{5,24},{6,112},{7,56},{8,0},{9... | collective-permute-start | bytes 1572872 | tf_op jit(solution)/shard_map/ppermute | solution.py:474
  50.8 2.9 %collective-permute-start.9 = (f32[2,8,64,128]{3,2,1,0:T(8,128)S(1)}, f32[2,8,64,128]{3,2,1,0:T(8,128)S(1)}, u32[]{:S(2)}, u32[]{:S(2)}) collective-permute-start(f32[2,8,64,128]{3,2,1,0:T(8,128)S(1)} %get-tuple-element.51), channel_id=1, source_target_pairs={{0,32},{1,104},{2,64},{3,8},{4,96},{5,40},{6,0},{7,72},{8,48},{9,1... | collective-permute-start | bytes 1572872 | tf_op jit(solution)/shard_map/ppermute | solution.py:474
  55.1 2.7 %collective-permute-start.10 = (f32[2,8,64,128]{3,2,1,0:T(8,128)S(1)}, f32[2,8,64,128]{3,2,1,0:T(8,128)S(1)}, u32[]{:S(2)}, u32[]{:S(2)}) collective-permute-start(f32[2,8,64,128]{3,2,1,0:T(8,128)S(1)} %get-tuple-element.54), channel_id=1, source_target_pairs={{0,48},{1,120},{2,80},{3,24},{4,112},{5,56},{6,16},{7,88},{8,32},{... | collective-permute-start | bytes 1572872 | tf_op jit(solution)/shard_map/ppermute | solution.py:474
  57.7 8.9 %collective-permute-start.11 = (f32[2,8,64,128]{3,2,1,0:T(8,128)S(1)}, f32[2,8,64,128]{3,2,1,0:T(8,128)S(1)}, u32[]{:S(2)}, u32[]{:S(2)}) collective-permute-start(f32[2,8,64,128]{3,2,1,0:T(8,128)S(1)} %get-tuple-element.55), channel_id=1, source_target_pairs={{0,64},{1,8},{2,96},{3,40},{4,0},{5,72},{6,32},{7,104},{8,80},{9,2... | collective-permute-start | bytes 1572872 | tf_op jit(solution)/shard_map/ppermute | solution.py:474
  66.7 8.0 %collective-permute-start.12 = (f32[2,8,64,128]{3,2,1,0:T(8,128)S(1)}, f32[2,8,64,128]{3,2,1,0:T(8,128)S(1)}, u32[]{:S(2)}, u32[]{:S(2)}) collective-permute-start(f32[2,8,64,128]{3,2,1,0:T(8,128)S(1)} %get-tuple-element.56), channel_id=1, source_target_pairs={{0,80},{1,24},{2,112},{3,56},{4,16},{5,88},{6,48},{7,120},{8,64},{... | collective-permute-start | bytes 1572872 | tf_op jit(solution)/shard_map/ppermute | solution.py:474
  74.7 11.5 %collective-permute-start.13 = (f32[2,8,64,128]{3,2,1,0:T(8,128)S(1)}, f32[2,8,64,128]{3,2,1,0:T(8,128)S(1)}, u32[]{:S(2)}, u32[]{:S(2)}) collective-permute-start(f32[2,8,64,128]{3,2,1,0:T(8,128)S(1)} %get-tuple-element.57), channel_id=1, source_target_pairs={{0,96},{1,40},{2,0},{3,72},{4,32},{5,104},{6,64},{7,8},{8,112},{9,... | collective-permute-start | bytes 1572872 | tf_op jit(solution)/shard_map/ppermute | solution.py:474
  86.3 5.9 %shard_map.78 = (f32[64,64,256]{2,1,0:T(8,128)S(1)}, f32[8,64,256]{2,1,0:T(8,128)S(1)}) custom-call(bf16[64,288]{1,0:T(8,128)(2,1)S(1)} %get-tuple-element.42.refs_2_.table_ref.refs_0_, f32[64,64,256]{2,1,0:T(8,128)S(1)} %copy-done.2, f32[8,64,128]{2,1,0:T(8,128)S(1)} %collective-permute-done.left_ref, f32[8,64,128]{2,1,0:T(8,128)} %collective-permute-done.1.right_ref, ...), custom_call_target="tpu_custom_call" | custom-call | bytes 12000000 | tf_op jit(solution)/shard_map/pallas_call | solution.py:195
  92.2 7.4 %shard_map.79.blur_ref = f32[64,64,256]{2,1,0:T(8,128)S(1)} custom-call(bf16[768,256]{1,0:T(8,128)(2,1)S(1)} %get-tuple-element.39.u_ref, bf16[768,256]{1,0:T(8,128)(2,1)S(1)} %get-tuple-element.40.e_ref, bf16[64,192]{1,0:T(8,128)(2,1)S(1)} %get-tuple-element.41.m_ref, f32[8,64,256]{2,1,0:T(8,128)S(1)} %get-tuple-element.52.edge_ref, ...), custom_call_target="tpu_custom_call" | custom-call | bytes 24000000 | tf_op jit(solution)/shard_map/pallas_call | solution.py:222
  99.6 3.8 %collective-permute-done.12.refs_5_ = f32[2,8,64,128]{3,2,1,0:T(8,128)S(1)} collective-permute-done((f32[2,8,64,128]{3,2,1,0:T(8,128)S(1)}, f32[2,8,64,128]{3,2,1,0:T(8,128)S(1)}, u32[]{:S(2)}, u32[]{:S(2)}) %collective-permute-start.12) | collective-permute-done | bytes 524320 | tf_op jit(solution)/shard_map/ppermute | solution.py:474
  103.3 2.8 %collective-permute-done.14.refs_7_ = f32[2,8,64,128]{3,2,1,0:T(8,128)S(1)} collective-permute-done((f32[2,8,64,128]{3,2,1,0:T(8,128)S(1)}, f32[2,8,64,128]{3,2,1,0:T(8,128)S(1)}, u32[]{:S(2)}, u32[]{:S(2)}) %collective-permute-start.14) | collective-permute-done | bytes 524320 | tf_op jit(solution)/shard_map/ppermute | solution.py:474
  108.6 3.8 %collective-permute-start.19 = (f32[16,64,256]{2,1,0:T(8,128)S(1)}, f32[16,64,256]{2,1,0:T(8,128)S(1)}, u32[]{:S(2)}, u32[]{:S(2)}) collective-permute-start(f32[16,64,256]{2,1,0:T(8,128)S(1)} %get-tuple-element.61), channel_id=1, source_target_pairs={{0,8},{1,9},{2,10},{3,11},{4,12},{5,13},{6,14},{7,15},{8,16},{9,17... | collective-permute-start | bytes 3145736 | tf_op jit(solution)/shard_map/ppermute | solution.py:340
  112.4 3.6 %collective-permute-start.20 = (f32[16,64,256]{2,1,0:T(8,128)S(1)}, f32[16,64,256]{2,1,0:T(8,128)S(1)}, u32[]{:S(2)}, u32[]{:S(2)}) collective-permute-start(f32[16,64,256]{2,1,0:T(8,128)S(1)} %get-tuple-element.62), channel_id=1, source_target_pairs={{8,0},{9,1},{10,2},{11,3},{12,4},{13,5},{14,6},{15,7},{16,8},{17,9... | collective-permute-start | bytes 3145736 | tf_op jit(solution)/shard_map/ppermute | solution.py:340
  116.0 11.0 %collective-permute-start.15 = (f32[8,64,128]{2,1,0:T(8,128)S(1)}, f32[8,64,128]{2,1,0:T(8,128)S(1)}, u32[]{:S(2)}, u32[]{:S(2)}) collective-permute-start(f32[8,64,128]{2,1,0:T(8,128)S(1)} %get-tuple-element.59), channel_id=1, source_target_pairs={{0,1},{1,2},{2,3},{3,4},{4,5},{5,6},{6,7},{8,9},{9,10},{10,11},{11... | collective-permute-start | bytes 786440 | tf_op jit(solution)/shard_map/ppermute | solution.py:340
  130.3 4.7 %collective-permute-done.16 = f32[8,64,128]{2,1,0:T(8,128)S(1)} collective-permute-done((f32[8,64,128]{2,1,0:T(8,128)S(1)}, f32[8,64,128]{2,1,0:T(8,128)S(1)}, u32[]{:S(2)}, u32[]{:S(2)}) %collective-permute-start.16) | collective-permute-done | bytes 262176 | tf_op jit(solution)/shard_map/ppermute | solution.py:340
  136.9 3.5 %collective-permute-start.17 = (f32[2,64,256]{2,1,0:T(8,128)S(1)}, f32[2,64,256]{2,1,0:T(8,128)S(1)}, u32[]{:S(2)}, u32[]{:S(2)}) collective-permute-start(f32[2,64,256]{2,1,0:T(8,128)S(1)} %get-tuple-element.68), channel_id=1, source_target_pairs={{0,8},{1,9},{2,10},{3,11},{4,12},{5,13},{6,14},{7,15},{8,16},{9,17... | collective-permute-start | bytes 393224 | tf_op jit(solution)/shard_map/ppermute | solution.py:340
  140.5 9.4 %shard_map.82.part_ref = f32[64,64,256]{2,1,0:T(8,128)} custom-call(bf16[768,256]{1,0:T(8,128)(2,1)S(1)} %get-tuple-element.35.u_ref, bf16[768,256]{1,0:T(8,128)(2,1)S(1)} %get-tuple-element.36.e_ref, bf16[64,192]{1,0:T(8,128)(2,1)S(1)} %get-tuple-element.37.m_ref, bf16[64,192]{1,0:T(8,128)(2,1)S(1)} %get-tuple-element.63.a_ref, ...), custom_call_target="tpu_custom_call" | custom-call | bytes 30000000 | tf_op jit(solution)/shard_map/pallas_call | solution.py:292
  149.9 6.1 %shard_map.83 = f32[64,64,256]{2,1,0:T(8,128)} custom-call(bf16[768,256]{1,0:T(8,128)(2,1)S(1)} %get-tuple-element.35.u_ref, bf16[768,256]{1,0:T(8,128)(2,1)S(1)} %get-tuple-element.36.e_ref, bf16[64,192]{1,0:T(8,128)(2,1)S(1)} %get-tuple-element.37.m_ref, bf16[2,16,48]{2,1,0:T(8,128)(2,1)S(1)} %get-tuple-element.38.a_ref, ...), custom_call_target="tpu_custom_call", output_to_operand_aliasing={{}: (9, {})} | custom-call | bytes 18000000 | tf_op jit(solution)/shard_map/pallas_call | solution.py:325
  (55 shorter events, 31.5 us)
Async XLA Ops:
  6.9 31.8 %copy-start.6 = (f32[32]{0:T(128)S(1)}, f32[32]{0:T(128)}, u32[]{:S(2)}) copy-start(f32[32]{0:T(128)} %pr_ref.1) | copy-start | bytes 388
  7.0 31.8 %copy-start.7 = (f32[32]{0:T(128)S(1)}, f32[32]{0:T(128)}, u32[]{:S(2)}) copy-start(f32[32]{0:T(128)} %pu_ref.1) | copy-start | bytes 388
  8.8 33.7 %collective-permute-start.6 = (f32[8,8,64,128]{3,2,1,0:T(8,128)}, f32[8,8,64,128]{3,2,1,0:T(8,128)}, u32[]{:S(2)}, u32[]{:S(2)}) collective-permute-start(f32[8,8,64,128]{3,2,1,0:T(8,128)} %get-tuple-element.48), channel_id=1, source_target_pairs={{0,1},{1,0},{2,3},{3,2},{4,5},{5,4},{6,7},{7,6},{8,9},{9,8},{10,11... | collective-permute-start | bytes 6291464 | tf_op jit(solution)/shard_map/ppermute | solution.py:468
  9.6 32.9 %collective-permute-start.2 = (f32[64,16,256]{2,1,0:T(8,128)}, f32[64,16,256]{2,1,0:T(8,128)S(1)}, u32[]{:S(2)}, u32[]{:S(2)}) collective-permute-start(f32[64,16,256]{2,1,0:T(8,128)} %get-tuple-element.46), channel_id=1, source_target_pairs={{0,8},{1,9},{2,10},{3,11},{4,12},{5,13},{6,14},{7,15},{8,16},{9,17... | collective-permute-start | bytes 3145736 | tf_op jit(solution)/shard_map/ppermute | solution.py:340
  12.8 29.7 %collective-permute-start.3 = (f32[64,16,256]{2,1,0:T(8,128)}, f32[64,16,256]{2,1,0:T(8,128)}, u32[]{:S(2)}, u32[]{:S(2)}) collective-permute-start(f32[64,16,256]{2,1,0:T(8,128)} %get-tuple-element.43.refs_0_), channel_id=1, source_target_pairs={{8,0},{9,1},{10,2},{11,3},{12,4},{13,5},{14,6},{15,7},{16,8},{17,9... | collective-permute-start | bytes 3145736 | tf_op jit(solution)/shard_map/ppermute | solution.py:340
  17.0 7.3 %collective-permute-start = (f32[8,64,128]{2,1,0:T(8,128)}, f32[8,64,128]{2,1,0:T(8,128)S(1)}, u32[]{:S(2)}, u32[]{:S(2)}) collective-permute-start(f32[8,64,128]{2,1,0:T(8,128)} %get-tuple-element.44), channel_id=1, source_target_pairs={{0,1},{1,2},{2,3},{3,4},{4,5},{5,6},{6,7},{8,9},{9,10},{10,11},{11... | collective-permute-start | bytes 786440 | tf_op jit(solution)/shard_map/ppermute | solution.py:340
  20.7 8.3 %collective-permute-start.1 = (f32[8,64,128]{2,1,0:T(8,128)}, f32[8,64,128]{2,1,0:T(8,128)}, u32[]{:S(2)}, u32[]{:S(2)}) collective-permute-start(f32[8,64,128]{2,1,0:T(8,128)} %get-tuple-element.45.refs_0_), channel_id=1, source_target_pairs={{1,0},{2,1},{3,2},{4,3},{5,4},{6,5},{7,6},{9,8},{10,9},{11,10},{12... | collective-permute-start | bytes 786440 | tf_op jit(solution)/shard_map/ppermute | solution.py:340
  30.7 11.8 %collective-permute-start.5 = (f32[8,16,256]{2,1,0:T(8,128)}, f32[8,16,256]{2,1,0:T(8,128)S(1)}, u32[]{:S(2)}, u32[]{:S(2)}) collective-permute-start(f32[8,16,256]{2,1,0:T(8,128)} %get-tuple-element.69), channel_id=1, source_target_pairs={{8,0},{9,1},{10,2},{11,3},{12,4},{13,5},{14,6},{15,7},{16,8},{17,9... | collective-permute-start | bytes 393224 | tf_op jit(solution)/shard_map/ppermute | solution.py:340
  33.2 9.3 %collective-permute-start.4 = (f32[8,16,256]{2,1,0:T(8,128)}, f32[8,16,256]{2,1,0:T(8,128)}, u32[]{:S(2)}, u32[]{:S(2)}) collective-permute-start(f32[8,16,256]{2,1,0:T(8,128)} %get-tuple-element.70), channel_id=1, source_target_pairs={{0,8},{1,9},{2,10},{3,11},{4,12},{5,13},{6,14},{7,15},{8,16},{9,17... | collective-permute-start | bytes 393224 | tf_op jit(solution)/shard_map/ppermute | solution.py:340
  42.5 43.8 %copy-start.2 = (f32[64,64,256]{2,1,0:T(8,128)S(1)}, f32[64,64,256]{2,1,0:T(8,128)}, u32[]{:S(2)}) copy-start(f32[64,64,256]{2,1,0:T(8,128)} %est_ref.5) | copy-start | bytes 12582916
  43.9 22.8 %collective-permute-start.7 = (f32[2,8,64,128]{3,2,1,0:T(8,128)S(1)}, f32[2,8,64,128]{3,2,1,0:T(8,128)S(1)}, u32[]{:S(2)}, u32[]{:S(2)}) collective-permute-start(f32[2,8,64,128]{3,2,1,0:T(8,128)S(1)} %get-tuple-element.49), channel_id=1, source_target_pairs={{0,0},{1,72},{2,32},{3,104},{4,64},{5,8},{6,96},{7,40},{8,16},{9,8... | collective-permute-start | bytes 1572872 | tf_op jit(solution)/shard_map/ppermute | solution.py:474
  47.8 26.9 %collective-permute-start.8 = (f32[2,8,64,128]{3,2,1,0:T(8,128)S(1)}, f32[2,8,64,128]{3,2,1,0:T(8,128)S(1)}, u32[]{:S(2)}, u32[]{:S(2)}) collective-permute-start(f32[2,8,64,128]{3,2,1,0:T(8,128)S(1)} %get-tuple-element.50), channel_id=1, source_target_pairs={{0,16},{1,88},{2,48},{3,120},{4,80},{5,24},{6,112},{7,56},{8,0},{9... | collective-permute-start | bytes 1572872 | tf_op jit(solution)/shard_map/ppermute | solution.py:474
  50.8 35.4 %collective-permute-start.9 = (f32[2,8,64,128]{3,2,1,0:T(8,128)S(1)}, f32[2,8,64,128]{3,2,1,0:T(8,128)S(1)}, u32[]{:S(2)}, u32[]{:S(2)}) collective-permute-start(f32[2,8,64,128]{3,2,1,0:T(8,128)S(1)} %get-tuple-element.51), channel_id=1, source_target_pairs={{0,32},{1,104},{2,64},{3,8},{4,96},{5,40},{6,0},{7,72},{8,48},{9,1... | collective-permute-start | bytes 1572872 | tf_op jit(solution)/shard_map/ppermute | solution.py:474
  55.1 44.5 %collective-permute-start.10 = (f32[2,8,64,128]{3,2,1,0:T(8,128)S(1)}, f32[2,8,64,128]{3,2,1,0:T(8,128)S(1)}, u32[]{:S(2)}, u32[]{:S(2)}) collective-permute-start(f32[2,8,64,128]{3,2,1,0:T(8,128)S(1)} %get-tuple-element.54), channel_id=1, source_target_pairs={{0,48},{1,120},{2,80},{3,24},{4,112},{5,56},{6,16},{7,88},{8,32},{... | collective-permute-start | bytes 1572872 | tf_op jit(solution)/shard_map/ppermute | solution.py:474
  57.7 41.8 %collective-permute-start.11 = (f32[2,8,64,128]{3,2,1,0:T(8,128)S(1)}, f32[2,8,64,128]{3,2,1,0:T(8,128)S(1)}, u32[]{:S(2)}, u32[]{:S(2)}) collective-permute-start(f32[2,8,64,128]{3,2,1,0:T(8,128)S(1)} %get-tuple-element.55), channel_id=1, source_target_pairs={{0,64},{1,8},{2,96},{3,40},{4,0},{5,72},{6,32},{7,104},{8,80},{9,2... | collective-permute-start | bytes 1572872 | tf_op jit(solution)/shard_map/ppermute | solution.py:474
  66.7 36.6 %collective-permute-start.12 = (f32[2,8,64,128]{3,2,1,0:T(8,128)S(1)}, f32[2,8,64,128]{3,2,1,0:T(8,128)S(1)}, u32[]{:S(2)}, u32[]{:S(2)}) collective-permute-start(f32[2,8,64,128]{3,2,1,0:T(8,128)S(1)} %get-tuple-element.56), channel_id=1, source_target_pairs={{0,80},{1,24},{2,112},{3,56},{4,16},{5,88},{6,48},{7,120},{8,64},{... | collective-permute-start | bytes 1572872 | tf_op jit(solution)/shard_map/ppermute | solution.py:474
  74.7 28.6 %collective-permute-start.13 = (f32[2,8,64,128]{3,2,1,0:T(8,128)S(1)}, f32[2,8,64,128]{3,2,1,0:T(8,128)S(1)}, u32[]{:S(2)}, u32[]{:S(2)}) collective-permute-start(f32[2,8,64,128]{3,2,1,0:T(8,128)S(1)} %get-tuple-element.57), channel_id=1, source_target_pairs={{0,96},{1,40},{2,0},{3,72},{4,32},{5,104},{6,64},{7,8},{8,112},{9,... | collective-permute-start | bytes 1572872 | tf_op jit(solution)/shard_map/ppermute | solution.py:474
  86.2 19.9 %collective-permute-start.14 = (f32[2,8,64,128]{3,2,1,0:T(8,128)S(1)}, f32[2,8,64,128]{3,2,1,0:T(8,128)S(1)}, u32[]{:S(2)}, u32[]{:S(2)}) collective-permute-start(f32[2,8,64,128]{3,2,1,0:T(8,128)S(1)} %get-tuple-element.58), channel_id=1, source_target_pairs={{0,112},{1,56},{2,16},{3,88},{4,48},{5,120},{6,80},{7,24},{8,96},{... | collective-permute-start | bytes 1572872 | tf_op jit(solution)/shard_map/ppermute | solution.py:474
  108.6 41.3 %collective-permute-start.19 = (f32[16,64,256]{2,1,0:T(8,128)S(1)}, f32[16,64,256]{2,1,0:T(8,128)S(1)}, u32[]{:S(2)}, u32[]{:S(2)}) collective-permute-start(f32[16,64,256]{2,1,0:T(8,128)S(1)} %get-tuple-element.61), channel_id=1, source_target_pairs={{0,8},{1,9},{2,10},{3,11},{4,12},{5,13},{6,14},{7,15},{8,16},{9,17... | collective-permute-start | bytes 3145736 | tf_op jit(solution)/shard_map/ppermute | solution.py:340
  112.4 37.6 %collective-permute-start.20 = (f32[16,64,256]{2,1,0:T(8,128)S(1)}, f32[16,64,256]{2,1,0:T(8,128)S(1)}, u32[]{:S(2)}, u32[]{:S(2)}) collective-permute-start(f32[16,64,256]{2,1,0:T(8,128)S(1)} %get-tuple-element.62), channel_id=1, source_target_pairs={{8,0},{9,1},{10,2},{11,3},{12,4},{13,5},{14,6},{15,7},{16,8},{17,9... | collective-permute-start | bytes 3145736 | tf_op jit(solution)/shard_map/ppermute | solution.py:340
  116.0 14.3 %collective-permute-start.15 = (f32[8,64,128]{2,1,0:T(8,128)S(1)}, f32[8,64,128]{2,1,0:T(8,128)S(1)}, u32[]{:S(2)}, u32[]{:S(2)}) collective-permute-start(f32[8,64,128]{2,1,0:T(8,128)S(1)} %get-tuple-element.59), channel_id=1, source_target_pairs={{0,1},{1,2},{2,3},{3,4},{4,5},{5,6},{6,7},{8,9},{9,10},{10,11},{11... | collective-permute-start | bytes 786440 | tf_op jit(solution)/shard_map/ppermute | solution.py:340
  126.9 8.0 %collective-permute-start.16 = (f32[8,64,128]{2,1,0:T(8,128)S(1)}, f32[8,64,128]{2,1,0:T(8,128)S(1)}, u32[]{:S(2)}, u32[]{:S(2)}) collective-permute-start(f32[8,64,128]{2,1,0:T(8,128)S(1)} %get-tuple-element.60), channel_id=1, source_target_pairs={{1,0},{2,1},{3,2},{4,3},{5,4},{6,5},{7,6},{9,8},{10,9},{11,10},{12... | collective-permute-start | bytes 786440 | tf_op jit(solution)/shard_map/ppermute | solution.py:340
  135.0 14.9 %collective-permute-start.18 = (f32[2,64,256]{2,1,0:T(8,128)S(1)}, f32[2,64,256]{2,1,0:T(8,128)S(1)}, u32[]{:S(2)}, u32[]{:S(2)}) collective-permute-start(f32[2,64,256]{2,1,0:T(8,128)S(1)} %get-tuple-element.67), channel_id=1, source_target_pairs={{8,0},{9,1},{10,2},{11,3},{12,4},{13,5},{14,6},{15,7},{16,8},{17,9... | collective-permute-start | bytes 393224 | tf_op jit(solution)/shard_map/ppermute | solution.py:340
  136.9 13.0 %collective-permute-start.17 = (f32[2,64,256]{2,1,0:T(8,128)S(1)}, f32[2,64,256]{2,1,0:T(8,128)S(1)}, u32[]{:S(2)}, u32[]{:S(2)}) collective-permute-start(f32[2,64,256]{2,1,0:T(8,128)S(1)} %get-tuple-element.68), channel_id=1, source_target_pairs={{0,8},{1,9},{2,10},{3,11},{4,12},{5,13},{6,14},{7,15},{8,16},{9,17... | collective-permute-start | bytes 393224 | tf_op jit(solution)/shard_map/ppermute | solution.py:340
  (5 other events, 42.5 us)
